TPU v7x, 32 devices: a whole 2x2x4 slice. The times are simulated.
32 devices in a mesh: fsdp: 8 (over z, x), ctx: 2 (over core), tp: 2 (over y).
Axes of the slice: x: 2, y: 2, z: 4, core: 2. Of those that a mesh axis runs over, the one named last changes fastest.
Arguments:
- tokens: bfloat16 [4096, 768], P(('fsdp', 'ctx')), may hold values from -6 to 6
- cotangent: bfloat16 [4096, 768], P(('fsdp', 'ctx')), may hold values from -6 to 6
- w_query: bfloat16 [768, 768], P(('fsdp', 'ctx'), 'tp'), may hold values from -0.25 to 0.25
- w_key: bfloat16 [768, 768], P(('fsdp', 'ctx'), 'tp'), may hold values from -0.25 to 0.25
- w_value: bfloat16 [768, 768], P(('fsdp', 'ctx'), 'tp'), may hold values from -0.21875 to 0.21875
- w_output: bfloat16 [768, 768], P(('fsdp', 'ctx'), 'tp'), may hold values from -2 to 2
- w_router: bfloat16 [768, 32], P(('fsdp', 'ctx')), may hold values from -0.25 to 0.25
- gain_attn: bfloat16 [768], P(('fsdp', 'ctx')), may hold values from 0.5 to 1.5
- gain_moe: bfloat16 [768], P(('fsdp', 'ctx')), may hold values from 0.5 to 1.5
- rel_table: float32 [32, 12], P(None, 'tp'), may hold values from -6 to 6
- w_in: bfloat16 [32, 768, 3072], P(('fsdp', 'ctx'), None, 'tp'), may hold values from -0.21875 to 0.21875
- w_out: bfloat16 [32, 3072, 768], P(('fsdp', 'ctx'), 'tp'), may hold values from -6 to 6
- lengths: int32 [8, 4], P('fsdp'), may hold values from 0 to 512, as said below
- routes: int32 [4096, 1], P(('fsdp', 'ctx')), may hold values from 0 to 31; in each aligned block of 256 rows (0 to 255, 256 to 511, ...) at most 10 rows name the same one
- keep_mask: int32 [4096], P(('fsdp', 'ctx')), may hold values 0 or 1
Outputs:
- result: float32 [4096, 768], P(('fsdp', 'ctx'))
- tokens_grad: float32 [4096, 768], P(('fsdp', 'ctx'))
- w_query_grad: float32 [768, 768], P(('fsdp', 'ctx'), 'tp')
- w_key_grad: float32 [768, 768], P(('fsdp', 'ctx'), 'tp')
- w_value_grad: float32 [768, 768], P(('fsdp', 'ctx'), 'tp')
- w_output_grad: float32 [768, 768], P(('fsdp', 'ctx'), 'tp')
- w_router_grad: float32 [768, 32], P(('fsdp', 'ctx'))
- gain_attn_grad: float32 [768], P(('fsdp', 'ctx'))
- gain_moe_grad: float32 [768], P(('fsdp', 'ctx'))
- rel_table_grad: float32 [32, 12], P(None, 'tp')
- w_in_grad: float32 [32, 768, 3072], P(('fsdp', 'ctx'), None, 'tp')
- w_out_grad: float32 [32, 3072, 768], P(('fsdp', 'ctx'), 'tp')
Inputs may be any that keep to these rules, and one draw needn't show every extreme that they name: `lengths`: each row sums to 512. In one row a single sequence fills the whole pack and the other entries are 0. `routes`: within the 256 tokens of one device, at most 10 name one expert, a bound that some block reaches.
All inputs are finite; a program needn't handle non-finite values. No bound on the sum of `keep_mask` on one device may be relied on, other than what follows from the above.
Results may differ from a plain program's by a relative error of at most 0.015.
The roundings to bfloat16 on the way count: a program that leaves them out, or rounds other values in their place, can miss the bound.
Values may be sent and summed in bfloat16 or wider, within the bound.
No kernel may reach another device: no remote copies, remote signals or barrier semaphores. Data moves between devices by JAX's collectives and lax.ppermute only.
A program may use at most 128 MiB of HBM per device.

v0:
```python
import jax
import jax.numpy as jnp
from jax import lax
from jax.sharding import PartitionSpec as P

epsilon = 1e-06
masked_value = -1e30
bucket_edges = (12, 16, 23, 32, 46, 64, 91)
highest = lax.Precision.HIGHEST


def bucket_index(offset):
    side = jnp.where(offset > 0, 16, 0).astype(jnp.int32)
    distance = jnp.abs(offset)
    far_bucket = 8 + sum(((distance >= edge).astype(jnp.int32) for edge in bucket_edges))
    return side + jnp.where(distance < 8, distance, far_bucket)


def rms_scale(values):
    return lax.rsqrt(jnp.mean(values * values, axis=-1, keepdims=True) + epsilon)


def matmul(left, right):
    return jnp.dot(left, right, preferred_element_type=jnp.float32)


def matmul_nt(left, right):
    return lax.dot_general(
        left, right, (((1,), (1,)), ((), ())), preferred_element_type=jnp.float32
    )


def matmul_tn(left, right):
    return lax.dot_general(
        left, right, (((0,), (0,)), ((), ())), preferred_element_type=jnp.float32
    )


def smooth(values):
    return jax.nn.gelu(values, approximate=True)


def norm_back(grad_normed, normed, scale):
    return scale * (grad_normed - normed * jnp.mean(grad_normed * normed, axis=-1, keepdims=True))


def offset_picks(first_place, block_rows, span_width, bucket_count):
    offsets = jnp.arange(span_width, dtype=jnp.int32) - (block_rows - 1) - first_place
    bucket = bucket_index(offsets)
    return (bucket[:, None] == jnp.arange(bucket_count, dtype=jnp.int32)[None, :]).astype(
        jnp.float32
    )


def body(
    tokens,
    cotangent,
    w_query,
    w_key,
    w_value,
    w_output,
    w_router,
    gain_attn,
    gain_moe,
    rel_table,
    w_in,
    w_out,
    lengths,
    routes,
    keep_mask,
):
    tok_rows = tokens.shape[0]
    model_width = tokens.shape[1]
    ctx_count = lax.axis_size("ctx")
    ctx_place = lax.axis_index("ctx")
    tp_count = lax.axis_size("tp")
    tp_place = lax.axis_index("tp")
    owners = lax.axis_size(("fsdp", "ctx"))
    group_rows = tok_rows * ctx_count
    experts = w_router.shape[1]
    capacity = max(2, (5 * tok_rows + 4 * experts - 1) // (4 * experts))
    local_pieces = w_in.shape[0]
    split_count = owners * local_pieces // experts
    part_width = model_width // tp_count
    heads_local = rel_table.shape[1]
    head_size = w_query.shape[1] // heads_local
    local_width = heads_local * head_size
    bucket_count = rel_table.shape[0]
    block_count = max(1, tok_rows // 512)
    block_rows = tok_rows // block_count
    span_width = group_rows + block_rows
    wq_full, wk_full, wv_full, wo_full, wr_full, gain_one, gain_two = (
        lax.all_gather(w_query, ("fsdp", "ctx"), axis=0, tiled=True),
        lax.all_gather(w_key, ("fsdp", "ctx"), axis=0, tiled=True),
        lax.all_gather(w_value, ("fsdp", "ctx"), axis=0, tiled=True),
        lax.all_gather(w_output, ("fsdp", "ctx"), axis=0, tiled=True),
        lax.all_gather(w_router, ("fsdp", "ctx"), axis=0, tiled=True),
        lax.all_gather(gain_attn, ("fsdp", "ctx"), axis=0, tiled=True),
        lax.all_gather(gain_moe, ("fsdp", "ctx"), axis=0, tiled=True),
    )
    gain_one = gain_one.astype(jnp.float32)
    gain_two = gain_two.astype(jnp.float32)
    inputs = tokens.astype(jnp.float32)
    seq_ends = jnp.cumsum(lengths[0])
    positions = jnp.arange(group_rows, dtype=jnp.int32)
    segment = jnp.sum((positions[:, None] >= seq_ends[None, :]).astype(jnp.int32), axis=1)
    own_first = ctx_place * tok_rows
    own_segment = lax.dynamic_slice_in_dim(segment, own_first, tok_rows)
    scale_one = rms_scale(inputs)
    normed_one = inputs * scale_one
    hidden_one = (normed_one * gain_one).astype(jnp.bfloat16)
    queries = matmul(hidden_one, wq_full).astype(jnp.bfloat16)
    keys_own = matmul(hidden_one, wk_full).astype(jnp.bfloat16)
    values_own = matmul(hidden_one, wv_full).astype(jnp.bfloat16)
    keys_all, values_all = (
        lax.all_gather(keys_own, "ctx", axis=0, tiled=True),
        lax.all_gather(values_own, "ctx", axis=0, tiled=True),
    )
    key_heads = keys_all.reshape(group_rows, heads_local, head_size)
    value_heads = values_all.reshape(group_rows, heads_local, head_size)

    def block_scores(query_block, segment_block, first_row):
        first_place = own_first + first_row
        bucket_picks = offset_picks(first_place, block_rows, span_width, bucket_count)
        offset_bias = jnp.dot(bucket_picks, rel_table, precision=highest).T
        repeated = jnp.tile(offset_bias, (1, block_rows))[:, : block_rows * (span_width - 1)]
        score_bias = repeated.reshape(heads_local, block_rows, span_width - 1)[
            :, :, block_rows - 1 : block_rows - 1 + group_rows
        ]
        query_heads = query_block.reshape(block_rows, heads_local, head_size)
        scores = (
            jnp.einsum("qhd,khd->hqk", query_heads, key_heads, preferred_element_type=jnp.float32)
            + score_bias
        )
        same_doc = segment_block[:, None] == segment[None, :]
        return (jnp.where(same_doc[None], scores, masked_value), bucket_picks, query_heads)

    def forward_block(block_inputs):
        query_block, segment_block, first_row = block_inputs
        scores, bucket_picks, query_heads = block_scores(query_block, segment_block, first_row)
        row_max = jnp.max(scores, axis=-1, keepdims=True)
        exponent = jnp.exp(scores - row_max)
        row_total = jnp.sum(exponent, axis=-1, keepdims=True)
        chances = (exponent / row_total).astype(jnp.bfloat16)
        mixed_rows = jnp.einsum(
            "hqk,khd->qhd", chances, value_heads, preferred_element_type=jnp.float32
        )
        return (
            mixed_rows.reshape(block_rows, local_width),
            (row_max + jnp.log(row_total))[:, :, 0],
        )

    starts = jnp.arange(block_count, dtype=jnp.int32) * block_rows
    query_blocks = queries.reshape(block_count, block_rows, local_width)
    segment_blocks = own_segment.reshape(block_count, block_rows)
    mixed_blocks, log_totals = lax.map(forward_block, (query_blocks, segment_blocks, starts))
    attended = mixed_blocks.reshape(tok_rows, local_width).astype(jnp.bfloat16)
    branch = lax.psum(matmul_nt(attended, wo_full), "tp")
    middle = inputs + branch
    scale_two = rms_scale(middle)
    normed_two = middle * scale_two
    hidden_two = (normed_two * gain_two).astype(jnp.bfloat16)
    logits = matmul(hidden_two, wr_full)
    router_probs = jax.nn.softmax(logits, axis=-1)
    expert_pick = routes[:, 0]
    expert_ids = jnp.arange(experts, dtype=jnp.int32)
    onehot = expert_pick[:, None] == expert_ids[None, :]
    kept_rows = keep_mask.astype(jnp.float32)
    gate_value = jnp.sum(jnp.where(onehot, router_probs, 0.0), axis=1) * kept_rows
    chosen = onehot.astype(jnp.int32) * keep_mask[:, None]
    earlier = jnp.sum((jnp.cumsum(chosen, axis=0) - chosen) * chosen, axis=1)
    slot_place = jnp.where(keep_mask == 1, expert_pick * capacity + earlier, experts * capacity)
    slot_total = experts * capacity

    def to_owner_rows(slot_box):
        pieces = jnp.repeat(slot_box, split_count, axis=0).reshape(
            owners, local_pieces, capacity, model_width
        )
        pieces = lax.dynamic_slice_in_dim(pieces, tp_place * part_width, part_width, 3)
        arrived = lax.all_to_all(pieces, ("fsdp", "ctx"), split_axis=0, concat_axis=2, tiled=True)
        arrived = lax.all_gather(arrived, "tp", axis=3, tiled=True)
        return arrived.reshape(local_pieces, owners * capacity, model_width)

    def to_token_rows(partial_value):
        tp_share = lax.psum_scatter(partial_value, "tp", scatter_dimension=2, tiled=True).astype(
            jnp.bfloat16
        )
        outgoing = tp_share.reshape(1, local_pieces, owners * capacity, tp_share.shape[2])
        returned = lax.all_to_all(
            outgoing, ("fsdp", "ctx"), split_axis=2, concat_axis=0, tiled=True
        )
        returned = lax.all_gather(returned, "tp", axis=3, tiled=True)
        summed = jnp.sum(
            returned.reshape(experts, split_count, capacity, model_width), axis=1, dtype=jnp.float32
        )
        return summed.reshape(slot_total, model_width)

    outbox = (
        jnp.zeros((slot_total, model_width), jnp.bfloat16)
        .at[slot_place]
        .set(hidden_two, mode="drop")
    )
    slot_rows = to_owner_rows(outbox.reshape(experts, capacity, model_width))
    pre_act = jnp.einsum("lrd,ldf->lrf", slot_rows, w_in, preferred_element_type=jnp.float32)
    activity = smooth(pre_act).astype(jnp.bfloat16)
    expert_part = jnp.einsum("lrf,lfd->lrd", activity, w_out, preferred_element_type=jnp.float32)
    expert_rows = to_token_rows(expert_part)
    picked = jnp.take(expert_rows, slot_place, axis=0, mode="fill", fill_value=0.0)
    result = middle + gate_value[:, None] * picked
    upstream = cotangent.astype(jnp.float32)
    gate_grad = jnp.sum(upstream * picked, axis=1)
    moe_grad = (gate_value[:, None] * upstream).astype(jnp.bfloat16)
    grad_box = (
        jnp.zeros((slot_total, model_width), jnp.bfloat16).at[slot_place].set(moe_grad, mode="drop")
    )
    out_grad = to_owner_rows(grad_box.reshape(experts, capacity, model_width))
    w_out_grad = jnp.einsum("lrf,lrd->lfd", activity, out_grad, preferred_element_type=jnp.float32)
    act_grad = jnp.einsum("lrd,lfd->lrf", out_grad, w_out, preferred_element_type=jnp.float32)
    gelu_back = jax.vjp(smooth, pre_act)[1]
    pre_grad = gelu_back(act_grad)[0].astype(jnp.bfloat16)
    w_in_grad = jnp.einsum("lrd,lrf->ldf", slot_rows, pre_grad, preferred_element_type=jnp.float32)
    slot_grad = to_token_rows(
        jnp.einsum("lrf,ldf->lrd", pre_grad, w_in, preferred_element_type=jnp.float32)
    )
    hidden_two_grad = jnp.take(slot_grad, slot_place, axis=0, mode="fill", fill_value=0.0)
    prob_grad = jnp.where(onehot, (gate_grad * kept_rows)[:, None], 0.0)
    logit_grad = (
        router_probs * (prob_grad - jnp.sum(router_probs * prob_grad, axis=1, keepdims=True))
    ).astype(jnp.bfloat16)
    router_grad = matmul_tn(hidden_two, logit_grad)
    hidden_two_grad = hidden_two_grad + matmul_nt(logit_grad, wr_full)
    gain_two_grad = jnp.sum(hidden_two_grad * normed_two, axis=0)
    middle_grad = upstream + norm_back(hidden_two_grad * gain_two, normed_two, scale_two)
    branch_grad = middle_grad.astype(jnp.bfloat16)
    output_weight_grad = matmul_tn(branch_grad, attended)
    attended_grad = matmul(branch_grad, wo_full).astype(jnp.bfloat16)

    def backward_block(carry, block_inputs):
        key_acc, value_acc, table_acc = carry
        query_block, grad_block, total_block, segment_block, first_row = block_inputs
        scores, bucket_picks, query_heads = block_scores(query_block, segment_block, first_row)
        chances = jnp.exp(scores - total_block[:, :, None])
        grad_heads = grad_block.reshape(block_rows, heads_local, head_size)
        value_acc = value_acc + jnp.einsum(
            "hqk,qhd->khd",
            chances.astype(jnp.bfloat16),
            grad_heads,
            preferred_element_type=jnp.float32,
        )
        chance_grad = jnp.einsum(
            "qhd,khd->hqk", grad_heads, value_heads, preferred_element_type=jnp.float32
        )
        score_grad = (
            chances * (chance_grad - jnp.sum(chances * chance_grad, axis=-1, keepdims=True))
        ).astype(jnp.bfloat16)
        query_grad = jnp.einsum(
            "hqk,khd->qhd", score_grad, key_heads, preferred_element_type=jnp.float32
        )
        key_acc = key_acc + jnp.einsum(
            "hqk,qhd->khd", score_grad, query_heads, preferred_element_type=jnp.float32
        )
        shifted = jnp.pad(score_grad, ((0, 0), (0, 0), (block_rows - 1, 0)))
        flattened = jnp.pad(
            shifted.reshape(heads_local, block_rows * (span_width - 1)), ((0, 0), (0, block_rows))
        )
        diagonal = jnp.sum(
            flattened.reshape(heads_local, block_rows, span_width), axis=1, dtype=jnp.float32
        )
        table_acc = table_acc + jnp.dot(diagonal, bucket_picks, precision=highest)
        return ((key_acc, value_acc, table_acc), query_grad.reshape(block_rows, local_width))

    zero_keys = jnp.zeros((group_rows, heads_local, head_size), jnp.float32)
    zero_table = jnp.zeros((heads_local, bucket_count), jnp.float32)
    grad_blocks = attended_grad.reshape(block_count, block_rows, local_width)
    carried, query_grads = lax.scan(
        backward_block,
        (zero_keys, zero_keys, zero_table),
        (query_blocks, grad_blocks, log_totals, segment_blocks, starts),
    )
    key_grad_all, value_grad_all, table_grad = carried
    key_grad, value_grad = (
        lax.psum_scatter(
            key_grad_all.reshape(group_rows, local_width), "ctx", scatter_dimension=0, tiled=True
        ),
        lax.psum_scatter(
            value_grad_all.reshape(group_rows, local_width), "ctx", scatter_dimension=0, tiled=True
        ),
    )
    query_grad = query_grads.reshape(tok_rows, local_width).astype(jnp.bfloat16)
    key_grad = key_grad.astype(jnp.bfloat16)
    value_grad = value_grad.astype(jnp.bfloat16)
    query_weight_grad = matmul_tn(hidden_one, query_grad)
    key_weight_grad = matmul_tn(hidden_one, key_grad)
    value_weight_grad = matmul_tn(hidden_one, value_grad)
    hidden_one_part = (
        matmul_nt(query_grad, wq_full)
        + matmul_nt(key_grad, wk_full)
        + matmul_nt(value_grad, wv_full)
    )
    hidden_one_grad = lax.psum(hidden_one_part, "tp")
    gain_one_grad = jnp.sum(hidden_one_grad * normed_one, axis=0)
    input_grad = middle_grad + norm_back(hidden_one_grad * gain_one, normed_one, scale_one)
    shards = (
        lax.psum_scatter(query_weight_grad, ("fsdp", "ctx"), scatter_dimension=0, tiled=True),
        lax.psum_scatter(key_weight_grad, ("fsdp", "ctx"), scatter_dimension=0, tiled=True),
        lax.psum_scatter(value_weight_grad, ("fsdp", "ctx"), scatter_dimension=0, tiled=True),
        lax.psum_scatter(output_weight_grad, ("fsdp", "ctx"), scatter_dimension=0, tiled=True),
        lax.psum_scatter(router_grad, ("fsdp", "ctx"), scatter_dimension=0, tiled=True),
        lax.psum_scatter(gain_one_grad, ("fsdp", "ctx"), scatter_dimension=0, tiled=True),
        lax.psum_scatter(gain_two_grad, ("fsdp", "ctx"), scatter_dimension=0, tiled=True),
    )
    table_total = lax.psum(table_grad.T, ("fsdp", "ctx"))
    return (
        result,
        input_grad,
        shards[0],
        shards[1],
        shards[2],
        shards[3],
        shards[4],
        shards[5],
        shards[6],
        table_total,
        w_in_grad,
        w_out_grad,
    )


def solution(mesh):
    in_specs = (
        P(("fsdp", "ctx"), None),
        P(("fsdp", "ctx"), None),
        P(("fsdp", "ctx"), "tp"),
        P(("fsdp", "ctx"), "tp"),
        P(("fsdp", "ctx"), "tp"),
        P(("fsdp", "ctx"), "tp"),
        P(("fsdp", "ctx"), None),
        P(("fsdp", "ctx")),
        P(("fsdp", "ctx")),
        P(None, "tp"),
        P(("fsdp", "ctx"), None, "tp"),
        P(("fsdp", "ctx"), "tp", None),
        P("fsdp", None),
        P(("fsdp", "ctx"), None),
        P(("fsdp", "ctx")),
    )
    out_specs = (
        P(("fsdp", "ctx"), None),
        P(("fsdp", "ctx"), None),
        P(("fsdp", "ctx"), "tp"),
        P(("fsdp", "ctx"), "tp"),
        P(("fsdp", "ctx"), "tp"),
        P(("fsdp", "ctx"), "tp"),
        P(("fsdp", "ctx"), None),
        P(("fsdp", "ctx")),
        P(("fsdp", "ctx")),
        P(None, "tp"),
        P(("fsdp", "ctx"), None, "tp"),
        P(("fsdp", "ctx"), "tp", None),
    )
    return jax.shard_map(body, mesh=mesh, in_specs=in_specs, out_specs=out_specs, check_vma=False)
```

profile of v0, /device:TPU:0, one launch (start us, length us, event | category | flops | bytes accessed | tf_op | source)
XLA Modules:
  0.0 767.5 jit_solution(2999854586908157875)
XLA Ops:
  13.1 35.5 %all-reduce.7 = (bf16[768]{0:T(1024)(128)(2,1)S(1)}, bf16[768]{0:T(1024)(128)(2,1)}) all-reduce(bf16[768]{0:T(1024)(128)(2,1)S(1)} %dynamic-update-slice, bf16[768]{0:T(1024)(128)(2,1)S(1)} %dynamic-update-slice.1), channel_id=1, replica_groups=mesh['fsdp'=8,'ctx'=2,'tp'=2] {'fsdp','ctx'}, use_global_device_ids=true, to_apply=%add.2 | all-reduce | flops 1536 | bytes 6144
  49.4 19.2 %all_gather.42 = bf16[768,384]{1,0:T(8,128)(2,1)S(1)} all-gather(bf16[48,384]{1,0:T(8,128)(2,1)} %param.19), channel_id=1, replica_groups=mesh['fsdp'=8,'ctx'=2,'tp'=2] {'fsdp','ctx'}, dimensions={0}, use_global_device_ids=true | all-gather | bytes 626688 | tf_op jit(solution)/shard_map/all_gather | solution.py:93
  71.6 20.6 %all_gather.43 = bf16[768,384]{1,0:T(8,128)(2,1)S(1)} all-gather(bf16[48,384]{1,0:T(8,128)(2,1)S(1)} %copy-done.37), channel_id=1, replica_groups=mesh['fsdp'=8,'ctx'=2,'tp'=2] {'fsdp','ctx'}, dimensions={0}, use_global_device_ids=true | all-gather | bytes 626688 | tf_op jit(solution)/shard_map/all_gather | solution.py:94
  93.5 2.1 all_gather.44
  96.5 19.0 %all_gather.40 = bf16[768,384]{1,0:T(8,128)(2,1)S(1)} all-gather(bf16[48,384]{1,0:T(8,128)(2,1)S(1)} %copy-done.38), channel_id=1, replica_groups=mesh['fsdp'=8,'ctx'=2,'tp'=2] {'fsdp','ctx'}, dimensions={0}, use_global_device_ids=true | all-gather | bytes 626688 | tf_op jit(solution)/shard_map/all_gather | solution.py:95
  116.8 2.1 all_gather.41
  119.9 22.0 %all_gather.45 = bf16[768,384]{1,0:T(8,128)(2,1)} all-gather(bf16[48,384]{1,0:T(8,128)(2,1)S(1)} %copy-done.39), channel_id=1, replica_groups=mesh['fsdp'=8,'ctx'=2,'tp'=2] {'fsdp','ctx'}, dimensions={0}, use_global_device_ids=true | all-gather | bytes 626688 | tf_op jit(solution)/shard_map/all_gather | solution.py:96
  142.6 2.8 copy.99
  145.4 2.9 slice.26
  148.4 10.2 %reshape.283 = f32[6,256,767]{2,1,0:T(8,128)} reshape(f32[6,196352]{1,0:T(8,128)} %slice.26) | data formatting | bytes 9424896 | tf_op jit(solution)/shard_map/while/body/eval_jaxpr/reshape | solution.py:127
  158.5 3.7 fusion.87
  168.0 1.9 reduce-window.19
  169.9 1.5 slice_reduce_fusion
  175.4 22.8 %all-reduce.11.cloned.1.call-done = f32[256,768]{1,0:T(8,128)} async-done(((f32[256,768]{1,0:T(8,128)}), f32[256,768]{1,0:T(8,128)}) %all-reduce.11.cloned.1.call-update) | async-done | bytes 786448 | tf_op jit(solution)/shard_map/psum | solution.py:158
  198.2 2.1 multiply_reduce_fusion.3
  200.4 3.1 scatter_custom_fusion
  203.4 2.0 reshape_reshape_broadcast_in_dim_reshape.6
  206.7 15.2 %all_to_all.72 = bf16[16,2,10,384]{3,1,2,0:T(2,128)(2,1)S(1)} all-to-all(bf16[16,2,10,384]{3,1,2,0:T(2,128)(2,1)S(1)} %copy.85), channel_id=1, replica_groups=mesh['fsdp'=8,'ctx'=2,'tp'=2] {'fsdp','ctx'}, dimensions={0} | all-to-all | bytes 491520 | tf_op jit(solution)/shard_map/all_to_all | solution.py:180
  221.9 8.5 %all_gather.48 = bf16[1,2,160,768]{3,2,1,0:T(8,128)(2,1)S(1)} all-gather(bf16[1,2,160,384]{3,2,1,0:T(8,128)(2,1)S(1)} %copy.86), channel_id=1, replica_groups=mesh['fsdp'=8,'ctx'=2,'tp'=2] {'tp'}, dimensions={3}, use_global_device_ids=true | all-gather | bytes 737280 | tf_op jit(solution)/shard_map/all_gather | solution.py:181
  231.3 3.3 fusion.36
  235.9 2.1 fusion.78
  238.0 19.5 %all-gather.2 = bf16[16,48,32]{1,2,0:T(8,128)(2,1)S(1)} all-gather(bf16[1,48,32]{1,2,0:T(8,128)(2,1)} %bitcast.149), channel_id=1, replica_groups=mesh['fsdp'=8,'ctx'=2,'tp'=2] {'fsdp','ctx'}, dimensions={0}, use_global_device_ids=true | all-gather | bytes 52224 | tf_op jit(solution)/shard_map/all_gather | solution.py:97
  258.2 1.7 reshape.345
  263.1 4.2 all-to-all-start.1
  271.6 5.5 all-to-all-done.1
  278.0 8.4 %all-gather = bf16[16,1,2,10,768]{4,0,3,2,1:T(8,128)(2,1)S(1)} all-gather(bf16[16,1,2,10,384]{4,0,3,2,1:T(8,128)(2,1)S(1)} %bitcast.137), channel_id=2, replica_groups=mesh['fsdp'=8,'ctx'=2,'tp'=2] {'tp'}, dimensions={4}, use_global_device_ids=true | all-gather | bytes 737280 | tf_op jit(solution)/shard_map/all_gather | solution.py:192
  287.8 2.4 reshape.293
  290.2 3.6 gather_fusion
  293.8 1.5 fusion.27
  298.1 2.9 scatter_custom_fusion.1
  301.0 2.0 reshape_reshape_broadcast_in_dim_reshape.7
  304.4 13.0 %all_to_all.73 = bf16[16,2,10,384]{3,1,2,0:T(2,128)(2,1)S(1)} all-to-all(bf16[16,2,10,384]{3,1,2,0:T(2,128)(2,1)S(1)} %copy.90), channel_id=1, replica_groups=mesh['fsdp'=8,'ctx'=2,'tp'=2] {'fsdp','ctx'}, dimensions={0} | all-to-all | bytes 491520 | tf_op jit(solution)/shard_map/all_to_all | solution.py:180
  317.5 8.8 %all_gather.50 = bf16[1,2,160,768]{3,2,1,0:T(8,128)(2,1)S(1)} all-gather(bf16[1,2,160,384]{3,2,1,0:T(8,128)(2,1)S(1)} %copy.91), channel_id=1, replica_groups=mesh['fsdp'=8,'ctx'=2,'tp'=2] {'tp'}, dimensions={3}, use_global_device_ids=true | all-gather | bytes 737280 | tf_op jit(solution)/shard_map/all_gather | solution.py:181
  326.4 4.7 fusion.9
  332.0 2.6 fusion.90
  334.7 17.4 %reduce-scatter.14.cloned.1.call-done = f32[2,160,384]{2,1,0:T(8,128)} async-done(((f32[2,160,768]{2,1,0:T(8,128)}), f32[2,160,384]{2,1,0:T(8,128)}) %reduce-scatter.14.cloned.1.call-update) | async-done | bytes 491536 | tf_op jit(solution)/shard_map/reduce_scatter | solution.py:185
  354.0 5.6 all-to-all-start.3
  360.4 9.1 %all-to-all-done.3 = bf16[1,2,160,384]{3,1,0,2:T(2,128)(2,1)} async-done(((bf16[1,2,160,384]{3,1,0,2:T(2,128)(2,1)}), bf16[1,2,160,384]{3,1,0,2:T(2,128)(2,1)}, u32[]{:S(2)}, u32[]{:S(2)}) %all-to-all-start.3) | async-done | bytes 245792 | tf_op jit(solution)/shard_map/all_to_all | solution.py:189
  370.5 8.4 %all-gather.1 = bf16[16,1,2,10,768]{4,0,3,2,1:T(8,128)(2,1)S(1)} all-gather(bf16[16,1,2,10,384]{4,0,3,2,1:T(8,128)(2,1)S(1)} %bitcast.139), channel_id=3, replica_groups=mesh['fsdp'=8,'ctx'=2,'tp'=2] {'tp'}, dimensions={4}, use_global_device_ids=true | all-gather | bytes 737280 | tf_op jit(solution)/shard_map/all_gather | solution.py:192
  380.2 2.5 reshape.294
  382.7 3.6 gather_fusion.1
  386.3 2.6 multiply_reduce_fusion.1
  392.1 1.7 copy.95
  393.8 2.2 multiply_reduce_fusion
  399.4 2.5 fusion.10
  402.0 2.3 fusion.73
  406.5 2.3 convolution_add_fusion.1
  408.8 8.0 %reduce-scatter.18.cloned.1.call-done = f32[256,384]{0,1:T(8,128)} async-done(((f32[512,384]{0,1:T(8,128)}), f32[256,384]{0,1:T(8,128)}) %reduce-scatter.18.cloned.1.call-update) | async-done | bytes 393232 | tf_op jit(solution)/shard_map/reduce_scatter | solution.py:285
  416.8 2.8 convolution_add_fusion
  422.8 2.7 fusion.50
  426.3 51.0 %reduce-scatter.28.cloned.1.call-done = f32[48,32]{1,0:T(8,128)} async-done(((f32[768,32]{1,0:T(8,128)}), f32[48,32]{1,0:T(8,128)}) %reduce-scatter.28.cloned.1.call-update) | async-done | bytes 6160
  478.8 6.5 fusion.34
  485.3 5.3 fusion.28
  490.6 2.3 pad.10
  492.9 6.0 reshape.363
  498.9 5.8 reshape.292
  504.7 1.5 fusion.53
  506.3 2.2 pad_convert_fusion
  510.1 3.0 all-reduce.13.cloned.1.call-done
  514.5 61.3 %all-reduce.6 = (f32[768]{0:T(1024)S(1)}, f32[768]{0:T(1024)S(1)}, f32[32,6]{0,1:T(8,128)}) all-reduce(f32[768]{0:T(1024)S(1)} %get-tuple-element.73, f32[768]{0:T(1024)S(1)} %copy-done.45, f32[32,6]{0,1:T(8,128)S(1)} %fusion.41), channel_id=13, replica_groups=mesh['fsdp'=8,'ctx'=2,'tp'=2] {'fsdp','ctx'}, use_global_device_ids=true, to_apply=%region_31.33.clone | all-reduce | flops 1728 | bytes 13824
  577.0 2.3 fusion.23
  579.3 58.2 %reduce-scatter.20.cloned.1.call-done = f32[48,384]{1,0:T(8,128)} async-done(((f32[768,384]{1,0:T(8,128)}), f32[48,384]{1,0:T(8,128)}) %reduce-scatter.20.cloned.1.call-update) | async-done | bytes 73744 | tf_op jit(solution)/shard_map/reduce_scatter | solution.py:304
  637.5 61.5 %reduce-scatter.24.cloned.1.call-done = f32[48,384]{1,0:T(8,128)} async-done(((f32[768,384]{1,0:T(8,128)}), f32[48,384]{1,0:T(8,128)}) %reduce-scatter.24.cloned.1.call-update) | async-done | bytes 73744 | tf_op jit(solution)/shard_map/reduce_scatter | solution.py:306
  699.0 61.8 %reduce-scatter.22.cloned.1.call-done = f32[48,384]{1,0:T(8,128)} async-done(((f32[768,384]{1,0:T(8,128)}), f32[48,384]{1,0:T(8,128)}) %reduce-scatter.22.cloned.1.call-update) | async-done | bytes 73744 | tf_op jit(solution)/shard_map/reduce_scatter | solution.py:305
  (209 shorter events, 65.7 us)
Async XLA Ops:
  7.2 134.7 %copy-start = (f32[32,6]{0,1:T(8,128)S(1)}, f32[32,6]{0,1:T(8,128)}, u32[]{:S(2)}) copy-start(f32[32,6]{0,1:T(8,128)} %param.26) | copy-start | bytes 2308
  7.2 85.8 %copy-start.5 = (bf16[256,768]{1,0:T(8,128)(2,1)S(1)}, bf16[256,768]{1,0:T(8,128)(2,1)}, u32[]{:S(2)}) copy-start(bf16[256,768]{1,0:T(8,128)(2,1)} %param.17) | copy-start | bytes 1179652
  7.2 64.4 %copy-start.37 = (bf16[48,384]{1,0:T(8,128)(2,1)S(1)}, bf16[48,384]{1,0:T(8,128)(2,1)}, u32[]{:S(2)}) copy-start(bf16[48,384]{1,0:T(8,128)(2,1)} %param.20) | copy-start | bytes 110596
  7.2 191.0 %all-reduce.11.cloned.1.call-start = ((), (), s32[]{:S(2)}) async-start(), calls=%async_computation.13 | async-start | bytes 1572864 | tf_op jit(solution)/shard_map/psum | solution.py:158
  7.3 134.5 %copy-start.50 = (s32[768]{0:T(1024)}, s32[768]{0:T(1024)S(1)}, u32[]{:S(2)}) copy-start(s32[768]{0:T(1024)S(1)} %fusion.63) | copy-start | bytes 9220
  9.3 106.3 %copy-start.33 = (f32[256]{0:T(256)}, f32[256]{0:T(256)S(1)}, u32[]{:S(2)}) copy-start(f32[256]{0:T(256)S(1)} %add_rsqrt_fusion.1) | copy-start | bytes 3076
  70.8 25.7 %copy-start.38 = (bf16[48,384]{1,0:T(8,128)(2,1)S(1)}, bf16[48,384]{1,0:T(8,128)(2,1)}, u32[]{:S(2)}) copy-start(bf16[48,384]{1,0:T(8,128)(2,1)} %param.21) | copy-start | bytes 110596
  92.2 0.8 copy-start.21
  95.6 24.3 %copy-start.39 = (bf16[48,384]{1,0:T(8,128)(2,1)S(1)}, bf16[48,384]{1,0:T(8,128)(2,1)}, u32[]{:S(2)}) copy-start(bf16[48,384]{1,0:T(8,128)(2,1)} %param.22) | copy-start | bytes 110596
  115.6 0.8 copy-start.20
  162.3 2.2 copy-start.32
  162.3 1.0 copy-start.28
  163.2 1.3 copy-start.40
  163.3 1.9 copy-start.14
  164.5 3.0 copy-start.35
  164.5 3.0 copy-start.42
  166.4 94.7 %reduce-scatter.12.cloned.1.call-start = ((), (), s32[]{:S(2)}) async-start(), calls=%async_computation.14 | async-start | bytes 1474560 | tf_op jit(solution)/shard_map/reduce_scatter | solution.py:185
  200.4 67.0 %copy-start.43 = (f32[256]{0:T(256)}, f32[256]{0:T(256)S(1)}, u32[]{:S(2)}) copy-start(f32[256]{0:T(256)S(1)} %add_rsqrt_fusion) | copy-start | bytes 3076
  221.9 14.0 %slice-start.2 = ((s8[4718592]{0:T(1024)(128)(4,1)}), s8[4194304]{0:T(1024)(128)(4,1)S(1)}, s32[]{:S(2)}) async-start(s8[4718592]{0:T(1024)(128)(4,1)} %bitcast.151), calls=%async_computation.26 | async-start | bytes 8388608
  231.3 4.6 slice-start.3
  234.6 1.3 copy-start.6
  263.1 14.0 %all-to-all-start.1 = ((bf16[1,2,160,384]{3,1,0,2:T(2,128)(2,1)}), bf16[1,2,160,384]{3,1,0,2:T(2,128)(2,1)}, u32[]{:S(2)}, u32[]{:S(2)}) async-start(bf16[1,2,160,384]{3,1,0,2:T(2,128)(2,1)} %copy.87), calls=%async_computation.2 | async-start | bytes 491520 | tf_op jit(solution)/shard_map/all_to_all | solution.py:189
  267.3 84.8 %reduce-scatter.14.cloned.1.call-start = ((), (), s32[]{:S(2)}) async-start(), calls=%async_computation.15 | async-start | bytes 1474560 | tf_op jit(solution)/shard_map/reduce_scatter | solution.py:185
  270.4 25.6 %copy-start.41 = (f32[256]{0:T(256)}, f32[256]{0:T(256)S(1)}, u32[]{:S(2)}) copy-start(f32[256]{0:T(256)S(1)} %get-tuple-element.106) | copy-start | bytes 3076
  296.0 1.4 copy-start.46
  298.1 19.4 %copy-start.47 = (f32[256]{0:T(256)}, f32[256]{0:T(256)S(1)}, u32[]{:S(2)}) copy-start(f32[256]{0:T(256)S(1)} %convert_multiply_fusion.5) | copy-start | bytes 3076
  303.1 23.3 %copy-start.7 = (f32[2,160,1536]{2,1,0:T(8,128)S(1)}, f32[2,160,1536]{2,1,0:T(8,128)}, u32[]{:S(2)}) copy-start(f32[2,160,1536]{2,1,0:T(8,128)} %copy-done.6) | copy-start | bytes 5898244
  304.4 27.6 %slice-start = ((s8[4718592]{0:T(1024)(128)(4,1)}), s8[4194304]{0:T(1024)(128)(4,1)S(1)}, s32[]{:S(2)}) async-start(s8[4718592]{0:T(1024)(128)(4,1)} %bitcast.120), calls=%async_computation.24 | async-start | bytes 8388608
  326.4 4.7 copy-start.24
  326.4 5.7 slice-start.1
  331.1 1.0 copy-start.16
  354.0 15.5 %all-to-all-start.3 = ((bf16[1,2,160,384]{3,1,0,2:T(2,128)(2,1)}), bf16[1,2,160,384]{3,1,0,2:T(2,128)(2,1)}, u32[]{:S(2)}, u32[]{:S(2)}) async-start(bf16[1,2,160,384]{3,1,0,2:T(2,128)(2,1)} %copy.92), calls=%async_computation.5 | async-start | bytes 491520 | tf_op jit(solution)/shard_map/all_to_all | solution.py:189
  359.6 46.8 %reduce-scatter.16.cloned.1.call-start = ((), (), s32[]{:S(2)}) async-start(), calls=%async_computation.16 | async-start | bytes 1179648 | tf_op jit(solution)/shard_map/reduce_scatter | solution.py:282
  386.3 2.6 copy-start.4
  386.3 2.6 copy-start.13
  386.3 2.6 copy-start.18
  386.3 2.6 copy-start.44
  386.3 2.6 copy-start.48
  386.3 2.6 copy-start.49
  389.0 2.1 copy-start.15
  390.2 0.9 copy-start.11
  396.0 2.0 copy-start.26
  396.8 1.1 copy-start.2
  399.3 2.6 copy-start.36
  399.3 17.5 %reduce-scatter.18.cloned.1.call-start = ((), (), s32[]{:S(2)}) async-start(), calls=%async_computation.17 | async-start | bytes 1179648 | tf_op jit(solution)/shard_map/reduce_scatter | solution.py:285
  401.9 2.5 copy-start.3
  401.9 2.5 copy-start.19
  401.9 75.5 %reduce-scatter.28.cloned.1.call-start = ((), (), s32[]{:S(2)}) async-start(), calls=%async_computation.23 | async-start | bytes 417792
  404.3 2.2 copy-start.22
  404.3 108.7 %all-reduce.13.cloned.1.call-start = ((), (), s32[]{:S(2)}) async-start(), calls=%async_computation.18 | async-start | bytes 1572864 | tf_op jit(solution)/shard_map/psum | solution.py:300
  408.8 10.9 %copy-start.12 = (f32[256,768]{1,0:T(8,128)S(1)}, f32[256,768]{1,0:T(8,128)}, u32[]{:S(2)}) copy-start(f32[256,768]{1,0:T(8,128)} %copy-done.11) | copy-start | bytes 2359300
  408.8 10.9 %copy-start.31 = (bf16[6,64,256]{2,1,0:T(8,128)(2,1)S(1)}, bf16[6,64,256]{2,1,0:T(8,128)(2,1)}, u32[]{:S(2)}) copy-start(bf16[6,64,256]{2,1,0:T(8,128)(2,1)} %copy-done.30) | copy-start | bytes 589828
  419.6 1.6 copy-start.34
  419.6 159.7 %reduce-scatter.26.cloned.1.call-start = ((), (), s32[]{:S(2)}) async-start(), calls=%async_computation.22 | async-start | bytes 1253376 | tf_op jit(solution)/shard_map/reduce_scatter | solution.py:307
  421.2 216.3 %reduce-scatter.20.cloned.1.call-start = ((), (), s32[]{:S(2)}) async-start(), calls=%async_computation.19 | async-start | bytes 1253376 | tf_op jit(solution)/shard_map/reduce_scatter | solution.py:304
  422.7 56.0 %copy-start.10 = (bf16[1,2,160,768]{3,2,1,0:T(8,128)(2,1)S(1)}, bf16[1,2,160,768]{3,2,1,0:T(8,128)(2,1)}, u32[]{:S(2)}) copy-start(bf16[1,2,160,768]{3,2,1,0:T(8,128)(2,1)} %copy-done.9) | copy-start | bytes 1474564
  422.7 276.2 %reduce-scatter.24.cloned.1.call-start = ((), (), s32[]{:S(2)}) async-start(), calls=%async_computation.21 | async-start | bytes 1253376 | tf_op jit(solution)/shard_map/reduce_scatter | solution.py:306
  425.5 335.3 %reduce-scatter.22.cloned.1.call-start = ((), (), s32[]{:S(2)}) async-start(), calls=%async_computation.20 | async-start | bytes 1253376 | tf_op jit(solution)/shard_map/reduce_scatter | solution.py:305
  478.8 6.5 copy-start.8
  478.8 6.5 copy-start.25
  498.9 5.8 copy-start.27
  508.4 1.3 copy-start.51
  508.5 6.1 copy-start.45
  509.7 251.0 %copy-start.1 = (f32[32,6]{0,1:T(8,128)S(1)}, f32[32,6]{0,1:T(8,128)}, u32[]{:S(2)}) copy-start(f32[32,6]{0,1:T(8,128)} %param.26) | copy-start | bytes 2308
  (5 other events, 3.6 us)
Sparse Core Ops, SparseCore 0:
  166.5 31.6 all-reduce.10
  238.1 17.2 reduce-scatter.11
  334.8 17.2 reduce-scatter.13
  399.4 5.8 reduce-scatter.15
  407.4 9.3 reduce-scatter.17
  420.6 56.7 reduce-scatter.27
  479.6 33.3 all-reduce.12
  517.7 58.1 reduce-scatter.25
  580.5 56.9 reduce-scatter.19
  642.0 56.9 reduce-scatter.23
  703.6 57.1 reduce-scatter.21
where the time goes:
time: 773 us; the launch traced here: 767 us
  waiting for transfers between devices  298 us (39%)
  blocking collectives  264 us (34%)
  local copies, waits for them, and re-layouts  80.7 us (10%)
  matrix products  60.8 us (8%)
  other arithmetic  37.2 us (5%)
  between operations  16 us (2%)
  starting transfers between devices  10.7 us (1%)
    unnamed x2, blocking collectives  96.8 us
    reduce_scatter x1, waiting for transfers between devices, body(): lax.psum_scatter(key_weight_grad, ('fsdp', 'ctx'), scatter_dimension=0, t...  61.8 us
    reduce_scatter x1, waiting for transfers between devices, body(): lax.psum_scatter(value_weight_grad, ('fsdp', 'ctx'), scatter_dimension=0,...  61.5 us
    reduce_scatter x1, waiting for transfers between devices, body(): lax.psum_scatter(query_weight_grad, ('fsdp', 'ctx'), scatter_dimension=0,...  58.2 us
    unnamed x12, waiting for transfers between devices  51.2 us
    all_to_all x2, blocking collectives, to_owner_rows(): lax.all_to_all(pieces, ('fsdp', 'ctx'), split_axis=0, concat_axis=2, tile...  28.2 us
    unnamed x124, local copies, waits for them, and re-layouts  26.3 us
    psum x1, waiting for transfers between devices, body(): branch = lax.psum(matmul_nt(attended, wo_full), 'tp')  22.8 us
  transfers between devices with their start and end apart: 13, of which 10 were waited for; matrix products, arithmetic and copies ran while one was open for 9% of the time, Pallas kernels for 0%

commit v1 on v0

v1 whole, which is shorter than its diff:
```python
import functools

import jax
import jax.numpy as jnp
import numpy as np
from jax import lax
from jax.experimental import pallas as pl
from jax.experimental.pallas import tpu as pltpu
from jax.sharding import PartitionSpec as P

epsilon = 1e-06
masked_value = -1e30
bucket_edges = (12, 16, 23, 32, 46, 64, 91)
highest = lax.Precision.HIGHEST
LANES = 128
STRIP = 128
HEAD_SIZE = 64
VMEM_BYTES = 50 * 1024 * 1024
f32 = jnp.float32
bf16 = jnp.bfloat16
vmem = pl.BlockSpec(memory_space=pltpu.VMEM)
smem = pl.BlockSpec(memory_space=pltpu.SMEM)


def mm(left, right):
    return jnp.dot(left, right, preferred_element_type=f32)


def mm_nt(left, right):
    return lax.dot_general(left, right, (((1,), (1,)), ((), ())), preferred_element_type=f32)


def mm_tn(left, right):
    return lax.dot_general(left, right, (((0,), (0,)), ((), ())), preferred_element_type=f32)


def rms_scale(values):
    return lax.rsqrt(jnp.mean(values * values, axis=-1, keepdims=True) + epsilon)


def iota(shape, dim):
    return lax.broadcasted_iota(jnp.int32, shape, dim)


def bucket_index(offset):
    side = jnp.where(offset > 0, 16, 0).astype(jnp.int32)
    distance = jnp.abs(offset)
    far_bucket = 8 + sum(((distance >= edge).astype(jnp.int32) for edge in bucket_edges))
    return side + jnp.where(distance < 8, distance, far_bucket)


def kernel_call(body, outs, in_specs, out_specs=None, scratch=(), grid=None, flops=0, moved=0):
    extra = {} if grid is None else {"grid": grid}
    return pl.pallas_call(
        body,
        out_shape=outs,
        in_specs=in_specs,
        out_specs=[vmem] * len(outs) if out_specs is None else out_specs,
        scratch_shapes=list(scratch),
        compiler_params=pltpu.CompilerParams(vmem_limit_bytes=VMEM_BYTES),
        cost_estimate=pl.CostEstimate(flops=flops, bytes_accessed=moved, transcendentals=0),
        **extra,
    )


def shape(dims, dtype):
    return jax.ShapeDtypeStruct(tuple(dims), dtype)


def segments(lengths_ref, rows, dim):
    dims = (rows, 1) if dim == 0 else (1, rows)
    places = iota(dims, dim)
    total = jnp.zeros(dims, jnp.int32)
    end = 0
    for entry in range(lengths_ref.shape[1]):
        end = end + lengths_ref[0, entry]
        total = total + (places >= end).astype(jnp.int32)
    return total


def skew(values, right):
    rows, lanes = values.shape
    row = lax.rem(iota((rows, 1), 0), STRIP)
    step = 1
    while step < STRIP:
        moved = pltpu.roll(values, step if right else lanes - step, 1)
        values = jnp.where((row & step) > 0, moved, values)
        step *= 2
    return values


def bias_strips(table_ref, first_head, heads, strip_ref):
    lanes = 4 * STRIP
    bucket = bucket_index(iota((1, lanes), 1) - 2 * STRIP)
    for head in range(heads):
        line = jnp.zeros((1, lanes), f32)
        for entry in range(table_ref.shape[0]):
            line = jnp.where(bucket == entry, table_ref[entry, first_head + head], line)
        strip = skew(jnp.broadcast_to(line, (STRIP, lanes)), True)
        strip_ref[head] = strip[:, STRIP:]


def bias_row(strip_ref, table_ref, head, first_head, block, blocks):
    buckets = table_ref.shape[0]
    parts = []
    for other in range(blocks):
        gap = other - block
        if abs(gap) <= 1:
            parts.append(strip_ref[head, :, (gap + 1) * STRIP : (gap + 2) * STRIP])
        else:
            entry = buckets - 1 if gap > 0 else buckets // 2 - 1
            parts.append(jnp.full((STRIP, STRIP), table_ref[entry, first_head + head], f32))
    return jnp.concatenate(parts, axis=1)


def head_mask(head, lanes):
    lane = iota((1, lanes), 1)
    return (lane >= head * HEAD_SIZE) & (lane < (head + 1) * HEAD_SIZE)


def pick_head(values, head, lanes):
    return jnp.where(head_mask(head, lanes), values, 0.0).astype(bf16)


def attention_forward(heads, extra_rows, *refs):
    (meta, offsets, lengths, table, x_own, x_other) = refs[:6]
    pieces = refs[6 : 6 + extra_rows]
    (h1, q_out, k_out, v_out, o_own, o_other, lse, wall, gains, strips, o_all) = refs[6 + extra_rows :]
    place = meta[0]
    rows = x_own.shape[0]
    group = 2 * rows
    first_head = place * heads
    for index, piece in enumerate(pieces):
        start = pl.multiple_of(offsets[index], 16)
        wall[pl.ds(start, piece.shape[0]), :] = piece[...]
    width = wall.shape[1]
    extras = wall[:, width - LANES :].astype(f32).T
    gain_at = LANES // 2 + 32
    gains[...] = extras[gain_at : gain_at + 8]
    gain_one = gains[0:1]
    for source, start in ((x_own, place * rows), (x_other, (1 - place) * rows)):
        values = source[...].astype(f32)
        h1[pl.ds(pl.multiple_of(start, 16), rows), :] = (
            values * rms_scale(values) * gain_one
        ).astype(bf16)
    qkv = mm(h1[...], wall[...])
    lanes = q_out.shape[1]
    q_out[...] = qkv[:, :lanes].astype(bf16)
    k_out[...] = pltpu.roll(qkv[:, LANES : LANES + lanes], lanes - LANES // 2, 1).astype(bf16)
    v_out[...] = qkv[:, width - lanes :].astype(bf16)
    bias_strips(table, first_head, heads, strips)
    segment_row = segments(lengths, group, 1)
    segment_column = segments(lengths, group, 0)
    keys = k_out[...]
    lane = iota((1, LANES), 1)
    blocks = group // STRIP
    values_of = [pick_head(v_out[...], head, lanes) for head in range(heads)]
    for block in range(blocks):
        first = block * STRIP
        same = segment_column[first : first + STRIP] == segment_row
        total = jnp.zeros((STRIP, lanes), f32)
        totals = jnp.zeros((STRIP, LANES), f32)
        for head in range(heads):
            query = pick_head(q_out[first : first + STRIP, :], head, lanes)
            scores = mm_nt(query, keys) + bias_row(strips, table, head, first_head, block, blocks)
            scores = jnp.where(same, scores, masked_value)
            top = jnp.max(scores, axis=1, keepdims=True)
            raised = jnp.exp(scores - top)
            mass = jnp.sum(raised, axis=1, keepdims=True)
            chances = (raised * (1.0 / mass)).astype(bf16)
            total = total + mm(chances, values_of[head])
            totals = jnp.where(lane == head, top + jnp.log(mass), totals)
        o_all[first : first + STRIP, :] = total.astype(bf16)
        lse[first : first + STRIP, :] = totals
    o_own[...] = o_all[pl.ds(pl.multiple_of(place * rows, 16), rows), :]
    o_other[...] = o_all[pl.ds(pl.multiple_of((1 - place) * rows, 16), rows), :]


def assemble(count, *refs):
    offsets = refs[0]
    out = refs[-1]
    for index in range(count):
        piece = refs[1 + index]
        out[pl.ds(pl.multiple_of(offsets[index], 16), piece.shape[0]), :] = piece[...]


def routed(hidden, extras, routes_column, keep_column, experts):
    logits = mm(hidden, extras)
    lane = iota((1, LANES), 1) - LANES // 2
    valid = (lane >= 0) & (lane < experts)
    logits = jnp.where(valid, logits, masked_value)
    raised = jnp.where(valid, jnp.exp(logits - jnp.max(logits, axis=1, keepdims=True)), 0.0)
    probs = raised / jnp.sum(raised, axis=1, keepdims=True)
    onehot = lane == routes_column
    kept = keep_column.astype(f32)
    gate = jnp.sum(jnp.where(onehot, probs, 0.0), axis=1, keepdims=True) * kept
    return probs, onehot, kept, gate


def slots_by_row(routes_row, keep_row, experts, capacity):
    count = routes_row.shape[1]
    chosen = ((iota((experts, count), 0) == routes_row) & (keep_row == 1)).astype(f32)
    before = (iota((count, count), 0) < iota((count, count), 1)).astype(bf16)
    earlier = mm(chosen.astype(bf16), before)
    rank = jnp.sum(earlier * chosen, axis=0, keepdims=True).astype(jnp.int32)
    return jnp.where(keep_row == 1, routes_row * capacity + rank, -2)


def slots_by_column(routes_column, keep_column, experts, capacity):
    count = routes_column.shape[0]
    chosen = ((iota((count, experts), 1) == routes_column) & (keep_column == 1)).astype(f32)
    before = (iota((count, count), 1) < iota((count, count), 0)).astype(bf16)
    earlier = mm(before, chosen.astype(bf16))
    rank = jnp.sum(earlier * chosen, axis=1, keepdims=True).astype(jnp.int32)
    return jnp.where(keep_column == 1, routes_column * capacity + rank, -2)


def to_experts(experts, capacity, *refs):
    (x_own, cotangent, o_own, o_tp, o_ctx, o_far, wo_own, wo_ctx, extras, gains) = refs[:10]
    (routes_row, routes_column, keep_row, keep_column, slot_h, slot_d) = refs[10:16]
    middle_out, sends = refs[16:]
    lanes = o_own.shape[1]
    branch = None
    for near, far, weights in ((o_own, o_tp, wo_own), (o_ctx, o_far, wo_ctx)):
        shifted = pltpu.roll(far[...].astype(f32), LANES // 2, 1).astype(bf16)
        part = mm_nt(near[...], weights[:, :lanes]) + mm_nt(shifted, weights[:, LANES : LANES + lanes])
        branch = part if branch is None else branch + part
    middle = x_own[...].astype(f32) + branch
    middle_out[...] = middle
    hidden = (middle * rms_scale(middle) * gains[1:2]).astype(bf16)
    _, _, _, gate = routed(hidden, extras[...], routes_column[...], keep_column[...], experts)
    out_grad = (gate * cotangent[...].astype(f32)).astype(bf16)
    slot = slots_by_row(routes_row[...], keep_row[...], experts, capacity)
    pick_h = (slot_h[...] == slot).astype(f32).astype(bf16)
    pick_d = (slot_d[...] == slot).astype(f32).astype(bf16)
    sends[...] = (mm(pick_h, hidden) + mm(pick_d, out_grad)).astype(bf16)


def gelu_both(value):
    scale = 0.7978845608028654
    cubic = 0.044715
    square = value * value
    inner = jnp.tanh(scale * value * (1.0 + cubic * square))
    half = 0.5 * (1.0 + inner)
    slope = half + 0.5 * value * (1.0 - inner * inner) * scale * (1.0 + 3.0 * cubic * square)
    return value * half, slope


def expert_kernel(owners, kinds_rows, chunks, group_owners, *refs):
    (rows_in, base_column, base_row, w_in, w_out) = refs[:5]
    (out, x_out, dy_out, act_out, dpre_out, acc_y, acc_x, full) = refs[5:]
    piece = pl.program_id(0)
    chunk = pl.program_id(1)
    pieces = pl.num_programs(0)
    capacity = kinds_rows
    per_owner = rows_in.shape[0] // owners
    span = group_owners * per_owner
    half = group_owners * capacity
    groups = owners // group_owners

    @pl.when(chunk == 0)
    def _():
        pick = (base_column[...] + piece * capacity == iota((2 * half, span), 1)).astype(f32).astype(bf16)
        for group in range(groups):
            got = mm(pick, rows_in[group * span : (group + 1) * span, :]).astype(bf16)
            x_out[0, group * half : (group + 1) * half, :] = got[:half]
            dy_out[0, group * half : (group + 1) * half, :] = got[half:]
        acc_y[...] = jnp.zeros_like(acc_y)
        acc_x[...] = jnp.zeros_like(acc_x)

    pre = mm(x_out[0], w_in[0])
    act, slope = gelu_both(pre)
    act = act.astype(bf16)
    act_out[0] = act
    acc_y[...] += mm(act, w_out[0])
    dpre = (mm_nt(dy_out[0], w_out[0]) * slope).astype(bf16)
    dpre_out[0] = dpre
    acc_x[...] += mm_nt(dpre, w_in[0])

    @pl.when(chunk == chunks - 1)
    def _():
        pick = (base_row[...] + piece * capacity == iota((span, 2 * half), 0)).astype(f32).astype(bf16)
        for group in range(groups):
            here = slice(group * half, (group + 1) * half)
            both = jnp.concatenate([acc_y[here].astype(bf16), acc_x[here].astype(bf16)], axis=0)
            part = mm(pick, both)
            there = slice(group * span, (group + 1) * span)
            full[there] = jnp.where(piece == 0, part, full[there] + part)

    @pl.when((chunk == chunks - 1) & (piece == pieces - 1))
    def _():
        width = out.shape[2]
        shares = out.shape[0] // owners
        for owner in range(owners):
            for share in range(shares):
                out[owner * shares + share] = full[
                    owner * per_owner : (owner + 1) * per_owner, share * width : (share + 1) * width
                ].astype(bf16)


def weight_grads(x_rows, dpre, act, dy):
    w_in_grad = jnp.einsum("lrd,lrf->ldf", x_rows, dpre, preferred_element_type=f32)
    w_out_grad = jnp.einsum("lrf,lrd->lfd", act, dy, preferred_element_type=f32)
    return w_in_grad, w_out_grad


def from_experts(experts, capacity, *refs):
    rows_in, routes_column, keep_column, slot_y, slot_x, out = refs
    slot = slots_by_column(routes_column[...], keep_column[...], experts, capacity)
    width = rows_in.shape[1]
    pick_y = (slot == slot_y[...]).astype(f32).astype(bf16)
    pick_x = (slot == slot_x[...]).astype(f32).astype(bf16)
    out[:, :width] = mm(pick_y, rows_in[...]).astype(bf16)
    out[:, width:] = mm(pick_x, rows_in[...]).astype(bf16)


def middle_backward(experts, *refs):
    (meta, both_own, both_tp, middle_ref, cotangent, extras, gains, routes_column, keep_column) = refs[:9]
    (result, dmiddle_out, branch_grad, router_grad, gain_grad) = refs[9:]
    share = meta[1]
    width = both_own.shape[1] // 2
    own = both_own[...].astype(f32)
    other = both_tp[...].astype(f32)
    first = jnp.where(share == 0, own, other)
    second = jnp.where(share == 0, other, own)
    picked = jnp.concatenate([first[:, :width], second[:, :width]], axis=1)
    slot_grad = jnp.concatenate([first[:, width:], second[:, width:]], axis=1)
    middle = middle_ref[...]
    scale = rms_scale(middle)
    normed = middle * scale
    gain = gains[1:2]
    hidden = (normed * gain).astype(bf16)
    probs, onehot, kept, gate = routed(
        hidden, extras[...], routes_column[...], keep_column[...], experts
    )
    result[...] = middle + gate * picked
    upstream = cotangent[...].astype(f32)
    gate_grad = jnp.sum(upstream * picked, axis=1, keepdims=True)
    prob_grad = jnp.where(onehot, gate_grad * kept, 0.0)
    logit_grad = (
        probs * (prob_grad - jnp.sum(probs * prob_grad, axis=1, keepdims=True))
    ).astype(bf16)
    router_grad[...] = mm_tn(hidden, logit_grad).astype(bf16)
    hidden_grad = slot_grad + mm_nt(logit_grad, extras[...])
    gain_grad[...] = jnp.broadcast_to(
        jnp.sum(hidden_grad * normed, axis=0, keepdims=True), gain_grad.shape
    )
    grad = hidden_grad * gain
    dmiddle = upstream + scale * (grad - normed * jnp.mean(grad * normed, axis=1, keepdims=True))
    dmiddle_out[...] = dmiddle
    branch_grad[...] = dmiddle.astype(bf16)


def output_grads(*refs):
    (db_own, db_other, o_own, o_other, router_grad, out) = refs
    both = mm_tn(db_own[...], o_own[...]) + mm_tn(db_other[...], o_other[...])
    width = out.shape[1]
    out[:, : width - LANES] = both[:, : width - LANES].astype(bf16)
    out[:, width - LANES :] = (
        both[:, width - LANES :] + router_grad[...].astype(f32)
    ).astype(bf16)


def attention_backward(heads, heads_all, *refs):
    (meta, lengths, table, x_own, x_other, h1, q_in, k_in, v_in, lse, db_own, db_other) = refs[:12]
    (wo_own, wall, gain_two) = refs[12:15]
    (payload, dh1_own, dh1_other, small) = refs[15:19]
    (strips, sums, do_all, dq, dk, dv, dqkv, dh1) = refs[19:]
    place, share = meta[0], meta[1]
    rows = x_own.shape[0]
    group = 2 * rows
    lanes = q_in.shape[1]
    first_head = place * heads
    own_at = pl.ds(pl.multiple_of(place * rows, 16), rows)
    other_at = pl.ds(pl.multiple_of((1 - place) * rows, 16), rows)
    weights = wo_own[:, :lanes]
    do_all[own_at, :] = mm(db_own[...], weights).astype(bf16)
    do_all[other_at, :] = mm(db_other[...], weights).astype(bf16)
    bias_strips(table, first_head, heads, strips)
    segment_row = segments(lengths, group, 1)
    segment_column = segments(lengths, group, 0)
    blocks = group // STRIP
    sums[...] = jnp.zeros_like(sums)
    keys = k_in[...]
    values = v_in[...]
    ahead = [jnp.zeros((STRIP, STRIP), f32) for _ in range(heads)]
    behind = [jnp.zeros((STRIP, STRIP), f32) for _ in range(heads)]
    for block in range(blocks):
        at = slice(block * STRIP, (block + 1) * STRIP)
        same = segment_column[at] == segment_row
        dq_total = jnp.zeros((STRIP, lanes), f32)
        for head in range(heads):
            query = pick_head(q_in[at, :], head, lanes)
            scores = mm_nt(query, keys) + bias_row(strips, table, head, first_head, block, blocks)
            scores = jnp.where(same, scores, masked_value)
            chances = jnp.exp(scores - lse[at, head : head + 1])
            grad = pick_head(do_all[at, :], head, lanes)
            chance_grad = mm_nt(grad, values)
            mean = jnp.sum(chances * chance_grad, axis=1, keepdims=True)
            score_grad = (chances * (chance_grad - mean)).astype(bf16)
            dv_part = mm_tn(chances.astype(bf16), grad)
            dk_part = mm_tn(score_grad, query)
            if block == 0 and head == 0:
                dv[...] = dv_part
                dk[...] = dk_part
            else:
                dv[...] += dv_part
                dk[...] += dk_part
            dq_total = dq_total + mm(score_grad, pick_head(keys, head, lanes))
            rounded = score_grad.astype(f32)
            for other in range(blocks):
                gap = other - block
                part = rounded[:, other * STRIP : (other + 1) * STRIP]
                if abs(gap) <= 1:
                    sums[head, :, (gap + 2) * STRIP : (gap + 3) * STRIP] += part
                elif gap > 0:
                    ahead[head] = ahead[head] + part
                else:
                    behind[head] = behind[head] + part
        dq[at, :] = dq_total
    half = LANES // 2
    dqkv[:, :LANES] = dq[:, :LANES].astype(bf16)
    shifted = pltpu.roll(dk[...], half, 1)
    dqkv[:, LANES : 2 * LANES] = (dq[:, LANES:] + shifted[:, :LANES]).astype(bf16)
    dqkv[:, 2 * LANES : 3 * LANES] = shifted[:, LANES:].astype(bf16)
    dqkv[:, 3 * LANES :] = dv[...].astype(bf16)
    payload[...] = mm_tn(h1[...], dqkv[...]).astype(bf16)
    dh1[...] = mm_nt(dqkv[...], wall[...])
    gain_part = None
    for source, at, target in ((x_own, own_at, dh1_own), (x_other, other_at, dh1_other)):
        values = source[...].astype(f32)
        grad = dh1[at, :]
        target[...] = grad.astype(bf16)
        part = jnp.sum(grad * (values * rms_scale(values)), axis=0, keepdims=True)
        gain_part = part if gain_part is None else gain_part + part
    buckets = table.shape[0]
    spread = skew(sums[...].reshape(heads * STRIP, 4 * STRIP), False)
    diagonals = jnp.sum(spread.reshape(heads, STRIP, 4 * STRIP), axis=1)
    picks = (bucket_index(iota((4 * STRIP, 1), 0) - 2 * STRIP) == iota((1, LANES), 1)).astype(f32)
    in_buckets = jnp.dot(diagonals, picks, precision=highest, preferred_element_type=f32)
    lane = iota((1, LANES), 1)
    row = iota((16, 1), 0)
    table_grad = jnp.zeros((16, LANES), f32)
    for head in range(heads):
        line = in_buckets[head : head + 1]
        line = line + jnp.where(lane == buckets - 1, jnp.sum(ahead[head]), 0.0)
        line = line + jnp.where(lane == buckets // 2 - 1, jnp.sum(behind[head]), 0.0)
        mine = share * (heads_all // 2) + first_head + head
        table_grad = table_grad + jnp.where(row == mine, line, 0.0)
    small[...] = jnp.zeros_like(small)
    small[:16, :] = table_grad
    gain_rows = gain_part.shape[1] // LANES
    once = jnp.where(share == 0, 1.0, 0.0)
    for index in range(gain_rows):
        at = slice(index * LANES, (index + 1) * LANES)
        small[16 + index : 17 + index, :] = gain_part[:, at]
        small[24 + index : 25 + index, :] = gain_two[0:1, at] * once


def input_backward(x_own, dmiddle, gains, near, far, out):
    values = x_own[...].astype(f32)
    scale = rms_scale(values)
    normed = values * scale
    grad = (near[...].astype(f32) + far[...].astype(f32)) * gains[0:1]
    out[...] = dmiddle[...] + scale * (
        grad - normed * jnp.mean(grad * normed, axis=1, keepdims=True)
    )


def swap(value, axis):
    return lax.ppermute(value, axis, [(0, 1), (1, 0)])


def ring_order(count):
    return list(range(0, count, 2)) + list(range(count - 1, 0, -2))


def ring_steps(count):
    order = ring_order(count)
    right = [(order[i], order[(i + 1) % count]) for i in range(count)]
    return order, right, [(b, a) for a, b in right]


def ring_place(count):
    order = ring_order(count)
    inverse = np.zeros(count, np.int32)
    inverse[order] = np.arange(count)
    return jnp.asarray(np.array(order, np.int32)), jnp.asarray(inverse)[lax.axis_index("fsdp")]


def ring_gather(shard, count):
    rows = shard.shape[0]
    order, right, left = ring_steps(count)
    table, place = ring_place(count)
    pieces = [shard]
    starts = [table[place] * rows]
    going_right, going_left = shard, shard
    for step in range(1, count // 2):
        going_right = lax.ppermute(going_right, "fsdp", right)
        going_left = lax.ppermute(going_left, "fsdp", left)
        pieces += [going_right, going_left]
        starts += [table[(place - step) % count] * rows, table[(place + step) % count] * rows]
    half = rows // 2
    pieces += [
        lax.ppermute(going_right[:half], "fsdp", right),
        lax.ppermute(going_left[half:], "fsdp", left),
    ]
    across = table[(place + count // 2) % count] * rows
    starts += [across, across + half]
    return pieces, jnp.stack(starts).astype(jnp.int32)


def gather_rows(shard, count):
    rows = shard.shape[0]
    if rows % 32 == 0 and count % 2 == 0:
        return ring_gather(shard, count)
    return [lax.all_gather(shard, "fsdp", axis=0, tiled=True)], jnp.zeros((1,), jnp.int32)


def sum_rows(payload, count):
    rows = payload.shape[0] // count
    if rows % 32 or count % 2:
        return lax.psum_scatter(payload.astype(f32), "fsdp", scatter_dimension=0, tiled=True)
    order, right, left = ring_steps(count)
    table, place = ring_place(count)
    half = rows // 2

    def mine(distance):
        start = table[(place + distance) % count] * rows
        return lax.dynamic_slice_in_dim(payload, start, rows, 0).astype(f32)

    across = mine(count // 2).astype(bf16)
    going_right, going_left = across[:half], across[half:]
    for step in range(count // 2, 0, -1):
        from_left = lax.ppermute(going_right, "fsdp", right).astype(f32)
        from_right = lax.ppermute(going_left, "fsdp", left).astype(f32)
        if step == count // 2:
            none = jnp.zeros_like(from_left)
            from_left = jnp.concatenate([from_left, none], axis=0)
            from_right = jnp.concatenate([none, from_right], axis=0)
        if step == 1:
            return mine(0) + from_left + from_right
        going_right = (mine(step - 1) + from_left).astype(bf16)
        going_left = (mine(1 - step) + from_right).astype(bf16)


def sum_everywhere(value, counts):
    for axis, count in counts:
        step = 1
        while step < count:
            pairs = [(i, i ^ step) for i in range(count)]
            value = value + lax.ppermute(value, axis, pairs)
            step *= 2
    return value


def body(
    tokens,
    cotangent,
    w_query,
    w_key,
    w_value,
    w_output,
    w_router,
    gain_attn,
    gain_moe,
    rel_table,
    w_in,
    w_out,
    lengths,
    routes,
    keep_mask,
):
    rows, model_width = tokens.shape
    fsdp_count = lax.axis_size("fsdp")
    owners = lax.axis_size(("fsdp", "ctx"))
    tp_count = lax.axis_size("tp")
    place = lax.axis_index("ctx")
    share = lax.axis_index("tp")
    fsdp_place = lax.axis_index("fsdp")
    group = 2 * rows
    experts = w_router.shape[1]
    capacity = max(2, (5 * rows + 4 * experts - 1) // (4 * experts))
    pieces = w_in.shape[0]
    split_count = owners * pieces // experts
    hidden_width = w_in.shape[2]
    heads = rel_table.shape[1] // 2
    heads_all = heads * 2 * tp_count
    width = heads * HEAD_SIZE
    lanes = width + HEAD_SIZE
    shard_rows = w_query.shape[0]
    buckets = rel_table.shape[0]
    meta = jnp.stack([place, share]).astype(jnp.int32)

    def columns(weight, which):
        return lax.dynamic_slice_in_dim(weight, which * width, width, 1)

    extras_width = HEAD_SIZE - experts - 2
    extras_shard = jnp.concatenate(
        [w_router, gain_attn[:, None], gain_moe[:, None], jnp.zeros((shard_rows, extras_width), bf16)],
        axis=1,
    )

    def shard_for(which):
        return jnp.concatenate(
            [columns(w_query, which), columns(w_key, which), columns(w_value, which), extras_shard],
            axis=1,
        )

    def in_order(own, other, axis):
        return jnp.where(
            place == 0,
            jnp.concatenate([own, other], axis=axis),
            jnp.concatenate([other, own], axis=axis),
        )

    shard = in_order(shard_for(place), swap(shard_for(1 - place), "ctx"), 0)
    x_other = swap(tokens, "ctx")
    wo_shard = in_order(columns(w_output, place), swap(columns(w_output, 1 - place), "ctx"), 0)
    wo_shard = jnp.concatenate([wo_shard, swap(wo_shard, "tp")], axis=1)

    wall_pieces, wall_starts = gather_rows(shard, fsdp_count)
    wo_shard, *_ = lax.optimization_barrier((wo_shard, *wall_pieces[-2:]))
    wo_pieces, wo_starts = gather_rows(wo_shard, fsdp_count)

    def full(dims, dtype):
        return shape(dims, dtype)

    wall_width = shard.shape[1]
    h1, q, k, v, o_own, o_other, lse, wall, gains = kernel_call(
        functools.partial(attention_forward, heads, len(wall_pieces)),
        [
            full((group, model_width), bf16),
            full((group, lanes), bf16),
            full((group, lanes), bf16),
            full((group, lanes), bf16),
            full((rows, lanes), bf16),
            full((rows, lanes), bf16),
            full((group, LANES), f32),
            full((model_width, wall_width), bf16),
            full((8, model_width), f32),
        ],
        [smem] * 4 + [vmem] * (2 + len(wall_pieces)),
        scratch=[pltpu.VMEM((heads, STRIP, 3 * STRIP), f32), pltpu.VMEM((group, lanes), bf16)],
        flops=2 * group * model_width * wall_width * 8,
        moved=8 * 1024 * 1024,
    )(meta, wall_starts, lengths, rel_table, tokens, x_other, *wall_pieces)

    wo_own = kernel_call(
        functools.partial(assemble, len(wo_pieces)),
        [full((model_width, wo_shard.shape[1]), bf16)],
        [smem] + [vmem] * len(wo_pieces),
        moved=1024 * 1024,
    )(wo_starts, *wo_pieces)[0]
    wo_ctx = swap(wo_own, "ctx")

    o_tp = swap(o_own, "tp")
    o_ctx = swap(o_other, "ctx")
    o_far = lax.ppermute(o_other, ("ctx", "tp"), [(i, 3 - i) for i in range(4)])

    per_owner = 2 * pieces * capacity
    owner_of = np.repeat(np.arange(owners), per_owner)
    inside = np.tile(np.arange(per_owner), owners)
    kind = inside // (pieces * capacity)
    piece_of = owner_of * pieces + (inside // capacity) % pieces
    slot_of = (piece_of // split_count) * capacity + inside % capacity
    slot_first = np.where(kind == 0, slot_of, -1).astype(np.int32)
    slot_second = np.where(kind == 1, slot_of, -1).astype(np.int32)
    routes_row = routes.reshape(1, rows)
    keep_row = keep_mask.reshape(1, rows)
    keep_column = keep_mask.reshape(rows, 1)
    extras = wall[:, wall_width - LANES :]

    middle, sends = kernel_call(
        functools.partial(to_experts, experts, capacity),
        [full((rows, model_width), f32), full((owners * per_owner, model_width), bf16)],
        [vmem] * 16,
        flops=2 * rows * model_width * (model_width + 2 * owners * per_owner),
        moved=6 * 1024 * 1024,
    )(
        tokens, cotangent, o_own, o_tp, o_ctx, o_far, wo_own, wo_ctx, extras, gains,
        routes_row, routes, keep_row, keep_column, slot_first[:, None], slot_second[:, None],
    )

    arrived = lax.all_to_all(
        sends.reshape(owners, per_owner, model_width),
        ("fsdp", "ctx"),
        split_axis=0,
        concat_axis=0,
        tiled=True,
    ).reshape(owners * per_owner, model_width)

    group_owners = min(16, owners)
    half = group_owners * capacity
    spot = np.arange(2 * half) % half
    base = (
        (spot // capacity) * per_owner
        + (np.arange(2 * half) // half) * pieces * capacity
        + spot % capacity
    ).astype(np.int32)
    chunk_width = 512 if hidden_width % 512 == 0 else hidden_width
    chunks = hidden_width // chunk_width
    slot_rows = owners * capacity
    part_width = model_width // tp_count
    whole = lambda *dims: pl.BlockSpec(dims, lambda i, j: (0,) * len(dims))
    outgoing, x_rows, dy_rows, act, dpre = kernel_call(
        functools.partial(expert_kernel, owners, capacity, chunks, group_owners),
        [
            full((owners * tp_count, per_owner, part_width), bf16),
            full((pieces, slot_rows, model_width), bf16),
            full((pieces, slot_rows, model_width), bf16),
            full((pieces, slot_rows, hidden_width), bf16),
            full((pieces, slot_rows, hidden_width), bf16),
        ],
        [
            whole(owners * per_owner, model_width),
            whole(2 * half, 1),
            whole(1, 2 * half),
            pl.BlockSpec((1, model_width, chunk_width), lambda i, j: (i, 0, j)),
            pl.BlockSpec((1, chunk_width, model_width), lambda i, j: (i, j, 0)),
        ],
        out_specs=[
            whole(owners * tp_count, per_owner, part_width),
            pl.BlockSpec((1, slot_rows, model_width), lambda i, j: (i, 0, 0)),
            pl.BlockSpec((1, slot_rows, model_width), lambda i, j: (i, 0, 0)),
            pl.BlockSpec((1, slot_rows, chunk_width), lambda i, j: (i, 0, j)),
            pl.BlockSpec((1, slot_rows, chunk_width), lambda i, j: (i, 0, j)),
        ],
        scratch=[
            pltpu.VMEM((slot_rows, model_width), f32),
            pltpu.VMEM((slot_rows, model_width), f32),
            pltpu.VMEM((owners * per_owner, model_width), f32),
        ],
        grid=(pieces, chunks),
        flops=8 * pieces * slot_rows * model_width * hidden_width,
        moved=12 * 1024 * 1024,
    )(arrived, base[:, None], base[None, :], w_in, w_out)

    returned = lax.all_to_all(
        outgoing, ("fsdp", "ctx", "tp"), split_axis=0, concat_axis=0, tiled=True
    ).reshape(owners * tp_count * per_owner, part_width)
    w_in_grad, w_out_grad = weight_grads(x_rows, dpre, act, dy_rows)

    back_first = np.repeat(slot_first.reshape(owners, 1, per_owner), tp_count, axis=1).reshape(1, -1)
    back_second = np.repeat(slot_second.reshape(owners, 1, per_owner), tp_count, axis=1).reshape(1, -1)
    both_own = kernel_call(
        functools.partial(from_experts, experts, capacity),
        [full((rows, 2 * part_width), bf16)],
        [vmem] * 5,
        flops=4 * rows * returned.shape[0] * part_width,
        moved=2 * 1024 * 1024,
    )(returned, routes, keep_column, back_first, back_second)[0]
    both_tp = swap(both_own, "tp")

    result, middle_grad, db_own, router_grad, gain_two_part = kernel_call(
        functools.partial(middle_backward, experts),
        [
            full((rows, model_width), f32),
            full((rows, model_width), f32),
            full((rows, model_width), bf16),
            full((model_width, LANES), bf16),
            full((8, model_width), f32),
        ],
        [smem] + [vmem] * 8,
        flops=6 * rows * LANES * model_width,
        moved=6 * 1024 * 1024,
    )(meta, both_own, both_tp, middle, cotangent, extras, gains, routes, keep_column)
    db_other = swap(db_own, "ctx")

    payload_one = kernel_call(
        output_grads,
        [full((model_width, lanes), bf16)],
        [vmem] * 5,
        flops=2 * group * lanes * model_width,
        moved=2 * 1024 * 1024,
    )(db_own, db_other, o_own, o_other, router_grad)[0]
    sums_one = sum_rows(payload_one, fsdp_count)

    payload_two, dh1_own, dh1_other, small = kernel_call(
        functools.partial(attention_backward, heads, heads_all),
        [
            full((model_width, wall_width), bf16),
            full((rows, model_width), bf16),
            full((rows, model_width), bf16),
            full((32, LANES), f32),
        ],
        [smem] * 3 + [vmem] * 12,
        scratch=[
            pltpu.VMEM((heads, STRIP, 3 * STRIP), f32),
            pltpu.VMEM((heads, STRIP, 4 * STRIP), f32),
            pltpu.VMEM((group, lanes), bf16),
            pltpu.VMEM((group, lanes), f32),
            pltpu.VMEM((group, lanes), f32),
            pltpu.VMEM((group, lanes), f32),
            pltpu.VMEM((group, wall_width), bf16),
            pltpu.VMEM((group, model_width), f32),
        ],
        flops=2 * group * model_width * wall_width * 12,
        moved=8 * 1024 * 1024,
    )(
        meta, lengths, rel_table, tokens, x_other, h1, q, k, v, lse, db_own, db_other,
        wo_own, wall, gain_two_part,
    )

    dh1_sum = (dh1_own.astype(f32) + swap(dh1_other, "ctx").astype(f32)).astype(bf16)
    dh1_far = swap(dh1_sum, "tp")
    sums_two = sum_rows(payload_two[:, : 3 * width], fsdp_count)
    small = sum_everywhere(small, (("ctx", 2), ("tp", tp_count), ("fsdp", fsdp_count)))

    input_grad = kernel_call(
        input_backward,
        [full((rows, model_width), f32)],
        [vmem] * 5,
        moved=4 * 1024 * 1024,
    )(tokens, middle_grad, gains, dh1_sum, dh1_far)[0]

    def own_rows(sums):
        own = lax.dynamic_slice_in_dim(sums, place * shard_rows, shard_rows, 0)
        other = lax.dynamic_slice_in_dim(sums, (1 - place) * shard_rows, shard_rows, 0)
        return own, swap(other, "ctx")

    one_own, one_other = own_rows(sums_one)
    two_own, two_other = own_rows(sums_two)
    grads = [
        in_order(two_own[:, at : at + width], two_other[:, at : at + width], 1)
        for at in (0, width, 2 * width)
    ]
    output_grad = in_order(one_own[:, :width], one_other[:, :width], 1)
    router_total = (one_own + one_other)[:, width : width + experts]
    first_row = (fsdp_place * 2 + place) * shard_rows
    gain_rows = model_width // LANES

    def gain_of(first):
        line = small[first : first + gain_rows].reshape(model_width)
        return lax.dynamic_slice_in_dim(line, first_row, shard_rows, 0)

    table_total = lax.dynamic_slice_in_dim(small, share * 2 * heads, 2 * heads, 0)[:, :buckets].T
    return (
        result,
        input_grad,
        grads[0],
        grads[1],
        grads[2],
        output_grad,
        router_total,
        gain_of(16),
        gain_of(24),
        table_total,
        w_in_grad,
        w_out_grad,
    )


def solution(mesh):
    in_specs = (
        P(("fsdp", "ctx"), None),
        P(("fsdp", "ctx"), None),
        P(("fsdp", "ctx"), "tp"),
        P(("fsdp", "ctx"), "tp"),
        P(("fsdp", "ctx"), "tp"),
        P(("fsdp", "ctx"), "tp"),
        P(("fsdp", "ctx"), None),
        P(("fsdp", "ctx")),
        P(("fsdp", "ctx")),
        P(None, "tp"),
        P(("fsdp", "ctx"), None, "tp"),
        P(("fsdp", "ctx"), "tp", None),
        P("fsdp", None),
        P(("fsdp", "ctx"), None),
        P(("fsdp", "ctx")),
    )
    out_specs = (
        P(("fsdp", "ctx"), None),
        P(("fsdp", "ctx"), None),
        P(("fsdp", "ctx"), "tp"),
        P(("fsdp", "ctx"), "tp"),
        P(("fsdp", "ctx"), "tp"),
        P(("fsdp", "ctx"), "tp"),
        P(("fsdp", "ctx"), None),
        P(("fsdp", "ctx")),
        P(("fsdp", "ctx")),
        P(None, "tp"),
        P(("fsdp", "ctx"), None, "tp"),
        P(("fsdp", "ctx"), "tp", None),
    )
    return jax.shard_map(body, mesh=mesh, in_specs=in_specs, out_specs=out_specs, check_vma=False)
```

time: 773 us -> 268 us (0.35)
  waiting for transfers between devices: 298 us -> 55.4 us
  blocking collectives: 264 us -> 58.2 us
  matrix products: 60.8 us -> 11.6 us
  local copies, waits for them, and re-layouts: 80.7 us -> 32.9 us
  Pallas kernels: 0 us -> 41.7 us
  starting transfers between devices: 10.7 us -> 45.3 us
  other arithmetic: 37.2 us -> 6.34 us
    reduce_scatter x8 -> x0, waiting for transfers between devices: 207 us -> none  [the longest x1 61.8 us: body(): lax.psum_scatter(key_weight_grad, ('fsdp', 'ctx'), scatter_dimension=0, t...]
    all_gather x11 -> x0, blocking collectives: 139 us -> none  [the longest x1 22 us: body(): lax.all_gather(w_output, ('fsdp', 'ctx'), axis=0, tiled=True)]
    unnamed x2 -> x0, blocking collectives: 96.8 us -> none
    ppermute x0 -> x51, waiting for transfers between devices: none -> 55.4 us  [the longest x8 14.6 us: sum_rows(): from_right = lax.ppermute(going_left, 'fsdp', left).astype(f32)]
    unnamed x12 -> x0, waiting for transfers between devices: 51.2 us -> none
    dot_general x28 -> x2, matrix products: 58.5 us -> 11.6 us  [the longest x1 6.38 us: weight_grads(): jnp.einsum('lrd,lrf->ldf', x_rows, dpre, preferred_element_type=f32)]
    ppermute x0 -> x51, starting transfers between devices: none -> 45.3 us  [the longest x6 10.9 us: ring_gather(): going_left = lax.ppermute(going_left, 'fsdp', left)]
    pallas_call x0 -> x9, Pallas kernels: none -> 41.7 us  [the longest x1 11.9 us: body(): kernel_call(functools.partial(expert_kernel, owners, capacity, chunks, gr...]
  transfers between devices with their start and end apart: 13 -> 51, of which waited for: 10 -> 26; matrix products, arithmetic and copies ran while one was open for 9% -> 10% of each run, Pallas kernels for 0% -> 3%
where the time goes in v1:
time: 268 us; the launch traced here: 267 us
  blocking collectives  58.2 us (22%)
  waiting for transfers between devices  55.4 us (21%)
  starting transfers between devices  45.3 us (17%)
  Pallas kernels  41.7 us (16%)
  local copies, waits for them, and re-layouts  32.9 us (12%)
  between operations  15 us (6%)
  matrix products  11.6 us (4%)
  other arithmetic  6.34 us (2%)
    all_to_all x1, blocking collectives, body(): lax.all_to_all(outgoing, ('fsdp', 'ctx', 'tp'), split_axis=0, concat_axis...  29.5 us
    all_to_all x1, blocking collectives, body(): lax.all_to_all(sends.reshape(owners, per_owner, model_width), ('fsdp', 'c...  28.7 us
    unnamed x114, local copies, waits for them, and re-layouts  22.3 us
    ppermute x8, waiting for transfers between devices, sum_rows(): from_right = lax.ppermute(going_left, 'fsdp', left).astype(f32)  14.6 us
    ppermute x13, waiting for transfers between devices, swap(): return lax.ppermute(value, axis, [(0, 1), (1, 0)])  14.2 us
    ppermute x6, waiting for transfers between devices, ring_gather(): going_left = lax.ppermute(going_left, 'fsdp', left)  12.8 us
    pallas_call x1, Pallas kernels, body(): kernel_call(functools.partial(expert_kernel, owners, capacity, chunks, gr...  11.9 us
    pallas_call x1, Pallas kernels, body(): kernel_call(functools.partial(attention_backward, heads, heads_all), [ful...  11.6 us
  transfers between devices with their start and end apart: 51, of which 26 were waited for; matrix products, arithmetic and copies ran while one was open for 10% of the time, Pallas kernels for 3%

profile of v1, /device:TPU:0, one launch (start us, length us, event | category | flops | bytes accessed | tf_op | source)
XLA Modules:
  0.0 266.5 jit_solution(10225316833157803833)
XLA Ops:
  4.0 1.0 constant_dynamic-slice_fusion.14
  6.6 2.9 %collective-permute-start.3 = (bf16[96,640]{1,0:T(8,128)(2,1)S(1)}, bf16[96,640]{1,0:T(8,128)(2,1)S(1)}, u32[]{:S(2)}, u32[]{:S(2)}) collective-permute-start(bf16[96,640]{1,0:T(8,128)(2,1)S(1)} %maximum_select_fusion.refs_6_), channel_id=1, source_target_pairs={{8,0},{16,8},{24,16},{28,24},{20,28},{12,20},{4,12},{0,4},{9,1},{1... | collective-permute-start | bytes 368648 | tf_op jit(solution)/shard_map/ppermute | solution.py:500
  9.6 3.6 %collective-permute-done.3.refs_8_ = bf16[96,640]{1,0:T(8,128)(2,1)S(1)} collective-permute-done((bf16[96,640]{1,0:T(8,128)(2,1)S(1)}, bf16[96,640]{1,0:T(8,128)(2,1)S(1)}, u32[]{:S(2)}, u32[]{:S(2)}) %collective-permute-start.3) | collective-permute-done | bytes 122912 | tf_op jit(solution)/shard_map/ppermute | solution.py:500
  13.2 1.7 collective-permute-start.5
  16.2 1.9 collective-permute-done.5.refs_10_
  18.1 1.7 collective-permute-start.7
  21.4 1.7 collective-permute-start.14
  23.2 1.5 collective-permute-start.9
  25.8 1.9 collective-permute-done.9.refs_14_
  28.3 1.3 collective-permute-done.8.refs_13_
  29.5 1.6 collective-permute-start.16
  31.6 2.3 collective-permute-done.16.refs_3_
  33.9 1.6 collective-permute-start.18
  36.3 2.7 %collective-permute-done.18.refs_5_ = bf16[96,384]{1,0:T(8,128)(2,1)S(1)} collective-permute-done((bf16[96,384]{1,0:T(8,128)(2,1)S(1)}, bf16[96,384]{1,0:T(8,128)(2,1)S(1)}, u32[]{:S(2)}, u32[]{:S(2)}) %collective-permute-start.18) | collective-permute-done | bytes 73760 | tf_op jit(solution)/shard_map/ppermute | solution.py:500
  39.0 1.6 collective-permute-start.20
  41.0 2.3 collective-permute-done.20.refs_7_
  43.3 1.6 collective-permute-start.22
  45.4 1.2 dynamic_slice.201
  54.6 1.7 fusion.2
  62.9 1.0 copy-done.1
  71.7 6.6 %shard_map.364 = (bf16[512,768]{1,0:T(8,128)(2,1)S(1)}, bf16[512,256]{1,0:T(8,128)(2,1)S(1)}, bf16[512,256]{1,0:T(8,128)(2,1)S(1)}, bf16[512,256]{1,0:T(8,128)(2...) custom-call(s32[2]{0:T(128)S(1)} %pad_add_fusion.refs_0_, ...), custom_call_target="tpu_custom_call" | custom-call | flops 4026531840 | bytes 8388608 | tf_op jit(solution)/shard_map/pallas_call | solution.py:630
  81.9 1.5 collective-permute-start.10
  84.4 0.9 slice.70.refs_8_.refs_5_
  85.3 2.9 %collective-permute-done.10.refs_3_ = bf16[256,256]{1,0:T(8,128)(2,1)S(1)} collective-permute-done((bf16[256,256]{1,0:T(8,128)(2,1)S(1)}, bf16[256,256]{1,0:T(8,128)(2,1)S(1)}, u32[]{:S(2)}, u32[]{:S(2)}) %collective-permute-start.10) | collective-permute-done | bytes 131104 | tf_op jit(solution)/shard_map/ppermute | solution.py:471
  88.2 2.1 collective-permute-done.12.refs_5_
  90.4 4.0 %shard_map.366 = (f32[256,768]{1,0:T(8,128)}, bf16[640,768]{1,0:T(8,128)(2,1)}) custom-call(bf16[256,768]{1,0:T(8,128)(2,1)S(1)} %copy-done.2, bf16[256,768]{1,0:T(8,128)(2,1)S(1)} %copy-done, bf16[256,256]{1,0:T(8,128)(2,1)S(1)} %get-tuple-element.38.refs_2_, bf16[256,256]{1,0:T(8,128)(2,1)S(1)} %collective-permute-done.10.refs_3_, ...), custom_call_target="tpu_custom_call" | custom-call | flops 805306368 | bytes 6291456 | tf_op jit(solution)/shard_map/pallas_call | solution.py:674
  94.5 28.7 %all_to_all.10 = bf16[16,40,768]{2,1,0:T(8,128)(2,1)} all-to-all(bf16[16,40,768]{2,1,0:T(8,128)(2,1)} %bitcast.42), channel_id=1, replica_groups=mesh['fsdp'=8,'ctx'=2,'tp'=2] {'fsdp','ctx'}, dimensions={0} | all-to-all | bytes 1966080 | tf_op jit(solution)/shard_map/all_to_all | solution.py:685
  124.8 11.9 %shard_map.367 = (bf16[32,40,384]{2,1,0:T(8,128)(2,1)S(1)}, bf16[2,160,768]{2,1,0:T(8,128)(2,1)S(1)}, bf16[2,160,768]{2,1,0:T(8,128)(2,1)S(1)}, bf16[2,160,1536]...) custom-call(bf16[640,768]{1,0:T(8,128)(2,1)} %bitcast.43, s32[320,1]{1,0:T(8,128)S(1)} %copy-done.41, s32[1,320]{1,0:T(1,128)S(1)} %copy-done.44, ...), custom_call_target="tpu_custom_call" | custom-call | flops 3019898880 | bytes 12582912 | tf_op jit(solution)/shard_map/pallas_call | solution.py:706
  136.7 0.9 copy-done.3
  137.6 29.5 %all_to_all.11 = bf16[32,40,384]{2,1,0:T(8,128)(2,1)S(1)} all-to-all(bf16[32,40,384]{2,1,0:T(8,128)(2,1)S(1)} %get-tuple-element.44), channel_id=1, replica_groups=mesh['fsdp'=8,'ctx'=2,'tp'=2] {'fsdp','ctx','tp'}, dimensions={0} | all-to-all | bytes 1966080 | tf_op jit(solution)/shard_map/all_to_all | solution.py:739
  167.1 2.0 shard_map.368.refs_1_
  169.2 1.5 collective-permute-start.24
  171.3 9.3 %collective-permute-done.24.refs_2_ = bf16[256,768]{1,0:T(8,128)(2,1)} collective-permute-done((bf16[256,768]{1,0:T(8,128)(2,1)}, bf16[256,768]{1,0:T(8,128)(2,1)}, u32[]{:S(2)}, u32[]{:S(2)}) %collective-permute-start.24) | collective-permute-done | bytes 393248 | tf_op jit(solution)/shard_map/ppermute | solution.py:471
  180.7 1.1 copy-done.6
  181.8 3.4 %shard_map.369 = (f32[256,768]{1,0:T(8,128)}, f32[256,768]{1,0:T(8,128)S(1)}, bf16[256,768]{1,0:T(8,128)(2,1)S(1)}, bf16[768,128]{1,0:T(8,128)(2,1)S(1)}, f32[8,768]{1,0:T(8,128)S(1)}) custom-call(s32[2]{0:T(128)S(1)} %copy-done.26, bf16[256,768]{1,0:T(8,128)(2,1)} %shard_map.368.refs_1_, bf16[256,768]{1,0:T(8,128)(2,1)} %collective-permute-done.24.refs_2_, ...), custom_call_target="tpu_custom_call" | custom-call | flops 150994944 | bytes 6291456 | tf_op jit(solution)/shard_map/pallas_call | solution.py:755
  186.1 6.4 %fusion.3 = f32[2,768,1536]{2,1,0:T(8,128)} fusion(bf16[2,160,768]{2,1,0:T(8,128)(2,1)S(1)} %get-tuple-element.60, bf16[2,160,1536]{2,1,0:T(8,128)(2,1)} %copy-done.3), kind=kOutput, calls=%fused_computation.47 | convolution fusion | flops 754974720 | bytes 10911744 | tf_op jit(solution)/shard_map/lrd,lrf->ldf/dot_general | solution.py:302
  192.5 11.6 %shard_map.370 = (bf16[768,640]{1,0:T(8,128)(2,1)}, bf16[256,768]{1,0:T(8,128)(2,1)S(1)}, bf16[256,768]{1,0:T(8,128)(2,1)}, f32[32,128]{1,0:T(8,128)S(1)}) custom-call(s32[2]{0:T(128)S(1)} %copy-done.26, s32[1,4]{1,0:T(1,128)S(1)} %copy-done.40, f32[32,6]{1,0:T(8,128)S(1)} %copy.59.refs_3_.refs_2_, bf16[256,768]{1,0:T(8,128)(2,1)S(1)} %copy-done.2, ...), custom_call_target="tpu_custom_call" | custom-call | flops 6039797760 | bytes 8388608 | tf_op jit(solution)/shard_map/pallas_call | solution.py:779
  206.0 1.1 collective-permute-start.37
  207.1 1.0 collective-permute-start.47
  208.1 5.2 %fusion.4 = f32[2,1536,768]{2,1,0:T(8,128)} fusion(bf16[2,160,1536]{2,1,0:T(8,128)(2,1)S(1)} %get-tuple-element.62, bf16[2,160,768]{2,1,0:T(8,128)(2,1)S(1)} %copy-done.8), kind=kOutput, calls=%fused_computation.48 | convolution fusion | flops 754974720 | bytes 10911744 | tf_op jit(solution)/shard_map/lrf,lrd->lfd/dot_general | solution.py:303
  214.2 1.7 collective-permute-start.48
  216.0 2.1 collective-permute-done.48
  218.1 1.1 collective-permute-start.49
  219.2 1.0 collective-permute-start.28
  220.2 1.1 collective-permute-start.32
  221.9 1.0 collective-permute-start.50
  224.4 2.3 collective-permute-done.50
  227.7 1.1 collective-permute-start.42
  228.9 3.0 %collective-permute-done.42 = bf16[96,256]{1,0:T(8,128)(2,1)S(1)} collective-permute-done((bf16[96,256]{1,0:T(8,128)(2,1)S(1)}, bf16[96,256]{1,0:T(8,128)(2,1)S(1)}, u32[]{:S(2)}, u32[]{:S(2)}) %collective-permute-start.42) | collective-permute-done | bytes 49184 | tf_op jit(solution)/shard_map/ppermute | solution.py:536
  231.9 1.1 collective-permute-start.43
  236.3 1.1 collective-permute-start.44
  237.4 1.1 collective-permute-start.30
  238.9 1.6 collective-permute-done.44
  240.6 1.7 collective-permute-done.30
  242.4 1.1 collective-permute-start.31
  243.5 1.0 collective-permute-start.33
  245.3 3.1 %collective-permute-done.33 = bf16[96,576]{1,0:T(8,128)(2,1)S(1)} collective-permute-done((bf16[96,576]{1,0:T(8,128)(2,1)S(1)}, bf16[96,576]{1,0:T(8,128)(2,1)S(1)}, u32[]{:S(2)}, u32[]{:S(2)}) %collective-permute-start.33) | collective-permute-done | bytes 110624 | tf_op jit(solution)/shard_map/ppermute | solution.py:536
  249.3 1.1 collective-permute-start.34
  251.1 3.7 %collective-permute-done.34 = bf16[96,576]{1,0:T(8,128)(2,1)S(1)} collective-permute-done((bf16[96,576]{1,0:T(8,128)(2,1)S(1)}, bf16[96,576]{1,0:T(8,128)(2,1)S(1)}, u32[]{:S(2)}, u32[]{:S(2)}) %collective-permute-start.34) | collective-permute-done | bytes 110624 | tf_op jit(solution)/shard_map/ppermute | solution.py:536
  256.6 1.4 collective-permute-start.27
  258.0 2.7 %collective-permute-done.35 = bf16[96,576]{1,0:T(8,128)(2,1)S(1)} collective-permute-done((bf16[96,576]{1,0:T(8,128)(2,1)S(1)}, bf16[96,576]{1,0:T(8,128)(2,1)S(1)}, u32[]{:S(2)}, u32[]{:S(2)}) %collective-permute-start.35) | collective-permute-done | bytes 110624 | tf_op jit(solution)/shard_map/ppermute | solution.py:536
  260.6 0.9 convert_add_fusion
  261.8 1.2 collective-permute-done.36
  265.3 1.3 shard_map.371
  (220 shorter events, 44.7 us)
Async XLA Ops:
  0.6 89.7 %copy-start.11 = (s32[640,1]{1,0:T(8,128)S(1)}, s32[640,1]{1,0:T(8,128)}, u32[]{:S(2)}) copy-start(s32[640,1]{1,0:T(8,128)} %constant.236.clone.refs_15_) | copy-start | bytes 7684
  0.7 89.7 %copy-start.12 = (s32[640,1]{1,0:T(8,128)S(1)}, s32[640,1]{1,0:T(8,128)}, u32[]{:S(2)}) copy-start(s32[640,1]{1,0:T(8,128)} %constant.235.clone.refs_14_) | copy-start | bytes 7684
  0.7 89.7 %copy-start.2 = (bf16[256,768]{1,0:T(8,128)(2,1)S(1)}, bf16[256,768]{1,0:T(8,128)(2,1)}, u32[]{:S(2)}) copy-start(bf16[256,768]{1,0:T(8,128)(2,1)} %x_own.1) | copy-start | bytes 1179652
  0.7 83.4 %copy-start.23 = (s32[256]{0:T(256)S(1)}, s32[256]{0:T(256)}, u32[]{:S(2)}) copy-start(s32[256]{0:T(256)} %param.43) | copy-start | bytes 3076
  0.7 83.5 %copy-start.21 = (s32[256,1]{0,1:T(1,128)S(1)}, s32[256,1]{0,1:T(1,128)}, u32[]{:S(2)}) copy-start(s32[256,1]{0,1:T(1,128)} %param.42) | copy-start | bytes 3076
  0.7 89.7 %copy-start = (bf16[256,768]{1,0:T(8,128)(2,1)S(1)}, bf16[256,768]{1,0:T(8,128)(2,1)}, u32[]{:S(2)}) copy-start(bf16[256,768]{1,0:T(8,128)(2,1)} %refs_4_.6) | copy-start | bytes 1179652
  5.1 1.4 collective-permute-start.1
  6.6 6.6 %collective-permute-start.3 = (bf16[96,640]{1,0:T(8,128)(2,1)S(1)}, bf16[96,640]{1,0:T(8,128)(2,1)S(1)}, u32[]{:S(2)}, u32[]{:S(2)}) collective-permute-start(bf16[96,640]{1,0:T(8,128)(2,1)S(1)} %maximum_select_fusion.refs_6_), channel_id=1, source_target_pairs={{8,0},{16,8},{24,16},{28,24},{20,28},{12,20},{4,12},{0,4},{9,1},{1... | collective-permute-start | bytes 368648 | tf_op jit(solution)/shard_map/ppermute | solution.py:500
  9.5 5.4 %collective-permute-start.2 = (bf16[96,640]{1,0:T(8,128)(2,1)S(1)}, bf16[96,640]{1,0:T(8,128)(2,1)S(1)}, u32[]{:S(2)}, u32[]{:S(2)}) collective-permute-start(bf16[96,640]{1,0:T(8,128)(2,1)S(1)} %maximum_select_fusion.refs_6_), channel_id=1, source_target_pairs={{0,8},{8,16},{16,24},{24,28},{28,20},{20,12},{12,4},{4,0},{1,9},{9... | collective-permute-start | bytes 368648 | tf_op jit(solution)/shard_map/ppermute | solution.py:499
  13.2 4.9 %collective-permute-start.5 = (bf16[96,640]{1,0:T(8,128)(2,1)S(1)}, bf16[96,640]{1,0:T(8,128)(2,1)S(1)}, u32[]{:S(2)}, u32[]{:S(2)}) collective-permute-start(bf16[96,640]{1,0:T(8,128)(2,1)S(1)} %collective-permute-done.3.refs_8_), channel_id=1, source_target_pairs={{8,0},{16,8},{24,16},{28,24},{20,28},{12,20},{4,12},{0,4},{9,1},{1... | collective-permute-start | bytes 368648 | tf_op jit(solution)/shard_map/ppermute | solution.py:500
  14.8 5.5 %collective-permute-start.4 = (bf16[96,640]{1,0:T(8,128)(2,1)S(1)}, bf16[96,640]{1,0:T(8,128)(2,1)S(1)}, u32[]{:S(2)}, u32[]{:S(2)}) collective-permute-start(bf16[96,640]{1,0:T(8,128)(2,1)S(1)} %collective-permute-done.2.refs_7_), channel_id=1, source_target_pairs={{0,8},{8,16},{16,24},{24,28},{28,20},{20,12},{12,4},{4,0},{1,9},{9... | collective-permute-start | bytes 368648 | tf_op jit(solution)/shard_map/ppermute | solution.py:499
  16.1 5.3 %collective-permute-start.13 = (bf16[48,192]{1,0:T(8,128)(2,1)S(1)}, bf16[48,192]{1,0:T(8,128)(2,1)S(1)}, u32[]{:S(2)}, u32[]{:S(2)}) collective-permute-start(bf16[48,192]{1,0:T(8,128)(2,1)S(1)} %get-tuple-element.103), channel_id=1, source_target_pairs={{0,2},{2,0},{1,3},{3,1},{4,6},{6,4},{5,7},{7,5},{8,10},{10,8},{9,1... | collective-permute-start | bytes 55304 | tf_op jit(solution)/shard_map/ppermute | solution.py:471
  18.1 5.1 %collective-permute-start.7 = (bf16[96,640]{1,0:T(8,128)(2,1)S(1)}, bf16[96,640]{1,0:T(8,128)(2,1)S(1)}, u32[]{:S(2)}, u32[]{:S(2)}) collective-permute-start(bf16[96,640]{1,0:T(8,128)(2,1)S(1)} %collective-permute-done.5.refs_10_), channel_id=1, source_target_pairs={{8,0},{16,8},{24,16},{28,24},{20,28},{12,20},{4,12},{0,4},{9,1},{1... | collective-permute-start | bytes 368648 | tf_op jit(solution)/shard_map/ppermute | solution.py:500
  20.4 4.9 %collective-permute-start.6 = (bf16[96,640]{1,0:T(8,128)(2,1)S(1)}, bf16[96,640]{1,0:T(8,128)(2,1)S(1)}, u32[]{:S(2)}, u32[]{:S(2)}) collective-permute-start(bf16[96,640]{1,0:T(8,128)(2,1)S(1)} %collective-permute-done.4.refs_9_), channel_id=1, source_target_pairs={{0,8},{8,16},{16,24},{24,28},{28,20},{20,12},{12,4},{4,0},{1,9},{9... | collective-permute-start | bytes 368648 | tf_op jit(solution)/shard_map/ppermute | solution.py:499
  21.4 4.3 %collective-permute-start.14 = (bf16[96,192]{1,0:T(8,128)(2,1)S(1)}, bf16[96,192]{1,0:T(8,128)(2,1)S(1)}, u32[]{:S(2)}, u32[]{:S(2)}) collective-permute-start(bf16[96,192]{1,0:T(8,128)(2,1)S(1)} %maximum_select_fusion.5), channel_id=1, source_target_pairs={{0,1},{1,0},{2,3},{3,2},{4,5},{5,4},{6,7},{7,6},{8,9},{9,8},{10,11... | collective-permute-start | bytes 110600 | tf_op jit(solution)/shard_map/ppermute | solution.py:471
  23.2 39.8 %collective-permute-start = (bf16[256,768]{1,0:T(8,128)(2,1)}, bf16[256,768]{1,0:T(8,128)(2,1)}, u32[]{:S(2)}, u32[]{:S(2)}) collective-permute-start(bf16[256,768]{1,0:T(8,128)(2,1)} %x_own.1), channel_id=1, source_target_pairs={{0,2},{2,0},{1,3},{3,1},{4,6},{6,4},{5,7},{7,5},{8,10},{10,8},{9,1... | collective-permute-start | bytes 1179656 | tf_op jit(solution)/shard_map/ppermute | solution.py:471
  23.2 4.5 %collective-permute-start.9 = (bf16[48,640]{1,0:T(8,128)(2,1)S(1)}, bf16[48,640]{1,0:T(8,128)(2,1)S(1)}, u32[]{:S(2)}, u32[]{:S(2)}) collective-permute-start(bf16[48,640]{1,0:T(8,128)(2,1)S(1)} %slice.89), channel_id=1, source_target_pairs={{8,0},{16,8},{24,16},{28,24},{20,28},{12,20},{4,12},{0,4},{9,1},{1... | collective-permute-start | bytes 184328 | tf_op jit(solution)/shard_map/ppermute | solution.py:506
  25.3 4.3 %collective-permute-start.8 = (bf16[48,640]{1,0:T(8,128)(2,1)S(1)}, bf16[48,640]{1,0:T(8,128)(2,1)S(1)}, u32[]{:S(2)}, u32[]{:S(2)}) collective-permute-start(bf16[48,640]{1,0:T(8,128)(2,1)S(1)} %slice.88), channel_id=1, source_target_pairs={{0,8},{8,16},{16,24},{24,28},{28,20},{20,12},{12,4},{4,0},{1,9},{9... | collective-permute-start | bytes 184328 | tf_op jit(solution)/shard_map/ppermute | solution.py:505
  29.5 4.4 %collective-permute-start.16 = (bf16[96,384]{1,0:T(8,128)(2,1)S(1)}, bf16[96,384]{1,0:T(8,128)(2,1)S(1)}, u32[]{:S(2)}, u32[]{:S(2)}) collective-permute-start(bf16[96,384]{1,0:T(8,128)(2,1)S(1)} %pad_maximum_fusion.refs_1_), channel_id=1, source_target_pairs={{8,0},{16,8},{24,16},{28,24},{20,28},{12,20},{4,12},{0,4},{9,1},{1... | collective-permute-start | bytes 221192 | tf_op jit(solution)/shard_map/ppermute | solution.py:500
  31.1 4.7 %collective-permute-start.15 = (bf16[96,384]{1,0:T(8,128)(2,1)S(1)}, bf16[96,384]{1,0:T(8,128)(2,1)S(1)}, u32[]{:S(2)}, u32[]{:S(2)}) collective-permute-start(bf16[96,384]{1,0:T(8,128)(2,1)S(1)} %pad_maximum_fusion.refs_1_), channel_id=1, source_target_pairs={{0,8},{8,16},{16,24},{24,28},{28,20},{20,12},{12,4},{4,0},{1,9},{9... | collective-permute-start | bytes 221192 | tf_op jit(solution)/shard_map/ppermute | solution.py:499
  33.9 5.1 %collective-permute-start.18 = (bf16[96,384]{1,0:T(8,128)(2,1)S(1)}, bf16[96,384]{1,0:T(8,128)(2,1)S(1)}, u32[]{:S(2)}, u32[]{:S(2)}) collective-permute-start(bf16[96,384]{1,0:T(8,128)(2,1)S(1)} %collective-permute-done.16.refs_3_), channel_id=1, source_target_pairs={{8,0},{16,8},{24,16},{28,24},{20,28},{12,20},{4,12},{0,4},{9,1},{1... | collective-permute-start | bytes 221192 | tf_op jit(solution)/shard_map/ppermute | solution.py:500
  35.8 4.7 %collective-permute-start.17 = (bf16[96,384]{1,0:T(8,128)(2,1)S(1)}, bf16[96,384]{1,0:T(8,128)(2,1)S(1)}, u32[]{:S(2)}, u32[]{:S(2)}) collective-permute-start(bf16[96,384]{1,0:T(8,128)(2,1)S(1)} %collective-permute-done.15.refs_2_), channel_id=1, source_target_pairs={{0,8},{8,16},{16,24},{24,28},{28,20},{20,12},{12,4},{4,0},{1,9},{9... | collective-permute-start | bytes 221192 | tf_op jit(solution)/shard_map/ppermute | solution.py:499
  39.0 4.4 %collective-permute-start.20 = (bf16[96,384]{1,0:T(8,128)(2,1)S(1)}, bf16[96,384]{1,0:T(8,128)(2,1)S(1)}, u32[]{:S(2)}, u32[]{:S(2)}) collective-permute-start(bf16[96,384]{1,0:T(8,128)(2,1)S(1)} %collective-permute-done.18.refs_5_), channel_id=1, source_target_pairs={{8,0},{16,8},{24,16},{28,24},{20,28},{12,20},{4,12},{0,4},{9,1},{1... | collective-permute-start | bytes 221192 | tf_op jit(solution)/shard_map/ppermute | solution.py:500
  40.6 4.4 %collective-permute-start.19 = (bf16[96,384]{1,0:T(8,128)(2,1)S(1)}, bf16[96,384]{1,0:T(8,128)(2,1)S(1)}, u32[]{:S(2)}, u32[]{:S(2)}) collective-permute-start(bf16[96,384]{1,0:T(8,128)(2,1)S(1)} %collective-permute-done.17.refs_4_), channel_id=1, source_target_pairs={{0,8},{8,16},{16,24},{24,28},{28,20},{20,12},{12,4},{4,0},{1,9},{9... | collective-permute-start | bytes 221192 | tf_op jit(solution)/shard_map/ppermute | solution.py:499
  43.3 18.8 %collective-permute-start.22 = (bf16[48,384]{1,0:T(8,128)(2,1)S(1)}, bf16[48,384]{1,0:T(8,128)(2,1)S(1)}, u32[]{:S(2)}, u32[]{:S(2)}) collective-permute-start(bf16[48,384]{1,0:T(8,128)(2,1)S(1)} %slice.91), channel_id=1, source_target_pairs={{8,0},{16,8},{24,16},{28,24},{20,28},{12,20},{4,12},{0,4},{9,1},{1... | collective-permute-start | bytes 110600 | tf_op jit(solution)/shard_map/ppermute | solution.py:506
  44.9 17.2 %collective-permute-start.21 = (bf16[48,384]{1,0:T(8,128)(2,1)S(1)}, bf16[48,384]{1,0:T(8,128)(2,1)S(1)}, u32[]{:S(2)}, u32[]{:S(2)}) collective-permute-start(bf16[48,384]{1,0:T(8,128)(2,1)S(1)} %slice.90), channel_id=1, source_target_pairs={{0,8},{8,16},{16,24},{24,28},{28,20},{20,12},{12,4},{4,0},{1,9},{9... | collective-permute-start | bytes 110600 | tf_op jit(solution)/shard_map/ppermute | solution.py:505
  62.8 27.6 %collective-permute-start.23 = (bf16[768,384]{1,0:T(8,128)(2,1)S(1)}, bf16[768,384]{1,0:T(8,128)(2,1)S(1)}, u32[]{:S(2)}, u32[]{:S(2)}) collective-permute-start(bf16[768,384]{1,0:T(8,128)(2,1)S(1)} %shard_map.365.refs_6_.refs_12_), channel_id=1, source_target_pairs={{0,2},{2,0},{1,3},{3,1},{4,6},{6,4},{5,7},{7,5},{8,10},{10,8},{9,1... | collective-permute-start | bytes 1769480 | tf_op jit(solution)/shard_map/ppermute | solution.py:471
  81.9 6.3 %collective-permute-start.10 = (bf16[256,256]{1,0:T(8,128)(2,1)S(1)}, bf16[256,256]{1,0:T(8,128)(2,1)S(1)}, u32[]{:S(2)}, u32[]{:S(2)}) collective-permute-start(bf16[256,256]{1,0:T(8,128)(2,1)S(1)} %get-tuple-element.38.refs_2_), channel_id=1, source_target_pairs={{0,1},{1,0},{2,3},{3,2},{4,5},{5,4},{6,7},{7,6},{8,9},{9,8},{10,11... | collective-permute-start | bytes 393224 | tf_op jit(solution)/shard_map/ppermute | solution.py:471
  83.5 6.9 %collective-permute-start.12 = (bf16[256,256]{1,0:T(8,128)(2,1)S(1)}, bf16[256,256]{1,0:T(8,128)(2,1)}, u32[]{:S(2)}, u32[]{:S(2)}) collective-permute-start(bf16[256,256]{1,0:T(8,128)(2,1)S(1)} %get-tuple-element.39.refs_3_), channel_id=1, source_target_pairs={{0,3},{1,2},{2,1},{3,0},{4,7},{5,6},{6,5},{7,4},{8,11},{9,10},{10,... | collective-permute-start | bytes 393224 | tf_op jit(solution)/shard_map/ppermute | solution.py:659
  83.8 6.6 %collective-permute-start.11 = (bf16[256,256]{1,0:T(8,128)(2,1)S(1)}, bf16[256,256]{1,0:T(8,128)(2,1)}, u32[]{:S(2)}, u32[]{:S(2)}) collective-permute-start(bf16[256,256]{1,0:T(8,128)(2,1)S(1)} %get-tuple-element.39.refs_3_), channel_id=1, source_target_pairs={{0,2},{2,0},{1,3},{3,1},{4,6},{6,4},{5,7},{7,5},{8,10},{10,8},{9,1... | collective-permute-start | bytes 393224 | tf_op jit(solution)/shard_map/ppermute | solution.py:471
  85.3 81.8 %copy-start.42 = (s32[1,1280]{1,0:T(1,128)S(1)}, s32[1,1280]{1,0:T(1,128)}, u32[]{:S(2)}) copy-start(s32[1,1280]{1,0:T(1,128)} %constant.240.clone.refs_4_) | copy-start | bytes 15364
  85.3 81.8 %copy-start.43 = (s32[1,1280]{1,0:T(1,128)S(1)}, s32[1,1280]{1,0:T(1,128)}, u32[]{:S(2)}) copy-start(s32[1,1280]{1,0:T(1,128)} %constant.239.clone.refs_3_) | copy-start | bytes 15364
  94.5 86.2 %copy-start.26 = (s32[2]{0:T(128)S(1)}, s32[2]{0:T(128)}, u32[]{:S(2)}) copy-start(s32[2]{0:T(128)} %copy-done.25) | copy-start | bytes 28
  124.8 55.9 %copy-start.14 = (f32[8,768]{1,0:T(8,128)S(1)}, f32[8,768]{1,0:T(8,128)}, u32[]{:S(2)}) copy-start(f32[8,768]{1,0:T(8,128)} %copy-done.13) | copy-start | bytes 73732
  137.6 54.8 %copy-start.40 = (s32[1,4]{1,0:T(1,128)S(1)}, s32[1,4]{1,0:T(1,128)}, u32[]{:S(2)}) copy-start(s32[1,4]{1,0:T(1,128)} %refs_1_.5) | copy-start | bytes 52
  169.2 11.5 %collective-permute-start.24 = (bf16[256,768]{1,0:T(8,128)(2,1)}, bf16[256,768]{1,0:T(8,128)(2,1)}, u32[]{:S(2)}, u32[]{:S(2)}) collective-permute-start(bf16[256,768]{1,0:T(8,128)(2,1)} %shard_map.368.refs_1_), channel_id=1, source_target_pairs={{0,1},{1,0},{2,3},{3,2},{4,5},{5,4},{6,7},{7,6},{8,9},{9,8},{10,11... | collective-permute-start | bytes 1179656 | tf_op jit(solution)/shard_map/ppermute | solution.py:471
  186.0 6.4 %collective-permute-start.25 = (bf16[256,768]{1,0:T(8,128)(2,1)S(1)}, bf16[256,768]{1,0:T(8,128)(2,1)S(1)}, u32[]{:S(2)}, u32[]{:S(2)}) collective-permute-start(bf16[256,768]{1,0:T(8,128)(2,1)S(1)} %get-tuple-element.53.refs_10_.refs_0_), channel_id=1, source_target_pairs={{0,2},{2,0},{1,3},{3,1},{4,6},{6,4},{5,7},{7,5},{8,10},{10,8},{9,1... | collective-permute-start | bytes 1179656 | tf_op jit(solution)/shard_map/ppermute | solution.py:471
  204.8 51.7 %copy-start.10 = (bf16[256,768]{1,0:T(8,128)(2,1)S(1)}, bf16[256,768]{1,0:T(8,128)(2,1)}, u32[]{:S(2)}) copy-start(bf16[256,768]{1,0:T(8,128)(2,1)} %copy-done.9) | copy-start | bytes 1179652
  204.8 2.3 collective-permute-start.46
  205.9 59.3 %copy-start.5 = (f32[256,768]{1,0:T(8,128)S(1)}, f32[256,768]{1,0:T(8,128)}, u32[]{:S(2)}) copy-start(f32[256,768]{1,0:T(8,128)} %copy-done.4) | copy-start | bytes 2359300
  206.0 9.9 %collective-permute-start.37 = (bf16[48,256]{1,0:T(8,128)(2,1)S(1)}, bf16[48,256]{1,0:T(8,128)(2,1)S(1)}, u32[]{:S(2)}, u32[]{:S(2)}) collective-permute-start(bf16[48,256]{1,0:T(8,128)(2,1)S(1)} %get-tuple-element.94), channel_id=1, source_target_pairs={{0,8},{8,16},{16,24},{24,28},{28,20},{20,12},{12,4},{4,0},{1,9},{9... | collective-permute-start | bytes 73736 | tf_op jit(solution)/shard_map/ppermute | solution.py:535
  207.1 7.1 %collective-permute-start.47 = (f32[32,128]{1,0:T(8,128)S(1)}, f32[32,128]{1,0:T(8,128)S(1)}, u32[]{:S(2)}, u32[]{:S(2)}) collective-permute-start(f32[32,128]{1,0:T(8,128)S(1)} %add.553), channel_id=1, source_target_pairs={{0,1},{1,0},{2,3},{3,2},{4,5},{5,4},{6,7},{7,6},{8,9},{9,8},{10,11... | collective-permute-start | bytes 49160 | tf_op jit(solution)/shard_map/ppermute | solution.py:552
  213.4 14.3 %collective-permute-start.41 = (bf16[48,256]{1,0:T(8,128)(2,1)S(1)}, bf16[48,256]{1,0:T(8,128)(2,1)S(1)}, u32[]{:S(2)}, u32[]{:S(2)}) collective-permute-start(bf16[48,256]{1,0:T(8,128)(2,1)S(1)} %get-tuple-element.95), channel_id=1, source_target_pairs={{8,0},{16,8},{24,16},{28,24},{20,28},{12,20},{4,12},{0,4},{9,1},{1... | collective-permute-start | bytes 73736 | tf_op jit(solution)/shard_map/ppermute | solution.py:536
  214.2 3.9 %collective-permute-start.48 = (f32[32,128]{1,0:T(8,128)S(1)}, f32[32,128]{1,0:T(8,128)S(1)}, u32[]{:S(2)}, u32[]{:S(2)}) collective-permute-start(f32[32,128]{1,0:T(8,128)S(1)} %add.554), channel_id=1, source_target_pairs={{0,4},{4,0},{8,12},{12,8},{16,20},{20,16},{24,28},{28,24},{1,5},{5... | collective-permute-start | bytes 49160 | tf_op jit(solution)/shard_map/ppermute | solution.py:552
  215.9 5.9 %collective-permute-start.38 = (bf16[96,256]{1,0:T(8,128)(2,1)S(1)}, bf16[96,256]{1,0:T(8,128)(2,1)S(1)}, u32[]{:S(2)}, u32[]{:S(2)}) collective-permute-start(bf16[96,256]{1,0:T(8,128)(2,1)S(1)} %add_convert_fusion.12), channel_id=1, source_target_pairs={{0,8},{8,16},{16,24},{24,28},{28,20},{20,12},{12,4},{4,0},{1,9},{9... | collective-permute-start | bytes 147464 | tf_op jit(solution)/shard_map/ppermute | solution.py:535
  218.1 3.7 %collective-permute-start.49 = (f32[32,128]{1,0:T(8,128)S(1)}, f32[32,128]{1,0:T(8,128)S(1)}, u32[]{:S(2)}, u32[]{:S(2)}) collective-permute-start(f32[32,128]{1,0:T(8,128)S(1)} %add.555), channel_id=1, source_target_pairs={{0,8},{4,12},{8,0},{12,4},{16,24},{20,28},{24,16},{28,20},{1,9},{5... | collective-permute-start | bytes 49160 | tf_op jit(solution)/shard_map/ppermute | solution.py:552
  219.2 4.3 %collective-permute-start.28 = (bf16[48,576]{1,0:T(8,128)(2,1)S(1)}, bf16[48,576]{1,0:T(8,128)(2,1)S(1)}, u32[]{:S(2)}, u32[]{:S(2)}) collective-permute-start(bf16[48,576]{1,0:T(8,128)(2,1)S(1)} %get-tuple-element.90), channel_id=1, source_target_pairs={{0,8},{8,16},{16,24},{24,28},{28,20},{20,12},{12,4},{4,0},{1,9},{9... | collective-permute-start | bytes 165896 | tf_op jit(solution)/shard_map/ppermute | solution.py:535
  220.2 20.4 %collective-permute-start.32 = (bf16[48,576]{1,0:T(8,128)(2,1)S(1)}, bf16[48,576]{1,0:T(8,128)(2,1)S(1)}, u32[]{:S(2)}, u32[]{:S(2)}) collective-permute-start(bf16[48,576]{1,0:T(8,128)(2,1)S(1)} %get-tuple-element.91), channel_id=1, source_target_pairs={{8,0},{16,8},{24,16},{28,24},{20,28},{12,20},{4,12},{0,4},{9,1},{1... | collective-permute-start | bytes 165896 | tf_op jit(solution)/shard_map/ppermute | solution.py:536
  221.8 34.6 %collective-permute-start.26 = (bf16[256,768]{1,0:T(8,128)(2,1)}, bf16[256,768]{1,0:T(8,128)(2,1)S(1)}, u32[]{:S(2)}, u32[]{:S(2)}) collective-permute-start(bf16[256,768]{1,0:T(8,128)(2,1)} %get-tuple-element.56), channel_id=1, source_target_pairs={{0,2},{2,0},{1,3},{3,1},{4,6},{6,4},{5,7},{7,5},{8,10},{10,8},{9,1... | collective-permute-start | bytes 1179656 | tf_op jit(solution)/shard_map/ppermute | solution.py:471
  221.9 4.9 %collective-permute-start.50 = (f32[32,128]{1,0:T(8,128)S(1)}, f32[32,128]{1,0:T(8,128)S(1)}, u32[]{:S(2)}, u32[]{:S(2)}) collective-permute-start(f32[32,128]{1,0:T(8,128)S(1)} %add.556), channel_id=1, source_target_pairs={{0,16},{4,20},{8,24},{12,28},{16,0},{20,4},{24,8},{28,12},{1,17},{... | collective-permute-start | bytes 49160 | tf_op jit(solution)/shard_map/ppermute | solution.py:552
  223.5 4.2 %collective-permute-start.39 = (bf16[96,256]{1,0:T(8,128)(2,1)S(1)}, bf16[96,256]{1,0:T(8,128)(2,1)S(1)}, u32[]{:S(2)}, u32[]{:S(2)}) collective-permute-start(bf16[96,256]{1,0:T(8,128)(2,1)S(1)} %add_convert_fusion.11), channel_id=1, source_target_pairs={{0,8},{8,16},{16,24},{24,28},{28,20},{20,12},{12,4},{4,0},{1,9},{9... | collective-permute-start | bytes 147464 | tf_op jit(solution)/shard_map/ppermute | solution.py:535
  226.7 10.6 %collective-permute-start.29 = (bf16[96,576]{1,0:T(8,128)(2,1)S(1)}, bf16[96,576]{1,0:T(8,128)(2,1)S(1)}, u32[]{:S(2)}, u32[]{:S(2)}) collective-permute-start(bf16[96,576]{1,0:T(8,128)(2,1)S(1)} %add_convert_fusion.6), channel_id=1, source_target_pairs={{0,8},{8,16},{16,24},{24,28},{28,20},{20,12},{12,4},{4,0},{1,9},{9... | collective-permute-start | bytes 331784 | tf_op jit(solution)/shard_map/ppermute | solution.py:535
  227.7 4.1 %collective-permute-start.42 = (bf16[96,256]{1,0:T(8,128)(2,1)S(1)}, bf16[96,256]{1,0:T(8,128)(2,1)S(1)}, u32[]{:S(2)}, u32[]{:S(2)}) collective-permute-start(bf16[96,256]{1,0:T(8,128)(2,1)S(1)} %get-tuple-element.93), channel_id=1, source_target_pairs={{8,0},{16,8},{24,16},{28,24},{20,28},{12,20},{4,12},{0,4},{9,1},{1... | collective-permute-start | bytes 147464 | tf_op jit(solution)/shard_map/ppermute | solution.py:536
  231.9 4.4 %collective-permute-start.43 = (bf16[96,256]{1,0:T(8,128)(2,1)S(1)}, bf16[96,256]{1,0:T(8,128)(2,1)S(1)}, u32[]{:S(2)}, u32[]{:S(2)}) collective-permute-start(bf16[96,256]{1,0:T(8,128)(2,1)S(1)} %add_convert_fusion.8), channel_id=1, source_target_pairs={{8,0},{16,8},{24,16},{28,24},{20,28},{12,20},{4,12},{0,4},{9,1},{1... | collective-permute-start | bytes 147464 | tf_op jit(solution)/shard_map/ppermute | solution.py:536
  234.8 4.1 %collective-permute-start.40 = (bf16[96,256]{1,0:T(8,128)(2,1)S(1)}, bf16[96,256]{1,0:T(8,128)(2,1)S(1)}, u32[]{:S(2)}, u32[]{:S(2)}) collective-permute-start(bf16[96,256]{1,0:T(8,128)(2,1)S(1)} %get-tuple-element.92), channel_id=1, source_target_pairs={{0,8},{8,16},{16,24},{24,28},{28,20},{20,12},{12,4},{4,0},{1,9},{9... | collective-permute-start | bytes 147464 | tf_op jit(solution)/shard_map/ppermute | solution.py:535
  236.3 4.1 %collective-permute-start.44 = (bf16[96,256]{1,0:T(8,128)(2,1)S(1)}, bf16[96,256]{1,0:T(8,128)(2,1)S(1)}, u32[]{:S(2)}, u32[]{:S(2)}) collective-permute-start(bf16[96,256]{1,0:T(8,128)(2,1)S(1)} %add_convert_fusion.7), channel_id=1, source_target_pairs={{8,0},{16,8},{24,16},{28,24},{20,28},{12,20},{4,12},{0,4},{9,1},{1... | collective-permute-start | bytes 147464 | tf_op jit(solution)/shard_map/ppermute | solution.py:536
  237.4 4.9 %collective-permute-start.30 = (bf16[96,576]{1,0:T(8,128)(2,1)S(1)}, bf16[96,576]{1,0:T(8,128)(2,1)S(1)}, u32[]{:S(2)}, u32[]{:S(2)}) collective-permute-start(bf16[96,576]{1,0:T(8,128)(2,1)S(1)} %add_convert_fusion.5), channel_id=1, source_target_pairs={{0,8},{8,16},{16,24},{24,28},{28,20},{20,12},{12,4},{4,0},{1,9},{9... | collective-permute-start | bytes 331784 | tf_op jit(solution)/shard_map/ppermute | solution.py:535
  240.5 4.0 %collective-permute-start.45 = (f32[48,256]{1,0:T(8,128)S(1)}, f32[48,256]{1,0:T(8,128)S(1)}, u32[]{:S(2)}, u32[]{:S(2)}) collective-permute-start(f32[48,256]{1,0:T(8,128)S(1)} %constant_dynamic-slice_fusion.9), channel_id=1, source_target_pairs={{0,2},{2,0},{1,3},{3,1},{4,6},{6,4},{5,7},{7,5},{8,10},{10,8},{9,1... | collective-permute-start | bytes 147464 | tf_op jit(solution)/shard_map/ppermute | solution.py:471
  242.4 15.5 %collective-permute-start.31 = (bf16[96,576]{1,0:T(8,128)(2,1)S(1)}, bf16[96,576]{1,0:T(8,128)(2,1)S(1)}, u32[]{:S(2)}, u32[]{:S(2)}) collective-permute-start(bf16[96,576]{1,0:T(8,128)(2,1)S(1)} %get-tuple-element.88), channel_id=1, source_target_pairs={{0,8},{8,16},{16,24},{24,28},{28,20},{20,12},{12,4},{4,0},{1,9},{9... | collective-permute-start | bytes 331784 | tf_op jit(solution)/shard_map/ppermute | solution.py:535
  243.5 4.9 %collective-permute-start.33 = (bf16[96,576]{1,0:T(8,128)(2,1)S(1)}, bf16[96,576]{1,0:T(8,128)(2,1)S(1)}, u32[]{:S(2)}, u32[]{:S(2)}) collective-permute-start(bf16[96,576]{1,0:T(8,128)(2,1)S(1)} %get-tuple-element.89), channel_id=1, source_target_pairs={{8,0},{16,8},{24,16},{28,24},{20,28},{12,20},{4,12},{0,4},{9,1},{1... | collective-permute-start | bytes 331784 | tf_op jit(solution)/shard_map/ppermute | solution.py:536
  249.3 5.5 %collective-permute-start.34 = (bf16[96,576]{1,0:T(8,128)(2,1)S(1)}, bf16[96,576]{1,0:T(8,128)(2,1)S(1)}, u32[]{:S(2)}, u32[]{:S(2)}) collective-permute-start(bf16[96,576]{1,0:T(8,128)(2,1)S(1)} %add_convert_fusion.2), channel_id=1, source_target_pairs={{8,0},{16,8},{24,16},{28,24},{20,28},{12,20},{4,12},{0,4},{9,1},{1... | collective-permute-start | bytes 331784 | tf_op jit(solution)/shard_map/ppermute | solution.py:536
  255.7 4.9 %collective-permute-start.35 = (bf16[96,576]{1,0:T(8,128)(2,1)S(1)}, bf16[96,576]{1,0:T(8,128)(2,1)S(1)}, u32[]{:S(2)}, u32[]{:S(2)}) collective-permute-start(bf16[96,576]{1,0:T(8,128)(2,1)S(1)} %add_convert_fusion.1), channel_id=1, source_target_pairs={{8,0},{16,8},{24,16},{28,24},{20,28},{12,20},{4,12},{0,4},{9,1},{1... | collective-permute-start | bytes 331784 | tf_op jit(solution)/shard_map/ppermute | solution.py:536
  256.6 8.7 %collective-permute-start.27 = (bf16[256,768]{1,0:T(8,128)(2,1)S(1)}, bf16[256,768]{1,0:T(8,128)(2,1)S(1)}, u32[]{:S(2)}, u32[]{:S(2)}) collective-permute-start(bf16[256,768]{1,0:T(8,128)(2,1)S(1)} %add_convert_fusion.near), channel_id=1, source_target_pairs={{0,1},{1,0},{2,3},{3,2},{4,5},{5,4},{6,7},{7,6},{8,9},{9,8},{10,11... | collective-permute-start | bytes 1179656 | tf_op jit(solution)/shard_map/ppermute | solution.py:471
  261.6 1.4 collective-permute-start.36
  (42 other events, 359.5 us)

commit v2 on v1

--- a/solution.py
+++ b/solution.py
@@ -15,7 +15,7 @@
 LANES = 128
 STRIP = 128
 HEAD_SIZE = 64
-VMEM_BYTES = 50 * 1024 * 1024
+VMEM_BYTES = 60 * 1024 * 1024
 f32 = jnp.float32
 bf16 = jnp.bfloat16
 vmem = pl.BlockSpec(memory_space=pltpu.VMEM)
@@ -122,20 +122,69 @@
     return jnp.where(head_mask(head, lanes), values, 0.0).astype(bf16)
 
 
-def attention_forward(heads, extra_rows, *refs):
-    (meta, offsets, lengths, table, x_own, x_other) = refs[:6]
-    pieces = refs[6 : 6 + extra_rows]
-    (h1, q_out, k_out, v_out, o_own, o_other, lse, wall, gains, strips, o_all) = refs[6 + extra_rows :]
+def half_columns(weight, which):
+    values = weight[...].astype(f32)
+    width = values.shape[1] // 2
+    lanes = width + HEAD_SIZE
+    high = pltpu.roll(values[:, LANES : LANES + lanes], lanes - HEAD_SIZE, 1)
+    picked = jnp.where(which == 0, values[:, :lanes], high)
+    return jnp.where(iota((1, lanes), 1) < width, picked, 0.0)
+
+
+def join(first, second):
+    moved = pltpu.roll(second, HEAD_SIZE, 1)
+    return first[:, :LANES], first[:, LANES:] + moved[:, :LANES], moved[:, LANES:]
+
+
+def pack_rows(*refs):
+    (meta, w_query, w_key, w_value, w_output, w_router, gain_one, gain_two, out) = refs
+    rows = w_query.shape[0]
+    experts = w_router.shape[1]
+    width = w_query.shape[1] // 2
+    lanes = width + HEAD_SIZE
+    lane = iota((1, lanes), 1)
+    diagonal = iota((rows, rows), 0) == iota((rows, rows), 1)
+    placing = (iota((experts, lanes), 0) + width == iota((experts, lanes), 1)).astype(f32)
+    extras = mm(w_router[...], placing.astype(bf16))
+    for index, gain in enumerate((gain_one, gain_two)):
+        column = jnp.sum(
+            jnp.where(diagonal, jnp.broadcast_to(gain[...].astype(f32), (rows, rows)), 0.0),
+            axis=1,
+            keepdims=True,
+        )
+        extras = extras + jnp.where(lane == width + experts + index, column, 0.0)
+    at = 0
+    for which in (meta[0], 1 - meta[0]):
+        blocks = join(half_columns(w_query, which), half_columns(w_key, which))
+        for block in blocks:
+            out[:, at : at + LANES] = block.astype(bf16)
+            at += LANES
+        out[:, at : at + lanes] = (half_columns(w_value, which) + extras).astype(bf16)
+        at += lanes
+    out[:, at:] = w_output[...]
+
+
+def interleave(out, lanes, own, other, place, count):
+    rows = own.shape[0] // count
+    for index in range(count):
+        here = slice(index * rows, (index + 1) * rows)
+        first = pl.multiple_of((2 * index + place) * rows, 16)
+        second = pl.multiple_of((2 * index + 1 - place) * rows, 16)
+        out[pl.ds(first, rows), lanes] = own[here, :]
+        out[pl.ds(second, rows), lanes] = other[here, :]
+
+
+def attention_forward(heads, experts, count, *refs):
+    (meta, lengths, table, x_own, x_other, rows_own, rows_other) = refs[:7]
+    (h1, q_out, k_out, v_out, o_own, o_other, lse, wall, gains, strips, o_all) = refs[7:]
     place = meta[0]
     rows = x_own.shape[0]
     group = 2 * rows
     first_head = place * heads
-    for index, piece in enumerate(pieces):
-        start = pl.multiple_of(offsets[index], 16)
-        wall[pl.ds(start, piece.shape[0]), :] = piece[...]
+    interleave(wall, slice(None), rows_own, rows_other, meta[2], count)
     width = wall.shape[1]
     extras = wall[:, width - LANES :].astype(f32).T
-    gain_at = LANES // 2 + 32
+    gain_at = HEAD_SIZE + experts
     gains[...] = extras[gain_at : gain_at + 8]
     gain_one = gains[0:1]
     for source, start in ((x_own, place * rows), (x_other, (1 - place) * rows)):
@@ -146,7 +195,7 @@
     qkv = mm(h1[...], wall[...])
     lanes = q_out.shape[1]
     q_out[...] = qkv[:, :lanes].astype(bf16)
-    k_out[...] = pltpu.roll(qkv[:, LANES : LANES + lanes], lanes - LANES // 2, 1).astype(bf16)
+    k_out[...] = pltpu.roll(qkv[:, LANES : LANES + lanes], lanes - HEAD_SIZE, 1).astype(bf16)
     v_out[...] = qkv[:, width - lanes :].astype(bf16)
     bias_strips(table, first_head, heads, strips)
     segment_row = segments(lengths, group, 1)
@@ -176,17 +225,9 @@
     o_other[...] = o_all[pl.ds(pl.multiple_of((1 - place) * rows, 16), rows), :]
 
 
-def assemble(count, *refs):
-    offsets = refs[0]
-    out = refs[-1]
-    for index in range(count):
-        piece = refs[1 + index]
-        out[pl.ds(pl.multiple_of(offsets[index], 16), piece.shape[0]), :] = piece[...]
-
-
 def routed(hidden, extras, routes_column, keep_column, experts):
     logits = mm(hidden, extras)
-    lane = iota((1, LANES), 1) - LANES // 2
+    lane = iota((1, LANES), 1) - HEAD_SIZE
     valid = (lane >= 0) & (lane < experts)
     logits = jnp.where(valid, logits, masked_value)
     raised = jnp.where(valid, jnp.exp(logits - jnp.max(logits, axis=1, keepdims=True)), 0.0)
@@ -215,16 +256,23 @@
     return jnp.where(keep_column == 1, routes_column * capacity + rank, -2)
 
 
-def to_experts(experts, capacity, *refs):
-    (x_own, cotangent, o_own, o_tp, o_ctx, o_far, wo_own, wo_ctx, extras, gains) = refs[:10]
-    (routes_row, routes_column, keep_row, keep_column, slot_h, slot_d) = refs[10:16]
-    middle_out, sends = refs[16:]
-    lanes = o_own.shape[1]
-    branch = None
-    for near, far, weights in ((o_own, o_tp, wo_own), (o_ctx, o_far, wo_ctx)):
-        shifted = pltpu.roll(far[...].astype(f32), LANES // 2, 1).astype(bf16)
-        part = mm_nt(near[...], weights[:, :lanes]) + mm_nt(shifted, weights[:, LANES : LANES + lanes])
-        branch = part if branch is None else branch + part
+def heads_of(own, other, place):
+    own = own[...].astype(f32)
+    other = other[...].astype(f32)
+    first = jnp.where(place == 0, own, other)
+    second = jnp.where(place == 0, other, own)
+    return jnp.concatenate(join(first, second), axis=1).astype(bf16)
+
+
+def to_experts(experts, capacity, count, *refs):
+    (meta, x_own, cotangent, o_own, o_tp, o_ctx, o_far, wo_own, wo_tp, wo_ctx, wo_far) = refs[:11]
+    (extras, gains, routes_row, routes_column, keep_row, keep_column, slot_h, slot_d) = refs[11:19]
+    middle_out, sends, wo_out, wo_other = refs[19:]
+    place, start = meta[0], meta[2]
+    interleave(wo_out, slice(None), wo_own, wo_ctx, start, count)
+    interleave(wo_other, slice(None), wo_tp, wo_far, start, count)
+    branch = mm_nt(heads_of(o_own, o_ctx, place), wo_out[...])
+    branch = branch + mm_nt(heads_of(o_tp, o_far, place), wo_other[...])
     middle = x_own[...].astype(f32) + branch
     middle_out[...] = middle
     hidden = (middle * rms_scale(middle) * gains[1:2]).astype(bf16)
@@ -314,9 +362,13 @@
     out[:, width:] = mm(pick_x, rows_in[...]).astype(bf16)
 
 
+def column_of(line):
+    return jnp.broadcast_to(line, (LANES, line.shape[1])).T[:, :1]
+
+
 def middle_backward(experts, *refs):
     (meta, both_own, both_tp, middle_ref, cotangent, extras, gains, routes_column, keep_column) = refs[:9]
-    (result, dmiddle_out, branch_grad, router_grad, gain_grad) = refs[9:]
+    (result, dmiddle_out, branch_grad, router_grad) = refs[9:]
     share = meta[1]
     width = both_own.shape[1] // 2
     own = both_own[...].astype(f32)
@@ -340,42 +392,34 @@
     logit_grad = (
         probs * (prob_grad - jnp.sum(probs * prob_grad, axis=1, keepdims=True))
     ).astype(bf16)
-    router_grad[...] = mm_tn(hidden, logit_grad).astype(bf16)
     hidden_grad = slot_grad + mm_nt(logit_grad, extras[...])
-    gain_grad[...] = jnp.broadcast_to(
-        jnp.sum(hidden_grad * normed, axis=0, keepdims=True), gain_grad.shape
-    )
+    gain_grad = column_of(jnp.sum(hidden_grad * normed, axis=0, keepdims=True))
+    lane = iota((1, LANES), 1)
+    router_grad[...] = jnp.where(
+        lane == HEAD_SIZE + experts, gain_grad, mm_tn(hidden, logit_grad)
+    ).astype(bf16)
     grad = hidden_grad * gain
     dmiddle = upstream + scale * (grad - normed * jnp.mean(grad * normed, axis=1, keepdims=True))
     dmiddle_out[...] = dmiddle
     branch_grad[...] = dmiddle.astype(bf16)
 
 
-def output_grads(*refs):
-    (db_own, db_other, o_own, o_other, router_grad, out) = refs
-    both = mm_tn(db_own[...], o_own[...]) + mm_tn(db_other[...], o_other[...])
-    width = out.shape[1]
-    out[:, : width - LANES] = both[:, : width - LANES].astype(bf16)
-    out[:, width - LANES :] = (
-        both[:, width - LANES :] + router_grad[...].astype(f32)
-    ).astype(bf16)
-
-
-def attention_backward(heads, heads_all, *refs):
+def attention_backward(heads, shard, *refs):
     (meta, lengths, table, x_own, x_other, h1, q_in, k_in, v_in, lse, db_own, db_other) = refs[:12]
-    (wo_own, wall, gain_two) = refs[12:15]
-    (payload, dh1_own, dh1_other, small) = refs[15:19]
-    (strips, sums, do_all, dq, dk, dv, dqkv, dh1) = refs[19:]
-    place, share = meta[0], meta[1]
+    (o_own, o_other, wo_ref, wall, router_grad) = refs[12:17]
+    (payload, dh1_own, dh1_other) = refs[17:20]
+    (strips, sums, do_all, dq, dk, dv, dqkv, dh1) = refs[20:]
+    place = meta[0]
     rows = x_own.shape[0]
     group = 2 * rows
     lanes = q_in.shape[1]
     first_head = place * heads
     own_at = pl.ds(pl.multiple_of(place * rows, 16), rows)
     other_at = pl.ds(pl.multiple_of((1 - place) * rows, 16), rows)
-    weights = wo_own[:, :lanes]
-    do_all[own_at, :] = mm(db_own[...], weights).astype(bf16)
-    do_all[other_at, :] = mm(db_other[...], weights).astype(bf16)
+    for source, at in ((db_own, own_at), (db_other, other_at)):
+        both = mm(source[...], wo_ref[...])
+        high = pltpu.roll(both[:, LANES : LANES + lanes], lanes - HEAD_SIZE, 1)
+        do_all[at, :] = jnp.where(place == 0, both[:, :lanes], high).astype(bf16)
     bias_strips(table, first_head, heads, strips)
     segment_row = segments(lengths, group, 1)
     segment_column = segments(lengths, group, 0)
@@ -418,13 +462,12 @@
                 else:
                     behind[head] = behind[head] + part
         dq[at, :] = dq_total
-    half = LANES // 2
+    half = HEAD_SIZE
     dqkv[:, :LANES] = dq[:, :LANES].astype(bf16)
     shifted = pltpu.roll(dk[...], half, 1)
     dqkv[:, LANES : 2 * LANES] = (dq[:, LANES:] + shifted[:, :LANES]).astype(bf16)
     dqkv[:, 2 * LANES : 3 * LANES] = shifted[:, LANES:].astype(bf16)
     dqkv[:, 3 * LANES :] = dv[...].astype(bf16)
-    payload[...] = mm_tn(h1[...], dqkv[...]).astype(bf16)
     dh1[...] = mm_nt(dqkv[...], wall[...])
     gain_part = None
     for source, at, target in ((x_own, own_at, dh1_own), (x_other, other_at, dh1_other)):
@@ -439,22 +482,58 @@
     picks = (bucket_index(iota((4 * STRIP, 1), 0) - 2 * STRIP) == iota((1, LANES), 1)).astype(f32)
     in_buckets = jnp.dot(diagonals, picks, precision=highest, preferred_element_type=f32)
     lane = iota((1, LANES), 1)
-    row = iota((16, 1), 0)
-    table_grad = jnp.zeros((16, LANES), f32)
+    row = lax.rem(iota((wall.shape[0], 1), 0), shard)
+    riders = jnp.where(lane == HEAD_SIZE, column_of(gain_part), 0.0)
     for head in range(heads):
         line = in_buckets[head : head + 1]
         line = line + jnp.where(lane == buckets - 1, jnp.sum(ahead[head]), 0.0)
         line = line + jnp.where(lane == buckets // 2 - 1, jnp.sum(behind[head]), 0.0)
-        mine = share * (heads_all // 2) + first_head + head
-        table_grad = table_grad + jnp.where(row == mine, line, 0.0)
-    small[...] = jnp.zeros_like(small)
-    small[:16, :] = table_grad
-    gain_rows = gain_part.shape[1] // LANES
-    once = jnp.where(share == 0, 1.0, 0.0)
-    for index in range(gain_rows):
-        at = slice(index * LANES, (index + 1) * LANES)
-        small[16 + index : 17 + index, :] = gain_part[:, at]
-        small[24 + index : 25 + index, :] = gain_two[0:1, at] * once
+        riders = riders + jnp.where(row == head, pltpu.roll(line, HEAD_SIZE + 1, 1), 0.0)
+    width = wall.shape[1]
+    grads = mm_tn(h1[...], dqkv[...])
+    payload[:, : width - LANES] = grads[:, : width - LANES].astype(bf16)
+    payload[:, width - LANES : width] = (grads[:, width - LANES :] + riders).astype(bf16)
+    grads = mm_tn(db_own[...], o_own[...]) + mm_tn(db_other[...], o_other[...])
+    payload[:, width : width + lanes - LANES] = grads[:, : lanes - LANES].astype(bf16)
+    payload[:, width + lanes - LANES :] = (
+        grads[:, lanes - LANES :] + router_grad[...].astype(f32)
+    ).astype(bf16)
+
+
+def shards_of_sums(experts, buckets, heads, *refs):
+    (meta, sums, other, from_tp, from_far) = refs[:5]
+    (query_out, key_out, value_out, output_out, router_out, gain_one, gain_two, table) = refs[5:]
+    place = meta[0]
+    rows, width = query_out.shape[0], query_out.shape[1] // 2
+    lanes = width + HEAD_SIZE
+    wide = 3 * width + HEAD_SIZE
+    own = jnp.where(place == 0, sums[:rows, :], sums[rows : 2 * rows, :])
+    more = other[:rows, :]
+    lane = iota((1, lanes), 1)
+    for at, moved, out in (
+        (0, False, query_out),
+        (LANES, True, key_out),
+        (2 * width, False, value_out),
+        (wide, False, output_out),
+    ):
+        parts = [values[:, at : at + lanes] for values in (own, more)]
+        if moved:
+            parts = [pltpu.roll(part, lanes - HEAD_SIZE, 1) for part in parts]
+        parts = [jnp.where(lane < width, part, 0.0) for part in parts]
+        first = jnp.where(place == 0, parts[0], parts[1])
+        second = jnp.where(place == 0, parts[1], parts[0])
+        for index, block in enumerate(join(first, second)):
+            out[:, index * LANES : (index + 1) * LANES] = block
+    total = (own + more)[:, wide + lanes - LANES :]
+    router_out[...] = total
+    gain_two[...] = total.T[HEAD_SIZE + experts : HEAD_SIZE + experts + 1, :]
+    line = (own + more)[:, wide - LANES : wide] + (from_tp[...] + from_far[...])
+    gain_one[...] = line.T[HEAD_SIZE : HEAD_SIZE + 1, :]
+    own_lines = pltpu.roll(sums[:8, wide - LANES : wide], LANES - HEAD_SIZE - 1, 1)
+    other_lines = pltpu.roll(other[rows : rows + 8, wide - LANES : wide], LANES - HEAD_SIZE - 1, 1)
+    table[...] = jnp.zeros_like(table)
+    table[:heads, :] = jnp.where(place == 0, own_lines, other_lines)[:heads]
+    table[heads : 2 * heads, :] = jnp.where(place == 0, other_lines, own_lines)[:heads]
 
 
 def input_backward(x_own, dmiddle, gains, near, far, out):
@@ -486,35 +565,6 @@
     inverse = np.zeros(count, np.int32)
     inverse[order] = np.arange(count)
     return jnp.asarray(np.array(order, np.int32)), jnp.asarray(inverse)[lax.axis_index("fsdp")]
-
-
-def ring_gather(shard, count):
-    rows = shard.shape[0]
-    order, right, left = ring_steps(count)
-    table, place = ring_place(count)
-    pieces = [shard]
-    starts = [table[place] * rows]
-    going_right, going_left = shard, shard
-    for step in range(1, count // 2):
-        going_right = lax.ppermute(going_right, "fsdp", right)
-        going_left = lax.ppermute(going_left, "fsdp", left)
-        pieces += [going_right, going_left]
-        starts += [table[(place - step) % count] * rows, table[(place + step) % count] * rows]
-    half = rows // 2
-    pieces += [
-        lax.ppermute(going_right[:half], "fsdp", right),
-        lax.ppermute(going_left[half:], "fsdp", left),
-    ]
-    across = table[(place + count // 2) % count] * rows
-    starts += [across, across + half]
-    return pieces, jnp.stack(starts).astype(jnp.int32)
-
-
-def gather_rows(shard, count):
-    rows = shard.shape[0]
-    if rows % 32 == 0 and count % 2 == 0:
-        return ring_gather(shard, count)
-    return [lax.all_gather(shard, "fsdp", axis=0, tiled=True)], jnp.zeros((1,), jnp.int32)
 
 
 def sum_rows(payload, count):
@@ -542,16 +592,6 @@
             return mine(0) + from_left + from_right
         going_right = (mine(step - 1) + from_left).astype(bf16)
         going_left = (mine(1 - step) + from_right).astype(bf16)
-
-
-def sum_everywhere(value, counts):
-    for axis, count in counts:
-        step = 1
-        while step < count:
-            pairs = [(i, i ^ step) for i in range(count)]
-            value = value + lax.ppermute(value, axis, pairs)
-            step *= 2
-    return value
 
 
 def body(
@@ -592,20 +632,29 @@
     buckets = rel_table.shape[0]
     meta = jnp.stack([place, share]).astype(jnp.int32)
 
-    def columns(weight, which):
-        return lax.dynamic_slice_in_dim(weight, which * width, width, 1)
-
-    extras_width = HEAD_SIZE - experts - 2
-    extras_shard = jnp.concatenate(
-        [w_router, gain_attn[:, None], gain_moe[:, None], jnp.zeros((shard_rows, extras_width), bf16)],
-        axis=1,
-    )
-
-    def shard_for(which):
-        return jnp.concatenate(
-            [columns(w_query, which), columns(w_key, which), columns(w_value, which), extras_shard],
-            axis=1,
-        )
+    def full(dims, dtype):
+        return shape(dims, dtype)
+
+    wide = 3 * width + HEAD_SIZE
+    packed = kernel_call(
+        pack_rows,
+        [full((shard_rows, 2 * wide + 2 * width), bf16)],
+        [smem] + [vmem] * 7,
+        moved=512 * 1024,
+    )(meta, w_query, w_key, w_value, w_output, w_router, gain_attn[None, :], gain_moe[None, :])[0]
+    x_other = swap(tokens, "ctx")
+    gathered = lax.all_gather(packed, "fsdp", axis=0, tiled=True)
+    rows_own, rows_other = gathered[:, :wide], swap(gathered[:, wide : 2 * wide], "ctx")
+    wo_own = gathered[:, 2 * wide :]
+    count = fsdp_count
+    start = place
+
+    def ordered(own, other):
+        if shard_rows % 16 == 0:
+            return own, other
+        dims = (fsdp_count, 1, shard_rows, own.shape[1])
+        pair = in_order(own.reshape(dims), other.reshape(dims), 1).reshape(2 * own.shape[0], -1)
+        return pair[: own.shape[0]], pair[own.shape[0] :]
 
     def in_order(own, other, axis):
         return jnp.where(
@@ -614,21 +663,12 @@
             jnp.concatenate([other, own], axis=axis),
         )
 
-    shard = in_order(shard_for(place), swap(shard_for(1 - place), "ctx"), 0)
-    x_other = swap(tokens, "ctx")
-    wo_shard = in_order(columns(w_output, place), swap(columns(w_output, 1 - place), "ctx"), 0)
-    wo_shard = jnp.concatenate([wo_shard, swap(wo_shard, "tp")], axis=1)
-
-    wall_pieces, wall_starts = gather_rows(shard, fsdp_count)
-    wo_shard, *_ = lax.optimization_barrier((wo_shard, *wall_pieces[-2:]))
-    wo_pieces, wo_starts = gather_rows(wo_shard, fsdp_count)
-
-    def full(dims, dtype):
-        return shape(dims, dtype)
-
-    wall_width = shard.shape[1]
+    if shard_rows % 16:
+        count, start = 1, 0 * place
+    meta = jnp.stack([place, share, start]).astype(jnp.int32)
+    rows_own, rows_other = ordered(rows_own, rows_other)
     h1, q, k, v, o_own, o_other, lse, wall, gains = kernel_call(
-        functools.partial(attention_forward, heads, len(wall_pieces)),
+        functools.partial(attention_forward, heads, experts, count),
         [
             full((group, model_width), bf16),
             full((group, lanes), bf16),
@@ -637,22 +677,19 @@
             full((rows, lanes), bf16),
             full((rows, lanes), bf16),
             full((group, LANES), f32),
-            full((model_width, wall_width), bf16),
+            full((model_width, wide), bf16),
             full((8, model_width), f32),
         ],
-        [smem] * 4 + [vmem] * (2 + len(wall_pieces)),
+        [smem] * 3 + [vmem] * 4,
         scratch=[pltpu.VMEM((heads, STRIP, 3 * STRIP), f32), pltpu.VMEM((group, lanes), bf16)],
-        flops=2 * group * model_width * wall_width * 8,
+        flops=2 * group * model_width * wide * 8,
         moved=8 * 1024 * 1024,
-    )(meta, wall_starts, lengths, rel_table, tokens, x_other, *wall_pieces)
-
-    wo_own = kernel_call(
-        functools.partial(assemble, len(wo_pieces)),
-        [full((model_width, wo_shard.shape[1]), bf16)],
-        [smem] + [vmem] * len(wo_pieces),
-        moved=1024 * 1024,
-    )(wo_starts, *wo_pieces)[0]
+    )(meta, lengths, rel_table, tokens, x_other, rows_own, rows_other)
+    wo_tp = swap(wo_own, "tp")
     wo_ctx = swap(wo_own, "ctx")
+    wo_far = swap(wo_tp, "ctx")
+    wo_own, wo_ctx = ordered(wo_own, wo_ctx)
+    wo_tp, wo_far = ordered(wo_tp, wo_far)
 
     o_tp = swap(o_own, "tp")
     o_ctx = swap(o_other, "ctx")
@@ -669,17 +706,22 @@
     routes_row = routes.reshape(1, rows)
     keep_row = keep_mask.reshape(1, rows)
     keep_column = keep_mask.reshape(rows, 1)
-    extras = wall[:, wall_width - LANES :]
-
-    middle, sends = kernel_call(
-        functools.partial(to_experts, experts, capacity),
-        [full((rows, model_width), f32), full((owners * per_owner, model_width), bf16)],
-        [vmem] * 16,
+    extras = wall[:, wide - LANES :]
+
+    middle, sends, wo_full = kernel_call(
+        functools.partial(to_experts, experts, capacity, count),
+        [
+            full((rows, model_width), f32),
+            full((owners * per_owner, model_width), bf16),
+            full((model_width, 2 * width), bf16),
+        ],
+        [smem] + [vmem] * 18,
+        scratch=[pltpu.VMEM((model_width, 2 * width), bf16)],
         flops=2 * rows * model_width * (model_width + 2 * owners * per_owner),
         moved=6 * 1024 * 1024,
     )(
-        tokens, cotangent, o_own, o_tp, o_ctx, o_far, wo_own, wo_ctx, extras, gains,
-        routes_row, routes, keep_row, keep_column, slot_first[:, None], slot_second[:, None],
+        meta, tokens, cotangent, o_own, o_tp, o_ctx, o_far, wo_own, wo_tp, wo_ctx, wo_far, extras,
+        gains, routes_row, routes, keep_row, keep_column, slot_first[:, None], slot_second[:, None],
     )
 
     arrived = lax.all_to_all(
@@ -740,6 +782,7 @@
         outgoing, ("fsdp", "ctx", "tp"), split_axis=0, concat_axis=0, tiled=True
     ).reshape(owners * tp_count * per_owner, part_width)
     w_in_grad, w_out_grad = weight_grads(x_rows, dpre, act, dy_rows)
+    returned, w_in_grad, w_out_grad = lax.optimization_barrier((returned, w_in_grad, w_out_grad))
 
     back_first = np.repeat(slot_first.reshape(owners, 1, per_owner), tp_count, axis=1).reshape(1, -1)
     back_second = np.repeat(slot_second.reshape(owners, 1, per_owner), tp_count, axis=1).reshape(1, -1)
@@ -752,14 +795,13 @@
     )(returned, routes, keep_column, back_first, back_second)[0]
     both_tp = swap(both_own, "tp")
 
-    result, middle_grad, db_own, router_grad, gain_two_part = kernel_call(
+    result, middle_grad, db_own, router_grad = kernel_call(
         functools.partial(middle_backward, experts),
         [
             full((rows, model_width), f32),
             full((rows, model_width), f32),
             full((rows, model_width), bf16),
             full((model_width, LANES), bf16),
-            full((8, model_width), f32),
         ],
         [smem] + [vmem] * 8,
         flops=6 * rows * LANES * model_width,
@@ -767,24 +809,14 @@
     )(meta, both_own, both_tp, middle, cotangent, extras, gains, routes, keep_column)
     db_other = swap(db_own, "ctx")
 
-    payload_one = kernel_call(
-        output_grads,
-        [full((model_width, lanes), bf16)],
-        [vmem] * 5,
-        flops=2 * group * lanes * model_width,
-        moved=2 * 1024 * 1024,
-    )(db_own, db_other, o_own, o_other, router_grad)[0]
-    sums_one = sum_rows(payload_one, fsdp_count)
-
-    payload_two, dh1_own, dh1_other, small = kernel_call(
-        functools.partial(attention_backward, heads, heads_all),
+    payload, dh1_own, dh1_other = kernel_call(
+        functools.partial(attention_backward, heads, model_width // fsdp_count),
         [
-            full((model_width, wall_width), bf16),
+            full((model_width, wide + lanes), bf16),
             full((rows, model_width), bf16),
             full((rows, model_width), bf16),
-            full((32, LANES), f32),
         ],
-        [smem] * 3 + [vmem] * 12,
+        [smem] * 3 + [vmem] * 14,
         scratch=[
             pltpu.VMEM((heads, STRIP, 3 * STRIP), f32),
             pltpu.VMEM((heads, STRIP, 4 * STRIP), f32),
@@ -792,21 +824,19 @@
             pltpu.VMEM((group, lanes), f32),
             pltpu.VMEM((group, lanes), f32),
             pltpu.VMEM((group, lanes), f32),
-            pltpu.VMEM((group, wall_width), bf16),
+            pltpu.VMEM((group, wide), bf16),
             pltpu.VMEM((group, model_width), f32),
         ],
-        flops=2 * group * model_width * wall_width * 12,
+        flops=2 * group * model_width * wide * 12,
         moved=8 * 1024 * 1024,
     )(
         meta, lengths, rel_table, tokens, x_other, h1, q, k, v, lse, db_own, db_other,
-        wo_own, wall, gain_two_part,
+        o_own, o_other, wo_full, wall, router_grad,
     )
 
     dh1_sum = (dh1_own.astype(f32) + swap(dh1_other, "ctx").astype(f32)).astype(bf16)
     dh1_far = swap(dh1_sum, "tp")
-    sums_two = sum_rows(payload_two[:, : 3 * width], fsdp_count)
-    small = sum_everywhere(small, (("ctx", 2), ("tp", tp_count), ("fsdp", fsdp_count)))
-
+    sums = sum_rows(payload, fsdp_count)
     input_grad = kernel_call(
         input_backward,
         [full((rows, model_width), f32)],
@@ -814,38 +844,36 @@
         moved=4 * 1024 * 1024,
     )(tokens, middle_grad, gains, dh1_sum, dh1_far)[0]
 
-    def own_rows(sums):
-        own = lax.dynamic_slice_in_dim(sums, place * shard_rows, shard_rows, 0)
-        other = lax.dynamic_slice_in_dim(sums, (1 - place) * shard_rows, shard_rows, 0)
-        return own, swap(other, "ctx")
-
-    one_own, one_other = own_rows(sums_one)
-    two_own, two_other = own_rows(sums_two)
-    grads = [
-        in_order(two_own[:, at : at + width], two_other[:, at : at + width], 1)
-        for at in (0, width, 2 * width)
-    ]
-    output_grad = in_order(one_own[:, :width], one_other[:, :width], 1)
-    router_total = (one_own + one_other)[:, width : width + experts]
-    first_row = (fsdp_place * 2 + place) * shard_rows
-    gain_rows = model_width // LANES
-
-    def gain_of(first):
-        line = small[first : first + gain_rows].reshape(model_width)
-        return lax.dynamic_slice_in_dim(line, first_row, shard_rows, 0)
-
-    table_total = lax.dynamic_slice_in_dim(small, share * 2 * heads, 2 * heads, 0)[:, :buckets].T
+    not_own = lax.dynamic_slice_in_dim(sums, (1 - place) * shard_rows, shard_rows, 0)
+    riders = slice(wide - LANES, wide)
+    own_riders = lax.dynamic_slice_in_dim(sums, place * shard_rows, shard_rows, 0)[:, riders]
+    other = swap(jnp.concatenate([not_own, sums[:8]], axis=0), "ctx")
+    from_tp = swap(own_riders, "tp")
+    from_far = lax.ppermute(not_own[:, riders], ("ctx", "tp"), [(i, 3 - i) for i in range(4)])
+    shard = full((shard_rows, 2 * width), f32)
+    query_grad, key_grad, value_grad, output_grad, router_sum, gain_one, gain_two, table_grad = kernel_call(
+        functools.partial(shards_of_sums, experts, buckets, heads),
+        [shard] * 4
+        + [
+            full((shard_rows, LANES), f32),
+            full((1, shard_rows), f32),
+            full((1, shard_rows), f32),
+            full((8, LANES), f32),
+        ],
+        [smem] + [vmem] * 4,
+        moved=1024 * 1024,
+    )(meta, sums, other, from_tp, from_far)
     return (
         result,
         input_grad,
-        grads[0],
-        grads[1],
-        grads[2],
+        query_grad,
+        key_grad,
+        value_grad,
         output_grad,
-        router_total,
-        gain_of(16),
-        gain_of(24),
-        table_total,
+        router_sum[:, HEAD_SIZE : HEAD_SIZE + experts],
+        gain_one.reshape(shard_rows),
+        gain_two.reshape(shard_rows),
+        table_grad[: 2 * heads, :buckets].T,
         w_in_grad,
         w_out_grad,
     )

time: 268 us -> 268 us (level)
  waiting for transfers between devices: 55.4 us -> 98.2 us
  blocking collectives: 58.2 us -> 28 us
  starting transfers between devices: 45.3 us -> 23.4 us
  local copies, waits for them, and re-layouts: 32.9 us -> 19.6 us
  Pallas kernels: 41.7 us -> 53.5 us
  between operations: 15 us -> 26.1 us
    all_gather x0 -> x1, waiting for transfers between devices: none -> 44.6 us  [body(): gathered = lax.all_gather(packed, 'fsdp', axis=0, tiled=True)]
    all_to_all x1 -> x0, blocking collectives: 29.5 us -> none  [body(): lax.all_to_all(outgoing, ('fsdp', 'ctx', 'tp'), split_axis=0, concat_axis...]
    ppermute x21 -> x1, starting transfers between devices: 22.5 us -> 0.61 us  [body(): lax.ppermute(not_own[:, riders], ('ctx', 'tp'), [(i, 3 - i) for i in rang...]
    ppermute x21 -> x1, waiting for transfers between devices: 21.8 us -> 0.01 us  [body(): lax.ppermute(not_own[:, riders], ('ctx', 'tp'), [(i, 3 - i) for i in rang...]
    all_to_all x0 -> x1, waiting for transfers between devices: none -> 14.2 us  [body(): lax.all_to_all(outgoing, ('fsdp', 'ctx', 'tp'), split_axis=0, concat_axis...]
    unnamed x114 -> x64, local copies, waits for them, and re-layouts: 22.3 us -> 9.78 us
    pallas_call x5, Pallas kernels: 23.2 us -> 30 us  [the longest x1 13.9 us: body(): kernel_call(functools.partial(attention_backward, heads, model_width // f...]
    ppermute x13, waiting for transfers between devices: 14.2 us -> 20.2 us  [swap(): return lax.ppermute(value, axis, [(0, 1), (1, 0)])]
  transfers between devices with their start and end apart: 51 -> 25, of which waited for: 26 -> 14; matrix products, arithmetic and copies ran while one was open for 10% -> 7% of each run, Pallas kernels for 3% -> 4%
where the time goes in v2:
time: 268 us; the launch traced here: 266 us
  waiting for transfers between devices  98.2 us (37%)
  Pallas kernels  53.5 us (20%)
  blocking collectives  28 us (10%)
  between operations  26.1 us (10%)
  starting transfers between devices  23.4 us (9%)
  local copies, waits for them, and re-layouts  19.6 us (7%)
  matrix products  10.4 us (4%)
  other arithmetic  7.17 us (3%)
    all_gather x1, waiting for transfers between devices, body(): gathered = lax.all_gather(packed, 'fsdp', axis=0, tiled=True)  44.6 us
    all_to_all x1, blocking collectives, body(): lax.all_to_all(sends.reshape(owners, per_owner, model_width), ('fsdp', 'c...  28 us
    ppermute x13, waiting for transfers between devices, swap(): return lax.ppermute(value, axis, [(0, 1), (1, 0)])  20.2 us
    all_to_all x1, waiting for transfers between devices, body(): lax.all_to_all(outgoing, ('fsdp', 'ctx', 'tp'), split_axis=0, concat_axis...  14.2 us
    pallas_call x1, Pallas kernels, body(): kernel_call(functools.partial(attention_backward, heads, model_width // f...  13.9 us
    pallas_call x1, Pallas kernels, body(): kernel_call(functools.partial(expert_kernel, owners, capacity, chunks, gr...  13.2 us
    unnamed x64, local copies, waits for them, and re-layouts  9.78 us
    ppermute x4, waiting for transfers between devices, sum_rows(): from_right = lax.ppermute(going_left, 'fsdp', left).astype(f32)  9.09 us
  transfers between devices with their start and end apart: 25, of which 14 were waited for; matrix products, arithmetic and copies ran while one was open for 7% of the time, Pallas kernels for 4%

profile of v2, /device:TPU:0, one launch (start us, length us, event | category | flops | bytes accessed | tf_op | source)
XLA Modules:
  0.0 266.5 jit_solution(15103961321901898437)
XLA Ops:
  7.2 1.4 copy.42.refs_5_
  9.2 1.8 shard_map.310
  11.0 44.6 %all-gather.2.cloned.1.call-done = bf16[384,1664]{1,0:T(8,128)(2,1)} async-done(((bf16[48,1664]{1,0:T(8,128)(2,1)}), bf16[384,1664]{1,0:T(8,128)(2,1)}) %all-gather.2.cloned.1.call-update) | async-done | bytes 1277968 | tf_op jit(solution)/shard_map/all_gather | solution.py:646
  55.7 2.0 fusion
  58.2 1.0 slice.46.refs_7_
  59.2 1.5 collective-permute-start.5
  60.8 0.7 copy.43.refs_2_
  62.1 6.2 %collective-permute-done.5.refs_8_ = bf16[384,384]{1,0:T(8,128)(2,1)S(1)} collective-permute-done((bf16[384,384]{1,0:T(8,128)(2,1)S(1)}, bf16[384,384]{1,0:T(8,128)(2,1)S(1)}, u32[]{:S(2)}, u32[]{:S(2)}) %collective-permute-start.5) | collective-permute-done | bytes 294944 | tf_op jit(solution)/shard_map/ppermute | solution.py:550
  68.3 0.8 copy-done.26
  69.2 7.0 %shard_map.311 = (bf16[512,768]{1,0:T(8,128)(2,1)}, bf16[512,256]{1,0:T(8,128)(2,1)}, bf16[512,256]{1,0:T(8,128)(2,1)}, bf16[512,256]{1,0:T(8,128)(2,1)}, bf16[2...) custom-call(s32[3]{0:T(128)} %pad_add_fusion.refs_0_, ...), custom_call_target="tpu_custom_call" | custom-call | flops 4026531840 | bytes 8388608 | tf_op jit(solution)/shard_map/pallas_call | solution.py:670
  76.2 1.5 collective-permute-start.2
  78.4 0.8 copy.44.refs_14_.refs_1_.refs_7_
  79.2 0.8 copy.45.refs_16_.refs_2_.refs_8_
  80.0 1.6 slice.36.refs_11_.refs_5_
  81.7 1.1 collective-permute-done.2.refs_4_
  82.8 1.9 collective-permute-done.4.refs_6_
  84.7 0.6 copy-done.18
  85.3 5.4 %shard_map.312 = (f32[256,768]{1,0:T(8,128)}, bf16[640,768]{1,0:T(8,128)(2,1)}, bf16[768,384]{1,0:T(8,128)(2,1)}) custom-call(s32[3]{0:T(128)} %pad_add_fusion.refs_0_, bf16[256,768]{1,0:T(8,128)(2,1)} %x_own.1, bf16[256,768]{1,0:T(8,128)(2,1)} %refs_4_.6, bf16[256,256]{1,0:T(8,128)(2,1)} %get-tuple-element.47.refs_3_.refs_12_, bf16[256,256]{1,0:T(8,128)(2,1)} %copy-done.16, ...), custom_call_target="tpu_custom_call" | custom-call | flops 805306368 | bytes 6291456 | tf_op jit(solution)/shard_map/pallas_call | solution.py:711
  90.8 28.0 %all_to_all.10 = bf16[16,40,768]{2,1,0:T(8,128)(2,1)} all-to-all(bf16[16,40,768]{2,1,0:T(8,128)(2,1)} %bitcast.28), channel_id=1, replica_groups=mesh['fsdp'=8,'ctx'=2,'tp'=2] {'fsdp','ctx'}, dimensions={0} | all-to-all | bytes 1966080 | tf_op jit(solution)/shard_map/all_to_all | solution.py:727
  118.7 13.2 %shard_map.313 = (bf16[32,40,384]{2,1,0:T(8,128)(2,1)}, bf16[2,160,768]{2,1,0:T(8,128)(2,1)}, bf16[2,160,768]{2,1,0:T(8,128)(2,1)}, bf16[2,160,1536]{2,1,0:T(8,128)(2,1)}, bf16[2,160,1536]{2,1,0:T(8,128)(2,1)}) custom-call(bf16[640,768]{1,0:T(8,128)(2,1)} %bitcast.29, s32[320,1]{1,0:T(8,128)} %constant.104.clone.refs_1_, s32[1,320]{1,0:T(1,128)} %constant.105.clone.refs_2_, ...), custom_call_target="tpu_custom_call" | custom-call | flops 3019898880 | bytes 12582912 | tf_op jit(solution)/shard_map/pallas_call | solution.py:748
  132.0 4.8 %all-to-all-start.1 = ((bf16[32,40,384]{2,1,0:T(8,128)(2,1)}), bf16[32,40,384]{2,1,0:T(8,128)(2,1)S(1)}, u32[]{:S(2)}, u32[]{:S(2)}) async-start(bf16[32,40,384]{2,1,0:T(8,128)(2,1)} %get-tuple-element.52), calls=%async_computation.1 | async-start | bytes 1966080 | tf_op jit(solution)/shard_map/all_to_all | solution.py:781
  136.8 5.2 %fusion.3 = f32[2,768,1536]{2,1,0:T(8,128)} fusion(bf16[2,160,768]{2,1,0:T(8,128)(2,1)S(1)} %copy-done.8, bf16[2,160,1536]{2,1,0:T(8,128)(2,1)S(1)} %copy-done.6), kind=kOutput, calls=%fused_computation.18 | convolution fusion | flops 754974720 | bytes 10911744 | tf_op jit(solution)/shard_map/lrd,lrf->ldf/dot_general | solution.py:350
  142.0 5.3 %fusion.4 = f32[2,1536,768]{2,1,0:T(8,128)} fusion(bf16[2,160,1536]{2,1,0:T(8,128)(2,1)S(1)} %copy-done.5, bf16[2,160,768]{2,1,0:T(8,128)(2,1)S(1)} %copy-done.7), kind=kOutput, calls=%fused_computation.19 | convolution fusion | flops 754974720 | bytes 10911744 | tf_op jit(solution)/shard_map/lrf,lrd->lfd/dot_general | solution.py:351
  147.3 14.2 %all-to-all-done.1 = bf16[32,40,384]{2,1,0:T(8,128)(2,1)S(1)} async-done(((bf16[32,40,384]{2,1,0:T(8,128)(2,1)}), bf16[32,40,384]{2,1,0:T(8,128)(2,1)S(1)}, u32[]{:S(2)}, u32[]{:S(2)}) %all-to-all-start.1) | async-done | bytes 983072 | tf_op jit(solution)/shard_map/all_to_all | solution.py:781
  161.4 1.0 copy-done.4
  162.4 3.4 %shard_map.314.refs_1_ = bf16[256,768]{1,0:T(8,128)(2,1)} custom-call(bf16[1280,384]{1,0:T(8,128)(2,1)} %bitcast.27, s32[256,1]{1,0:T(8,128)} %copy.44.refs_14_.refs_1_.refs_7_, s32[256,1]{1,0:T(8,128)} %copy.45.refs_16_.refs_2_.refs_8_, s32[1,1280]{1,0:T(1,128)} %constant.106.clone.refs_3_, s32[1,1280]{1,0:T(1,128)} %constant.107.clone.refs_4_), custom_call_target="tpu_custom_call" | custom-call | flops 503316480 | bytes 2097152 | tf_op jit(solution)/shard_map/pallas_call | solution.py:789
  165.8 1.5 collective-permute-start.8
  167.3 9.9 %collective-permute-done.8.refs_2_ = bf16[256,768]{1,0:T(8,128)(2,1)S(1)} collective-permute-done((bf16[256,768]{1,0:T(8,128)(2,1)}, bf16[256,768]{1,0:T(8,128)(2,1)S(1)}, u32[]{:S(2)}, u32[]{:S(2)}) %collective-permute-start.8) | collective-permute-done | bytes 393248 | tf_op jit(solution)/shard_map/ppermute | solution.py:550
  177.2 0.8 copy-done.11
  178.0 4.2 %shard_map.315 = (f32[256,768]{1,0:T(8,128)}, f32[256,768]{1,0:T(8,128)}, bf16[256,768]{1,0:T(8,128)(2,1)}, bf16[768,128]{1,0:T(8,128)(2,1)}) custom-call(s32[3]{0:T(128)} %pad_add_fusion.refs_0_, bf16[256,768]{1,0:T(8,128)(2,1)} %shard_map.314.refs_1_, bf16[256,768]{1,0:T(8,128)(2,1)} %copy-done.11, f32[256,768]{1,0:T(8,128)} %get-tuple-element.58.refs_3_, ...), custom_call_target="tpu_custom_call" | custom-call | flops 150994944 | bytes 6291456 | tf_op jit(solution)/shard_map/pallas_call | solution.py:798
  189.3 0.7 fusion.2
  190.7 0.7 copy-done.27
  191.5 13.9 %shard_map.316 = (bf16[768,896]{1,0:T(8,128)(2,1)}, bf16[256,768]{1,0:T(8,128)(2,1)}, bf16[256,768]{1,0:T(8,128)(2,1)}) custom-call(s32[3]{0:T(128)} %pad_add_fusion.refs_0_, s32[1,4]{1,0:T(1,128)} %refs_1_.9, f32[32,6]{1,0:T(8,128)} %copy.43.refs_2_, bf16[256,768]{1,0:T(8,128)(2,1)} %x_own.1, bf16[256,768]{1,0:T(8,128)(2,1)} %copy-done.26, ...), custom_call_target="tpu_custom_call" | custom-call | flops 6039797760 | bytes 8388608 | tf_op jit(solution)/shard_map/pallas_call | solution.py:812
  205.3 1.0 constant_dynamic-slice_fusion
  206.3 1.3 collective-permute-start.12
  208.2 3.1 %collective-permute-done.12 = bf16[48,896]{1,0:T(8,128)(2,1)S(1)} collective-permute-done((bf16[48,896]{1,0:T(8,128)(2,1)S(1)}, bf16[48,896]{1,0:T(8,128)(2,1)S(1)}, u32[]{:S(2)}, u32[]{:S(2)}) %collective-permute-start.12) | collective-permute-done | bytes 86048 | tf_op jit(solution)/shard_map/ppermute | solution.py:585
  211.3 0.9 add_convert_fusion.6
  212.3 1.1 collective-permute-start.13
  214.0 4.3 %collective-permute-done.13 = bf16[96,896]{1,0:T(8,128)(2,1)S(1)} collective-permute-done((bf16[96,896]{1,0:T(8,128)(2,1)S(1)}, bf16[96,896]{1,0:T(8,128)(2,1)S(1)}, u32[]{:S(2)}, u32[]{:S(2)}) %collective-permute-start.13) | collective-permute-done | bytes 172064 | tf_op jit(solution)/shard_map/ppermute | solution.py:585
  218.3 1.0 add_convert_fusion.5
  219.3 0.9 collective-permute-start.14
  220.2 1.1 collective-permute-start.16
  222.6 2.1 collective-permute-done.16
  224.7 1.1 add_convert_fusion.4
  225.8 1.8 collective-permute-start.17
  228.2 3.1 %collective-permute-done.17 = bf16[96,896]{1,0:T(8,128)(2,1)S(1)} collective-permute-done((bf16[96,896]{1,0:T(8,128)(2,1)S(1)}, bf16[96,896]{1,0:T(8,128)(2,1)S(1)}, u32[]{:S(2)}, u32[]{:S(2)}) %collective-permute-start.17) | collective-permute-done | bytes 172064 | tf_op jit(solution)/shard_map/ppermute | solution.py:586
  231.3 1.0 add_convert_fusion.2
  232.2 1.8 collective-permute-start.18
  235.7 2.0 collective-permute-done.18
  237.7 1.0 add_convert_fusion.1
  238.7 1.8 collective-permute-start.19
  240.6 0.8 collective-permute-start.11
  241.4 0.8 collective-permute-done.15
  242.2 1.9 collective-permute-done.19
  244.1 1.0 convert_add_fusion.refs_1_
  245.3 1.2 collective-permute-start.21
  247.1 3.0 %collective-permute-done.11.far = bf16[256,768]{1,0:T(8,128)(2,1)S(1)} collective-permute-done((bf16[256,768]{1,0:T(8,128)(2,1)S(1)}, bf16[256,768]{1,0:T(8,128)(2,1)S(1)}, u32[]{:S(2)}, u32[]{:S(2)}) %collective-permute-start.11) | collective-permute-done | bytes 393248 | tf_op jit(solution)/shard_map/ppermute | solution.py:550
  250.1 0.7 copy-done.10
  250.9 2.7 %shard_map.317 = f32[256,768]{1,0:T(8,128)} custom-call(bf16[256,768]{1,0:T(8,128)(2,1)} %x_own.1, f32[256,768]{1,0:T(8,128)} %get-tuple-element.60.dmiddle, f32[8,768]{1,0:T(8,128)} %get-tuple-element.50.refs_12_.refs_6_.gains, bf16[256,768]{1,0:T(8,128)(2,1)} %copy-done.2, bf16[256,768]{1,0:T(8,128)(2,1)} %copy-done.10), custom_call_target="tpu_custom_call" | custom-call | bytes 4194304 | tf_op jit(solution)/shard_map/pallas_call | solution.py:840
  254.3 0.7 copy-done.15
  254.9 2.0 shard_map.318
  256.9 0.8 slice.42
  257.7 0.7 copy.51
  258.4 1.3 slice_bitcast_fusion
  (85 shorter events, 5.1 us)
Async XLA Ops:
  7.2 50.5 %copy-start.1 = (bf16[256,768]{1,0:T(8,128)(2,1)S(1)}, bf16[256,768]{1,0:T(8,128)(2,1)}, u32[]{:S(2)}) copy-start(bf16[256,768]{1,0:T(8,128)(2,1)} %x_own.1) | copy-start | bytes 1179652
  7.2 48.5 %all-gather.2.cloned.1.call-start = ((), (), s32[]{:S(2)}) async-start(), calls=%async_computation.2 | async-start | bytes 1437696 | tf_op jit(solution)/shard_map/all_gather | solution.py:646
  11.0 49.8 %copy-start.24 = (f32[32,6]{0,1:T(8,128)S(1)}, f32[32,6]{0,1:T(8,128)}, u32[]{:S(2)}) copy-start(f32[32,6]{0,1:T(8,128)} %param.32) | copy-start | bytes 2308
  57.7 10.5 %collective-permute-start.1 = (bf16[384,640]{1,0:T(8,128)(2,1)S(1)}, bf16[384,640]{1,0:T(8,128)(2,1)S(1)}, u32[]{:S(2)}, u32[]{:S(2)}) collective-permute-start(bf16[384,640]{1,0:T(8,128)(2,1)S(1)} %get-tuple-element.110), channel_id=1, source_target_pairs={{0,2},{2,0},{1,3},{3,1},{4,6},{6,4},{5,7},{7,5},{8,10},{10,8},{9,1... | collective-permute-start | bytes 1474568 | tf_op jit(solution)/shard_map/ppermute | solution.py:550
  57.7 10.5 %collective-permute-start = (bf16[256,768]{1,0:T(8,128)(2,1)S(1)}, bf16[256,768]{1,0:T(8,128)(2,1)S(1)}, u32[]{:S(2)}, u32[]{:S(2)}) collective-permute-start(bf16[256,768]{1,0:T(8,128)(2,1)S(1)} %copy-done.1), channel_id=1, source_target_pairs={{0,2},{2,0},{1,3},{3,1},{4,6},{6,4},{5,7},{7,5},{8,10},{10,8},{9,1... | collective-permute-start | bytes 1179656 | tf_op jit(solution)/shard_map/ppermute | solution.py:550
  59.2 17.0 %copy-start.3 = (bf16[384,384]{1,0:T(8,128)(2,1)}, bf16[384,384]{1,0:T(8,128)(2,1)S(1)}, u32[]{:S(2)}) copy-start(bf16[384,384]{1,0:T(8,128)(2,1)S(1)} %slice.46.refs_7_) | copy-start | bytes 884740
  59.2 9.0 %collective-permute-start.5 = (bf16[384,384]{1,0:T(8,128)(2,1)S(1)}, bf16[384,384]{1,0:T(8,128)(2,1)S(1)}, u32[]{:S(2)}, u32[]{:S(2)}) collective-permute-start(bf16[384,384]{1,0:T(8,128)(2,1)S(1)} %slice.46.refs_7_), channel_id=1, source_target_pairs={{0,1},{1,0},{2,3},{3,2},{4,5},{5,4},{6,7},{7,6},{8,9},{9,8},{10,11... | collective-permute-start | bytes 884744 | tf_op jit(solution)/shard_map/ppermute | solution.py:550
  62.1 19.6 %collective-permute-start.6 = (bf16[384,384]{1,0:T(8,128)(2,1)S(1)}, bf16[384,384]{1,0:T(8,128)(2,1)S(1)}, u32[]{:S(2)}, u32[]{:S(2)}) collective-permute-start(bf16[384,384]{1,0:T(8,128)(2,1)S(1)} %slice.46.refs_7_), channel_id=1, source_target_pairs={{0,2},{2,0},{1,3},{3,1},{4,6},{6,4},{5,7},{7,5},{8,10},{10,8},{9,1... | collective-permute-start | bytes 884744 | tf_op jit(solution)/shard_map/ppermute | solution.py:550
  68.2 8.0 %copy-start.12 = (bf16[384,384]{1,0:T(8,128)(2,1)}, bf16[384,384]{1,0:T(8,128)(2,1)S(1)}, u32[]{:S(2)}) copy-start(bf16[384,384]{1,0:T(8,128)(2,1)S(1)} %collective-permute-done.5.refs_8_) | copy-start | bytes 884740
  68.2 13.5 %collective-permute-start.7 = (bf16[384,384]{1,0:T(8,128)(2,1)S(1)}, bf16[384,384]{1,0:T(8,128)(2,1)S(1)}, u32[]{:S(2)}, u32[]{:S(2)}) collective-permute-start(bf16[384,384]{1,0:T(8,128)(2,1)S(1)} %collective-permute-done.5.refs_8_), channel_id=1, source_target_pairs={{0,2},{2,0},{1,3},{3,1},{4,6},{6,4},{5,7},{7,5},{8,10},{10,8},{9,1... | collective-permute-start | bytes 884744 | tf_op jit(solution)/shard_map/ppermute | solution.py:550
  68.2 0.8 copy-start.26
  68.2 0.9 copy-start.25
  69.2 9.2 %copy-start.22 = (s32[256,1]{0,1:T(1,128)S(1)}, s32[256,1]{0,1:T(1,128)}, u32[]{:S(2)}) copy-start(s32[256,1]{0,1:T(1,128)} %param.36) | copy-start | bytes 3076
  69.2 10.0 %copy-start.23 = (s32[256]{0:T(256)S(1)}, s32[256]{0:T(256)}, u32[]{:S(2)}) copy-start(s32[256]{0:T(256)} %param.37) | copy-start | bytes 3076
  76.2 6.6 %collective-permute-start.2 = (bf16[256,256]{1,0:T(8,128)(2,1)}, bf16[256,256]{1,0:T(8,128)(2,1)S(1)}, u32[]{:S(2)}, u32[]{:S(2)}) collective-permute-start(bf16[256,256]{1,0:T(8,128)(2,1)} %get-tuple-element.47.refs_3_.refs_12_), channel_id=1, source_target_pairs={{0,1},{1,0},{2,3},{3,2},{4,5},{5,4},{6,7},{7,6},{8,9},{9,8},{10,11... | collective-permute-start | bytes 393224 | tf_op jit(solution)/shard_map/ppermute | solution.py:550
  77.7 5.1 %collective-permute-start.3 = (bf16[256,256]{1,0:T(8,128)(2,1)}, bf16[256,256]{1,0:T(8,128)(2,1)S(1)}, u32[]{:S(2)}, u32[]{:S(2)}) collective-permute-start(bf16[256,256]{1,0:T(8,128)(2,1)} %get-tuple-element.48.refs_13_), channel_id=1, source_target_pairs={{0,2},{2,0},{1,3},{3,1},{4,6},{6,4},{5,7},{7,5},{8,10},{10,8},{9,1... | collective-permute-start | bytes 393224 | tf_op jit(solution)/shard_map/ppermute | solution.py:550
  77.9 6.8 %collective-permute-start.4 = (bf16[256,256]{1,0:T(8,128)(2,1)}, bf16[256,256]{1,0:T(8,128)(2,1)S(1)}, u32[]{:S(2)}, u32[]{:S(2)}) collective-permute-start(bf16[256,256]{1,0:T(8,128)(2,1)} %get-tuple-element.48.refs_13_), channel_id=1, source_target_pairs={{0,3},{1,2},{2,1},{3,0},{4,7},{5,6},{6,5},{7,4},{8,11},{9,10},{10,... | collective-permute-start | bytes 393224 | tf_op jit(solution)/shard_map/ppermute | solution.py:696
  81.7 3.0 %copy-start.13 = (bf16[384,384]{1,0:T(8,128)(2,1)}, bf16[384,384]{1,0:T(8,128)(2,1)S(1)}, u32[]{:S(2)}) copy-start(bf16[384,384]{1,0:T(8,128)(2,1)S(1)} %collective-permute-done.6.refs_9_) | copy-start | bytes 884740
  81.7 3.0 %copy-start.14 = (bf16[384,384]{1,0:T(8,128)(2,1)}, bf16[384,384]{1,0:T(8,128)(2,1)S(1)}, u32[]{:S(2)}) copy-start(bf16[384,384]{1,0:T(8,128)(2,1)S(1)} %collective-permute-done.7.refs_10_) | copy-start | bytes 884740
  82.8 1.9 copy-start.16
  82.8 1.9 copy-start.17
  84.7 0.6 copy-start.18
  132.0 4.8 %copy-start.6 = (bf16[2,160,1536]{2,1,0:T(8,128)(2,1)S(1)}, bf16[2,160,1536]{2,1,0:T(8,128)(2,1)}, u32[]{:S(2)}) copy-start(bf16[2,160,1536]{2,1,0:T(8,128)(2,1)} %get-tuple-element.54) | copy-start | bytes 2949124
  132.0 4.8 %copy-start.8 = (bf16[2,160,768]{2,1,0:T(8,128)(2,1)S(1)}, bf16[2,160,768]{2,1,0:T(8,128)(2,1)}, u32[]{:S(2)}) copy-start(bf16[2,160,768]{2,1,0:T(8,128)(2,1)} %get-tuple-element.53) | copy-start | bytes 1474564
  132.0 29.4 %all-to-all-start.1 = ((bf16[32,40,384]{2,1,0:T(8,128)(2,1)}), bf16[32,40,384]{2,1,0:T(8,128)(2,1)S(1)}, u32[]{:S(2)}, u32[]{:S(2)}) async-start(bf16[32,40,384]{2,1,0:T(8,128)(2,1)} %get-tuple-element.52), calls=%async_computation.1 | async-start | bytes 1966080 | tf_op jit(solution)/shard_map/all_to_all | solution.py:781
  136.8 5.2 %copy-start.5 = (bf16[2,160,1536]{2,1,0:T(8,128)(2,1)S(1)}, bf16[2,160,1536]{2,1,0:T(8,128)(2,1)}, u32[]{:S(2)}) copy-start(bf16[2,160,1536]{2,1,0:T(8,128)(2,1)} %get-tuple-element.55) | copy-start | bytes 2949124
  136.8 5.2 %copy-start.7 = (bf16[2,160,768]{2,1,0:T(8,128)(2,1)S(1)}, bf16[2,160,768]{2,1,0:T(8,128)(2,1)}, u32[]{:S(2)}) copy-start(bf16[2,160,768]{2,1,0:T(8,128)(2,1)} %get-tuple-element.56) | copy-start | bytes 1474564
  161.4 1.0 copy-start.4
  165.8 16.3 %copy-start.29 = (s32[8]{0:T(128)S(1)}, s32[8]{0:T(128)}, u32[]{:S(2)}) copy-start(s32[8]{0:T(128)} %constant.109.clone) | copy-start | bytes 100
  165.8 23.5 %copy-start.19 = (s32[8]{0:T(128)S(1)}, s32[8]{0:T(128)}, u32[]{:S(2)}) copy-start(s32[8]{0:T(128)} %constant.108.clone) | copy-start | bytes 100
  165.8 11.4 %collective-permute-start.8 = (bf16[256,768]{1,0:T(8,128)(2,1)}, bf16[256,768]{1,0:T(8,128)(2,1)S(1)}, u32[]{:S(2)}, u32[]{:S(2)}) collective-permute-start(bf16[256,768]{1,0:T(8,128)(2,1)} %shard_map.314.refs_1_), channel_id=1, source_target_pairs={{0,1},{1,0},{2,3},{3,2},{4,5},{5,4},{6,7},{7,6},{8,9},{9,8},{10,11... | collective-permute-start | bytes 1179656 | tf_op jit(solution)/shard_map/ppermute | solution.py:550
  177.2 0.8 copy-start.11
  182.1 8.6 %collective-permute-start.9 = (bf16[256,768]{1,0:T(8,128)(2,1)}, bf16[256,768]{1,0:T(8,128)(2,1)S(1)}, u32[]{:S(2)}, u32[]{:S(2)}) collective-permute-start(bf16[256,768]{1,0:T(8,128)(2,1)} %get-tuple-element.66.refs_10_), channel_id=1, source_target_pairs={{0,2},{2,0},{1,3},{3,1},{4,6},{6,4},{5,7},{7,5},{8,10},{10,8},{9,1... | collective-permute-start | bytes 1179656 | tf_op jit(solution)/shard_map/ppermute | solution.py:550
  190.7 0.8 copy-start.27
  205.3 28.7 %copy-start.28 = (bf16[256,768]{1,0:T(8,128)(2,1)S(1)}, bf16[256,768]{1,0:T(8,128)(2,1)}, u32[]{:S(2)}) copy-start(bf16[256,768]{1,0:T(8,128)(2,1)} %get-tuple-element.70) | copy-start | bytes 1179652
  206.3 5.0 %collective-permute-start.12 = (bf16[48,896]{1,0:T(8,128)(2,1)S(1)}, bf16[48,896]{1,0:T(8,128)(2,1)S(1)}, u32[]{:S(2)}, u32[]{:S(2)}) collective-permute-start(bf16[48,896]{1,0:T(8,128)(2,1)S(1)} %get-tuple-element.108), channel_id=1, source_target_pairs={{0,8},{8,16},{16,24},{24,28},{28,20},{20,12},{12,4},{4,0},{1,9},{9... | collective-permute-start | bytes 258056 | tf_op jit(solution)/shard_map/ppermute | solution.py:585
  212.3 28.2 %copy-start.9 = (bf16[256,768]{1,0:T(8,128)(2,1)S(1)}, bf16[256,768]{1,0:T(8,128)(2,1)}, u32[]{:S(2)}) copy-start(bf16[256,768]{1,0:T(8,128)(2,1)} %get-tuple-element.69) | copy-start | bytes 1179652
  212.3 6.0 %collective-permute-start.13 = (bf16[96,896]{1,0:T(8,128)(2,1)S(1)}, bf16[96,896]{1,0:T(8,128)(2,1)S(1)}, u32[]{:S(2)}, u32[]{:S(2)}) collective-permute-start(bf16[96,896]{1,0:T(8,128)(2,1)S(1)} %add_convert_fusion.6), channel_id=1, source_target_pairs={{0,8},{8,16},{16,24},{24,28},{28,20},{20,12},{12,4},{4,0},{1,9},{9... | collective-permute-start | bytes 516104 | tf_op jit(solution)/shard_map/ppermute | solution.py:585
  219.3 5.5 %collective-permute-start.14 = (bf16[96,896]{1,0:T(8,128)(2,1)S(1)}, bf16[96,896]{1,0:T(8,128)(2,1)S(1)}, u32[]{:S(2)}, u32[]{:S(2)}) collective-permute-start(bf16[96,896]{1,0:T(8,128)(2,1)S(1)} %add_convert_fusion.5), channel_id=1, source_target_pairs={{0,8},{8,16},{16,24},{24,28},{28,20},{20,12},{12,4},{4,0},{1,9},{9... | collective-permute-start | bytes 516104 | tf_op jit(solution)/shard_map/ppermute | solution.py:585
  220.2 4.5 %collective-permute-start.16 = (bf16[48,896]{1,0:T(8,128)(2,1)S(1)}, bf16[48,896]{1,0:T(8,128)(2,1)S(1)}, u32[]{:S(2)}, u32[]{:S(2)}) collective-permute-start(bf16[48,896]{1,0:T(8,128)(2,1)S(1)} %get-tuple-element.109), channel_id=1, source_target_pairs={{8,0},{16,8},{24,16},{28,24},{20,28},{12,20},{4,12},{0,4},{9,1},{1... | collective-permute-start | bytes 258056 | tf_op jit(solution)/shard_map/ppermute | solution.py:586
  225.8 5.5 %collective-permute-start.17 = (bf16[96,896]{1,0:T(8,128)(2,1)S(1)}, bf16[96,896]{1,0:T(8,128)(2,1)S(1)}, u32[]{:S(2)}, u32[]{:S(2)}) collective-permute-start(bf16[96,896]{1,0:T(8,128)(2,1)S(1)} %get-tuple-element.107), channel_id=1, source_target_pairs={{8,0},{16,8},{24,16},{28,24},{20,28},{12,20},{4,12},{0,4},{9,1},{1... | collective-permute-start | bytes 516104 | tf_op jit(solution)/shard_map/ppermute | solution.py:586
  232.2 5.5 %collective-permute-start.18 = (bf16[96,896]{1,0:T(8,128)(2,1)S(1)}, bf16[96,896]{1,0:T(8,128)(2,1)S(1)}, u32[]{:S(2)}, u32[]{:S(2)}) collective-permute-start(bf16[96,896]{1,0:T(8,128)(2,1)S(1)} %add_convert_fusion.2), channel_id=1, source_target_pairs={{8,0},{16,8},{24,16},{28,24},{20,28},{12,20},{4,12},{0,4},{9,1},{1... | collective-permute-start | bytes 516104 | tf_op jit(solution)/shard_map/ppermute | solution.py:586
  234.0 6.4 %collective-permute-start.10 = (bf16[256,768]{1,0:T(8,128)(2,1)S(1)}, bf16[256,768]{1,0:T(8,128)(2,1)S(1)}, u32[]{:S(2)}, u32[]{:S(2)}) collective-permute-start(bf16[256,768]{1,0:T(8,128)(2,1)S(1)} %copy-done.28), channel_id=1, source_target_pairs={{0,2},{2,0},{1,3},{3,1},{4,6},{6,4},{5,7},{7,5},{8,10},{10,8},{9,1... | collective-permute-start | bytes 1179656 | tf_op jit(solution)/shard_map/ppermute | solution.py:550
  235.4 6.8 %collective-permute-start.15 = (bf16[96,896]{1,0:T(8,128)(2,1)S(1)}, bf16[96,896]{1,0:T(8,128)(2,1)S(1)}, u32[]{:S(2)}, u32[]{:S(2)}) collective-permute-start(bf16[96,896]{1,0:T(8,128)(2,1)S(1)} %get-tuple-element.106), channel_id=1, source_target_pairs={{0,8},{8,16},{16,24},{24,28},{28,20},{20,12},{12,4},{4,0},{1,9},{9... | collective-permute-start | bytes 516104 | tf_op jit(solution)/shard_map/ppermute | solution.py:585
  238.7 5.5 %collective-permute-start.19 = (bf16[96,896]{1,0:T(8,128)(2,1)S(1)}, bf16[96,896]{1,0:T(8,128)(2,1)S(1)}, u32[]{:S(2)}, u32[]{:S(2)}) collective-permute-start(bf16[96,896]{1,0:T(8,128)(2,1)S(1)} %add_convert_fusion.1), channel_id=1, source_target_pairs={{8,0},{16,8},{24,16},{28,24},{20,28},{12,20},{4,12},{0,4},{9,1},{1... | collective-permute-start | bytes 516104 | tf_op jit(solution)/shard_map/ppermute | solution.py:586
  240.6 9.6 %copy-start.2 = (bf16[256,768]{1,0:T(8,128)(2,1)}, bf16[256,768]{1,0:T(8,128)(2,1)S(1)}, u32[]{:S(2)}) copy-start(bf16[256,768]{1,0:T(8,128)(2,1)S(1)} %add_convert_fusion.near) | copy-start | bytes 1179652
  240.6 9.6 %collective-permute-start.11 = (bf16[256,768]{1,0:T(8,128)(2,1)S(1)}, bf16[256,768]{1,0:T(8,128)(2,1)S(1)}, u32[]{:S(2)}, u32[]{:S(2)}) collective-permute-start(bf16[256,768]{1,0:T(8,128)(2,1)S(1)} %add_convert_fusion.near), channel_id=1, source_target_pairs={{0,1},{1,0},{2,3},{3,2},{4,5},{5,4},{6,7},{7,6},{8,9},{9,8},{10,11... | collective-permute-start | bytes 1179656 | tf_op jit(solution)/shard_map/ppermute | solution.py:550
  245.1 8.5 %copy-start = (f32[96,896]{1,0:T(8,128)}, f32[96,896]{1,0:T(8,128)S(1)}, u32[]{:S(2)}) copy-start(f32[96,896]{1,0:T(8,128)S(1)} %convert_add_fusion.refs_1_) | copy-start | bytes 1032196
  245.2 8.5 %collective-permute-start.20 = (f32[56,896]{1,0:T(8,128)S(1)}, f32[56,896]{1,0:T(8,128)S(1)}, u32[]{:S(2)}, u32[]{:S(2)}) collective-permute-start(f32[56,896]{1,0:T(8,128)S(1)} %pad_maximum_fusion), channel_id=1, source_target_pairs={{0,2},{2,0},{1,3},{3,1},{4,6},{6,4},{5,7},{7,5},{8,10},{10,8},{9,1... | collective-permute-start | bytes 602120 | tf_op jit(solution)/shard_map/ppermute | solution.py:550
  245.3 8.3 %collective-permute-start.21 = (f32[48,128]{1,0:T(8,128)S(1)}, f32[48,128]{1,0:T(8,128)S(1)}, u32[]{:S(2)}, u32[]{:S(2)}) collective-permute-start(f32[48,128]{1,0:T(8,128)S(1)} %get-tuple-element.113), channel_id=1, source_target_pairs={{0,1},{1,0},{2,3},{3,2},{4,5},{5,4},{6,7},{7,6},{8,9},{9,8},{10,11... | collective-permute-start | bytes 73736 | tf_op jit(solution)/shard_map/ppermute | solution.py:550
  246.5 7.1 %collective-permute-start.22 = (f32[48,128]{1,0:T(8,128)S(1)}, f32[48,128]{1,0:T(8,128)S(1)}, u32[]{:S(2)}, u32[]{:S(2)}) collective-permute-start(f32[48,128]{1,0:T(8,128)S(1)} %get-tuple-element.112), channel_id=1, source_target_pairs={{0,3},{1,2},{2,1},{3,0},{4,7},{5,6},{6,5},{7,4},{8,11},{9,10},{10,... | collective-permute-start | bytes 73736 | tf_op jit(solution)/shard_map/ppermute | solution.py:852
  250.1 0.7 copy-start.10
  253.6 0.6 copy-start.20
  253.7 0.6 copy-start.21
  254.3 0.7 copy-start.15
Sparse Core Ops, SparseCore 0:
  11.2 44.4 all-gather.1

commit v3 on v2

--- a/solution.py
+++ b/solution.py
@@ -94,14 +94,14 @@
     bucket = bucket_index(iota((1, lanes), 1) - 2 * STRIP)
     for head in range(heads):
         line = jnp.zeros((1, lanes), f32)
-        for entry in range(table_ref.shape[0]):
-            line = jnp.where(bucket == entry, table_ref[entry, first_head + head], line)
+        for entry in range(table_ref.shape[1]):
+            line = jnp.where(bucket == entry, table_ref[first_head + head, entry], line)
         strip = skew(jnp.broadcast_to(line, (STRIP, lanes)), True)
         strip_ref[head] = strip[:, STRIP:]
 
 
 def bias_row(strip_ref, table_ref, head, first_head, block, blocks):
-    buckets = table_ref.shape[0]
+    buckets = table_ref.shape[1]
     parts = []
     for other in range(blocks):
         gap = other - block
@@ -109,7 +109,7 @@
             parts.append(strip_ref[head, :, (gap + 1) * STRIP : (gap + 2) * STRIP])
         else:
             entry = buckets - 1 if gap > 0 else buckets // 2 - 1
-            parts.append(jnp.full((STRIP, STRIP), table_ref[entry, first_head + head], f32))
+            parts.append(jnp.full((STRIP, STRIP), table_ref[first_head + head, entry], f32))
     return jnp.concatenate(parts, axis=1)
 
 
@@ -137,15 +137,15 @@
 
 
 def pack_rows(*refs):
-    (meta, w_query, w_key, w_value, w_output, w_router, gain_one, gain_two, out) = refs
+    (meta, w_query, w_key, w_value, w_output, w_router, gain_one, gain_two, own, send, output) = refs
     rows = w_query.shape[0]
-    experts = w_router.shape[1]
+    experts = w_router.shape[0]
     width = w_query.shape[1] // 2
     lanes = width + HEAD_SIZE
     lane = iota((1, lanes), 1)
     diagonal = iota((rows, rows), 0) == iota((rows, rows), 1)
     placing = (iota((experts, lanes), 0) + width == iota((experts, lanes), 1)).astype(f32)
-    extras = mm(w_router[...], placing.astype(bf16))
+    extras = mm_tn(w_router[...], placing.astype(bf16))
     for index, gain in enumerate((gain_one, gain_two)):
         column = jnp.sum(
             jnp.where(diagonal, jnp.broadcast_to(gain[...].astype(f32), (rows, rows)), 0.0),
@@ -153,15 +153,32 @@
             keepdims=True,
         )
         extras = extras + jnp.where(lane == width + experts + index, column, 0.0)
-    at = 0
-    for which in (meta[0], 1 - meta[0]):
-        blocks = join(half_columns(w_query, which), half_columns(w_key, which))
-        for block in blocks:
+    for which, out in ((meta[0], own), (1 - meta[0], send)):
+        at = 0
+        for block in join(half_columns(w_query, which), half_columns(w_key, which)):
             out[:, at : at + LANES] = block.astype(bf16)
             at += LANES
-        out[:, at : at + lanes] = (half_columns(w_value, which) + extras).astype(bf16)
-        at += lanes
-    out[:, at:] = w_output[...]
+        out[:, at:] = (half_columns(w_value, which) + extras).astype(bf16)
+    output[:rows, :] = half_columns(w_output, 0).astype(bf16)
+    output[rows:, :] = half_columns(w_output, 1).astype(bf16)
+
+
+def put_in_rows(count, *refs):
+    starts, meta = refs[:2]
+    shards = refs[2 : 2 + count]
+    wall, output = refs[2 + count :]
+    wide = wall.shape[1]
+    place = meta[0]
+    for index, shard in enumerate(shards):
+        rows = shard.shape[0] // 2
+        first = starts[index]
+        for half, core in ((0, place), (1, 1 - place)):
+            at = pl.multiple_of((2 * first + core) * rows, 16)
+            wall[pl.ds(at, rows), :] = shard[half * rows : (half + 1) * rows, :wide]
+        blocks = join(shard[:rows, wide:].astype(f32), shard[rows:, wide:].astype(f32))
+        at = pl.multiple_of(first * rows, 16)
+        for block, values in enumerate(blocks):
+            output[pl.ds(at, rows), block * LANES : (block + 1) * LANES] = values.astype(bf16)
 
 
 def interleave(out, lanes, own, other, place, count):
@@ -174,14 +191,13 @@
         out[pl.ds(second, rows), lanes] = other[here, :]
 
 
-def attention_forward(heads, experts, count, *refs):
-    (meta, lengths, table, x_own, x_other, rows_own, rows_other) = refs[:7]
-    (h1, q_out, k_out, v_out, o_own, o_other, lse, wall, gains, strips, o_all) = refs[7:]
+def attention_forward(heads, experts, *refs):
+    (meta, lengths, table, x_own, x_other, wall) = refs[:6]
+    (h1, q_out, k_out, v_out, o_own, o_other, o_all, lse, gains, strips) = refs[6:]
     place = meta[0]
     rows = x_own.shape[0]
     group = 2 * rows
     first_head = place * heads
-    interleave(wall, slice(None), rows_own, rows_other, meta[2], count)
     width = wall.shape[1]
     extras = wall[:, width - LANES :].astype(f32).T
     gain_at = HEAD_SIZE + experts
@@ -225,6 +241,14 @@
     o_other[...] = o_all[pl.ds(pl.multiple_of((1 - place) * rows, 16), rows), :]
 
 
+def column_of(line):
+    return jnp.broadcast_to(line, (LANES, line.shape[1])).T[:, :1]
+
+
+def columns_of(*lines):
+    return [column_of(line[...].astype(f32)).astype(jnp.int32) for line in lines]
+
+
 def routed(hidden, extras, routes_column, keep_column, experts):
     logits = mm(hidden, extras)
     lane = iota((1, LANES), 1) - HEAD_SIZE
@@ -247,15 +271,6 @@
     return jnp.where(keep_row == 1, routes_row * capacity + rank, -2)
 
 
-def slots_by_column(routes_column, keep_column, experts, capacity):
-    count = routes_column.shape[0]
-    chosen = ((iota((count, experts), 1) == routes_column) & (keep_column == 1)).astype(f32)
-    before = (iota((count, count), 1) < iota((count, count), 0)).astype(bf16)
-    earlier = mm(before, chosen.astype(bf16))
-    rank = jnp.sum(earlier * chosen, axis=1, keepdims=True).astype(jnp.int32)
-    return jnp.where(keep_column == 1, routes_column * capacity + rank, -2)
-
-
 def heads_of(own, other, place):
     own = own[...].astype(f32)
     other = other[...].astype(f32)
@@ -266,8 +281,9 @@
 
 def to_experts(experts, capacity, count, *refs):
     (meta, x_own, cotangent, o_own, o_tp, o_ctx, o_far, wo_own, wo_tp, wo_ctx, wo_far) = refs[:11]
-    (extras, gains, routes_row, routes_column, keep_row, keep_column, slot_h, slot_d) = refs[11:19]
-    middle_out, sends, wo_out, wo_other = refs[19:]
+    (extras, gains, routes_row, keep_row, slot_h, slot_d) = refs[11:17]
+    middle_out, sends, wo_out, wo_other = refs[17:]
+    routes_column, keep_column = columns_of(routes_row, keep_row)
     place, start = meta[0], meta[2]
     interleave(wo_out, slice(None), wo_own, wo_ctx, start, count)
     interleave(wo_other, slice(None), wo_tp, wo_far, start, count)
@@ -276,7 +292,7 @@
     middle = x_own[...].astype(f32) + branch
     middle_out[...] = middle
     hidden = (middle * rms_scale(middle) * gains[1:2]).astype(bf16)
-    _, _, _, gate = routed(hidden, extras[...], routes_column[...], keep_column[...], experts)
+    _, _, _, gate = routed(hidden, extras[...], routes_column, keep_column, experts)
     out_grad = (gate * cotangent[...].astype(f32)).astype(bf16)
     slot = slots_by_row(routes_row[...], keep_row[...], experts, capacity)
     pick_h = (slot_h[...] == slot).astype(f32).astype(bf16)
@@ -353,8 +369,9 @@
 
 
 def from_experts(experts, capacity, *refs):
-    rows_in, routes_column, keep_column, slot_y, slot_x, out = refs
-    slot = slots_by_column(routes_column[...], keep_column[...], experts, capacity)
+    rows_in, routes_row, keep_row, slot_y, slot_x, out = refs
+    slot = column_of(slots_by_row(routes_row[...], keep_row[...], experts, capacity).astype(f32))
+    slot = slot.astype(jnp.int32)
     width = rows_in.shape[1]
     pick_y = (slot == slot_y[...]).astype(f32).astype(bf16)
     pick_x = (slot == slot_x[...]).astype(f32).astype(bf16)
@@ -362,12 +379,9 @@
     out[:, width:] = mm(pick_x, rows_in[...]).astype(bf16)
 
 
-def column_of(line):
-    return jnp.broadcast_to(line, (LANES, line.shape[1])).T[:, :1]
-
-
 def middle_backward(experts, *refs):
-    (meta, both_own, both_tp, middle_ref, cotangent, extras, gains, routes_column, keep_column) = refs[:9]
+    (meta, both_own, both_tp, middle_ref, cotangent, extras, gains, routes_row, keep_row) = refs[:9]
+    routes_column, keep_column = columns_of(routes_row, keep_row)
     (result, dmiddle_out, branch_grad, router_grad) = refs[9:]
     share = meta[1]
     width = both_own.shape[1] // 2
@@ -382,9 +396,7 @@
     normed = middle * scale
     gain = gains[1:2]
     hidden = (normed * gain).astype(bf16)
-    probs, onehot, kept, gate = routed(
-        hidden, extras[...], routes_column[...], keep_column[...], experts
-    )
+    probs, onehot, kept, gate = routed(hidden, extras[...], routes_column, keep_column, experts)
     result[...] = middle + gate * picked
     upstream = cotangent[...].astype(f32)
     gate_grad = jnp.sum(upstream * picked, axis=1, keepdims=True)
@@ -405,9 +417,9 @@
 
 
 def attention_backward(heads, shard, *refs):
-    (meta, lengths, table, x_own, x_other, h1, q_in, k_in, v_in, lse, db_own, db_other) = refs[:12]
-    (o_own, o_other, wo_ref, wall, router_grad) = refs[12:17]
-    (payload, dh1_own, dh1_other) = refs[17:20]
+    (meta, lengths, table, x_own, x_other, h1, q_in, k_in, v_in, lse, db) = refs[:11]
+    (o_all, wo_ref, wall, router_grad) = refs[11:15]
+    (payload, top_out, bottom_out, dh1_own, dh1_other) = refs[15:20]
     (strips, sums, do_all, dq, dk, dv, dqkv, dh1) = refs[20:]
     place = meta[0]
     rows = x_own.shape[0]
@@ -416,10 +428,9 @@
     first_head = place * heads
     own_at = pl.ds(pl.multiple_of(place * rows, 16), rows)
     other_at = pl.ds(pl.multiple_of((1 - place) * rows, 16), rows)
-    for source, at in ((db_own, own_at), (db_other, other_at)):
-        both = mm(source[...], wo_ref[...])
-        high = pltpu.roll(both[:, LANES : LANES + lanes], lanes - HEAD_SIZE, 1)
-        do_all[at, :] = jnp.where(place == 0, both[:, :lanes], high).astype(bf16)
+    both = mm(db[...], wo_ref[...])
+    high = pltpu.roll(both[:, LANES : LANES + lanes], lanes - HEAD_SIZE, 1)
+    do_all[...] = jnp.where(place == 0, both[:, :lanes], high).astype(bf16)
     bias_strips(table, first_head, heads, strips)
     segment_row = segments(lengths, group, 1)
     segment_column = segments(lengths, group, 0)
@@ -476,7 +487,7 @@
         target[...] = grad.astype(bf16)
         part = jnp.sum(grad * (values * rms_scale(values)), axis=0, keepdims=True)
         gain_part = part if gain_part is None else gain_part + part
-    buckets = table.shape[0]
+    buckets = table.shape[1]
     spread = skew(sums[...].reshape(heads * STRIP, 4 * STRIP), False)
     diagonals = jnp.sum(spread.reshape(heads, STRIP, 4 * STRIP), axis=1)
     picks = (bucket_index(iota((4 * STRIP, 1), 0) - 2 * STRIP) == iota((1, LANES), 1)).astype(f32)
@@ -493,21 +504,57 @@
     grads = mm_tn(h1[...], dqkv[...])
     payload[:, : width - LANES] = grads[:, : width - LANES].astype(bf16)
     payload[:, width - LANES : width] = (grads[:, width - LANES :] + riders).astype(bf16)
-    grads = mm_tn(db_own[...], o_own[...]) + mm_tn(db_other[...], o_other[...])
+    grads = mm_tn(db[...], o_all[...])
     payload[:, width : width + lanes - LANES] = grads[:, : lanes - LANES].astype(bf16)
     payload[:, width + lanes - LANES :] = (
         grads[:, lanes - LANES :] + router_grad[...].astype(f32)
     ).astype(bf16)
+    half = top_out.shape[0]
+    across = pl.multiple_of(meta[3] * shard if 2 * half == shard else 0 * meta[3], 16)
+    top_out[...] = payload[pl.ds(across, half), :]
+    bottom_out[...] = payload[pl.ds(across + half, half), :]
+
+
+def ring_add(places, right_mine, left_mine, from_left, from_right, right_out, left_out):
+    rows = right_mine.shape[0]
+    span = from_left.shape[0]
+    right_out[...] = right_mine[...]
+    left_out[...] = left_mine[...]
+    top, bottom = slice(0, span), slice(rows - span, rows)
+    right_out[top] = (right_mine[top].astype(f32) + from_left[...].astype(f32)).astype(bf16)
+    left_out[bottom] = (left_mine[bottom].astype(f32) + from_right[...].astype(f32)).astype(bf16)
+
+
+def ring_end(at, place, sums, own, send, table, riders_own, riders_other):
+    rows = own.shape[0]
+    first, second = sums[:rows, :], sums[rows : 2 * rows, :]
+    mine = jnp.where(place == 0, first, second)
+    other = jnp.where(place == 0, second, first)
+    own[...] = mine
+    send[:rows, :] = other
+    send[rows:, :] = sums[:8, :]
+    table[...] = sums[:8, at : at + LANES]
+    riders_own[...] = mine[:, at : at + LANES]
+    riders_other[...] = other[:, at : at + LANES]
+
+
+def ring_last(at, places, mine, from_left, from_right, own, send, table, riders_own, riders_other):
+    total = mine[...].astype(f32) + from_left[...].astype(f32) + from_right[...].astype(f32)
+    ring_end(at, places[2], total, own, send, table, riders_own, riders_other)
+
+
+def ring_whole(at, places, sums, own, send, table, riders_own, riders_other):
+    ring_end(at, places[2], sums[...], own, send, table, riders_own, riders_other)
 
 
 def shards_of_sums(experts, buckets, heads, *refs):
-    (meta, sums, other, from_tp, from_far) = refs[:5]
-    (query_out, key_out, value_out, output_out, router_out, gain_one, gain_two, table) = refs[5:]
+    (meta, own_ref, other, own_top, from_tp, from_far) = refs[:6]
+    (query_out, key_out, value_out, output_out, router_out, gain_one, gain_two, table) = refs[6:]
     place = meta[0]
     rows, width = query_out.shape[0], query_out.shape[1] // 2
     lanes = width + HEAD_SIZE
     wide = 3 * width + HEAD_SIZE
-    own = jnp.where(place == 0, sums[:rows, :], sums[rows : 2 * rows, :])
+    own = own_ref[...]
     more = other[:rows, :]
     lane = iota((1, lanes), 1)
     for at, moved, out in (
@@ -524,16 +571,17 @@
         second = jnp.where(place == 0, parts[1], parts[0])
         for index, block in enumerate(join(first, second)):
             out[:, index * LANES : (index + 1) * LANES] = block
-    total = (own + more)[:, wide + lanes - LANES :]
-    router_out[...] = total
-    gain_two[...] = total.T[HEAD_SIZE + experts : HEAD_SIZE + experts + 1, :]
+    total = (own + more)[:, wide + lanes - LANES :].T
+    router_out[...] = total[HEAD_SIZE : HEAD_SIZE + experts, :]
+    gain_two[...] = total[HEAD_SIZE + experts : HEAD_SIZE + experts + 1, :]
     line = (own + more)[:, wide - LANES : wide] + (from_tp[...] + from_far[...])
     gain_one[...] = line.T[HEAD_SIZE : HEAD_SIZE + 1, :]
-    own_lines = pltpu.roll(sums[:8, wide - LANES : wide], LANES - HEAD_SIZE - 1, 1)
-    other_lines = pltpu.roll(other[rows : rows + 8, wide - LANES : wide], LANES - HEAD_SIZE - 1, 1)
-    table[...] = jnp.zeros_like(table)
-    table[:heads, :] = jnp.where(place == 0, own_lines, other_lines)[:heads]
-    table[heads : 2 * heads, :] = jnp.where(place == 0, other_lines, own_lines)[:heads]
+    own_lines = own_top[...]
+    other_lines = other[rows : rows + 8, wide - LANES : wide]
+    own_lines = pltpu.roll(own_lines, LANES - HEAD_SIZE - 1, 1)
+    other_lines = pltpu.roll(other_lines, LANES - HEAD_SIZE - 1, 1)
+    table[:heads, :] = jnp.where(place == 0, own_lines, other_lines)[:heads, :buckets]
+    table[heads : 2 * heads, :] = jnp.where(place == 0, other_lines, own_lines)[:heads, :buckets]
 
 
 def input_backward(x_own, dmiddle, gains, near, far, out):
@@ -567,31 +615,69 @@
     return jnp.asarray(np.array(order, np.int32)), jnp.asarray(inverse)[lax.axis_index("fsdp")]
 
 
-def sum_rows(payload, count):
-    rows = payload.shape[0] // count
-    if rows % 32 or count % 2:
-        return lax.psum_scatter(payload.astype(f32), "fsdp", scatter_dimension=0, tiled=True)
+def ring_gather(shard, count):
     order, right, left = ring_steps(count)
     table, place = ring_place(count)
+    shards = [shard]
+    places = [table[place]]
+    going_right, going_left = shard, shard
+    for step in range(1, count // 2):
+        going_right = lax.ppermute(going_right, "fsdp", right)
+        going_left = lax.ppermute(going_left, "fsdp", left)
+        shards += [going_right, going_left]
+        places += [table[(place - step) % count], table[(place + step) % count]]
+    shards.append(lax.ppermute(going_right, "fsdp", right))
+    places.append(table[(place + count // 2) % count])
+    return shards, jnp.stack(places).astype(jnp.int32)
+
+
+def ring_sums(payload, top, bottom, count, at, place, side):
+    rows = payload.shape[0] // count
+    lanes = payload.shape[1]
     half = rows // 2
-
-    def mine(distance):
-        start = table[(place + distance) % count] * rows
-        return lax.dynamic_slice_in_dim(payload, start, rows, 0).astype(f32)
-
-    across = mine(count // 2).astype(bf16)
-    going_right, going_left = across[:half], across[half:]
+    outs = [
+        shape((half, lanes), f32),
+        shape((half + 8, lanes), f32),
+        shape((8, LANES), f32),
+        shape((half, LANES), f32),
+        shape((half, LANES), f32),
+    ]
+    zero = jnp.zeros((), jnp.int32)
+    if rows % 32 or count % 2:
+        sums = lax.psum_scatter(payload.astype(f32), "fsdp", scatter_dimension=0, tiled=True)
+        places = jnp.stack([zero, zero, place]).astype(jnp.int32)
+        return kernel_call(functools.partial(ring_whole, at), outs, [smem, vmem])(places, sums)
+    order, right, left = ring_steps(count)
+    table, spot = ring_place(count)
+    going_right, going_left = top, bottom
+    spec = lambda which: pl.BlockSpec((rows, lanes), lambda i, places: (places[which], 0))
+    params = pltpu.CompilerParams(vmem_limit_bytes=VMEM_BYTES)
     for step in range(count // 2, 0, -1):
-        from_left = lax.ppermute(going_right, "fsdp", right).astype(f32)
-        from_right = lax.ppermute(going_left, "fsdp", left).astype(f32)
-        if step == count // 2:
-            none = jnp.zeros_like(from_left)
-            from_left = jnp.concatenate([from_left, none], axis=0)
-            from_right = jnp.concatenate([none, from_right], axis=0)
-        if step == 1:
-            return mine(0) + from_left + from_right
-        going_right = (mine(step - 1) + from_left).astype(bf16)
-        going_left = (mine(1 - step) + from_right).astype(bf16)
+        from_left = lax.ppermute(going_right, "fsdp", right)
+        from_right = lax.ppermute(going_left, "fsdp", left)
+        places = [table[(spot + step - 1) % count], table[(spot + 1 - step) % count], place]
+        places = jnp.stack(places).astype(jnp.int32)
+        whole = lambda dims: pl.BlockSpec(dims, lambda i, places: (0, 0))
+        last = step == 1
+        if last:
+            side, from_left, from_right = lax.optimization_barrier((side, from_left, from_right))
+        step_outs = outs if last else [shape((rows, lanes), bf16)] * 2
+        out = pl.pallas_call(
+            functools.partial(ring_last, at) if last else ring_add,
+            grid_spec=pltpu.PrefetchScalarGridSpec(
+                num_scalar_prefetch=1,
+                grid=(1,),
+                in_specs=([spec(0)] if last else [spec(0), spec(1)])
+                + [whole(from_left.shape), whole(from_right.shape)],
+                out_specs=[whole(o.shape) for o in step_outs],
+            ),
+            out_shape=step_outs,
+            compiler_params=params,
+            cost_estimate=pl.CostEstimate(flops=0, bytes_accessed=1024 * 1024, transcendentals=0),
+        )(places, *([payload] if last else [payload, payload]), from_left, from_right)
+        if last:
+            return out
+        going_right, going_left = out
 
 
 def body(
@@ -630,27 +716,32 @@
     lanes = width + HEAD_SIZE
     shard_rows = w_query.shape[0]
     buckets = rel_table.shape[0]
-    meta = jnp.stack([place, share]).astype(jnp.int32)
 
     def full(dims, dtype):
         return shape(dims, dtype)
 
     wide = 3 * width + HEAD_SIZE
-    packed = kernel_call(
+    aligned = shard_rows % 16 == 0 and fsdp_count % 2 == 0
+    count = fsdp_count if aligned else 1
+    start = place if aligned else 0 * place
+    across = ring_place(fsdp_count)[1] + fsdp_count // 2
+    across = ring_place(fsdp_count)[0][across % fsdp_count]
+    meta = jnp.stack([place, share, start, across]).astype(jnp.int32)
+    table_rows = rel_table.T
+    shard_own, shard_send, wo_shard = kernel_call(
         pack_rows,
-        [full((shard_rows, 2 * wide + 2 * width), bf16)],
+        [full((shard_rows, wide), bf16), full((shard_rows, wide), bf16), full((2 * shard_rows, lanes), bf16)],
         [smem] + [vmem] * 7,
         moved=512 * 1024,
-    )(meta, w_query, w_key, w_value, w_output, w_router, gain_attn[None, :], gain_moe[None, :])[0]
+    )(meta, w_query, w_key, w_value, w_output, w_router.T, gain_attn[None, :], gain_moe[None, :])
+    shard_other = swap(shard_send, "ctx")
+    shard = jnp.concatenate(
+        [jnp.concatenate([shard_own, shard_other], axis=0), wo_shard], axis=1
+    )
     x_other = swap(tokens, "ctx")
-    gathered = lax.all_gather(packed, "fsdp", axis=0, tiled=True)
-    rows_own, rows_other = gathered[:, :wide], swap(gathered[:, wide : 2 * wide], "ctx")
-    wo_own = gathered[:, 2 * wide :]
-    count = fsdp_count
-    start = place
 
     def ordered(own, other):
-        if shard_rows % 16 == 0:
+        if aligned:
             return own, other
         dims = (fsdp_count, 1, shard_rows, own.shape[1])
         pair = in_order(own.reshape(dims), other.reshape(dims), 1).reshape(2 * own.shape[0], -1)
@@ -663,12 +754,25 @@
             jnp.concatenate([other, own], axis=axis),
         )
 
-    if shard_rows % 16:
-        count, start = 1, 0 * place
-    meta = jnp.stack([place, share, start]).astype(jnp.int32)
-    rows_own, rows_other = ordered(rows_own, rows_other)
-    h1, q, k, v, o_own, o_other, lse, wall, gains = kernel_call(
-        functools.partial(attention_forward, heads, experts, count),
+    if aligned:
+        shards, places = ring_gather(shard, fsdp_count)
+        wall, wo_own = kernel_call(
+            functools.partial(put_in_rows, len(shards)),
+            [full((model_width, wide), bf16), full((model_width // 2, 2 * width), bf16)],
+            [smem, smem] + [vmem] * len(shards),
+            moved=4 * 1024 * 1024,
+        )(places, meta, *shards)
+    else:
+        both = lax.all_gather(shard, "fsdp", axis=0, tiled=False)
+        near, far = both[:, :shard_rows], both[:, shard_rows:]
+        wall = jnp.concatenate(
+            ordered(near[:, :, :wide].reshape(-1, wide), far[:, :, :wide].reshape(-1, wide)), axis=0
+        )
+        wo_own = jnp.concatenate([near[:, :, wide : wide + width], far[:, :, wide : wide + width]], axis=2)
+        wo_own = wo_own.reshape(-1, 2 * width)
+
+    h1, q, k, v, o_own, o_other, o_all, lse, gains = kernel_call(
+        functools.partial(attention_forward, heads, experts),
         [
             full((group, model_width), bf16),
             full((group, lanes), bf16),
@@ -676,15 +780,15 @@
             full((group, lanes), bf16),
             full((rows, lanes), bf16),
             full((rows, lanes), bf16),
+            full((group, lanes), bf16),
             full((group, LANES), f32),
-            full((model_width, wide), bf16),
             full((8, model_width), f32),
         ],
-        [smem] * 3 + [vmem] * 4,
-        scratch=[pltpu.VMEM((heads, STRIP, 3 * STRIP), f32), pltpu.VMEM((group, lanes), bf16)],
+        [smem] * 3 + [vmem] * 3,
+        scratch=[pltpu.VMEM((heads, STRIP, 3 * STRIP), f32)],
         flops=2 * group * model_width * wide * 8,
         moved=8 * 1024 * 1024,
-    )(meta, lengths, rel_table, tokens, x_other, rows_own, rows_other)
+    )(meta, lengths, table_rows, tokens, x_other, wall)
     wo_tp = swap(wo_own, "tp")
     wo_ctx = swap(wo_own, "ctx")
     wo_far = swap(wo_tp, "ctx")
@@ -705,7 +809,6 @@
     slot_second = np.where(kind == 1, slot_of, -1).astype(np.int32)
     routes_row = routes.reshape(1, rows)
     keep_row = keep_mask.reshape(1, rows)
-    keep_column = keep_mask.reshape(rows, 1)
     extras = wall[:, wide - LANES :]
 
     middle, sends, wo_full = kernel_call(
@@ -715,13 +818,13 @@
             full((owners * per_owner, model_width), bf16),
             full((model_width, 2 * width), bf16),
         ],
-        [smem] + [vmem] * 18,
+        [smem] + [vmem] * 16,
         scratch=[pltpu.VMEM((model_width, 2 * width), bf16)],
         flops=2 * rows * model_width * (model_width + 2 * owners * per_owner),
         moved=6 * 1024 * 1024,
     )(
         meta, tokens, cotangent, o_own, o_tp, o_ctx, o_far, wo_own, wo_tp, wo_ctx, wo_far, extras,
-        gains, routes_row, routes, keep_row, keep_column, slot_first[:, None], slot_second[:, None],
+        gains, routes_row, keep_row, slot_first[:, None], slot_second[:, None],
     )
 
     arrived = lax.all_to_all(
@@ -792,7 +895,7 @@
         [vmem] * 5,
         flops=4 * rows * returned.shape[0] * part_width,
         moved=2 * 1024 * 1024,
-    )(returned, routes, keep_column, back_first, back_second)[0]
+    )(returned, routes_row, keep_row, back_first, back_second)[0]
     both_tp = swap(both_own, "tp")
 
     result, middle_grad, db_own, router_grad = kernel_call(
@@ -806,17 +909,20 @@
         [smem] + [vmem] * 8,
         flops=6 * rows * LANES * model_width,
         moved=6 * 1024 * 1024,
-    )(meta, both_own, both_tp, middle, cotangent, extras, gains, routes, keep_column)
-    db_other = swap(db_own, "ctx")
-
-    payload, dh1_own, dh1_other = kernel_call(
+    )(meta, both_own, both_tp, middle, cotangent, extras, gains, routes_row, keep_row)
+    db = lax.all_gather(db_own, "ctx", axis=0, tiled=True)
+
+    half = model_width // fsdp_count // 2
+    payload, top, bottom, dh1_own, dh1_other = kernel_call(
         functools.partial(attention_backward, heads, model_width // fsdp_count),
         [
             full((model_width, wide + lanes), bf16),
+            full((half if aligned else 16, wide + lanes), bf16),
+            full((half if aligned else 16, wide + lanes), bf16),
             full((rows, model_width), bf16),
             full((rows, model_width), bf16),
         ],
-        [smem] * 3 + [vmem] * 14,
+        [smem] * 3 + [vmem] * 12,
         scratch=[
             pltpu.VMEM((heads, STRIP, 3 * STRIP), f32),
             pltpu.VMEM((heads, STRIP, 4 * STRIP), f32),
@@ -830,39 +936,39 @@
         flops=2 * group * model_width * wide * 12,
         moved=8 * 1024 * 1024,
     )(
-        meta, lengths, rel_table, tokens, x_other, h1, q, k, v, lse, db_own, db_other,
-        o_own, o_other, wo_full, wall, router_grad,
+        meta, lengths, table_rows, tokens, x_other, h1, q, k, v, lse, db,
+        o_all, wo_full, wall, router_grad,
     )
 
     dh1_sum = (dh1_own.astype(f32) + swap(dh1_other, "ctx").astype(f32)).astype(bf16)
     dh1_far = swap(dh1_sum, "tp")
-    sums = sum_rows(payload, fsdp_count)
+    own, send, own_lines, riders_own, riders_other = ring_sums(
+        payload, top, bottom, fsdp_count, wide - LANES, place, dh1_far
+    )
+    other = swap(send, "ctx")
+    from_tp = swap(riders_own, "tp")
+    from_far = lax.ppermute(riders_other, ("ctx", "tp"), [(i, 3 - i) for i in range(4)])
     input_grad = kernel_call(
         input_backward,
         [full((rows, model_width), f32)],
         [vmem] * 5,
         moved=4 * 1024 * 1024,
     )(tokens, middle_grad, gains, dh1_sum, dh1_far)[0]
-
-    not_own = lax.dynamic_slice_in_dim(sums, (1 - place) * shard_rows, shard_rows, 0)
-    riders = slice(wide - LANES, wide)
-    own_riders = lax.dynamic_slice_in_dim(sums, place * shard_rows, shard_rows, 0)[:, riders]
-    other = swap(jnp.concatenate([not_own, sums[:8]], axis=0), "ctx")
-    from_tp = swap(own_riders, "tp")
-    from_far = lax.ppermute(not_own[:, riders], ("ctx", "tp"), [(i, 3 - i) for i in range(4)])
+    other, input_grad = lax.optimization_barrier((other, input_grad))
+
     shard = full((shard_rows, 2 * width), f32)
     query_grad, key_grad, value_grad, output_grad, router_sum, gain_one, gain_two, table_grad = kernel_call(
         functools.partial(shards_of_sums, experts, buckets, heads),
         [shard] * 4
         + [
-            full((shard_rows, LANES), f32),
+            full((experts, shard_rows), f32),
             full((1, shard_rows), f32),
             full((1, shard_rows), f32),
-            full((8, LANES), f32),
+            full((2 * heads, buckets), f32),
         ],
-        [smem] + [vmem] * 4,
+        [smem] + [vmem] * 5,
         moved=1024 * 1024,
-    )(meta, sums, other, from_tp, from_far)
+    )(meta, own, other, own_lines, from_tp, from_far)
     return (
         result,
         input_grad,
@@ -870,10 +976,10 @@
         key_grad,
         value_grad,
         output_grad,
-        router_sum[:, HEAD_SIZE : HEAD_SIZE + experts],
+        router_sum.T,
         gain_one.reshape(shard_rows),
         gain_two.reshape(shard_rows),
-        table_grad[: 2 * heads, :buckets].T,
+        table_grad.T,
         w_in_grad,
         w_out_grad,
     )

time: 268 us -> 238 us (0.89)
  waiting for transfers between devices: 98.2 us -> 57.1 us
  between operations: 26.1 us -> 9.52 us
  Pallas kernels: 53.5 us -> 66.2 us
  starting transfers between devices: 23.4 us -> 30.7 us
  blocking collectives: 28 us -> 32.8 us
  other arithmetic: 7.17 us -> 10.1 us
    all_gather x1 -> x0, waiting for transfers between devices: 44.6 us -> none  [body(): gathered = lax.all_gather(packed, 'fsdp', axis=0, tiled=True)]
    pallas_call x2 -> x7, Pallas kernels: 8.78 us -> 21.6 us  [the longest x4 10.4 us: ring_sums(): pl.pallas_call(functools.partial(ring_last, at) if last else ring_add, gr...]
    another operation x2 -> x5, other arithmetic: 1.17 us -> 8.12 us  [the longest x4 6.88 us: ring_sums(): places = jnp.stack(places).astype(jnp.int32)]
    ppermute x9 -> x16, starting transfers between devices: 10.8 us -> 17.5 us  [the longest x3 6.31 us: ring_gather(): going_right = lax.ppermute(going_right, 'fsdp', right)]
    another operation x0 -> x1, local copies, waits for them, and re-layouts: none -> 5.75 us  [ring_gather(): return (shards, jnp.stack(places).astype(jnp.int32))]
    convert_element_type x5 -> x0, other arithmetic: 4.91 us -> none  [the longest x3 2.98 us: sum_rows(): going_right = (mine(step - 1) + from_left).astype(bf16)]
    slice x6 -> x0, local copies, waits for them, and re-layouts: 4.87 us -> none  [the longest x1 2.04 us: body(): gathered[:, wide:2 * wide]]
    all_gather x0 -> x1, blocking collectives: none -> 4.06 us  [body(): db = lax.all_gather(db_own, 'ctx', axis=0, tiled=True)]
  transfers between devices with their start and end apart: 25 -> 30, of which waited for: 14 -> 16; matrix products, arithmetic and copies ran while one was open for 7% -> 11% of each run, Pallas kernels for 4% -> 9%
where the time goes in v3:
time: 238 us; the launch traced here: 237 us
  Pallas kernels  66.2 us (28%)
  waiting for transfers between devices  57.1 us (24%)
  blocking collectives  32.8 us (14%)
  starting transfers between devices  30.7 us (13%)
  local copies, waits for them, and re-layouts  18.4 us (8%)
  matrix products  11.8 us (5%)
  other arithmetic  10.1 us (4%)
  between operations  9.52 us (4%)
    all_to_all x1, blocking collectives, body(): lax.all_to_all(sends.reshape(owners, per_owner, model_width), ('fsdp', 'c...  28.7 us
    ppermute x12, waiting for transfers between devices, swap(): return lax.ppermute(value, axis, [(0, 1), (1, 0)])  21.7 us
    pallas_call x1, Pallas kernels, body(): kernel_call(functools.partial(attention_backward, heads, model_width // f...  13.6 us
    pallas_call x1, Pallas kernels, body(): kernel_call(functools.partial(expert_kernel, owners, capacity, chunks, gr...  13.2 us
    all_to_all x1, waiting for transfers between devices, body(): lax.all_to_all(outgoing, ('fsdp', 'ctx', 'tp'), split_axis=0, concat_axis...  12.9 us
    ppermute x3, waiting for transfers between devices, ring_gather(): going_right = lax.ppermute(going_right, 'fsdp', right)  11.9 us
    pallas_call x4, Pallas kernels, ring_sums(): pl.pallas_call(functools.partial(ring_last, at) if last else ring_add, gr...  10.4 us
    unnamed x64, local copies, waits for them, and re-layouts  8.04 us
  transfers between devices with their start and end apart: 30, of which 16 were waited for; matrix products, arithmetic and copies ran while one was open for 11% of the time, Pallas kernels for 9%

profile of v3, /device:TPU:0, one launch (start us, length us, event | category | flops | bytes accessed | tf_op | source)
XLA Modules:
  0.0 236.5 jit_solution(13345970072415532201)
XLA Ops:
  0.6 1.2 dynamic_slice.58
  10.5 1.7 fusion
  12.2 1.2 pad_add_fusion.refs_0_.refs_1_
  13.4 1.7 shard_map.346
  15.6 1.1 collective-permute-done.1
  16.7 0.9 pad_maximum_fusion.refs_2_
  17.6 3.0 %collective-permute-start.2 = (bf16[96,896]{1,0:T(8,128)(2,1)S(1)}, bf16[96,896]{1,0:T(8,128)(2,1)S(1)}, u32[]{:S(2)}, u32[]{:S(2)}) collective-permute-start(bf16[96,896]{1,0:T(8,128)(2,1)S(1)} %pad_maximum_fusion.refs_2_), channel_id=1, source_target_pairs={{0,8},{8,16},{16,24},{24,28},{28,20},{20,12},{12,4},{4,0},{1,9},{9... | collective-permute-start | bytes 516104 | tf_op jit(solution)/shard_map/ppermute | solution.py:625
  20.5 4.6 %collective-permute-done.2.refs_3_ = bf16[96,896]{1,0:T(8,128)(2,1)S(1)} collective-permute-done((bf16[96,896]{1,0:T(8,128)(2,1)S(1)}, bf16[96,896]{1,0:T(8,128)(2,1)S(1)}, u32[]{:S(2)}, u32[]{:S(2)}) %collective-permute-start.2) | collective-permute-done | bytes 172064 | tf_op jit(solution)/shard_map/ppermute | solution.py:625
  25.2 1.8 collective-permute-start.4
  27.2 3.9 %collective-permute-done.4.refs_5_ = bf16[96,896]{1,0:T(8,128)(2,1)S(1)} collective-permute-done((bf16[96,896]{1,0:T(8,128)(2,1)S(1)}, bf16[96,896]{1,0:T(8,128)(2,1)S(1)}, u32[]{:S(2)}, u32[]{:S(2)}) %collective-permute-start.4) | collective-permute-done | bytes 172064 | tf_op jit(solution)/shard_map/ppermute | solution.py:625
  31.1 1.5 collective-permute-start.6
  33.1 3.4 %collective-permute-done.6.refs_7_ = bf16[96,896]{1,0:T(8,128)(2,1)S(1)} collective-permute-done((bf16[96,896]{1,0:T(8,128)(2,1)S(1)}, bf16[96,896]{1,0:T(8,128)(2,1)S(1)}, u32[]{:S(2)}, u32[]{:S(2)}) %collective-permute-start.6) | collective-permute-done | bytes 172064 | tf_op jit(solution)/shard_map/ppermute | solution.py:625
  36.5 1.6 collective-permute-start.8
  38.1 5.8 %stack.32.refs_0_ = s32[8]{0:T(128)} concatenate(s32[1]{0:T(128)} %get-tuple-element.133, s32[1]{0:T(128)} %get-tuple-element.132, s32[1]{0:T(128)} %get-tuple-element.131, s32[1]{0:T(128)} %get-tuple-element.130, s32[1]{0:T(128)} %get-tuple-element.129, s32[1]{0:T(128)} %get-tuple-element.128, s32[1]{0:T(128)} %get-tuple-element.127, s32[1]{0:T(128)} %get-tuple-element.135), dimensions={0} | concatenate | bytes 64 | tf_op jit(solution)/shard_map/stack | solution.py:631
  45.2 2.6 %shard_map.347 = (bf16[768,640]{1,0:T(8,128)(2,1)}, bf16[384,384]{1,0:T(8,128)(2,1)}) custom-call(s32[8]{0:T(128)} %stack.32.refs_0_, s32[4]{0:T(128)} %pad_add_fusion.refs_0_.refs_1_, bf16[96,896]{1,0:T(8,128)(2,1)} %copy-done.3, bf16[96,896]{1,0:T(8,128)(2,1)} %copy-done.11, bf16[96,896]{1,0:T(8,128)(2,1)} %copy-done.12, bf16[96,896]{1,0:T(8,128)(2,1)} %copy-done.13, ...), custom_call_target="tpu_custom_call" | custom-call | bytes 4194304 | tf_op jit(solution)/shard_map/pallas_call | solution.py:759
  47.8 1.5 collective-permute-start.12
  49.5 7.9 %collective-permute-done.12.refs_8_ = bf16[384,384]{1,0:T(8,128)(2,1)S(1)} collective-permute-done((bf16[384,384]{1,0:T(8,128)(2,1)}, bf16[384,384]{1,0:T(8,128)(2,1)S(1)}, u32[]{:S(2)}, u32[]{:S(2)}) %collective-permute-start.12) | collective-permute-done | bytes 294944 | tf_op jit(solution)/shard_map/ppermute | solution.py:598
  57.4 0.8 copy-done.31
  58.2 7.0 %shard_map.348 = (bf16[512,768]{1,0:T(8,128)(2,1)}, bf16[512,256]{1,0:T(8,128)(2,1)}, bf16[512,256]{1,0:T(8,128)(2,1)}, bf16[512,256]{1,0:T(8,128)(2,1)}, bf16[2...) custom-call(s32[4]{0:T(128)} %pad_add_fusion.refs_0_.refs_1_, ...), custom_call_target="tpu_custom_call" | custom-call | flops 4026531840 | bytes 8388608 | tf_op jit(solution)/shard_map/pallas_call | solution.py:774
  65.1 1.5 collective-permute-start.9
  67.3 1.6 slice.3.refs_11_.refs_5_
  68.9 2.7 %collective-permute-done.9.refs_4_ = bf16[256,256]{1,0:T(8,128)(2,1)S(1)} collective-permute-done((bf16[256,256]{1,0:T(8,128)(2,1)}, bf16[256,256]{1,0:T(8,128)(2,1)S(1)}, u32[]{:S(2)}, u32[]{:S(2)}) %collective-permute-start.9) | collective-permute-done | bytes 131104 | tf_op jit(solution)/shard_map/ppermute | solution.py:598
  71.6 1.9 collective-permute-done.11.refs_6_
  74.5 5.4 %shard_map.349 = (f32[256,768]{1,0:T(8,128)}, bf16[640,768]{1,0:T(8,128)(2,1)}, bf16[768,384]{1,0:T(8,128)(2,1)}) custom-call(s32[4]{0:T(128)} %pad_add_fusion.refs_0_.refs_1_, bf16[256,768]{1,0:T(8,128)(2,1)} %x_own.1, bf16[256,768]{1,0:T(8,128)(2,1)} %refs_4_.6, bf16[256,256]{1,0:T(8,128)(2,1)} %get-tuple-element.73.refs_3_, bf16[256,256]{1,0:T(8,128)(2,1)} %copy-done.24, ...), custom_call_target="tpu_custom_call" | custom-call | flops 805306368 | bytes 6291456 | tf_op jit(solution)/shard_map/pallas_call | solution.py:814
  79.9 28.7 %all_to_all.10 = bf16[16,40,768]{2,1,0:T(8,128)(2,1)} all-to-all(bf16[16,40,768]{2,1,0:T(8,128)(2,1)} %bitcast.22), channel_id=1, replica_groups=mesh['fsdp'=8,'ctx'=2,'tp'=2] {'fsdp','ctx'}, dimensions={0} | all-to-all | bytes 1966080 | tf_op jit(solution)/shard_map/all_to_all | solution.py:830
  108.6 13.2 %shard_map.350 = (bf16[32,40,384]{2,1,0:T(8,128)(2,1)}, bf16[2,160,768]{2,1,0:T(8,128)(2,1)}, bf16[2,160,768]{2,1,0:T(8,128)(2,1)}, bf16[2,160,1536]{2,1,0:T(8,128)(2,1)}, bf16[2,160,1536]{2,1,0:T(8,128)(2,1)}) custom-call(bf16[640,768]{1,0:T(8,128)(2,1)} %bitcast.23, s32[320,1]{1,0:T(8,128)} %constant.134.clone.refs_1_, s32[1,320]{1,0:T(1,128)} %constant.135.clone.refs_2_, ...), custom_call_target="tpu_custom_call" | custom-call | flops 3019898880 | bytes 12582912 | tf_op jit(solution)/shard_map/pallas_call | solution.py:851
  121.8 4.9 %all-to-all-start.1 = ((bf16[32,40,384]{2,1,0:T(8,128)(2,1)}), bf16[32,40,384]{2,1,0:T(8,128)(2,1)S(1)}, u32[]{:S(2)}, u32[]{:S(2)}) async-start(bf16[32,40,384]{2,1,0:T(8,128)(2,1)} %get-tuple-element.78), calls=%async_computation.1 | async-start | bytes 1966080 | tf_op jit(solution)/shard_map/all_to_all | solution.py:884
  126.7 6.5 %fusion.1 = f32[2,768,1536]{2,1,0:T(8,128)} fusion(bf16[2,160,768]{2,1,0:T(8,128)(2,1)} %get-tuple-element.79, bf16[2,160,1536]{2,1,0:T(8,128)(2,1)} %get-tuple-element.80), kind=kOutput, calls=%fused_computation.8 | convolution fusion | flops 754974720 | bytes 10911744 | tf_op jit(solution)/shard_map/lrd,lrf->ldf/dot_general | solution.py:366
  133.3 5.2 %fusion.2 = f32[2,1536,768]{2,1,0:T(8,128)} fusion(bf16[2,160,1536]{2,1,0:T(8,128)(2,1)S(1)} %copy-done.2, bf16[2,160,768]{2,1,0:T(8,128)(2,1)S(1)} %copy-done.4), kind=kOutput, calls=%fused_computation.9 | convolution fusion | flops 754974720 | bytes 10911744 | tf_op jit(solution)/shard_map/lrf,lrd->lfd/dot_general | solution.py:367
  138.5 12.9 %all-to-all-done.1 = bf16[32,40,384]{2,1,0:T(8,128)(2,1)S(1)} async-done(((bf16[32,40,384]{2,1,0:T(8,128)(2,1)}), bf16[32,40,384]{2,1,0:T(8,128)(2,1)S(1)}, u32[]{:S(2)}, u32[]{:S(2)}) %all-to-all-start.1) | async-done | bytes 983072 | tf_op jit(solution)/shard_map/all_to_all | solution.py:884
  151.4 1.0 copy-done.1
  152.4 3.2 %shard_map.351.refs_1_ = bf16[256,768]{1,0:T(8,128)(2,1)} custom-call(bf16[1280,384]{1,0:T(8,128)(2,1)} %bitcast.21, s32[1,256]{1,0:T(1,128)} %bitcast.26, s32[1,256]{1,0:T(1,128)} %bitcast.29, s32[1,1280]{1,0:T(1,128)} %constant.136.clone.refs_3_, s32[1,1280]{1,0:T(1,128)} %constant.137.clone.refs_4_), custom_call_target="tpu_custom_call" | custom-call | flops 503316480 | bytes 2097152 | tf_op jit(solution)/shard_map/pallas_call | solution.py:892
  155.6 1.5 collective-permute-start.15
  157.1 9.9 %collective-permute-done.15.refs_2_ = bf16[256,768]{1,0:T(8,128)(2,1)S(1)} collective-permute-done((bf16[256,768]{1,0:T(8,128)(2,1)}, bf16[256,768]{1,0:T(8,128)(2,1)S(1)}, u32[]{:S(2)}, u32[]{:S(2)}) %collective-permute-start.15) | collective-permute-done | bytes 393248 | tf_op jit(solution)/shard_map/ppermute | solution.py:598
  167.0 0.8 copy-done.6
  167.7 4.5 %shard_map.352 = (f32[256,768]{1,0:T(8,128)}, f32[256,768]{1,0:T(8,128)}, bf16[256,768]{1,0:T(8,128)(2,1)}, bf16[768,128]{1,0:T(8,128)(2,1)}) custom-call(s32[4]{0:T(128)} %pad_add_fusion.refs_0_.refs_1_, bf16[256,768]{1,0:T(8,128)(2,1)} %shard_map.351.refs_1_, bf16[256,768]{1,0:T(8,128)(2,1)} %copy-done.6, f32[256,768]{1,0:T(8,128)} %get-tuple-element.84.refs_3_, ...), custom_call_target="tpu_custom_call" | custom-call | flops 150994944 | bytes 6291456 | tf_op jit(solution)/shard_map/pallas_call | solution.py:901
  172.2 4.1 %all_gather.3.refs_10_ = bf16[512,768]{1,0:T(8,128)(2,1)} all-gather(bf16[256,768]{1,0:T(8,128)(2,1)} %get-tuple-element.91), channel_id=1, replica_groups=mesh['fsdp'=8,'ctx'=2,'tp'=2] {'ctx'}, dimensions={0}, use_global_device_ids=true | all-gather | bytes 1179648 | tf_op jit(solution)/shard_map/all_gather | solution.py:913
  176.2 13.6 %shard_map.353 = (bf16[768,896]{1,0:T(8,128)(2,1)}, bf16[48,896]{1,0:T(8,128)(2,1)}, bf16[48,896]{1,0:T(8,128)(2,1)}, bf16[256,768]{1,0:T(8,128)(2,1)}, bf16[256,768]{1,0:T(8,128)(2,1)}) custom-call(s32[4]{0:T(128)} %pad_add_fusion.refs_0_.refs_1_, s32[1,4]{1,0:T(1,128)} %refs_1_.8, f32[6,32]{1,0:T(8,128)} %bitcast.35, bf16[256,768]{1,0:T(8,128)(2,1)} %x_own.1, ...), custom_call_target="tpu_custom_call" | custom-call | flops 6039797760 | bytes 8388608 | tf_op jit(solution)/shard_map/pallas_call | solution.py:916
  190.2 1.1 collective-permute-start.18
  191.3 1.0 collective-permute-start.19
  192.3 1.9 add_add_fusion.3.places
  194.1 0.9 collective-permute-done.18.from_left
  195.0 1.0 collective-permute-done.19.from_right
  196.6 2.5 %shard_map.354 = (bf16[96,896]{1,0:T(8,128)(2,1)}, bf16[96,896]{1,0:T(8,128)(2,1)}) custom-call(s32[3]{0:T(128)} %add_add_fusion.3.places, bf16[768,896]{1,0:T(8,128)(2,1)} %get-tuple-element.95.right_mine.left_mine.mine, bf16[768,896]{1,0:T(8,128)(2,1)} %get-tuple-element.95.right_mine.left_mine.mine, bf16[48,896]{1,0:T(8,128)(2,1)} %copy-done.27, ...), custom_call_target="tpu_custom_call" | custom-call | bytes 1048576 | tf_op jit(solution)/shard_map/pallas_call | solution.py:665
  199.2 1.1 collective-permute-start.20
  200.3 0.9 collective-permute-start.21
  201.2 1.1 add_convert_fusion.near
  202.3 1.0 collective-permute-start.17
  203.3 1.9 add_add_fusion.2.places
  205.2 0.7 collective-permute-done.21.from_right
  206.6 2.6 %shard_map.355 = (bf16[96,896]{1,0:T(8,128)(2,1)}, bf16[96,896]{1,0:T(8,128)(2,1)}) custom-call(s32[3]{0:T(128)} %add_add_fusion.2.places, bf16[768,896]{1,0:T(8,128)(2,1)} %get-tuple-element.95.right_mine.left_mine.mine, bf16[768,896]{1,0:T(8,128)(2,1)} %get-tuple-element.95.right_mine.left_mine.mine, bf16[96,896]{1,0:T(8,128)(2,1)} %copy-done.20, ...), custom_call_target="tpu_custom_call" | custom-call | bytes 1048576 | tf_op jit(solution)/shard_map/pallas_call | solution.py:665
  209.9 1.4 collective-permute-start.23
  211.3 1.9 add_add_fusion.1.places
  213.2 1.7 collective-permute-done.22.from_left
  216.2 2.6 %shard_map.356 = (bf16[96,896]{1,0:T(8,128)(2,1)}, bf16[96,896]{1,0:T(8,128)(2,1)}) custom-call(s32[3]{0:T(128)} %add_add_fusion.1.places, bf16[768,896]{1,0:T(8,128)(2,1)} %get-tuple-element.95.right_mine.left_mine.mine, bf16[768,896]{1,0:T(8,128)(2,1)} %get-tuple-element.95.right_mine.left_mine.mine, bf16[96,896]{1,0:T(8,128)(2,1)} %copy-done.22, ...), custom_call_target="tpu_custom_call" | custom-call | bytes 1048576 | tf_op jit(solution)/shard_map/pallas_call | solution.py:665
  218.9 1.5 collective-permute-start.24
  220.9 1.2 add_add_fusion.places
  222.1 2.4 collective-permute-done.24.from_left
  224.5 1.5 collective-permute-done.25.from_right
  226.6 2.6 %shard_map.357 = (f32[48,896]{1,0:T(8,128)}, f32[56,896]{1,0:T(8,128)}, f32[8,128]{1,0:T(8,128)}, f32[48,128]{1,0:T(8,128)}, f32[48,128]{1,0:T(8,128)}) custom-call(s32[3]{0:T(128)} %add_add_fusion.places, bf16[768,896]{1,0:T(8,128)(2,1)} %get-tuple-element.95.right_mine.left_mine.mine, bf16[96,896]{1,0:T(8,128)(2,1)} %copy-done.17, bf16[96,896]{1,0:T(8,128)(2,1)} %copy-done.19), custom_call_target="tpu_custom_call" | custom-call | bytes 1048576 | tf_op jit(solution)/shard_map/pallas_call | solution.py:665
  229.2 1.1 collective-permute-start.27
  230.3 0.8 collective-permute-start.28
  231.1 2.7 %shard_map.358 = f32[256,768]{1,0:T(8,128)} custom-call(bf16[256,768]{1,0:T(8,128)(2,1)} %x_own.1, f32[256,768]{1,0:T(8,128)} %get-tuple-element.109.dmiddle, f32[8,768]{1,0:T(8,128)} %get-tuple-element.76.refs_12_.refs_6_.gains, bf16[256,768]{1,0:T(8,128)(2,1)} %copy-done, bf16[256,768]{1,0:T(8,128)(2,1)} %copy-done.5), custom_call_target="tpu_custom_call" | custom-call | bytes 4194304 | tf_op jit(solution)/shard_map/pallas_call | solution.py:951
  234.5 1.9 shard_map.359
  (89 shorter events, 9.9 us)
Async XLA Ops:
  15.1 1.6 collective-permute-start.1
  17.6 26.3 %copy-start.3 = (bf16[96,896]{1,0:T(8,128)(2,1)}, bf16[96,896]{1,0:T(8,128)(2,1)S(1)}, u32[]{:S(2)}) copy-start(bf16[96,896]{1,0:T(8,128)(2,1)S(1)} %pad_maximum_fusion.refs_2_) | copy-start | bytes 516100
  17.6 7.6 %collective-permute-start.2 = (bf16[96,896]{1,0:T(8,128)(2,1)S(1)}, bf16[96,896]{1,0:T(8,128)(2,1)S(1)}, u32[]{:S(2)}, u32[]{:S(2)}) collective-permute-start(bf16[96,896]{1,0:T(8,128)(2,1)S(1)} %pad_maximum_fusion.refs_2_), channel_id=1, source_target_pairs={{0,8},{8,16},{16,24},{24,28},{28,20},{20,12},{12,4},{4,0},{1,9},{9... | collective-permute-start | bytes 516104 | tf_op jit(solution)/shard_map/ppermute | solution.py:625
  20.5 6.4 %collective-permute-start.3 = (bf16[96,896]{1,0:T(8,128)(2,1)S(1)}, bf16[96,896]{1,0:T(8,128)(2,1)S(1)}, u32[]{:S(2)}, u32[]{:S(2)}) collective-permute-start(bf16[96,896]{1,0:T(8,128)(2,1)S(1)} %pad_maximum_fusion.refs_2_), channel_id=1, source_target_pairs={{8,0},{16,8},{24,16},{28,24},{20,28},{12,20},{4,12},{0,4},{9,1},{1... | collective-permute-start | bytes 516104 | tf_op jit(solution)/shard_map/ppermute | solution.py:626
  25.2 18.7 %copy-start.11 = (bf16[96,896]{1,0:T(8,128)(2,1)}, bf16[96,896]{1,0:T(8,128)(2,1)S(1)}, u32[]{:S(2)}) copy-start(bf16[96,896]{1,0:T(8,128)(2,1)S(1)} %collective-permute-done.2.refs_3_) | copy-start | bytes 516100
  25.2 5.9 %collective-permute-start.4 = (bf16[96,896]{1,0:T(8,128)(2,1)S(1)}, bf16[96,896]{1,0:T(8,128)(2,1)S(1)}, u32[]{:S(2)}, u32[]{:S(2)}) collective-permute-start(bf16[96,896]{1,0:T(8,128)(2,1)S(1)} %collective-permute-done.2.refs_3_), channel_id=1, source_target_pairs={{0,8},{8,16},{16,24},{24,28},{28,20},{20,12},{12,4},{4,0},{1,9},{9... | collective-permute-start | bytes 516104 | tf_op jit(solution)/shard_map/ppermute | solution.py:625
  27.0 16.9 %copy-start.12 = (bf16[96,896]{1,0:T(8,128)(2,1)}, bf16[96,896]{1,0:T(8,128)(2,1)S(1)}, u32[]{:S(2)}) copy-start(bf16[96,896]{1,0:T(8,128)(2,1)S(1)} %collective-permute-done.3.refs_4_) | copy-start | bytes 516100
  27.0 5.6 %collective-permute-start.5 = (bf16[96,896]{1,0:T(8,128)(2,1)S(1)}, bf16[96,896]{1,0:T(8,128)(2,1)S(1)}, u32[]{:S(2)}, u32[]{:S(2)}) collective-permute-start(bf16[96,896]{1,0:T(8,128)(2,1)S(1)} %collective-permute-done.3.refs_4_), channel_id=1, source_target_pairs={{8,0},{16,8},{24,16},{28,24},{20,28},{12,20},{4,12},{0,4},{9,1},{1... | collective-permute-start | bytes 516104 | tf_op jit(solution)/shard_map/ppermute | solution.py:626
  31.1 12.8 %copy-start.13 = (bf16[96,896]{1,0:T(8,128)(2,1)}, bf16[96,896]{1,0:T(8,128)(2,1)S(1)}, u32[]{:S(2)}) copy-start(bf16[96,896]{1,0:T(8,128)(2,1)S(1)} %collective-permute-done.4.refs_5_) | copy-start | bytes 516100
  31.1 5.4 %collective-permute-start.6 = (bf16[96,896]{1,0:T(8,128)(2,1)S(1)}, bf16[96,896]{1,0:T(8,128)(2,1)S(1)}, u32[]{:S(2)}, u32[]{:S(2)}) collective-permute-start(bf16[96,896]{1,0:T(8,128)(2,1)S(1)} %collective-permute-done.4.refs_5_), channel_id=1, source_target_pairs={{0,8},{8,16},{16,24},{24,28},{28,20},{20,12},{12,4},{4,0},{1,9},{9... | collective-permute-start | bytes 516104 | tf_op jit(solution)/shard_map/ppermute | solution.py:625
  32.6 11.3 %copy-start.14 = (bf16[96,896]{1,0:T(8,128)(2,1)}, bf16[96,896]{1,0:T(8,128)(2,1)S(1)}, u32[]{:S(2)}) copy-start(bf16[96,896]{1,0:T(8,128)(2,1)S(1)} %collective-permute-done.5.refs_6_) | copy-start | bytes 516100
  32.6 11.2 %collective-permute-start.7 = (bf16[96,896]{1,0:T(8,128)(2,1)S(1)}, bf16[96,896]{1,0:T(8,128)(2,1)S(1)}, u32[]{:S(2)}, u32[]{:S(2)}) collective-permute-start(bf16[96,896]{1,0:T(8,128)(2,1)S(1)} %collective-permute-done.5.refs_6_), channel_id=1, source_target_pairs={{8,0},{16,8},{24,16},{28,24},{20,28},{12,20},{4,12},{0,4},{9,1},{1... | collective-permute-start | bytes 516104 | tf_op jit(solution)/shard_map/ppermute | solution.py:626
  36.5 7.4 %copy-start.15 = (bf16[96,896]{1,0:T(8,128)(2,1)}, bf16[96,896]{1,0:T(8,128)(2,1)S(1)}, u32[]{:S(2)}) copy-start(bf16[96,896]{1,0:T(8,128)(2,1)S(1)} %collective-permute-done.6.refs_7_) | copy-start | bytes 516100
  36.5 7.4 %collective-permute-start.8 = (bf16[96,896]{1,0:T(8,128)(2,1)S(1)}, bf16[96,896]{1,0:T(8,128)(2,1)S(1)}, u32[]{:S(2)}, u32[]{:S(2)}) collective-permute-start(bf16[96,896]{1,0:T(8,128)(2,1)S(1)} %collective-permute-done.6.refs_7_), channel_id=1, source_target_pairs={{0,8},{8,16},{16,24},{24,28},{28,20},{20,12},{12,4},{4,0},{1,9},{9... | collective-permute-start | bytes 516104 | tf_op jit(solution)/shard_map/ppermute | solution.py:629
  38.1 19.3 %collective-permute-start = (bf16[256,768]{1,0:T(8,128)(2,1)}, bf16[256,768]{1,0:T(8,128)(2,1)S(1)}, u32[]{:S(2)}, u32[]{:S(2)}) collective-permute-start(bf16[256,768]{1,0:T(8,128)(2,1)} %x_own.1), channel_id=1, source_target_pairs={{0,2},{2,0},{1,3},{3,1},{4,6},{6,4},{5,7},{7,5},{8,10},{10,8},{9,1... | collective-permute-start | bytes 1179656 | tf_op jit(solution)/shard_map/ppermute | solution.py:598
  43.8 0.7 copy-start.16
  44.5 0.7 copy-start.18
  47.8 9.6 %collective-permute-start.12 = (bf16[384,384]{1,0:T(8,128)(2,1)}, bf16[384,384]{1,0:T(8,128)(2,1)S(1)}, u32[]{:S(2)}, u32[]{:S(2)}) collective-permute-start(bf16[384,384]{1,0:T(8,128)(2,1)} %get-tuple-element.75.refs_7_), channel_id=1, source_target_pairs={{0,1},{1,0},{2,3},{3,2},{4,5},{5,4},{6,7},{7,6},{8,9},{9,8},{10,11... | collective-permute-start | bytes 884744 | tf_op jit(solution)/shard_map/ppermute | solution.py:598
  49.3 24.3 %collective-permute-start.13 = (bf16[384,384]{1,0:T(8,128)(2,1)}, bf16[384,384]{1,0:T(8,128)(2,1)S(1)}, u32[]{:S(2)}, u32[]{:S(2)}) collective-permute-start(bf16[384,384]{1,0:T(8,128)(2,1)} %get-tuple-element.75.refs_7_), channel_id=1, source_target_pairs={{0,2},{2,0},{1,3},{3,1},{4,6},{6,4},{5,7},{7,5},{8,10},{10,8},{9,1... | collective-permute-start | bytes 884744 | tf_op jit(solution)/shard_map/ppermute | solution.py:598
  57.4 16.2 %copy-start.7 = (bf16[384,384]{1,0:T(8,128)(2,1)}, bf16[384,384]{1,0:T(8,128)(2,1)S(1)}, u32[]{:S(2)}) copy-start(bf16[384,384]{1,0:T(8,128)(2,1)S(1)} %collective-permute-done.12.refs_8_) | copy-start | bytes 884740
  57.4 16.2 %collective-permute-start.14 = (bf16[384,384]{1,0:T(8,128)(2,1)S(1)}, bf16[384,384]{1,0:T(8,128)(2,1)S(1)}, u32[]{:S(2)}, u32[]{:S(2)}) collective-permute-start(bf16[384,384]{1,0:T(8,128)(2,1)S(1)} %collective-permute-done.12.refs_8_), channel_id=1, source_target_pairs={{0,2},{2,0},{1,3},{3,1},{4,6},{6,4},{5,7},{7,5},{8,10},{10,8},{9,1... | collective-permute-start | bytes 884744 | tf_op jit(solution)/shard_map/ppermute | solution.py:598
  57.4 0.8 copy-start.31
  65.1 6.5 %collective-permute-start.9 = (bf16[256,256]{1,0:T(8,128)(2,1)}, bf16[256,256]{1,0:T(8,128)(2,1)S(1)}, u32[]{:S(2)}, u32[]{:S(2)}) collective-permute-start(bf16[256,256]{1,0:T(8,128)(2,1)} %get-tuple-element.73.refs_3_), channel_id=1, source_target_pairs={{0,1},{1,0},{2,3},{3,2},{4,5},{5,4},{6,7},{7,6},{8,9},{9,8},{10,11... | collective-permute-start | bytes 393224 | tf_op jit(solution)/shard_map/ppermute | solution.py:598
  66.6 6.9 %collective-permute-start.11 = (bf16[256,256]{1,0:T(8,128)(2,1)}, bf16[256,256]{1,0:T(8,128)(2,1)S(1)}, u32[]{:S(2)}, u32[]{:S(2)}) collective-permute-start(bf16[256,256]{1,0:T(8,128)(2,1)} %get-tuple-element.74), channel_id=1, source_target_pairs={{0,3},{1,2},{2,1},{3,0},{4,7},{5,6},{6,5},{7,4},{8,11},{9,10},{10,... | collective-permute-start | bytes 393224 | tf_op jit(solution)/shard_map/ppermute | solution.py:800
  66.9 6.6 %collective-permute-start.10 = (bf16[256,256]{1,0:T(8,128)(2,1)}, bf16[256,256]{1,0:T(8,128)(2,1)S(1)}, u32[]{:S(2)}, u32[]{:S(2)}) collective-permute-start(bf16[256,256]{1,0:T(8,128)(2,1)} %get-tuple-element.74), channel_id=1, source_target_pairs={{0,2},{2,0},{1,3},{3,1},{4,6},{6,4},{5,7},{7,5},{8,10},{10,8},{9,1... | collective-permute-start | bytes 393224 | tf_op jit(solution)/shard_map/ppermute | solution.py:598
  71.6 2.0 copy-start.24
  73.6 0.6 copy-start.25
  73.6 0.7 copy-start.26
  73.6 0.8 copy-start.8
  73.6 0.9 copy-start.9
  121.8 11.4 %copy-start.2 = (bf16[2,160,1536]{2,1,0:T(8,128)(2,1)S(1)}, bf16[2,160,1536]{2,1,0:T(8,128)(2,1)}, u32[]{:S(2)}) copy-start(bf16[2,160,1536]{2,1,0:T(8,128)(2,1)} %get-tuple-element.81) | copy-start | bytes 2949124
  121.8 11.4 %copy-start.4 = (bf16[2,160,768]{2,1,0:T(8,128)(2,1)S(1)}, bf16[2,160,768]{2,1,0:T(8,128)(2,1)}, u32[]{:S(2)}) copy-start(bf16[2,160,768]{2,1,0:T(8,128)(2,1)} %get-tuple-element.82) | copy-start | bytes 1474564
  121.8 29.5 %all-to-all-start.1 = ((bf16[32,40,384]{2,1,0:T(8,128)(2,1)}), bf16[32,40,384]{2,1,0:T(8,128)(2,1)S(1)}, u32[]{:S(2)}, u32[]{:S(2)}) async-start(bf16[32,40,384]{2,1,0:T(8,128)(2,1)} %get-tuple-element.78), calls=%async_computation.1 | async-start | bytes 1966080 | tf_op jit(solution)/shard_map/all_to_all | solution.py:884
  151.4 1.0 copy-start.1
  155.6 11.4 %collective-permute-start.15 = (bf16[256,768]{1,0:T(8,128)(2,1)}, bf16[256,768]{1,0:T(8,128)(2,1)S(1)}, u32[]{:S(2)}, u32[]{:S(2)}) collective-permute-start(bf16[256,768]{1,0:T(8,128)(2,1)} %shard_map.351.refs_1_), channel_id=1, source_target_pairs={{0,1},{1,0},{2,3},{3,2},{4,5},{5,4},{6,7},{7,6},{8,9},{9,8},{10,11... | collective-permute-start | bytes 1179656 | tf_op jit(solution)/shard_map/ppermute | solution.py:598
  167.0 0.8 copy-start.6
  189.8 11.3 %collective-permute-start.16 = (bf16[256,768]{1,0:T(8,128)(2,1)}, bf16[256,768]{1,0:T(8,128)(2,1)S(1)}, u32[]{:S(2)}, u32[]{:S(2)}) collective-permute-start(bf16[256,768]{1,0:T(8,128)(2,1)} %get-tuple-element.97), channel_id=1, source_target_pairs={{0,2},{2,0},{1,3},{3,1},{4,6},{6,4},{5,7},{7,5},{8,10},{10,8},{9,1... | collective-permute-start | bytes 1179656 | tf_op jit(solution)/shard_map/ppermute | solution.py:598
  190.2 4.8 %collective-permute-start.18 = (bf16[48,896]{1,0:T(8,128)(2,1)}, bf16[48,896]{1,0:T(8,128)(2,1)S(1)}, u32[]{:S(2)}, u32[]{:S(2)}) collective-permute-start(bf16[48,896]{1,0:T(8,128)(2,1)} %get-tuple-element.98), channel_id=1, source_target_pairs={{0,8},{8,16},{16,24},{24,28},{28,20},{20,12},{12,4},{4,0},{1,9},{9... | collective-permute-start | bytes 258056 | tf_op jit(solution)/shard_map/ppermute | solution.py:656
  191.3 4.7 %collective-permute-start.19 = (bf16[48,896]{1,0:T(8,128)(2,1)}, bf16[48,896]{1,0:T(8,128)(2,1)S(1)}, u32[]{:S(2)}, u32[]{:S(2)}) collective-permute-start(bf16[48,896]{1,0:T(8,128)(2,1)} %get-tuple-element.99), channel_id=1, source_target_pairs={{8,0},{16,8},{24,16},{28,24},{20,28},{12,20},{4,12},{0,4},{9,1},{1... | collective-permute-start | bytes 258056 | tf_op jit(solution)/shard_map/ppermute | solution.py:657
  195.0 1.0 copy-start.27
  196.0 0.6 copy-start.28
  199.2 6.0 %collective-permute-start.20 = (bf16[96,896]{1,0:T(8,128)(2,1)}, bf16[96,896]{1,0:T(8,128)(2,1)S(1)}, u32[]{:S(2)}, u32[]{:S(2)}) collective-permute-start(bf16[96,896]{1,0:T(8,128)(2,1)} %get-tuple-element.100), channel_id=1, source_target_pairs={{0,8},{8,16},{16,24},{24,28},{28,20},{20,12},{12,4},{4,0},{1,9},{9... | collective-permute-start | bytes 516104 | tf_op jit(solution)/shard_map/ppermute | solution.py:656
  200.3 5.6 %collective-permute-start.21 = (bf16[96,896]{1,0:T(8,128)(2,1)}, bf16[96,896]{1,0:T(8,128)(2,1)S(1)}, u32[]{:S(2)}, u32[]{:S(2)}) collective-permute-start(bf16[96,896]{1,0:T(8,128)(2,1)} %get-tuple-element.101), channel_id=1, source_target_pairs={{8,0},{16,8},{24,16},{28,24},{20,28},{12,20},{4,12},{0,4},{9,1},{1... | collective-permute-start | bytes 516104 | tf_op jit(solution)/shard_map/ppermute | solution.py:657
  202.3 28.8 %copy-start = (bf16[256,768]{1,0:T(8,128)(2,1)}, bf16[256,768]{1,0:T(8,128)(2,1)S(1)}, u32[]{:S(2)}) copy-start(bf16[256,768]{1,0:T(8,128)(2,1)S(1)} %add_convert_fusion.near) | copy-start | bytes 1179652
  202.3 23.7 %collective-permute-start.17 = (bf16[256,768]{1,0:T(8,128)(2,1)S(1)}, bf16[256,768]{1,0:T(8,128)(2,1)S(1)}, u32[]{:S(2)}, u32[]{:S(2)}) collective-permute-start(bf16[256,768]{1,0:T(8,128)(2,1)S(1)} %add_convert_fusion.near), channel_id=1, source_target_pairs={{0,1},{1,0},{2,3},{3,2},{4,5},{5,4},{6,7},{7,6},{8,9},{9,8},{10,11... | collective-permute-start | bytes 1179656 | tf_op jit(solution)/shard_map/ppermute | solution.py:598
  205.2 0.7 copy-start.20
  205.9 0.7 copy-start.21
  209.2 5.6 %collective-permute-start.22 = (bf16[96,896]{1,0:T(8,128)(2,1)}, bf16[96,896]{1,0:T(8,128)(2,1)S(1)}, u32[]{:S(2)}, u32[]{:S(2)}) collective-permute-start(bf16[96,896]{1,0:T(8,128)(2,1)} %get-tuple-element.102), channel_id=1, source_target_pairs={{0,8},{8,16},{16,24},{24,28},{28,20},{20,12},{12,4},{4,0},{1,9},{9... | collective-permute-start | bytes 516104 | tf_op jit(solution)/shard_map/ppermute | solution.py:656
  209.9 5.6 %collective-permute-start.23 = (bf16[96,896]{1,0:T(8,128)(2,1)}, bf16[96,896]{1,0:T(8,128)(2,1)S(1)}, u32[]{:S(2)}, u32[]{:S(2)}) collective-permute-start(bf16[96,896]{1,0:T(8,128)(2,1)} %get-tuple-element.103), channel_id=1, source_target_pairs={{8,0},{16,8},{24,16},{28,24},{20,28},{12,20},{4,12},{0,4},{9,1},{1... | collective-permute-start | bytes 516104 | tf_op jit(solution)/shard_map/ppermute | solution.py:657
  214.9 0.7 copy-start.22
  215.5 0.7 copy-start.23
  218.9 5.6 %collective-permute-start.24 = (bf16[96,896]{1,0:T(8,128)(2,1)}, bf16[96,896]{1,0:T(8,128)(2,1)S(1)}, u32[]{:S(2)}, u32[]{:S(2)}) collective-permute-start(bf16[96,896]{1,0:T(8,128)(2,1)} %get-tuple-element.104), channel_id=1, source_target_pairs={{0,8},{8,16},{16,24},{24,28},{28,20},{20,12},{12,4},{4,0},{1,9},{9... | collective-permute-start | bytes 516104 | tf_op jit(solution)/shard_map/ppermute | solution.py:656
  220.3 5.6 %collective-permute-start.25 = (bf16[96,896]{1,0:T(8,128)(2,1)}, bf16[96,896]{1,0:T(8,128)(2,1)S(1)}, u32[]{:S(2)}, u32[]{:S(2)}) collective-permute-start(bf16[96,896]{1,0:T(8,128)(2,1)} %get-tuple-element.105), channel_id=1, source_target_pairs={{8,0},{16,8},{24,16},{28,24},{20,28},{12,20},{4,12},{0,4},{9,1},{1... | collective-permute-start | bytes 516104 | tf_op jit(solution)/shard_map/ppermute | solution.py:657
  224.5 1.5 copy-start.17
  226.0 0.7 copy-start.19
  226.6 4.4 %copy-start.5 = (bf16[256,768]{1,0:T(8,128)(2,1)}, bf16[256,768]{1,0:T(8,128)(2,1)S(1)}, u32[]{:S(2)}) copy-start(bf16[256,768]{1,0:T(8,128)(2,1)S(1)} %collective-permute-done.17.far) | copy-start | bytes 1179652
  229.2 4.6 %collective-permute-start.26 = (f32[56,896]{1,0:T(8,128)}, f32[56,896]{1,0:T(8,128)S(1)}, u32[]{:S(2)}, u32[]{:S(2)}) collective-permute-start(f32[56,896]{1,0:T(8,128)} %get-tuple-element.108), channel_id=1, source_target_pairs={{0,2},{2,0},{1,3},{3,1},{4,6},{6,4},{5,7},{7,5},{8,10},{10,8},{9,1... | collective-permute-start | bytes 602120 | tf_op jit(solution)/shard_map/ppermute | solution.py:598
  229.2 4.6 %collective-permute-start.27 = (f32[48,128]{1,0:T(8,128)}, f32[48,128]{1,0:T(8,128)S(1)}, u32[]{:S(2)}, u32[]{:S(2)}) collective-permute-start(f32[48,128]{1,0:T(8,128)} %get-tuple-element.114), channel_id=1, source_target_pairs={{0,1},{1,0},{2,3},{3,2},{4,5},{5,4},{6,7},{7,6},{8,9},{9,8},{10,11... | collective-permute-start | bytes 73736 | tf_op jit(solution)/shard_map/ppermute | solution.py:598
  230.3 3.6 %collective-permute-start.28 = (f32[48,128]{1,0:T(8,128)}, f32[48,128]{1,0:T(8,128)S(1)}, u32[]{:S(2)}, u32[]{:S(2)}) collective-permute-start(f32[48,128]{1,0:T(8,128)} %get-tuple-element.115), channel_id=1, source_target_pairs={{0,3},{1,2},{2,1},{3,0},{4,7},{5,6},{6,5},{7,4},{8,11},{9,10},{10,... | collective-permute-start | bytes 73736 | tf_op jit(solution)/shard_map/ppermute | solution.py:950
  233.8 0.7 copy-start.10
  233.8 0.7 copy-start.29
  233.9 0.7 copy-start.30

commit v4 on v3

--- a/solution.py
+++ b/solution.py
@@ -15,7 +15,8 @@
 LANES = 128
 STRIP = 128
 HEAD_SIZE = 64
-VMEM_BYTES = 60 * 1024 * 1024
+VMEM_BYTES = 40 * 1024 * 1024
+SMALL_VMEM_BYTES = 16 * 1024 * 1024
 f32 = jnp.float32
 bf16 = jnp.bfloat16
 vmem = pl.BlockSpec(memory_space=pltpu.VMEM)
@@ -49,7 +50,7 @@
     return side + jnp.where(distance < 8, distance, far_bucket)
 
 
-def kernel_call(body, outs, in_specs, out_specs=None, scratch=(), grid=None, flops=0, moved=0):
+def kernel_call(body, outs, in_specs, out_specs=None, scratch=(), grid=None, flops=0, moved=0, small=False):
     extra = {} if grid is None else {"grid": grid}
     return pl.pallas_call(
         body,
@@ -57,7 +58,7 @@
         in_specs=in_specs,
         out_specs=[vmem] * len(outs) if out_specs is None else out_specs,
         scratch_shapes=list(scratch),
-        compiler_params=pltpu.CompilerParams(vmem_limit_bytes=VMEM_BYTES),
+        compiler_params=pltpu.CompilerParams(vmem_limit_bytes=SMALL_VMEM_BYTES if small else VMEM_BYTES),
         cost_estimate=pl.CostEstimate(flops=flops, bytes_accessed=moved, transcendentals=0),
         **extra,
     )
@@ -164,14 +165,14 @@
 
 
 def put_in_rows(count, *refs):
-    starts, meta = refs[:2]
-    shards = refs[2 : 2 + count]
-    wall, output = refs[2 + count :]
+    meta = refs[0]
+    shards = refs[1 : 1 + count]
+    wall, output = refs[1 + count :]
     wide = wall.shape[1]
     place = meta[0]
     for index, shard in enumerate(shards):
         rows = shard.shape[0] // 2
-        first = starts[index]
+        first = meta[4 + index]
         for half, core in ((0, place), (1, 1 - place)):
             at = pl.multiple_of((2 * first + core) * rows, 16)
             wall[pl.ds(at, rows), :] = shard[half * rows : (half + 1) * rows, :wide]
@@ -237,8 +238,10 @@
             totals = jnp.where(lane == head, top + jnp.log(mass), totals)
         o_all[first : first + STRIP, :] = total.astype(bf16)
         lse[first : first + STRIP, :] = totals
-    o_own[...] = o_all[pl.ds(pl.multiple_of(place * rows, 16), rows), :]
-    o_other[...] = o_all[pl.ds(pl.multiple_of((1 - place) * rows, 16), rows), :]
+    for out, start in ((o_own, place * rows), (o_other, (1 - place) * rows)):
+        values = o_all[pl.ds(pl.multiple_of(start, 16), rows), :].astype(f32)
+        for index, part in enumerate(join(values[: rows // 2], values[rows // 2 :])):
+            out[:, index * LANES : (index + 1) * LANES] = part.astype(bf16)
 
 
 def column_of(line):
@@ -271,9 +274,18 @@
     return jnp.where(keep_row == 1, routes_row * capacity + rank, -2)
 
 
+def unpacked(pair):
+    values = pair[...].astype(f32)
+    lanes = values.shape[1] - LANES
+    upper = jnp.where(iota((1, lanes), 1) < lanes - HEAD_SIZE, values[:, :lanes], 0.0)
+    lower = pltpu.roll(values[:, LANES:], lanes - HEAD_SIZE, 1)
+    lower = jnp.where(iota((1, lanes), 1) < lanes - HEAD_SIZE, lower, 0.0)
+    return jnp.concatenate([upper, lower], axis=0)
+
+
 def heads_of(own, other, place):
-    own = own[...].astype(f32)
-    other = other[...].astype(f32)
+    own = unpacked(own)
+    other = unpacked(other)
     first = jnp.where(place == 0, own, other)
     second = jnp.where(place == 0, other, own)
     return jnp.concatenate(join(first, second), axis=1).astype(bf16)
@@ -284,6 +296,7 @@
     (extras, gains, routes_row, keep_row, slot_h, slot_d) = refs[11:17]
     middle_out, sends, wo_out, wo_other = refs[17:]
     routes_column, keep_column = columns_of(routes_row, keep_row)
+    extras = extras[:, extras.shape[1] - LANES :]
     place, start = meta[0], meta[2]
     interleave(wo_out, slice(None), wo_own, wo_ctx, start, count)
     interleave(wo_other, slice(None), wo_tp, wo_far, start, count)
@@ -292,7 +305,7 @@
     middle = x_own[...].astype(f32) + branch
     middle_out[...] = middle
     hidden = (middle * rms_scale(middle) * gains[1:2]).astype(bf16)
-    _, _, _, gate = routed(hidden, extras[...], routes_column, keep_column, experts)
+    _, _, _, gate = routed(hidden, extras, routes_column, keep_column, experts)
     out_grad = (gate * cotangent[...].astype(f32)).astype(bf16)
     slot = slots_by_row(routes_row[...], keep_row[...], experts, capacity)
     pick_h = (slot_h[...] == slot).astype(f32).astype(bf16)
@@ -382,6 +395,7 @@
 def middle_backward(experts, *refs):
     (meta, both_own, both_tp, middle_ref, cotangent, extras, gains, routes_row, keep_row) = refs[:9]
     routes_column, keep_column = columns_of(routes_row, keep_row)
+    extras = extras[:, extras.shape[1] - LANES :]
     (result, dmiddle_out, branch_grad, router_grad) = refs[9:]
     share = meta[1]
     width = both_own.shape[1] // 2
@@ -396,7 +410,7 @@
     normed = middle * scale
     gain = gains[1:2]
     hidden = (normed * gain).astype(bf16)
-    probs, onehot, kept, gate = routed(hidden, extras[...], routes_column, keep_column, experts)
+    probs, onehot, kept, gate = routed(hidden, extras, routes_column, keep_column, experts)
     result[...] = middle + gate * picked
     upstream = cotangent[...].astype(f32)
     gate_grad = jnp.sum(upstream * picked, axis=1, keepdims=True)
@@ -404,7 +418,7 @@
     logit_grad = (
         probs * (prob_grad - jnp.sum(probs * prob_grad, axis=1, keepdims=True))
     ).astype(bf16)
-    hidden_grad = slot_grad + mm_nt(logit_grad, extras[...])
+    hidden_grad = slot_grad + mm_nt(logit_grad, extras)
     gain_grad = column_of(jnp.sum(hidden_grad * normed, axis=0, keepdims=True))
     lane = iota((1, LANES), 1)
     router_grad[...] = jnp.where(
@@ -540,11 +554,11 @@
 
 def ring_last(at, places, mine, from_left, from_right, own, send, table, riders_own, riders_other):
     total = mine[...].astype(f32) + from_left[...].astype(f32) + from_right[...].astype(f32)
-    ring_end(at, places[2], total, own, send, table, riders_own, riders_other)
+    ring_end(at, places[0], total, own, send, table, riders_own, riders_other)
 
 
 def ring_whole(at, places, sums, own, send, table, riders_own, riders_other):
-    ring_end(at, places[2], sums[...], own, send, table, riders_own, riders_other)
+    ring_end(at, places[0], sums[...], own, send, table, riders_own, riders_other)
 
 
 def shards_of_sums(experts, buckets, heads, *refs):
@@ -608,30 +622,38 @@
     return order, right, [(b, a) for a, b in right]
 
 
-def ring_place(count):
-    order = ring_order(count)
-    inverse = np.zeros(count, np.int32)
-    inverse[order] = np.arange(count)
-    return jnp.asarray(np.array(order, np.int32)), jnp.asarray(inverse)[lax.axis_index("fsdp")]
+def device_table(fsdp_count, ctx_count, tp_count, aligned):
+    order = ring_order(fsdp_count)
+    rows = []
+    for place in range(fsdp_count):
+        spot = order.index(place)
+        at = lambda distance: order[(spot + distance) % fsdp_count]
+        half = fsdp_count // 2
+        ring = [place]
+        for step in range(1, half):
+            ring += [at(-step), at(step)]
+        ring.append(at(half))
+        for step in range(half, 0, -1):
+            ring += [at(step - 1), at(1 - step)]
+        for core in range(ctx_count):
+            for share in range(tp_count):
+                rows.append([core, share, core if aligned else 0, at(half)] + (ring if aligned else []))
+    return np.array(rows, np.int32)
 
 
 def ring_gather(shard, count):
-    order, right, left = ring_steps(count)
-    table, place = ring_place(count)
+    _, right, left = ring_steps(count)
     shards = [shard]
-    places = [table[place]]
     going_right, going_left = shard, shard
     for step in range(1, count // 2):
         going_right = lax.ppermute(going_right, "fsdp", right)
         going_left = lax.ppermute(going_left, "fsdp", left)
         shards += [going_right, going_left]
-        places += [table[(place - step) % count], table[(place + step) % count]]
     shards.append(lax.ppermute(going_right, "fsdp", right))
-    places.append(table[(place + count // 2) % count])
-    return shards, jnp.stack(places).astype(jnp.int32)
-
-
-def ring_sums(payload, top, bottom, count, at, place, side):
+    return shards
+
+
+def ring_sums(payload, top, bottom, count, at, meta, side):
     rows = payload.shape[0] // count
     lanes = payload.shape[1]
     half = rows // 2
@@ -642,21 +664,17 @@
         shape((half, LANES), f32),
         shape((half, LANES), f32),
     ]
-    zero = jnp.zeros((), jnp.int32)
     if rows % 32 or count % 2:
         sums = lax.psum_scatter(payload.astype(f32), "fsdp", scatter_dimension=0, tiled=True)
-        places = jnp.stack([zero, zero, place]).astype(jnp.int32)
-        return kernel_call(functools.partial(ring_whole, at), outs, [smem, vmem])(places, sums)
-    order, right, left = ring_steps(count)
-    table, spot = ring_place(count)
+        return kernel_call(functools.partial(ring_whole, at), outs, [smem, vmem])(meta, sums)
+    _, right, left = ring_steps(count)
     going_right, going_left = top, bottom
     spec = lambda which: pl.BlockSpec((rows, lanes), lambda i, places: (places[which], 0))
-    params = pltpu.CompilerParams(vmem_limit_bytes=VMEM_BYTES)
+    params = pltpu.CompilerParams(vmem_limit_bytes=SMALL_VMEM_BYTES)
     for step in range(count // 2, 0, -1):
         from_left = lax.ppermute(going_right, "fsdp", right)
         from_right = lax.ppermute(going_left, "fsdp", left)
-        places = [table[(spot + step - 1) % count], table[(spot + 1 - step) % count], place]
-        places = jnp.stack(places).astype(jnp.int32)
+        which = 4 + count + 2 * (count // 2 - step)
         whole = lambda dims: pl.BlockSpec(dims, lambda i, places: (0, 0))
         last = step == 1
         if last:
@@ -667,14 +685,14 @@
             grid_spec=pltpu.PrefetchScalarGridSpec(
                 num_scalar_prefetch=1,
                 grid=(1,),
-                in_specs=([spec(0)] if last else [spec(0), spec(1)])
+                in_specs=([spec(which)] if last else [spec(which), spec(which + 1)])
                 + [whole(from_left.shape), whole(from_right.shape)],
                 out_specs=[whole(o.shape) for o in step_outs],
             ),
             out_shape=step_outs,
             compiler_params=params,
             cost_estimate=pl.CostEstimate(flops=0, bytes_accessed=1024 * 1024, transcendentals=0),
-        )(places, *([payload] if last else [payload, payload]), from_left, from_right)
+        )(meta, *([payload] if last else [payload, payload]), from_left, from_right)
         if last:
             return out
         going_right, going_left = out
@@ -723,10 +741,9 @@
     wide = 3 * width + HEAD_SIZE
     aligned = shard_rows % 16 == 0 and fsdp_count % 2 == 0
     count = fsdp_count if aligned else 1
-    start = place if aligned else 0 * place
-    across = ring_place(fsdp_count)[1] + fsdp_count // 2
-    across = ring_place(fsdp_count)[0][across % fsdp_count]
-    meta = jnp.stack([place, share, start, across]).astype(jnp.int32)
+    table = jnp.asarray(device_table(fsdp_count, 2, tp_count, aligned))
+    device = lax.axis_index(("fsdp", "ctx", "tp"))
+    meta = lax.dynamic_slice(table, (device, 0), (1, table.shape[1])).reshape(-1)
     table_rows = rel_table.T
     shard_own, shard_send, wo_shard = kernel_call(
         pack_rows,
@@ -755,13 +772,13 @@
         )
 
     if aligned:
-        shards, places = ring_gather(shard, fsdp_count)
+        shards = ring_gather(shard, fsdp_count)
         wall, wo_own = kernel_call(
             functools.partial(put_in_rows, len(shards)),
             [full((model_width, wide), bf16), full((model_width // 2, 2 * width), bf16)],
-            [smem, smem] + [vmem] * len(shards),
+            [smem] + [vmem] * len(shards),
             moved=4 * 1024 * 1024,
-        )(places, meta, *shards)
+        )(meta, *shards)
     else:
         both = lax.all_gather(shard, "fsdp", axis=0, tiled=False)
         near, far = both[:, :shard_rows], both[:, shard_rows:]
@@ -778,8 +795,8 @@
             full((group, lanes), bf16),
             full((group, lanes), bf16),
             full((group, lanes), bf16),
-            full((rows, lanes), bf16),
-            full((rows, lanes), bf16),
+            full((rows // 2, 2 * width), bf16),
+            full((rows // 2, 2 * width), bf16),
             full((group, lanes), bf16),
             full((group, LANES), f32),
             full((8, model_width), f32),
@@ -791,6 +808,7 @@
     )(meta, lengths, table_rows, tokens, x_other, wall)
     wo_tp = swap(wo_own, "tp")
     wo_ctx = swap(wo_own, "ctx")
+    wo_tp, gains = lax.optimization_barrier((wo_tp, gains))
     wo_far = swap(wo_tp, "ctx")
     wo_own, wo_ctx = ordered(wo_own, wo_ctx)
     wo_tp, wo_far = ordered(wo_tp, wo_far)
@@ -809,7 +827,6 @@
     slot_second = np.where(kind == 1, slot_of, -1).astype(np.int32)
     routes_row = routes.reshape(1, rows)
     keep_row = keep_mask.reshape(1, rows)
-    extras = wall[:, wide - LANES :]
 
     middle, sends, wo_full = kernel_call(
         functools.partial(to_experts, experts, capacity, count),
@@ -823,7 +840,7 @@
         flops=2 * rows * model_width * (model_width + 2 * owners * per_owner),
         moved=6 * 1024 * 1024,
     )(
-        meta, tokens, cotangent, o_own, o_tp, o_ctx, o_far, wo_own, wo_tp, wo_ctx, wo_far, extras,
+        meta, tokens, cotangent, o_own, o_tp, o_ctx, o_far, wo_own, wo_tp, wo_ctx, wo_far, wall,
         gains, routes_row, keep_row, slot_first[:, None], slot_second[:, None],
     )
 
@@ -843,7 +860,7 @@
         + (np.arange(2 * half) // half) * pieces * capacity
         + spot % capacity
     ).astype(np.int32)
-    chunk_width = 512 if hidden_width % 512 == 0 else hidden_width
+    chunk_width = 768 if hidden_width % 768 == 0 else hidden_width
     chunks = hidden_width // chunk_width
     slot_rows = owners * capacity
     part_width = model_width // tp_count
@@ -909,7 +926,7 @@
         [smem] + [vmem] * 8,
         flops=6 * rows * LANES * model_width,
         moved=6 * 1024 * 1024,
-    )(meta, both_own, both_tp, middle, cotangent, extras, gains, routes_row, keep_row)
+    )(meta, both_own, both_tp, middle, cotangent, wall, gains, routes_row, keep_row)
     db = lax.all_gather(db_own, "ctx", axis=0, tiled=True)
 
     half = model_width // fsdp_count // 2
@@ -943,7 +960,7 @@
     dh1_sum = (dh1_own.astype(f32) + swap(dh1_other, "ctx").astype(f32)).astype(bf16)
     dh1_far = swap(dh1_sum, "tp")
     own, send, own_lines, riders_own, riders_other = ring_sums(
-        payload, top, bottom, fsdp_count, wide - LANES, place, dh1_far
+        payload, top, bottom, fsdp_count, wide - LANES, meta, dh1_far
     )
     other = swap(send, "ctx")
     from_tp = swap(riders_own, "tp")

time: 238 us -> 201 us (0.84)
  Pallas kernels: 66.2 us -> 38.6 us
  other arithmetic: 10.1 us -> 0.11 us
  between operations: 9.52 us -> 1.01 us
  local copies, waits for them, and re-layouts: 18.4 us -> 26.4 us
  waiting for transfers between devices: 57.1 us -> 60.8 us
    unnamed x64 -> x98, local copies, waits for them, and re-layouts: 8.04 us -> 25.6 us
    another operation x5 -> x0, other arithmetic: 8.12 us -> none  [the longest x4 6.88 us: ring_sums(): places = jnp.stack(places).astype(jnp.int32)]
    pallas_call x4, Pallas kernels: 10.4 us -> 2.47 us  [ring_sums(): pl.pallas_call(functools.partial(ring_last, at) if last else ring_add, gr...]
    ppermute x4, waiting for transfers between devices: 4.94 us -> 11.9 us  [ring_sums(): from_left = lax.ppermute(going_right, 'fsdp', right)]
    ppermute x12, waiting for transfers between devices: 21.7 us -> 14.8 us  [swap(): return lax.ppermute(value, axis, [(0, 1), (1, 0)])]
    another operation x1 -> x0, local copies, waits for them, and re-layouts: 5.75 us -> none  [ring_gather(): return (shards, jnp.stack(places).astype(jnp.int32))]
    pallas_call x1, Pallas kernels: 13.2 us -> 9.2 us  [body(): kernel_call(functools.partial(expert_kernel, owners, capacity, chunks, gr...]
    pallas_call x1, Pallas kernels: 13.6 us -> 10.5 us  [body(): kernel_call(functools.partial(attention_backward, heads, model_width // f...]
  transfers between devices with their start and end apart: 30 -> 30, of which waited for: 16 -> 21; matrix products, arithmetic and copies ran while one was open for 11% -> 6% of each run, Pallas kernels for 9% -> 5%
where the time goes in v4:
time: 201 us; the launch traced here: 200 us
  waiting for transfers between devices  60.8 us (30%)
  Pallas kernels  38.6 us (19%)
  blocking collectives  31.9 us (16%)
  starting transfers between devices  29.6 us (15%)
  local copies, waits for them, and re-layouts  26.4 us (13%)
  matrix products  11.9 us (6%)
    all_to_all x1, blocking collectives, body(): lax.all_to_all(sends.reshape(owners, per_owner, model_width), ('fsdp', 'c...  29.5 us
    unnamed x98, local copies, waits for them, and re-layouts  25.6 us
    ppermute x12, waiting for transfers between devices, swap(): return lax.ppermute(value, axis, [(0, 1), (1, 0)])  14.8 us
    all_to_all x1, waiting for transfers between devices, body(): lax.all_to_all(outgoing, ('fsdp', 'ctx', 'tp'), split_axis=0, concat_axis...  12.7 us
    ppermute x4, waiting for transfers between devices, ring_sums(): from_left = lax.ppermute(going_right, 'fsdp', right)  11.9 us
    ppermute x3, waiting for transfers between devices, ring_gather(): going_right = lax.ppermute(going_right, 'fsdp', right)  10.9 us
    pallas_call x1, Pallas kernels, body(): kernel_call(functools.partial(attention_backward, heads, model_width // f...  10.5 us
    pallas_call x1, Pallas kernels, body(): kernel_call(functools.partial(expert_kernel, owners, capacity, chunks, gr...  9.2 us
  transfers between devices with their start and end apart: 30, of which 21 were waited for; matrix products, arithmetic and copies ran while one was open for 6% of the time, Pallas kernels for 5%

profile of v4, /device:TPU:0, one launch (start us, length us, event | category | flops | bytes accessed | tf_op | source)
XLA Modules:
  0.0 200.3 jit_solution(7566312536952627104)
XLA Ops:
  0.7 0.8 dynamic-slice_bitcast_fusion.refs_0_.places
  7.9 0.9 collective-permute-done.1
  8.8 3.0 %collective-permute-start.2 = (bf16[96,896]{1,0:T(8,128)(2,1)S(1)}, bf16[96,896]{1,0:T(8,128)(2,1)S(1)}, u32[]{:S(2)}, u32[]{:S(2)}) collective-permute-start(bf16[96,896]{1,0:T(8,128)(2,1)S(1)} %pad_maximum_fusion.refs_1_), channel_id=1, source_target_pairs={{0,8},{8,16},{16,24},{24,28},{28,20},{20,12},{12,4},{4,0},{1,9},{9... | collective-permute-start | bytes 516104 | tf_op jit(solution)/shard_map/ppermute | solution.py:649
  11.8 4.6 %collective-permute-done.2.refs_2_ = bf16[96,896]{1,0:T(8,128)(2,1)S(1)} collective-permute-done((bf16[96,896]{1,0:T(8,128)(2,1)S(1)}, bf16[96,896]{1,0:T(8,128)(2,1)S(1)}, u32[]{:S(2)}, u32[]{:S(2)}) %collective-permute-start.2) | collective-permute-done | bytes 172064 | tf_op jit(solution)/shard_map/ppermute | solution.py:649
  16.4 1.8 collective-permute-start.4
  18.4 3.9 %collective-permute-done.4.refs_4_ = bf16[96,896]{1,0:T(8,128)(2,1)S(1)} collective-permute-done((bf16[96,896]{1,0:T(8,128)(2,1)S(1)}, bf16[96,896]{1,0:T(8,128)(2,1)S(1)}, u32[]{:S(2)}, u32[]{:S(2)}) %collective-permute-start.4) | collective-permute-done | bytes 172064 | tf_op jit(solution)/shard_map/ppermute | solution.py:649
  22.3 1.5 collective-permute-start.6
  23.8 1.2 collective-permute-done.5.refs_5_
  25.3 2.4 %collective-permute-done.6.refs_6_ = bf16[96,896]{1,0:T(8,128)(2,1)S(1)} collective-permute-done((bf16[96,896]{1,0:T(8,128)(2,1)S(1)}, bf16[96,896]{1,0:T(8,128)(2,1)S(1)}, u32[]{:S(2)}, u32[]{:S(2)}) %collective-permute-start.6) | collective-permute-done | bytes 172064 | tf_op jit(solution)/shard_map/ppermute | solution.py:649
  27.7 1.5 collective-permute-start.8
  29.2 1.8 collective-permute-done.7.refs_7_
  31.0 2.1 %collective-permute-done.8.refs_8_ = bf16[96,896]{1,0:T(8,128)(2,1)S(1)} collective-permute-done((bf16[96,896]{1,0:T(8,128)(2,1)S(1)}, bf16[96,896]{1,0:T(8,128)(2,1)S(1)}, u32[]{:S(2)}, u32[]{:S(2)}) %collective-permute-start.8) | collective-permute-done | bytes 172064 | tf_op jit(solution)/shard_map/ppermute | solution.py:652
  34.0 1.5 collective-permute-start.12
  35.5 1.1 copy-done.1
  38.0 5.4 %shard_map.303 = (bf16[512,768]{1,0:T(8,128)(2,1)S(1)}, bf16[512,256]{1,0:T(8,128)(2,1)S(1)}, bf16[512,256]{1,0:T(8,128)(2,1)S(1)}, bf16[512,256]{1,0:T(8,128)(2...) custom-call(s32[20]{0:T(128)S(1)} %dynamic-slice_bitcast_fusion.refs, ...), custom_call_target="tpu_custom_call" | custom-call | flops 4026531840 | bytes 8388608 | tf_op jit(solution)/shard_map/pallas_call | solution.py:791
  43.4 0.9 copy-done.37
  47.9 1.1 collective-permute-start.11
  49.5 3.5 %collective-permute-done.9.refs_4_ = bf16[128,384]{1,0:T(8,128)(2,1)S(1)} collective-permute-done((bf16[128,384]{1,0:T(8,128)(2,1)S(1)}, bf16[128,384]{1,0:T(8,128)(2,1)S(1)}, u32[]{:S(2)}, u32[]{:S(2)}) %collective-permute-start.9) | collective-permute-done | bytes 98336 | tf_op jit(solution)/shard_map/ppermute | solution.py:612
  52.9 0.9 collective-permute-done.11.refs_6_
  53.9 2.9 %shard_map.304 = (f32[256,768]{1,0:T(8,128)S(1)}, bf16[640,768]{1,0:T(8,128)(2,1)S(1)}, bf16[768,384]{1,0:T(8,128)(2,1)S(1)}) custom-call(s32[20]{0:T(128)S(1)} %dynamic-slice_bitcast_fusion.refs_0_.places, bf16[256,768]{1,0:T(8,128)(2,1)S(1)} %copy-done.2, bf16[256,768]{1,0:T(8,128)(2,1)S(1)} %copy-done, bf16[128,384]{1,0:T(8,128)(2,1)S(1)} %get-tuple-element.75.refs_3_, ...), custom_call_target="tpu_custom_call" | custom-call | flops 805306368 | bytes 6291456 | tf_op jit(solution)/shard_map/pallas_call | solution.py:831
  56.8 0.9 copy-done.7
  57.7 0.8 copy-done.25
  58.5 29.5 %all_to_all.10 = bf16[16,40,768]{2,1,0:T(8,128)(2,1)S(1)} all-to-all(bf16[16,40,768]{2,1,0:T(8,128)(2,1)S(1)} %bitcast.20), channel_id=1, replica_groups=mesh['fsdp'=8,'ctx'=2,'tp'=2] {'fsdp','ctx'}, dimensions={0} | all-to-all | bytes 1966080 | tf_op jit(solution)/shard_map/all_to_all | solution.py:847
  88.1 9.2 %shard_map.305 = (bf16[32,40,384]{2,1,0:T(8,128)(2,1)S(1)}, bf16[2,160,768]{2,1,0:T(8,128)(2,1)S(1)}, bf16[2,160,768]{2,1,0:T(8,128)(2,1)S(1)}, bf16[2,160,1536]...) custom-call(bf16[640,768]{1,0:T(8,128)(2,1)S(1)} %bitcast.21, s32[320,1]{1,0:T(8,128)S(1)} %copy-done.33, ...), custom_call_target="tpu_custom_call" | custom-call | flops 3019898880 | bytes 12582912 | tf_op jit(solution)/shard_map/pallas_call | solution.py:868
  97.3 0.9 copy-done.3
  98.2 0.9 copy-done.4
  99.2 0.9 copy-done.6
  100.1 0.8 copy-done.9
  100.9 0.8 copy-done.11
  101.7 3.9 %all-to-all-start.1 = ((bf16[32,40,384]{2,1,0:T(8,128)(2,1)}), bf16[32,40,384]{2,1,0:T(8,128)(2,1)S(1)}, u32[]{:S(2)}, u32[]{:S(2)}) async-start(bf16[32,40,384]{2,1,0:T(8,128)(2,1)} %copy-done.3), calls=%async_computation.1 | async-start | bytes 1966080 | tf_op jit(solution)/shard_map/all_to_all | solution.py:901
  105.6 6.6 %fusion = f32[2,768,1536]{2,1,0:T(8,128)} fusion(bf16[2,160,768]{2,1,0:T(8,128)(2,1)} %copy-done.11, bf16[2,160,1536]{2,1,0:T(8,128)(2,1)} %copy-done.6), kind=kOutput, calls=%fused_computation.3 | convolution fusion | flops 754974720 | bytes 10911744 | tf_op jit(solution)/shard_map/lrd,lrf->ldf/dot_general | solution.py:379
  112.3 5.3 %fusion.1 = f32[2,1536,768]{2,1,0:T(8,128)} fusion(bf16[2,160,1536]{2,1,0:T(8,128)(2,1)S(1)} %copy-done.5, bf16[2,160,768]{2,1,0:T(8,128)(2,1)S(1)} %copy-done.10), kind=kOutput, calls=%fused_computation.4 | convolution fusion | flops 754974720 | bytes 10911744 | tf_op jit(solution)/shard_map/lrf,lrd->lfd/dot_general | solution.py:380
  117.5 12.7 %all-to-all-done.1 = bf16[32,40,384]{2,1,0:T(8,128)(2,1)S(1)} async-done(((bf16[32,40,384]{2,1,0:T(8,128)(2,1)}), bf16[32,40,384]{2,1,0:T(8,128)(2,1)S(1)}, u32[]{:S(2)}, u32[]{:S(2)}) %all-to-all-start.1) | async-done | bytes 983072 | tf_op jit(solution)/shard_map/all_to_all | solution.py:901
  130.3 1.2 shard_map.306.refs_1_
  131.5 1.5 collective-permute-start.15
  133.0 9.7 %collective-permute-done.15.refs_2_ = bf16[256,768]{1,0:T(8,128)(2,1)S(1)} collective-permute-done((bf16[256,768]{1,0:T(8,128)(2,1)S(1)}, bf16[256,768]{1,0:T(8,128)(2,1)S(1)}, u32[]{:S(2)}, u32[]{:S(2)}) %collective-permute-start.15) | collective-permute-done | bytes 393248 | tf_op jit(solution)/shard_map/ppermute | solution.py:612
  142.7 1.1 copy-done.8
  143.8 2.7 %shard_map.307 = (f32[256,768]{1,0:T(8,128)}, f32[256,768]{1,0:T(8,128)S(1)}, bf16[256,768]{1,0:T(8,128)(2,1)S(1)}, bf16[768,128]{1,0:T(8,128)(2,1)S(1)}) custom-call(s32[20]{0:T(128)S(1)} %dynamic-slice_bitcast_fusion.refs_0_.places, bf16[256,768]{1,0:T(8,128)(2,1)S(1)} %shard_map.306.refs_1_, bf16[256,768]{1,0:T(8,128)(2,1)S(1)} %collective-permute-done.15.refs_2_, ...), custom_call_target="tpu_custom_call" | custom-call | flops 150994944 | bytes 6291456 | tf_op jit(solution)/shard_map/pallas_call | solution.py:918
  146.6 2.4 %all_gather.3.refs_10_ = bf16[512,768]{1,0:T(8,128)(2,1)S(1)} all-gather(bf16[256,768]{1,0:T(8,128)(2,1)S(1)} %get-tuple-element.95), channel_id=1, replica_groups=mesh['fsdp'=8,'ctx'=2,'tp'=2] {'ctx'}, dimensions={0}, use_global_device_ids=true | all-gather | bytes 1179648 | tf_op jit(solution)/shard_map/all_gather | solution.py:930
  149.0 1.1 copy-done.26
  150.0 1.0 copy-done.28
  151.0 1.1 copy-done.38
  152.1 0.9 copy-done.42
  153.1 0.9 copy-done.44
  154.0 0.9 copy-done.46
  155.0 0.9 copy-done.48
  155.9 10.5 %shard_map.308 = (bf16[768,896]{1,0:T(8,128)(2,1)S(1)}, bf16[48,896]{1,0:T(8,128)(2,1)S(1)}, bf16[48,896]{1,0:T(8,128)(2,1)S(1)}, bf16[256,768]{1,0:T(8,128)(2,1)S(1)}, bf16[256,768]{1,0:T(8,128)(2,1)S(1)}) custom-call(s32[20]{0:T(128)S(1)} %dynamic-slice_bitcast_fusion.refs_0_.places, s32[1,4]{1,0:T(1,128)S(1)} %copy-done.32, f32[6,32]{1,0:T(8,128)S(1)} %bitcast.32, ...), custom_call_target="tpu_custom_call" | custom-call | flops 6039797760 | bytes 8388608 | tf_op jit(solution)/shard_map/pallas_call | solution.py:933
  166.6 1.1 collective-permute-start.18
  167.7 1.0 collective-permute-start.19
  168.6 2.8 %collective-permute-done.18.from_left = bf16[48,896]{1,0:T(8,128)(2,1)S(1)} collective-permute-done((bf16[48,896]{1,0:T(8,128)(2,1)S(1)}, bf16[48,896]{1,0:T(8,128)(2,1)S(1)}, u32[]{:S(2)}, u32[]{:S(2)}) %collective-permute-start.18) | collective-permute-done | bytes 86048 | tf_op jit(solution)/shard_map/ppermute | solution.py:675
  171.4 0.8 collective-permute-done.19.from_right
  172.8 1.2 collective-permute-start.20
  174.0 0.9 collective-permute-start.21
  175.0 1.0 collective-permute-start.17
  176.0 2.4 %collective-permute-done.20.from_left = bf16[96,896]{1,0:T(8,128)(2,1)S(1)} collective-permute-done((bf16[96,896]{1,0:T(8,128)(2,1)S(1)}, bf16[96,896]{1,0:T(8,128)(2,1)S(1)}, u32[]{:S(2)}, u32[]{:S(2)}) %collective-permute-start.20) | collective-permute-done | bytes 172064 | tf_op jit(solution)/shard_map/ppermute | solution.py:675
  178.4 1.0 collective-permute-done.21.from_right
  180.6 1.4 collective-permute-start.23
  182.1 3.4 %collective-permute-done.22.from_left = bf16[96,896]{1,0:T(8,128)(2,1)S(1)} collective-permute-done((bf16[96,896]{1,0:T(8,128)(2,1)S(1)}, bf16[96,896]{1,0:T(8,128)(2,1)S(1)}, u32[]{:S(2)}, u32[]{:S(2)}) %collective-permute-start.22) | collective-permute-done | bytes 172064 | tf_op jit(solution)/shard_map/ppermute | solution.py:675
  186.7 1.6 collective-permute-start.24
  188.8 3.4 %collective-permute-done.24.from_left = bf16[96,896]{1,0:T(8,128)(2,1)S(1)} collective-permute-done((bf16[96,896]{1,0:T(8,128)(2,1)S(1)}, bf16[96,896]{1,0:T(8,128)(2,1)S(1)}, u32[]{:S(2)}, u32[]{:S(2)}) %collective-permute-start.24) | collective-permute-done | bytes 172064 | tf_op jit(solution)/shard_map/ppermute | solution.py:675
  192.1 1.6 collective-permute-done.25.from_right
  194.4 1.1 collective-permute-start.27
  196.3 1.3 shard_map.313
  198.8 1.4 shard_map.314
  (115 shorter events, 19.6 us)
Async XLA Ops:
  0.6 53.2 %copy-start.12 = (s32[640,1]{1,0:T(8,128)S(1)}, s32[640,1]{1,0:T(8,128)}, u32[]{:S(2)}) copy-start(s32[640,1]{1,0:T(8,128)} %constant.36.clone.refs_16_) | copy-start | bytes 7684
  0.7 53.2 %copy-start.2 = (bf16[256,768]{1,0:T(8,128)(2,1)S(1)}, bf16[256,768]{1,0:T(8,128)(2,1)}, u32[]{:S(2)}) copy-start(bf16[256,768]{1,0:T(8,128)(2,1)} %x_own.1) | copy-start | bytes 1179652
  0.7 53.2 %copy-start = (bf16[256,768]{1,0:T(8,128)(2,1)S(1)}, bf16[256,768]{1,0:T(8,128)(2,1)}, u32[]{:S(2)}) copy-start(bf16[256,768]{1,0:T(8,128)(2,1)} %refs_4_.6) | copy-start | bytes 1179652
  0.7 53.2 %copy-start.13 = (s32[640,1]{1,0:T(8,128)S(1)}, s32[640,1]{1,0:T(8,128)}, u32[]{:S(2)}) copy-start(s32[640,1]{1,0:T(8,128)} %constant.35.clone.refs_15_) | copy-start | bytes 7684
  6.6 47.3 %copy-start.19 = (s32[256,1]{0,1:T(1,128)S(1)}, s32[256,1]{0,1:T(1,128)}, u32[]{:S(2)}) copy-start(s32[256,1]{0,1:T(1,128)} %param.35) | copy-start | bytes 3076
  6.6 47.3 %copy-start.20 = (s32[256]{0:T(256)S(1)}, s32[256]{0:T(256)}, u32[]{:S(2)}) copy-start(s32[256]{0:T(256)} %param.36) | copy-start | bytes 3076
  7.3 1.4 collective-permute-start.1
  8.8 7.6 %collective-permute-start.2 = (bf16[96,896]{1,0:T(8,128)(2,1)S(1)}, bf16[96,896]{1,0:T(8,128)(2,1)S(1)}, u32[]{:S(2)}, u32[]{:S(2)}) collective-permute-start(bf16[96,896]{1,0:T(8,128)(2,1)S(1)} %pad_maximum_fusion.refs_1_), channel_id=1, source_target_pairs={{0,8},{8,16},{16,24},{24,28},{28,20},{20,12},{12,4},{4,0},{1,9},{9... | collective-permute-start | bytes 516104 | tf_op jit(solution)/shard_map/ppermute | solution.py:649
  11.8 6.4 %collective-permute-start.3 = (bf16[96,896]{1,0:T(8,128)(2,1)S(1)}, bf16[96,896]{1,0:T(8,128)(2,1)S(1)}, u32[]{:S(2)}, u32[]{:S(2)}) collective-permute-start(bf16[96,896]{1,0:T(8,128)(2,1)S(1)} %pad_maximum_fusion.refs_1_), channel_id=1, source_target_pairs={{8,0},{16,8},{24,16},{28,24},{20,28},{12,20},{4,12},{0,4},{9,1},{1... | collective-permute-start | bytes 516104 | tf_op jit(solution)/shard_map/ppermute | solution.py:650
  16.4 5.9 %collective-permute-start.4 = (bf16[96,896]{1,0:T(8,128)(2,1)S(1)}, bf16[96,896]{1,0:T(8,128)(2,1)S(1)}, u32[]{:S(2)}, u32[]{:S(2)}) collective-permute-start(bf16[96,896]{1,0:T(8,128)(2,1)S(1)} %collective-permute-done.2.refs_2_), channel_id=1, source_target_pairs={{0,8},{8,16},{16,24},{24,28},{28,20},{20,12},{12,4},{4,0},{1,9},{9... | collective-permute-start | bytes 516104 | tf_op jit(solution)/shard_map/ppermute | solution.py:649
  18.2 17.3 %collective-permute-start = (bf16[256,768]{1,0:T(8,128)(2,1)}, bf16[256,768]{1,0:T(8,128)(2,1)S(1)}, u32[]{:S(2)}, u32[]{:S(2)}) collective-permute-start(bf16[256,768]{1,0:T(8,128)(2,1)} %x_own.1), channel_id=1, source_target_pairs={{0,2},{2,0},{1,3},{3,1},{4,6},{6,4},{5,7},{7,5},{8,10},{10,8},{9,1... | collective-permute-start | bytes 1179656 | tf_op jit(solution)/shard_map/ppermute | solution.py:612
  18.2 6.8 %collective-permute-start.5 = (bf16[96,896]{1,0:T(8,128)(2,1)S(1)}, bf16[96,896]{1,0:T(8,128)(2,1)S(1)}, u32[]{:S(2)}, u32[]{:S(2)}) collective-permute-start(bf16[96,896]{1,0:T(8,128)(2,1)S(1)} %collective-permute-done.3.refs_3_), channel_id=1, source_target_pairs={{8,0},{16,8},{24,16},{28,24},{20,28},{12,20},{4,12},{0,4},{9,1},{1... | collective-permute-start | bytes 516104 | tf_op jit(solution)/shard_map/ppermute | solution.py:650
  22.3 5.4 %collective-permute-start.6 = (bf16[96,896]{1,0:T(8,128)(2,1)S(1)}, bf16[96,896]{1,0:T(8,128)(2,1)S(1)}, u32[]{:S(2)}, u32[]{:S(2)}) collective-permute-start(bf16[96,896]{1,0:T(8,128)(2,1)S(1)} %collective-permute-done.4.refs_4_), channel_id=1, source_target_pairs={{0,8},{8,16},{16,24},{24,28},{28,20},{20,12},{12,4},{4,0},{1,9},{9... | collective-permute-start | bytes 516104 | tf_op jit(solution)/shard_map/ppermute | solution.py:649
  25.0 6.0 %collective-permute-start.7 = (bf16[96,896]{1,0:T(8,128)(2,1)S(1)}, bf16[96,896]{1,0:T(8,128)(2,1)S(1)}, u32[]{:S(2)}, u32[]{:S(2)}) collective-permute-start(bf16[96,896]{1,0:T(8,128)(2,1)S(1)} %collective-permute-done.5.refs_5_), channel_id=1, source_target_pairs={{8,0},{16,8},{24,16},{28,24},{20,28},{12,20},{4,12},{0,4},{9,1},{1... | collective-permute-start | bytes 516104 | tf_op jit(solution)/shard_map/ppermute | solution.py:650
  27.7 5.4 %collective-permute-start.8 = (bf16[96,896]{1,0:T(8,128)(2,1)S(1)}, bf16[96,896]{1,0:T(8,128)(2,1)S(1)}, u32[]{:S(2)}, u32[]{:S(2)}) collective-permute-start(bf16[96,896]{1,0:T(8,128)(2,1)S(1)} %collective-permute-done.6.refs_6_), channel_id=1, source_target_pairs={{0,8},{8,16},{16,24},{24,28},{28,20},{20,12},{12,4},{4,0},{1,9},{9... | collective-permute-start | bytes 516104 | tf_op jit(solution)/shard_map/ppermute | solution.py:652
  33.9 20.0 %collective-permute-start.13 = (bf16[384,384]{1,0:T(8,128)(2,1)S(1)}, bf16[384,384]{1,0:T(8,128)(2,1)S(1)}, u32[]{:S(2)}, u32[]{:S(2)}) collective-permute-start(bf16[384,384]{1,0:T(8,128)(2,1)S(1)} %get-tuple-element.77.refs_7_), channel_id=1, source_target_pairs={{0,2},{2,0},{1,3},{3,1},{4,6},{6,4},{5,7},{7,5},{8,10},{10,8},{9,1... | collective-permute-start | bytes 884744 | tf_op jit(solution)/shard_map/ppermute | solution.py:612
  34.0 13.2 %collective-permute-start.12 = (bf16[384,384]{1,0:T(8,128)(2,1)S(1)}, bf16[384,384]{1,0:T(8,128)(2,1)S(1)}, u32[]{:S(2)}, u32[]{:S(2)}) collective-permute-start(bf16[384,384]{1,0:T(8,128)(2,1)S(1)} %get-tuple-element.77.refs_7_), channel_id=1, source_target_pairs={{0,1},{1,0},{2,3},{3,2},{4,5},{5,4},{6,7},{7,6},{8,9},{9,8},{10,11... | collective-permute-start | bytes 884744 | tf_op jit(solution)/shard_map/ppermute | solution.py:612
  35.5 21.3 %copy-start.27 = (bf16[256,768]{1,0:T(8,128)(2,1)}, bf16[256,768]{1,0:T(8,128)(2,1)S(1)}, u32[]{:S(2)}) copy-start(bf16[256,768]{1,0:T(8,128)(2,1)S(1)} %collective-permute-done.refs_4_) | copy-start | bytes 1179652
  35.5 1.1 copy-start.1
  38.0 50.1 %copy-start.23 = (bf16[2,768,1536]{2,1,0:T(8,128)(2,1)S(1)}, bf16[2,768,1536]{2,1,0:T(8,128)(2,1)}, u32[]{:S(2)}) copy-start(bf16[2,768,1536]{2,1,0:T(8,128)(2,1)} %refs_3_.7) | copy-start | bytes 14155780
  38.0 50.1 %copy-start.24 = (bf16[2,1536,768]{2,1,0:T(8,128)(2,1)S(1)}, bf16[2,1536,768]{2,1,0:T(8,128)(2,1)}, u32[]{:S(2)}) copy-start(bf16[2,1536,768]{2,1,0:T(8,128)(2,1)} %refs_4_.5) | copy-start | bytes 14155780
  38.0 50.1 %copy-start.33 = (s32[320,1]{1,0:T(8,128)S(1)}, s32[320,1]{1,0:T(8,128)}, u32[]{:S(2)}) copy-start(s32[320,1]{1,0:T(8,128)} %constant.37.clone.refs_1_) | copy-start | bytes 3844
  38.0 50.1 %copy-start.36 = (s32[1,320]{1,0:T(1,128)S(1)}, s32[1,320]{1,0:T(1,128)}, u32[]{:S(2)}) copy-start(s32[1,320]{1,0:T(1,128)} %constant.38.clone.refs_2_) | copy-start | bytes 3844
  43.4 0.9 copy-start.37
  47.1 50.1 %copy-start.47 = (f32[512,128]{1,0:T(8,128)}, f32[512,128]{1,0:T(8,128)S(1)}, u32[]{:S(2)}) copy-start(f32[512,128]{1,0:T(8,128)S(1)} %get-tuple-element.94.refs_9_) | copy-start | bytes 786436
  47.1 6.7 %collective-permute-start.14 = (bf16[384,384]{1,0:T(8,128)(2,1)S(1)}, bf16[384,384]{1,0:T(8,128)(2,1)S(1)}, u32[]{:S(2)}, u32[]{:S(2)}) collective-permute-start(bf16[384,384]{1,0:T(8,128)(2,1)S(1)} %collective-permute-done.12.refs_8_), channel_id=1, source_target_pairs={{0,2},{2,0},{1,3},{3,1},{4,6},{6,4},{5,7},{7,5},{8,10},{10,8},{9,1... | collective-permute-start | bytes 884744 | tf_op jit(solution)/shard_map/ppermute | solution.py:612
  47.3 5.6 %collective-permute-start.9 = (bf16[128,384]{1,0:T(8,128)(2,1)S(1)}, bf16[128,384]{1,0:T(8,128)(2,1)S(1)}, u32[]{:S(2)}, u32[]{:S(2)}) collective-permute-start(bf16[128,384]{1,0:T(8,128)(2,1)S(1)} %get-tuple-element.75.refs_3_), channel_id=1, source_target_pairs={{0,1},{1,0},{2,3},{3,2},{4,5},{5,4},{6,7},{7,6},{8,9},{9,8},{10,11... | collective-permute-start | bytes 294920 | tf_op jit(solution)/shard_map/ppermute | solution.py:612
  47.9 6.0 %collective-permute-start.11 = (bf16[128,384]{1,0:T(8,128)(2,1)S(1)}, bf16[128,384]{1,0:T(8,128)(2,1)S(1)}, u32[]{:S(2)}, u32[]{:S(2)}) collective-permute-start(bf16[128,384]{1,0:T(8,128)(2,1)S(1)} %get-tuple-element.76), channel_id=1, source_target_pairs={{0,3},{1,2},{2,1},{3,0},{4,7},{5,6},{6,5},{7,4},{8,11},{9,10},{10,... | collective-permute-start | bytes 294920 | tf_op jit(solution)/shard_map/ppermute | solution.py:818
  49.0 4.9 %collective-permute-start.10 = (bf16[128,384]{1,0:T(8,128)(2,1)S(1)}, bf16[128,384]{1,0:T(8,128)(2,1)S(1)}, u32[]{:S(2)}, u32[]{:S(2)}) collective-permute-start(bf16[128,384]{1,0:T(8,128)(2,1)S(1)} %get-tuple-element.76), channel_id=1, source_target_pairs={{0,2},{2,0},{1,3},{3,1},{4,6},{6,4},{5,7},{7,5},{8,10},{10,8},{9,1... | collective-permute-start | bytes 294920 | tf_op jit(solution)/shard_map/ppermute | solution.py:612
  56.8 0.9 copy-start.7
  57.7 0.8 copy-start.25
  97.3 0.9 copy-start.3
  98.2 0.9 copy-start.4
  99.2 0.9 copy-start.6
  101.7 28.6 %all-to-all-start.1 = ((bf16[32,40,384]{2,1,0:T(8,128)(2,1)}), bf16[32,40,384]{2,1,0:T(8,128)(2,1)S(1)}, u32[]{:S(2)}, u32[]{:S(2)}) async-start(bf16[32,40,384]{2,1,0:T(8,128)(2,1)} %copy-done.3), calls=%async_computation.1 | async-start | bytes 1966080 | tf_op jit(solution)/shard_map/all_to_all | solution.py:901
  105.6 6.7 %copy-start.5 = (bf16[2,160,1536]{2,1,0:T(8,128)(2,1)S(1)}, bf16[2,160,1536]{2,1,0:T(8,128)(2,1)}, u32[]{:S(2)}) copy-start(bf16[2,160,1536]{2,1,0:T(8,128)(2,1)} %copy-done.4) | copy-start | bytes 2949124
  105.6 6.7 %copy-start.10 = (bf16[2,160,768]{2,1,0:T(8,128)(2,1)S(1)}, bf16[2,160,768]{2,1,0:T(8,128)(2,1)}, u32[]{:S(2)}) copy-start(bf16[2,160,768]{2,1,0:T(8,128)(2,1)} %copy-done.9) | copy-start | bytes 1474564
  105.6 24.6 %copy-start.34 = (s32[1,1280]{1,0:T(1,128)S(1)}, s32[1,1280]{1,0:T(1,128)}, u32[]{:S(2)}) copy-start(s32[1,1280]{1,0:T(1,128)} %constant.40.clone.refs_4_) | copy-start | bytes 15364
  105.6 24.6 %copy-start.35 = (s32[1,1280]{1,0:T(1,128)S(1)}, s32[1,1280]{1,0:T(1,128)}, u32[]{:S(2)}) copy-start(s32[1,1280]{1,0:T(1,128)} %constant.39.clone.refs_3_) | copy-start | bytes 15364
  112.3 36.7 %copy-start.30 = (f32[32,6]{0,1:T(8,128)S(1)}, f32[32,6]{0,1:T(8,128)}, u32[]{:S(2)}) copy-start(f32[32,6]{0,1:T(8,128)} %param.31) | copy-start | bytes 2308
  112.3 36.7 %copy-start.32 = (s32[1,4]{1,0:T(1,128)S(1)}, s32[1,4]{1,0:T(1,128)}, u32[]{:S(2)}) copy-start(s32[1,4]{1,0:T(1,128)} %refs_1_.8) | copy-start | bytes 52
  112.3 36.7 %copy-start.40 = (bf16[512,256]{1,0:T(8,128)(2,1)S(1)}, bf16[512,256]{1,0:T(8,128)(2,1)}, u32[]{:S(2)}) copy-start(bf16[512,256]{1,0:T(8,128)(2,1)} %copy-done.39) | copy-start | bytes 786436
  131.5 11.2 %collective-permute-start.15 = (bf16[256,768]{1,0:T(8,128)(2,1)S(1)}, bf16[256,768]{1,0:T(8,128)(2,1)S(1)}, u32[]{:S(2)}, u32[]{:S(2)}) collective-permute-start(bf16[256,768]{1,0:T(8,128)(2,1)S(1)} %shard_map.306.refs_1_), channel_id=1, source_target_pairs={{0,1},{1,0},{2,3},{3,2},{4,5},{5,4},{6,7},{7,6},{8,9},{9,8},{10,11... | collective-permute-start | bytes 1179656 | tf_op jit(solution)/shard_map/ppermute | solution.py:612
  142.7 1.1 copy-start.8
  148.9 1.1 copy-start.26
  150.0 1.0 copy-start.28
  151.0 1.1 copy-start.38
  152.1 0.9 copy-start.42
  153.1 0.9 copy-start.44
  154.0 0.9 copy-start.46
  155.0 0.9 copy-start.48
  166.4 8.5 %collective-permute-start.16 = (bf16[256,768]{1,0:T(8,128)(2,1)S(1)}, bf16[256,768]{1,0:T(8,128)(2,1)S(1)}, u32[]{:S(2)}, u32[]{:S(2)}) collective-permute-start(bf16[256,768]{1,0:T(8,128)(2,1)S(1)} %get-tuple-element.101), channel_id=1, source_target_pairs={{0,2},{2,0},{1,3},{3,1},{4,6},{6,4},{5,7},{7,5},{8,10},{10,8},{9,1... | collective-permute-start | bytes 1179656 | tf_op jit(solution)/shard_map/ppermute | solution.py:612
  166.6 4.8 %collective-permute-start.18 = (bf16[48,896]{1,0:T(8,128)(2,1)S(1)}, bf16[48,896]{1,0:T(8,128)(2,1)S(1)}, u32[]{:S(2)}, u32[]{:S(2)}) collective-permute-start(bf16[48,896]{1,0:T(8,128)(2,1)S(1)} %get-tuple-element.102), channel_id=1, source_target_pairs={{0,8},{8,16},{16,24},{24,28},{28,20},{20,12},{12,4},{4,0},{1,9},{9... | collective-permute-start | bytes 258056 | tf_op jit(solution)/shard_map/ppermute | solution.py:675
  167.7 4.5 %collective-permute-start.19 = (bf16[48,896]{1,0:T(8,128)(2,1)S(1)}, bf16[48,896]{1,0:T(8,128)(2,1)S(1)}, u32[]{:S(2)}, u32[]{:S(2)}) collective-permute-start(bf16[48,896]{1,0:T(8,128)(2,1)S(1)} %get-tuple-element.103), channel_id=1, source_target_pairs={{8,0},{16,8},{24,16},{28,24},{20,28},{12,20},{4,12},{0,4},{9,1},{1... | collective-permute-start | bytes 258056 | tf_op jit(solution)/shard_map/ppermute | solution.py:676
  172.8 5.6 %collective-permute-start.20 = (bf16[96,896]{1,0:T(8,128)(2,1)S(1)}, bf16[96,896]{1,0:T(8,128)(2,1)S(1)}, u32[]{:S(2)}, u32[]{:S(2)}) collective-permute-start(bf16[96,896]{1,0:T(8,128)(2,1)S(1)} %get-tuple-element.104), channel_id=1, source_target_pairs={{0,8},{8,16},{16,24},{24,28},{28,20},{20,12},{12,4},{4,0},{1,9},{9... | collective-permute-start | bytes 516104 | tf_op jit(solution)/shard_map/ppermute | solution.py:675
  174.0 5.4 %collective-permute-start.21 = (bf16[96,896]{1,0:T(8,128)(2,1)S(1)}, bf16[96,896]{1,0:T(8,128)(2,1)S(1)}, u32[]{:S(2)}, u32[]{:S(2)}) collective-permute-start(bf16[96,896]{1,0:T(8,128)(2,1)S(1)} %get-tuple-element.105), channel_id=1, source_target_pairs={{8,0},{16,8},{24,16},{28,24},{20,28},{12,20},{4,12},{0,4},{9,1},{1... | collective-permute-start | bytes 516104 | tf_op jit(solution)/shard_map/ppermute | solution.py:676
  175.0 18.8 %collective-permute-start.17 = (bf16[256,768]{1,0:T(8,128)(2,1)S(1)}, bf16[256,768]{1,0:T(8,128)(2,1)S(1)}, u32[]{:S(2)}, u32[]{:S(2)}) collective-permute-start(bf16[256,768]{1,0:T(8,128)(2,1)S(1)} %add_convert_fusion.near), channel_id=1, source_target_pairs={{0,1},{1,0},{2,3},{3,2},{4,5},{5,4},{6,7},{7,6},{8,9},{9,8},{10,11... | collective-permute-start | bytes 1179656 | tf_op jit(solution)/shard_map/ppermute | solution.py:612
  180.0 5.5 %collective-permute-start.22 = (bf16[96,896]{1,0:T(8,128)(2,1)S(1)}, bf16[96,896]{1,0:T(8,128)(2,1)S(1)}, u32[]{:S(2)}, u32[]{:S(2)}) collective-permute-start(bf16[96,896]{1,0:T(8,128)(2,1)S(1)} %get-tuple-element.106), channel_id=1, source_target_pairs={{0,8},{8,16},{16,24},{24,28},{28,20},{20,12},{12,4},{4,0},{1,9},{9... | collective-permute-start | bytes 516104 | tf_op jit(solution)/shard_map/ppermute | solution.py:675
  180.6 5.4 %collective-permute-start.23 = (bf16[96,896]{1,0:T(8,128)(2,1)S(1)}, bf16[96,896]{1,0:T(8,128)(2,1)S(1)}, u32[]{:S(2)}, u32[]{:S(2)}) collective-permute-start(bf16[96,896]{1,0:T(8,128)(2,1)S(1)} %get-tuple-element.107), channel_id=1, source_target_pairs={{8,0},{16,8},{24,16},{28,24},{20,28},{12,20},{4,12},{0,4},{9,1},{1... | collective-permute-start | bytes 516104 | tf_op jit(solution)/shard_map/ppermute | solution.py:676
  186.7 5.5 %collective-permute-start.24 = (bf16[96,896]{1,0:T(8,128)(2,1)S(1)}, bf16[96,896]{1,0:T(8,128)(2,1)S(1)}, u32[]{:S(2)}, u32[]{:S(2)}) collective-permute-start(bf16[96,896]{1,0:T(8,128)(2,1)S(1)} %get-tuple-element.108), channel_id=1, source_target_pairs={{0,8},{8,16},{16,24},{24,28},{28,20},{20,12},{12,4},{4,0},{1,9},{9... | collective-permute-start | bytes 516104 | tf_op jit(solution)/shard_map/ppermute | solution.py:675
  188.3 5.4 %collective-permute-start.25 = (bf16[96,896]{1,0:T(8,128)(2,1)S(1)}, bf16[96,896]{1,0:T(8,128)(2,1)S(1)}, u32[]{:S(2)}, u32[]{:S(2)}) collective-permute-start(bf16[96,896]{1,0:T(8,128)(2,1)S(1)} %get-tuple-element.109), channel_id=1, source_target_pairs={{8,0},{16,8},{24,16},{28,24},{20,28},{12,20},{4,12},{0,4},{9,1},{1... | collective-permute-start | bytes 516104 | tf_op jit(solution)/shard_map/ppermute | solution.py:676
  194.4 3.2 %collective-permute-start.26 = (f32[56,896]{1,0:T(8,128)S(1)}, f32[56,896]{1,0:T(8,128)S(1)}, u32[]{:S(2)}, u32[]{:S(2)}) collective-permute-start(f32[56,896]{1,0:T(8,128)S(1)} %get-tuple-element.112), channel_id=1, source_target_pairs={{0,2},{2,0},{1,3},{3,1},{4,6},{6,4},{5,7},{7,5},{8,10},{10,8},{9,1... | collective-permute-start | bytes 602120 | tf_op jit(solution)/shard_map/ppermute | solution.py:612
  194.4 3.9 %collective-permute-start.27 = (f32[48,128]{1,0:T(8,128)S(1)}, f32[48,128]{1,0:T(8,128)S(1)}, u32[]{:S(2)}, u32[]{:S(2)}) collective-permute-start(f32[48,128]{1,0:T(8,128)S(1)} %get-tuple-element.118), channel_id=1, source_target_pairs={{0,1},{1,0},{2,3},{3,2},{4,5},{5,4},{6,7},{7,6},{8,9},{9,8},{10,11... | collective-permute-start | bytes 73736 | tf_op jit(solution)/shard_map/ppermute | solution.py:612
  195.6 3.3 %collective-permute-start.28 = (f32[48,128]{1,0:T(8,128)S(1)}, f32[48,128]{1,0:T(8,128)S(1)}, u32[]{:S(2)}, u32[]{:S(2)}) collective-permute-start(f32[48,128]{1,0:T(8,128)S(1)} %get-tuple-element.119), channel_id=1, source_target_pairs={{0,3},{1,2},{2,1},{3,0},{4,7},{5,6},{6,5},{7,4},{8,11},{9,10},{10,... | collective-permute-start | bytes 73736 | tf_op jit(solution)/shard_map/ppermute | solution.py:967
  (15 other events, 10.8 us)

commit v5 on v4

--- a/solution.py
+++ b/solution.py
@@ -15,8 +15,7 @@
 LANES = 128
 STRIP = 128
 HEAD_SIZE = 64
-VMEM_BYTES = 40 * 1024 * 1024
-SMALL_VMEM_BYTES = 16 * 1024 * 1024
+MIB = 1024 * 1024
 f32 = jnp.float32
 bf16 = jnp.bfloat16
 vmem = pl.BlockSpec(memory_space=pltpu.VMEM)
@@ -50,7 +49,7 @@
     return side + jnp.where(distance < 8, distance, far_bucket)
 
 
-def kernel_call(body, outs, in_specs, out_specs=None, scratch=(), grid=None, flops=0, moved=0, small=False):
+def kernel_call(body, outs, in_specs, out_specs=None, scratch=(), grid=None, flops=0, moved=0, mib=16):
     extra = {} if grid is None else {"grid": grid}
     return pl.pallas_call(
         body,
@@ -58,7 +57,7 @@
         in_specs=in_specs,
         out_specs=[vmem] * len(outs) if out_specs is None else out_specs,
         scratch_shapes=list(scratch),
-        compiler_params=pltpu.CompilerParams(vmem_limit_bytes=SMALL_VMEM_BYTES if small else VMEM_BYTES),
+        compiler_params=pltpu.CompilerParams(vmem_limit_bytes=mib * MIB),
         cost_estimate=pl.CostEstimate(flops=flops, bytes_accessed=moved, transcendentals=0),
         **extra,
     )
@@ -68,15 +67,18 @@
     return jax.ShapeDtypeStruct(tuple(dims), dtype)
 
 
-def segments(lengths_ref, rows, dim):
-    dims = (rows, 1) if dim == 0 else (1, rows)
-    places = iota(dims, dim)
-    total = jnp.zeros(dims, jnp.int32)
+def segments(lengths_ref, columns, rows):
+    places = iota((rows, columns), 1)
+    total = jnp.zeros((rows, columns), jnp.int32)
     end = 0
     for entry in range(lengths_ref.shape[1]):
         end = end + lengths_ref[0, entry]
         total = total + (places >= end).astype(jnp.int32)
     return total
+
+
+def column_of(line):
+    return jnp.broadcast_to(line, (LANES, line.shape[1])).T[:, :1]
 
 
 def skew(values, right):
@@ -90,27 +92,34 @@
     return values
 
 
-def bias_strips(table_ref, first_head, heads, strip_ref):
+def attention_tables(heads, meta, lengths, table, strips, far, segment):
     lanes = 4 * STRIP
+    buckets = table.shape[1]
+    first_head = meta[0] * heads
     bucket = bucket_index(iota((1, lanes), 1) - 2 * STRIP)
+    far[...] = jnp.zeros_like(far)
     for head in range(heads):
         line = jnp.zeros((1, lanes), f32)
-        for entry in range(table_ref.shape[1]):
-            line = jnp.where(bucket == entry, table_ref[first_head + head, entry], line)
+        for entry in range(buckets):
+            line = jnp.where(bucket == entry, table[first_head + head, entry], line)
         strip = skew(jnp.broadcast_to(line, (STRIP, lanes)), True)
-        strip_ref[head] = strip[:, STRIP:]
-
-
-def bias_row(strip_ref, table_ref, head, first_head, block, blocks):
-    buckets = table_ref.shape[1]
+        strips[head] = strip[:, STRIP:]
+        far[2 * head : 2 * head + 1, :] = jnp.full((1, LANES), table[first_head + head, buckets - 1], f32)
+        far[2 * head + 1 : 2 * head + 2, :] = jnp.full(
+            (1, LANES), table[first_head + head, buckets // 2 - 1], f32
+        )
+    segment[...] = segments(lengths, segment.shape[1], segment.shape[0])
+
+
+def bias_row(strips, far, head, block, blocks):
     parts = []
     for other in range(blocks):
         gap = other - block
         if abs(gap) <= 1:
-            parts.append(strip_ref[head, :, (gap + 1) * STRIP : (gap + 2) * STRIP])
+            parts.append(strips[head, :, (gap + 1) * STRIP : (gap + 2) * STRIP])
         else:
-            entry = buckets - 1 if gap > 0 else buckets // 2 - 1
-            parts.append(jnp.full((STRIP, STRIP), table_ref[first_head + head, entry], f32))
+            row = 2 * head + (0 if gap > 0 else 1)
+            parts.append(jnp.broadcast_to(far[row : row + 1, :], (STRIP, STRIP)))
     return jnp.concatenate(parts, axis=1)
 
 
@@ -193,12 +202,11 @@
 
 
 def attention_forward(heads, experts, *refs):
-    (meta, lengths, table, x_own, x_other, wall) = refs[:6]
-    (h1, q_out, k_out, v_out, o_own, o_other, o_all, lse, gains, strips) = refs[6:]
+    (meta, x_own, x_other, wall, strips, far, segment) = refs[:7]
+    (h1, q_out, k_out, v_out, o_own, o_other, o_all, probs, gains) = refs[7:]
     place = meta[0]
     rows = x_own.shape[0]
     group = 2 * rows
-    first_head = place * heads
     width = wall.shape[1]
     extras = wall[:, width - LANES :].astype(f32).T
     gain_at = HEAD_SIZE + experts
@@ -214,38 +222,30 @@
     q_out[...] = qkv[:, :lanes].astype(bf16)
     k_out[...] = pltpu.roll(qkv[:, LANES : LANES + lanes], lanes - HEAD_SIZE, 1).astype(bf16)
     v_out[...] = qkv[:, width - lanes :].astype(bf16)
-    bias_strips(table, first_head, heads, strips)
-    segment_row = segments(lengths, group, 1)
-    segment_column = segments(lengths, group, 0)
+    segment_row = segment[0:1, :]
+    segment_column = column_of(segment_row.astype(f32)).astype(jnp.int32)
     keys = k_out[...]
-    lane = iota((1, LANES), 1)
     blocks = group // STRIP
     values_of = [pick_head(v_out[...], head, lanes) for head in range(heads)]
     for block in range(blocks):
         first = block * STRIP
         same = segment_column[first : first + STRIP] == segment_row
         total = jnp.zeros((STRIP, lanes), f32)
-        totals = jnp.zeros((STRIP, LANES), f32)
         for head in range(heads):
             query = pick_head(q_out[first : first + STRIP, :], head, lanes)
-            scores = mm_nt(query, keys) + bias_row(strips, table, head, first_head, block, blocks)
+            scores = mm_nt(query, keys) + bias_row(strips, far, head, block, blocks)
             scores = jnp.where(same, scores, masked_value)
             top = jnp.max(scores, axis=1, keepdims=True)
             raised = jnp.exp(scores - top)
             mass = jnp.sum(raised, axis=1, keepdims=True)
-            chances = (raised * (1.0 / mass)).astype(bf16)
-            total = total + mm(chances, values_of[head])
-            totals = jnp.where(lane == head, top + jnp.log(mass), totals)
+            chances = raised * (1.0 / mass)
+            probs[head, first : first + STRIP, :] = chances
+            total = total + mm(chances.astype(bf16), values_of[head])
         o_all[first : first + STRIP, :] = total.astype(bf16)
-        lse[first : first + STRIP, :] = totals
     for out, start in ((o_own, place * rows), (o_other, (1 - place) * rows)):
         values = o_all[pl.ds(pl.multiple_of(start, 16), rows), :].astype(f32)
         for index, part in enumerate(join(values[: rows // 2], values[rows // 2 :])):
             out[:, index * LANES : (index + 1) * LANES] = part.astype(bf16)
-
-
-def column_of(line):
-    return jnp.broadcast_to(line, (LANES, line.shape[1])).T[:, :1]
 
 
 def columns_of(*lines):
@@ -382,38 +382,49 @@
 
 
 def from_experts(experts, capacity, *refs):
-    rows_in, routes_row, keep_row, slot_y, slot_x, out = refs
+    meta, rows_in, cotangent, routes_row, keep_row, slot_y, slot_x, y_out, dx_out, gate_out = refs
     slot = column_of(slots_by_row(routes_row[...], keep_row[...], experts, capacity).astype(f32))
     slot = slot.astype(jnp.int32)
     width = rows_in.shape[1]
     pick_y = (slot == slot_y[...]).astype(f32).astype(bf16)
     pick_x = (slot == slot_x[...]).astype(f32).astype(bf16)
-    out[:, :width] = mm(pick_y, rows_in[...]).astype(bf16)
-    out[:, width:] = mm(pick_x, rows_in[...]).astype(bf16)
+    dx_out[...] = mm(pick_x, rows_in[...]).astype(bf16)
+    picked = mm(pick_y, rows_in[...]).astype(bf16)
+    y_out[...] = picked
+    upstream = jnp.where(meta[1] == 0, cotangent[:, :width], cotangent[:, width:])
+    part = jnp.sum(upstream.astype(f32) * picked.astype(f32), axis=1, keepdims=True)
+    gate_out[...] = jnp.broadcast_to(part, (part.shape[0], LANES)).T[:8]
+
+
+def add_expert(meta, middle, gate, y_own, y_tp, result):
+    width = y_own.shape[1]
+    share = meta[1]
+    own, other = y_own[...].astype(f32), y_tp[...].astype(f32)
+    gates = gate[:, :1]
+    result[:, :width] = middle[:, :width] + gates * jnp.where(share == 0, own, other)
+    result[:, width:] = middle[:, width:] + gates * jnp.where(share == 0, other, own)
 
 
 def middle_backward(experts, *refs):
-    (meta, both_own, both_tp, middle_ref, cotangent, extras, gains, routes_row, keep_row) = refs[:9]
+    (meta, dx_own, dx_tp, part_own, part_tp, middle_ref, cotangent, extras) = refs[:8]
+    (gains, routes_row, keep_row) = refs[8:11]
+    (dmiddle_out, branch_grad, router_grad, gate_out) = refs[11:]
     routes_column, keep_column = columns_of(routes_row, keep_row)
     extras = extras[:, extras.shape[1] - LANES :]
-    (result, dmiddle_out, branch_grad, router_grad) = refs[9:]
     share = meta[1]
-    width = both_own.shape[1] // 2
-    own = both_own[...].astype(f32)
-    other = both_tp[...].astype(f32)
-    first = jnp.where(share == 0, own, other)
-    second = jnp.where(share == 0, other, own)
-    picked = jnp.concatenate([first[:, :width], second[:, :width]], axis=1)
-    slot_grad = jnp.concatenate([first[:, width:], second[:, width:]], axis=1)
+    own, other = dx_own[...].astype(f32), dx_tp[...].astype(f32)
+    slot_grad = jnp.concatenate(
+        [jnp.where(share == 0, own, other), jnp.where(share == 0, other, own)], axis=1
+    )
     middle = middle_ref[...]
     scale = rms_scale(middle)
     normed = middle * scale
     gain = gains[1:2]
     hidden = (normed * gain).astype(bf16)
     probs, onehot, kept, gate = routed(hidden, extras, routes_column, keep_column, experts)
-    result[...] = middle + gate * picked
+    gate_out[...] = jnp.broadcast_to(gate, gate_out.shape)
     upstream = cotangent[...].astype(f32)
-    gate_grad = jnp.sum(upstream * picked, axis=1, keepdims=True)
+    gate_grad = column_of(part_own[0:1, :] + part_tp[0:1, :])
     prob_grad = jnp.where(onehot, gate_grad * kept, 0.0)
     logit_grad = (
         probs * (prob_grad - jnp.sum(probs * prob_grad, axis=1, keepdims=True))
@@ -430,24 +441,20 @@
     branch_grad[...] = dmiddle.astype(bf16)
 
 
-def attention_backward(heads, shard, *refs):
-    (meta, lengths, table, x_own, x_other, h1, q_in, k_in, v_in, lse, db) = refs[:11]
-    (o_all, wo_ref, wall, router_grad) = refs[11:15]
-    (payload, top_out, bottom_out, dh1_own, dh1_other) = refs[15:20]
-    (strips, sums, do_all, dq, dk, dv, dqkv, dh1) = refs[20:]
+def attention_backward(heads, buckets, shard, *refs):
+    (meta, x_own, x_other, h1, q_in, k_in, v_in, probs, db) = refs[:9]
+    (o_all, wo_ref, wall, router_grad) = refs[9:13]
+    (payload, top_out, bottom_out, dh1_own, dh1_other) = refs[13:18]
+    (sums, do_all, dq, dk, dv, dqkv, dh1) = refs[18:]
     place = meta[0]
     rows = x_own.shape[0]
     group = 2 * rows
     lanes = q_in.shape[1]
-    first_head = place * heads
     own_at = pl.ds(pl.multiple_of(place * rows, 16), rows)
     other_at = pl.ds(pl.multiple_of((1 - place) * rows, 16), rows)
     both = mm(db[...], wo_ref[...])
     high = pltpu.roll(both[:, LANES : LANES + lanes], lanes - HEAD_SIZE, 1)
     do_all[...] = jnp.where(place == 0, both[:, :lanes], high).astype(bf16)
-    bias_strips(table, first_head, heads, strips)
-    segment_row = segments(lengths, group, 1)
-    segment_column = segments(lengths, group, 0)
     blocks = group // STRIP
     sums[...] = jnp.zeros_like(sums)
     keys = k_in[...]
@@ -456,13 +463,10 @@
     behind = [jnp.zeros((STRIP, STRIP), f32) for _ in range(heads)]
     for block in range(blocks):
         at = slice(block * STRIP, (block + 1) * STRIP)
-        same = segment_column[at] == segment_row
         dq_total = jnp.zeros((STRIP, lanes), f32)
         for head in range(heads):
             query = pick_head(q_in[at, :], head, lanes)
-            scores = mm_nt(query, keys) + bias_row(strips, table, head, first_head, block, blocks)
-            scores = jnp.where(same, scores, masked_value)
-            chances = jnp.exp(scores - lse[at, head : head + 1])
+            chances = probs[head, at, :]
             grad = pick_head(do_all[at, :], head, lanes)
             chance_grad = mm_nt(grad, values)
             mean = jnp.sum(chances * chance_grad, axis=1, keepdims=True)
@@ -501,7 +505,6 @@
         target[...] = grad.astype(bf16)
         part = jnp.sum(grad * (values * rms_scale(values)), axis=0, keepdims=True)
         gain_part = part if gain_part is None else gain_part + part
-    buckets = table.shape[1]
     spread = skew(sums[...].reshape(heads * STRIP, 4 * STRIP), False)
     diagonals = jnp.sum(spread.reshape(heads, STRIP, 4 * STRIP), axis=1)
     picks = (bucket_index(iota((4 * STRIP, 1), 0) - 2 * STRIP) == iota((1, LANES), 1)).astype(f32)
@@ -670,7 +673,7 @@
     _, right, left = ring_steps(count)
     going_right, going_left = top, bottom
     spec = lambda which: pl.BlockSpec((rows, lanes), lambda i, places: (places[which], 0))
-    params = pltpu.CompilerParams(vmem_limit_bytes=SMALL_VMEM_BYTES)
+    params = pltpu.CompilerParams(vmem_limit_bytes=8 * MIB)
     for step in range(count // 2, 0, -1):
         from_left = lax.ppermute(going_right, "fsdp", right)
         from_right = lax.ppermute(going_left, "fsdp", left)
@@ -744,12 +747,12 @@
     table = jnp.asarray(device_table(fsdp_count, 2, tp_count, aligned))
     device = lax.axis_index(("fsdp", "ctx", "tp"))
     meta = lax.dynamic_slice(table, (device, 0), (1, table.shape[1])).reshape(-1)
-    table_rows = rel_table.T
     shard_own, shard_send, wo_shard = kernel_call(
         pack_rows,
         [full((shard_rows, wide), bf16), full((shard_rows, wide), bf16), full((2 * shard_rows, lanes), bf16)],
         [smem] + [vmem] * 7,
         moved=512 * 1024,
+        mib=60,
     )(meta, w_query, w_key, w_value, w_output, w_router.T, gain_attn[None, :], gain_moe[None, :])
     shard_other = swap(shard_send, "ctx")
     shard = jnp.concatenate(
@@ -771,6 +774,17 @@
             jnp.concatenate([other, own], axis=axis),
         )
 
+    strips, far, segment = kernel_call(
+        functools.partial(attention_tables, heads),
+        [
+            full((heads, STRIP, 3 * STRIP), f32),
+            full((8, LANES), f32),
+            full((8, group), jnp.int32),
+        ],
+        [smem] * 3,
+        moved=1024 * 1024,
+        mib=8,
+    )(meta, lengths, rel_table.T)
     if aligned:
         shards = ring_gather(shard, fsdp_count)
         wall, wo_own = kernel_call(
@@ -781,14 +795,14 @@
         )(meta, *shards)
     else:
         both = lax.all_gather(shard, "fsdp", axis=0, tiled=False)
-        near, far = both[:, :shard_rows], both[:, shard_rows:]
+        upper, lower = both[:, :shard_rows], both[:, shard_rows:]
         wall = jnp.concatenate(
-            ordered(near[:, :, :wide].reshape(-1, wide), far[:, :, :wide].reshape(-1, wide)), axis=0
+            ordered(upper[:, :, :wide].reshape(-1, wide), lower[:, :, :wide].reshape(-1, wide)), axis=0
         )
-        wo_own = jnp.concatenate([near[:, :, wide : wide + width], far[:, :, wide : wide + width]], axis=2)
+        wo_own = jnp.concatenate([upper[:, :, wide : wide + width], lower[:, :, wide : wide + width]], axis=2)
         wo_own = wo_own.reshape(-1, 2 * width)
 
-    h1, q, k, v, o_own, o_other, o_all, lse, gains = kernel_call(
+    h1, q, k, v, o_own, o_other, o_all, probs, gains = kernel_call(
         functools.partial(attention_forward, heads, experts),
         [
             full((group, model_width), bf16),
@@ -798,14 +812,13 @@
             full((rows // 2, 2 * width), bf16),
             full((rows // 2, 2 * width), bf16),
             full((group, lanes), bf16),
-            full((group, LANES), f32),
+            full((heads, group, group), f32),
             full((8, model_width), f32),
         ],
-        [smem] * 3 + [vmem] * 3,
-        scratch=[pltpu.VMEM((heads, STRIP, 3 * STRIP), f32)],
+        [smem] + [vmem] * 6,
         flops=2 * group * model_width * wide * 8,
         moved=8 * 1024 * 1024,
-    )(meta, lengths, table_rows, tokens, x_other, wall)
+    )(meta, tokens, x_other, wall, strips, far, segment)
     wo_tp = swap(wo_own, "tp")
     wo_ctx = swap(wo_own, "ctx")
     wo_tp, gains = lax.optimization_barrier((wo_tp, gains))
@@ -894,6 +907,7 @@
             pltpu.VMEM((owners * per_owner, model_width), f32),
         ],
         grid=(pieces, chunks),
+        mib=24,
         flops=8 * pieces * slot_rows * model_width * hidden_width,
         moved=12 * 1024 * 1024,
     )(arrived, base[:, None], base[None, :], w_in, w_out)
@@ -906,32 +920,45 @@
 
     back_first = np.repeat(slot_first.reshape(owners, 1, per_owner), tp_count, axis=1).reshape(1, -1)
     back_second = np.repeat(slot_second.reshape(owners, 1, per_owner), tp_count, axis=1).reshape(1, -1)
-    both_own = kernel_call(
+    y_own, dx_own, part_own = kernel_call(
         functools.partial(from_experts, experts, capacity),
-        [full((rows, 2 * part_width), bf16)],
-        [vmem] * 5,
+        [
+            full((rows, part_width), bf16),
+            full((rows, part_width), bf16),
+            full((8, rows), f32),
+        ],
+        [smem] + [vmem] * 6,
         flops=4 * rows * returned.shape[0] * part_width,
         moved=2 * 1024 * 1024,
-    )(returned, routes_row, keep_row, back_first, back_second)[0]
-    both_tp = swap(both_own, "tp")
-
-    result, middle_grad, db_own, router_grad = kernel_call(
+    )(meta, returned, cotangent, routes_row, keep_row, back_first, back_second)
+    dx_tp = swap(dx_own, "tp")
+    part_tp = swap(part_own, "tp")
+
+    middle_grad, db_own, router_grad, gate = kernel_call(
         functools.partial(middle_backward, experts),
         [
             full((rows, model_width), f32),
-            full((rows, model_width), f32),
             full((rows, model_width), bf16),
             full((model_width, LANES), bf16),
-        ],
-        [smem] + [vmem] * 8,
+            full((rows, LANES), f32),
+        ],
+        [smem] + [vmem] * 10,
         flops=6 * rows * LANES * model_width,
         moved=6 * 1024 * 1024,
-    )(meta, both_own, both_tp, middle, cotangent, wall, gains, routes_row, keep_row)
+    )(meta, dx_own, dx_tp, part_own, part_tp, middle, cotangent, wall, gains, routes_row, keep_row)
+    y_own, gate = lax.optimization_barrier((y_own, gate))
+    y_tp = swap(y_own, "tp")
+    result = kernel_call(
+        add_expert,
+        [full((rows, model_width), f32)],
+        [smem] + [vmem] * 4,
+        moved=4 * 1024 * 1024,
+    )(meta, middle, gate, y_own, y_tp)[0]
     db = lax.all_gather(db_own, "ctx", axis=0, tiled=True)
 
     half = model_width // fsdp_count // 2
     payload, top, bottom, dh1_own, dh1_other = kernel_call(
-        functools.partial(attention_backward, heads, model_width // fsdp_count),
+        functools.partial(attention_backward, heads, buckets, model_width // fsdp_count),
         [
             full((model_width, wide + lanes), bf16),
             full((half if aligned else 16, wide + lanes), bf16),
@@ -939,9 +966,8 @@
             full((rows, model_width), bf16),
             full((rows, model_width), bf16),
         ],
-        [smem] * 3 + [vmem] * 12,
+        [smem] + [vmem] * 12,
         scratch=[
-            pltpu.VMEM((heads, STRIP, 3 * STRIP), f32),
             pltpu.VMEM((heads, STRIP, 4 * STRIP), f32),
             pltpu.VMEM((group, lanes), bf16),
             pltpu.VMEM((group, lanes), f32),
@@ -951,10 +977,10 @@
             pltpu.VMEM((group, model_width), f32),
         ],
         flops=2 * group * model_width * wide * 12,
+        mib=20,
         moved=8 * 1024 * 1024,
     )(
-        meta, lengths, table_rows, tokens, x_other, h1, q, k, v, lse, db,
-        o_all, wo_full, wall, router_grad,
+        meta, tokens, x_other, h1, q, k, v, probs, db, o_all, wo_full, wall, router_grad,
     )
 
     dh1_sum = (dh1_own.astype(f32) + swap(dh1_other, "ctx").astype(f32)).astype(bf16)
@@ -971,7 +997,7 @@
         [vmem] * 5,
         moved=4 * 1024 * 1024,
     )(tokens, middle_grad, gains, dh1_sum, dh1_far)[0]
-    other, input_grad = lax.optimization_barrier((other, input_grad))
+    other, input_grad, result = lax.optimization_barrier((other, input_grad, result))
 
     shard = full((shard_rows, 2 * width), f32)
     query_grad, key_grad, value_grad, output_grad, router_sum, gain_one, gain_two, table_grad = kernel_call(

time: 201 us -> 200 us (level)
  waiting for transfers between devices: 60.8 us -> 56.5 us
  Pallas kernels: 38.6 us -> 42 us
  local copies, waits for them, and re-layouts: 26.4 us -> 23.8 us
    unnamed x98 -> x90, local copies, waits for them, and re-layouts: 25.6 us -> 22.5 us
    pallas_call x1 -> x3, Pallas kernels: 10.5 us -> 12.9 us  [the longest x1 9.04 us: body(): kernel_call(functools.partial(attention_backward, heads, buckets, model_w...]
    ppermute x1, waiting for transfers between devices: 2.12 us -> 0.01 us  [ring_gather(): shards.append(lax.ppermute(going_right, 'fsdp', right))]
    ppermute x12 -> x14, starting transfers between devices: 7.31 us -> 8.73 us  [swap(): return lax.ppermute(value, axis, [(0, 1), (1, 0)])]
    ppermute x12 -> x14, waiting for transfers between devices: 14.8 us -> 14.8 us  [swap(): return lax.ppermute(value, axis, [(0, 1), (1, 0)])]
  transfers between devices with their start and end apart: 30 -> 32, of which waited for: 21 -> 18; matrix products, arithmetic and copies ran while one was open for 6% -> 6% of each run, Pallas kernels for 5% -> 6%
where the time goes in v5:
time: 200 us; the launch traced here: 199 us
  waiting for transfers between devices  56.5 us (28%)
  Pallas kernels  42 us (21%)
  blocking collectives  31.5 us (16%)
  starting transfers between devices  31 us (16%)
  local copies, waits for them, and re-layouts  23.8 us (12%)
  matrix products  11.9 us (6%)
    all_to_all x1, blocking collectives, body(): lax.all_to_all(sends.reshape(owners, per_owner, model_width), ('fsdp', 'c...  29.1 us
    unnamed x90, local copies, waits for them, and re-layouts  22.5 us
    ppermute x14, waiting for transfers between devices, swap(): return lax.ppermute(value, axis, [(0, 1), (1, 0)])  14.8 us
    all_to_all x1, waiting for transfers between devices, body(): lax.all_to_all(outgoing, ('fsdp', 'ctx', 'tp'), split_axis=0, concat_axis...  12.7 us
    ppermute x4, waiting for transfers between devices, ring_sums(): from_left = lax.ppermute(going_right, 'fsdp', right)  11.9 us
    ppermute x3, waiting for transfers between devices, ring_gather(): going_right = lax.ppermute(going_right, 'fsdp', right)  10.9 us
    pallas_call x1, Pallas kernels, body(): kernel_call(functools.partial(expert_kernel, owners, capacity, chunks, gr...  9.22 us
    pallas_call x1, Pallas kernels, body(): kernel_call(functools.partial(attention_backward, heads, buckets, model_w...  9.04 us
  transfers between devices with their start and end apart: 32, of which 18 were waited for; matrix products, arithmetic and copies ran while one was open for 6% of the time, Pallas kernels for 6%

profile of v5, /device:TPU:0, one launch (start us, length us, event | category | flops | bytes accessed | tf_op | source)
XLA Modules:
  0.0 198.6 jit_solution(6448867976514915736)
XLA Ops:
  0.7 1.3 dynamic-slice_bitcast_fusion.refs_0_.meta.places
  2.0 1.7 shard_map.301
  4.2 1.1 collective-permute-done.1
  5.3 0.9 pad_maximum_fusion.refs_1_
  6.2 3.0 %collective-permute-start.2 = (bf16[96,896]{1,0:T(8,128)(2,1)S(1)}, bf16[96,896]{1,0:T(8,128)(2,1)S(1)}, u32[]{:S(2)}, u32[]{:S(2)}) collective-permute-start(bf16[96,896]{1,0:T(8,128)(2,1)S(1)} %pad_maximum_fusion.refs_1_), channel_id=1, source_target_pairs={{0,8},{8,16},{16,24},{24,28},{28,20},{20,12},{12,4},{4,0},{1,9},{9... | collective-permute-start | bytes 516104 | tf_op jit(solution)/shard_map/ppermute | solution.py:652
  9.1 4.6 %collective-permute-done.2.refs_2_ = bf16[96,896]{1,0:T(8,128)(2,1)S(1)} collective-permute-done((bf16[96,896]{1,0:T(8,128)(2,1)S(1)}, bf16[96,896]{1,0:T(8,128)(2,1)S(1)}, u32[]{:S(2)}, u32[]{:S(2)}) %collective-permute-start.2) | collective-permute-done | bytes 172064 | tf_op jit(solution)/shard_map/ppermute | solution.py:652
  13.7 1.8 collective-permute-start.4
  15.8 3.9 %collective-permute-done.4.refs_4_ = bf16[96,896]{1,0:T(8,128)(2,1)S(1)} collective-permute-done((bf16[96,896]{1,0:T(8,128)(2,1)S(1)}, bf16[96,896]{1,0:T(8,128)(2,1)S(1)}, u32[]{:S(2)}, u32[]{:S(2)}) %collective-permute-start.4) | collective-permute-done | bytes 172064 | tf_op jit(solution)/shard_map/ppermute | solution.py:652
  19.7 1.5 collective-permute-start.6
  21.2 1.2 collective-permute-done.5.refs_5_
  22.6 2.4 %collective-permute-done.6.refs_6_ = bf16[96,896]{1,0:T(8,128)(2,1)S(1)} collective-permute-done((bf16[96,896]{1,0:T(8,128)(2,1)S(1)}, bf16[96,896]{1,0:T(8,128)(2,1)S(1)}, u32[]{:S(2)}, u32[]{:S(2)}) %collective-permute-start.6) | collective-permute-done | bytes 172064 | tf_op jit(solution)/shard_map/ppermute | solution.py:652
  25.1 1.5 collective-permute-start.8
  28.6 2.3 %shard_map.303 = (f32[3,128,384]{2,1,0:T(8,128)S(1)}, f32[8,128]{1,0:T(8,128)S(1)}, s32[8,512]{1,0:T(8,128)S(1)}) custom-call(s32[20]{0:T(128)S(1)} %copy-done.15, s32[1,4]{1,0:T(1,128)S(1)} %copy-done.22, f32[6,32]{1,0:T(8,128)S(1)} %bitcast.22), custom_call_target="tpu_custom_call" | custom-call | bytes 1048576 | tf_op jit(solution)/shard_map/pallas_call | solution.py:777
  32.4 1.6 collective-permute-start.12
  34.0 1.1 copy-done.1
  35.8 5.1 %shard_map.304 = (bf16[512,768]{1,0:T(8,128)(2,1)S(1)}, bf16[512,256]{1,0:T(8,128)(2,1)S(1)}, bf16[512,256]{1,0:T(8,128)(2,1)S(1)}, bf16[512,256]{1,0:T(8,128)(2...) custom-call(s32[20]{0:T(128)S(1)} %copy-done.17, ...), custom_call_target="tpu_custom_call" | custom-call | flops 4026531840 | bytes 8388608 | tf_op jit(solution)/shard_map/pallas_call | solution.py:805
  40.8 1.6 copy-done.33
  42.4 0.9 copy-done.35
  44.1 1.2 collective-permute-start.11
  45.7 3.5 %collective-permute-done.9.refs_4_ = bf16[128,384]{1,0:T(8,128)(2,1)S(1)} collective-permute-done((bf16[128,384]{1,0:T(8,128)(2,1)S(1)}, bf16[128,384]{1,0:T(8,128)(2,1)S(1)}, u32[]{:S(2)}, u32[]{:S(2)}) %collective-permute-start.9) | collective-permute-done | bytes 98336 | tf_op jit(solution)/shard_map/ppermute | solution.py:615
  49.2 1.0 collective-permute-done.11.refs_6_
  50.2 2.9 %shard_map.305 = (f32[256,768]{1,0:T(8,128)S(1)}, bf16[640,768]{1,0:T(8,128)(2,1)S(1)}, bf16[768,384]{1,0:T(8,128)(2,1)S(1)}) custom-call(s32[20]{0:T(128)S(1)} %copy-done.17, bf16[256,768]{1,0:T(8,128)(2,1)S(1)} %copy-done.2, bf16[256,768]{1,0:T(8,128)(2,1)S(1)} %copy-done, bf16[128,384]{1,0:T(8,128)(2,1)S(1)} %get-tuple-element.92.refs_3_, ...), custom_call_target="tpu_custom_call" | custom-call | flops 805306368 | bytes 6291456 | tf_op jit(solution)/shard_map/pallas_call | solution.py:844
  53.1 29.1 %all_to_all.10 = bf16[16,40,768]{2,1,0:T(8,128)(2,1)S(1)} all-to-all(bf16[16,40,768]{2,1,0:T(8,128)(2,1)S(1)} %bitcast.20), channel_id=1, replica_groups=mesh['fsdp'=8,'ctx'=2,'tp'=2] {'fsdp','ctx'}, dimensions={0} | all-to-all | bytes 1966080 | tf_op jit(solution)/shard_map/all_to_all | solution.py:860
  82.3 9.2 %shard_map.306 = (bf16[32,40,384]{2,1,0:T(8,128)(2,1)S(1)}, bf16[2,160,768]{2,1,0:T(8,128)(2,1)S(1)}, bf16[2,160,768]{2,1,0:T(8,128)(2,1)S(1)}, bf16[2,160,1536]...) custom-call(bf16[640,768]{1,0:T(8,128)(2,1)S(1)} %bitcast.21, s32[320,1]{1,0:T(8,128)S(1)} %copy-done.29, ...), custom_call_target="tpu_custom_call" | custom-call | flops 3019898880 | bytes 12582912 | tf_op jit(solution)/shard_map/pallas_call | solution.py:881
  91.5 1.0 copy-done.3
  92.5 1.0 copy-done.4
  93.5 0.9 copy-done.6
  96.0 3.9 %all-to-all-start.1 = ((bf16[32,40,384]{2,1,0:T(8,128)(2,1)}), bf16[32,40,384]{2,1,0:T(8,128)(2,1)S(1)}, u32[]{:S(2)}, u32[]{:S(2)}) async-start(bf16[32,40,384]{2,1,0:T(8,128)(2,1)} %copy-done.3), calls=%async_computation.1 | async-start | bytes 1966080 | tf_op jit(solution)/shard_map/all_to_all | solution.py:915
  99.9 6.6 %fusion = f32[2,768,1536]{2,1,0:T(8,128)} fusion(bf16[2,160,768]{2,1,0:T(8,128)(2,1)} %copy-done.9, bf16[2,160,1536]{2,1,0:T(8,128)(2,1)} %copy-done.6), kind=kOutput, calls=%fused_computation.3 | convolution fusion | flops 754974720 | bytes 10911744 | tf_op jit(solution)/shard_map/lrd,lrf->ldf/dot_general | solution.py:379
  106.6 5.3 %fusion.1 = f32[2,1536,768]{2,1,0:T(8,128)} fusion(bf16[2,160,1536]{2,1,0:T(8,128)(2,1)S(1)} %copy-done.5, bf16[2,160,768]{2,1,0:T(8,128)(2,1)S(1)} %copy-done.8), kind=kOutput, calls=%fused_computation.4 | convolution fusion | flops 754974720 | bytes 10911744 | tf_op jit(solution)/shard_map/lrf,lrd->lfd/dot_general | solution.py:380
  111.8 12.7 %all-to-all-done.1 = bf16[32,40,384]{2,1,0:T(8,128)(2,1)S(1)} async-done(((bf16[32,40,384]{2,1,0:T(8,128)(2,1)}), bf16[32,40,384]{2,1,0:T(8,128)(2,1)S(1)}, u32[]{:S(2)}, u32[]{:S(2)}) %all-to-all-start.1) | async-done | bytes 983072 | tf_op jit(solution)/shard_map/all_to_all | solution.py:915
  125.9 1.9 shard_map.307
  127.8 1.5 collective-permute-start.15
  129.9 5.1 %collective-permute-done.16.refs_4_ = f32[8,256]{1,0:T(8,128)S(1)} collective-permute-done((f32[8,256]{1,0:T(8,128)S(1)}, f32[8,256]{1,0:T(8,128)S(1)}, u32[]{:S(2)}, u32[]{:S(2)}) %collective-permute-start.16) | collective-permute-done | bytes 8224 | tf_op jit(solution)/shard_map/ppermute | solution.py:615
  135.7 2.5 %shard_map.308 = (f32[256,768]{1,0:T(8,128)S(1)}, bf16[256,768]{1,0:T(8,128)(2,1)S(1)}, bf16[768,128]{1,0:T(8,128)(2,1)S(1)}, f32[256,128]{1,0:T(8,128)S(1)}) custom-call(s32[20]{0:T(128)S(1)} %copy-done.18, bf16[256,384]{1,0:T(8,128)(2,1)S(1)} %get-tuple-element.105.refs_1_, bf16[256,384]{1,0:T(8,128)(2,1)S(1)} %collective-permute-done.15.refs_2_, ...), custom_call_target="tpu_custom_call" | custom-call | flops 150994944 | bytes 6291456 | tf_op jit(solution)/shard_map/pallas_call | solution.py:937
  138.2 2.4 %all_gather.3.refs_8_ = bf16[512,768]{1,0:T(8,128)(2,1)S(1)} all-gather(bf16[256,768]{1,0:T(8,128)(2,1)S(1)} %get-tuple-element.108), channel_id=1, replica_groups=mesh['fsdp'=8,'ctx'=2,'tp'=2] {'ctx'}, dimensions={0}, use_global_device_ids=true | all-gather | bytes 1179648 | tf_op jit(solution)/shard_map/all_gather | solution.py:957
  140.6 1.1 copy-done.26
  141.6 1.0 copy-done.28
  142.6 1.9 copy-done.34
  144.5 1.1 copy-done.36
  145.7 0.9 copy-done.38
  146.6 0.9 copy-done.40
  147.6 0.9 copy-done.42
  148.5 0.9 copy-done.44
  149.5 9.0 %shard_map.309 = (bf16[768,896]{1,0:T(8,128)(2,1)S(1)}, bf16[48,896]{1,0:T(8,128)(2,1)S(1)}, bf16[48,896]{1,0:T(8,128)(2,1)S(1)}, bf16[256,768]{1,0:T(8,128)(2,1)S(1)}, bf16[256,768]{1,0:T(8,128)(2,1)S(1)}) custom-call(s32[20]{0:T(128)S(1)} %copy-done.18, bf16[256,768]{1,0:T(8,128)(2,1)S(1)} %copy-done.2, bf16[256,768]{1,0:T(8,128)(2,1)S(1)} %copy-done.28, ...), custom_call_target="tpu_custom_call" | custom-call | flops 6039797760 | bytes 8388608 | tf_op jit(solution)/shard_map/pallas_call | solution.py:960
  158.7 1.1 collective-permute-start.19
  159.8 1.0 collective-permute-start.20
  160.8 2.8 %collective-permute-done.19.from_left = bf16[48,896]{1,0:T(8,128)(2,1)S(1)} collective-permute-done((bf16[48,896]{1,0:T(8,128)(2,1)S(1)}, bf16[48,896]{1,0:T(8,128)(2,1)S(1)}, u32[]{:S(2)}, u32[]{:S(2)}) %collective-permute-start.19) | collective-permute-done | bytes 86048 | tf_op jit(solution)/shard_map/ppermute | solution.py:678
  164.9 1.2 collective-permute-start.21
  166.1 0.9 collective-permute-start.22
  167.1 1.0 collective-permute-start.18
  168.1 2.4 %collective-permute-done.21.from_left = bf16[96,896]{1,0:T(8,128)(2,1)S(1)} collective-permute-done((bf16[96,896]{1,0:T(8,128)(2,1)S(1)}, bf16[96,896]{1,0:T(8,128)(2,1)S(1)}, u32[]{:S(2)}, u32[]{:S(2)}) %collective-permute-start.21) | collective-permute-done | bytes 172064 | tf_op jit(solution)/shard_map/ppermute | solution.py:678
  170.5 1.0 collective-permute-done.22.from_right
  172.8 1.4 collective-permute-start.24
  174.2 3.4 %collective-permute-done.23.from_left = bf16[96,896]{1,0:T(8,128)(2,1)S(1)} collective-permute-done((bf16[96,896]{1,0:T(8,128)(2,1)S(1)}, bf16[96,896]{1,0:T(8,128)(2,1)S(1)}, u32[]{:S(2)}, u32[]{:S(2)}) %collective-permute-start.23) | collective-permute-done | bytes 172064 | tf_op jit(solution)/shard_map/ppermute | solution.py:678
  178.8 1.6 collective-permute-start.25
  180.9 3.4 %collective-permute-done.25.from_left = bf16[96,896]{1,0:T(8,128)(2,1)S(1)} collective-permute-done((bf16[96,896]{1,0:T(8,128)(2,1)S(1)}, bf16[96,896]{1,0:T(8,128)(2,1)S(1)}, u32[]{:S(2)}, u32[]{:S(2)}) %collective-permute-start.25) | collective-permute-done | bytes 172064 | tf_op jit(solution)/shard_map/ppermute | solution.py:678
  184.3 1.6 collective-permute-done.26.from_right
  186.6 1.1 collective-permute-start.28
  187.7 1.0 collective-permute-start.29
  189.2 5.1 %collective-permute-done.28.y_tp = bf16[256,384]{1,0:T(8,128)(2,1)S(1)} collective-permute-done((bf16[256,384]{1,0:T(8,128)(2,1)S(1)}, bf16[256,384]{1,0:T(8,128)(2,1)S(1)}, u32[]{:S(2)}, u32[]{:S(2)}) %collective-permute-start.28) | collective-permute-done | bytes 196640 | tf_op jit(solution)/shard_map/ppermute | solution.py:615
  194.3 1.6 shard_map.315
  195.9 1.3 shard_map.314
  197.2 1.4 shard_map.316
  (113 shorter events, 16.5 us)
Async XLA Ops:
  0.6 49.5 %copy-start.10 = (s32[640,1]{1,0:T(8,128)S(1)}, s32[640,1]{1,0:T(8,128)}, u32[]{:S(2)}) copy-start(s32[640,1]{1,0:T(8,128)} %constant.36.clone.refs_16_) | copy-start | bytes 7684
  0.7 49.5 %copy-start.11 = (s32[640,1]{1,0:T(8,128)S(1)}, s32[640,1]{1,0:T(8,128)}, u32[]{:S(2)}) copy-start(s32[640,1]{1,0:T(8,128)} %constant.35.clone.refs_15_) | copy-start | bytes 7684
  0.7 49.5 %copy-start.2 = (bf16[256,768]{1,0:T(8,128)(2,1)S(1)}, bf16[256,768]{1,0:T(8,128)(2,1)}, u32[]{:S(2)}) copy-start(bf16[256,768]{1,0:T(8,128)(2,1)} %x_own.1) | copy-start | bytes 1179652
  0.7 49.5 %copy-start = (bf16[256,768]{1,0:T(8,128)(2,1)S(1)}, bf16[256,768]{1,0:T(8,128)(2,1)}, u32[]{:S(2)}) copy-start(bf16[256,768]{1,0:T(8,128)(2,1)} %refs_6_.2) | copy-start | bytes 1179652
  3.7 1.6 collective-permute-start.1
  6.2 7.6 %collective-permute-start.2 = (bf16[96,896]{1,0:T(8,128)(2,1)S(1)}, bf16[96,896]{1,0:T(8,128)(2,1)S(1)}, u32[]{:S(2)}, u32[]{:S(2)}) collective-permute-start(bf16[96,896]{1,0:T(8,128)(2,1)S(1)} %pad_maximum_fusion.refs_1_), channel_id=1, source_target_pairs={{0,8},{8,16},{16,24},{24,28},{28,20},{20,12},{12,4},{4,0},{1,9},{9... | collective-permute-start | bytes 516104 | tf_op jit(solution)/shard_map/ppermute | solution.py:652
  9.1 6.4 %collective-permute-start.3 = (bf16[96,896]{1,0:T(8,128)(2,1)S(1)}, bf16[96,896]{1,0:T(8,128)(2,1)S(1)}, u32[]{:S(2)}, u32[]{:S(2)}) collective-permute-start(bf16[96,896]{1,0:T(8,128)(2,1)S(1)} %pad_maximum_fusion.refs_1_), channel_id=1, source_target_pairs={{8,0},{16,8},{24,16},{28,24},{20,28},{12,20},{4,12},{0,4},{9,1},{1... | collective-permute-start | bytes 516104 | tf_op jit(solution)/shard_map/ppermute | solution.py:653
  13.7 5.9 %collective-permute-start.4 = (bf16[96,896]{1,0:T(8,128)(2,1)S(1)}, bf16[96,896]{1,0:T(8,128)(2,1)S(1)}, u32[]{:S(2)}, u32[]{:S(2)}) collective-permute-start(bf16[96,896]{1,0:T(8,128)(2,1)S(1)} %collective-permute-done.2.refs_2_), channel_id=1, source_target_pairs={{0,8},{8,16},{16,24},{24,28},{28,20},{20,12},{12,4},{4,0},{1,9},{9... | collective-permute-start | bytes 516104 | tf_op jit(solution)/shard_map/ppermute | solution.py:652
  15.6 18.4 %collective-permute-start = (bf16[256,768]{1,0:T(8,128)(2,1)}, bf16[256,768]{1,0:T(8,128)(2,1)S(1)}, u32[]{:S(2)}, u32[]{:S(2)}) collective-permute-start(bf16[256,768]{1,0:T(8,128)(2,1)} %x_own.1), channel_id=1, source_target_pairs={{0,2},{2,0},{1,3},{3,1},{4,6},{6,4},{5,7},{7,5},{8,10},{10,8},{9,1... | collective-permute-start | bytes 1179656 | tf_op jit(solution)/shard_map/ppermute | solution.py:615
  15.6 6.8 %collective-permute-start.5 = (bf16[96,896]{1,0:T(8,128)(2,1)S(1)}, bf16[96,896]{1,0:T(8,128)(2,1)S(1)}, u32[]{:S(2)}, u32[]{:S(2)}) collective-permute-start(bf16[96,896]{1,0:T(8,128)(2,1)S(1)} %collective-permute-done.3.refs_3_), channel_id=1, source_target_pairs={{8,0},{16,8},{24,16},{28,24},{20,28},{12,20},{4,12},{0,4},{9,1},{1... | collective-permute-start | bytes 516104 | tf_op jit(solution)/shard_map/ppermute | solution.py:653
  19.7 5.4 %collective-permute-start.6 = (bf16[96,896]{1,0:T(8,128)(2,1)S(1)}, bf16[96,896]{1,0:T(8,128)(2,1)S(1)}, u32[]{:S(2)}, u32[]{:S(2)}) collective-permute-start(bf16[96,896]{1,0:T(8,128)(2,1)S(1)} %collective-permute-done.4.refs_4_), channel_id=1, source_target_pairs={{0,8},{8,16},{16,24},{24,28},{28,20},{20,12},{12,4},{4,0},{1,9},{9... | collective-permute-start | bytes 516104 | tf_op jit(solution)/shard_map/ppermute | solution.py:652
  22.4 8.5 %collective-permute-start.7 = (bf16[96,896]{1,0:T(8,128)(2,1)S(1)}, bf16[96,896]{1,0:T(8,128)(2,1)S(1)}, u32[]{:S(2)}, u32[]{:S(2)}) collective-permute-start(bf16[96,896]{1,0:T(8,128)(2,1)S(1)} %collective-permute-done.5.refs_5_), channel_id=1, source_target_pairs={{8,0},{16,8},{24,16},{28,24},{20,28},{12,20},{4,12},{0,4},{9,1},{1... | collective-permute-start | bytes 516104 | tf_op jit(solution)/shard_map/ppermute | solution.py:653
  25.1 5.8 %collective-permute-start.8 = (bf16[96,896]{1,0:T(8,128)(2,1)S(1)}, bf16[96,896]{1,0:T(8,128)(2,1)S(1)}, u32[]{:S(2)}, u32[]{:S(2)}) collective-permute-start(bf16[96,896]{1,0:T(8,128)(2,1)S(1)} %collective-permute-done.6.refs_6_), channel_id=1, source_target_pairs={{0,8},{8,16},{16,24},{24,28},{28,20},{20,12},{12,4},{4,0},{1,9},{9... | collective-permute-start | bytes 516104 | tf_op jit(solution)/shard_map/ppermute | solution.py:655
  31.5 18.7 %copy-start.20 = (s32[256,1]{0,1:T(1,128)S(1)}, s32[256,1]{0,1:T(1,128)}, u32[]{:S(2)}) copy-start(s32[256,1]{0,1:T(1,128)} %param.35) | copy-start | bytes 3076
  31.5 18.7 %copy-start.21 = (s32[256]{0:T(256)S(1)}, s32[256]{0:T(256)}, u32[]{:S(2)}) copy-start(s32[256]{0:T(256)} %param.36) | copy-start | bytes 3076
  32.3 17.9 %collective-permute-start.13 = (bf16[384,384]{1,0:T(8,128)(2,1)S(1)}, bf16[384,384]{1,0:T(8,128)(2,1)S(1)}, u32[]{:S(2)}, u32[]{:S(2)}) collective-permute-start(bf16[384,384]{1,0:T(8,128)(2,1)S(1)} %get-tuple-element.94.refs_7_), channel_id=1, source_target_pairs={{0,2},{2,0},{1,3},{3,1},{4,6},{6,4},{5,7},{7,5},{8,10},{10,8},{9,1... | collective-permute-start | bytes 884744 | tf_op jit(solution)/shard_map/ppermute | solution.py:615
  32.4 11.0 %collective-permute-start.12 = (bf16[384,384]{1,0:T(8,128)(2,1)S(1)}, bf16[384,384]{1,0:T(8,128)(2,1)S(1)}, u32[]{:S(2)}, u32[]{:S(2)}) collective-permute-start(bf16[384,384]{1,0:T(8,128)(2,1)S(1)} %get-tuple-element.94.refs_7_), channel_id=1, source_target_pairs={{0,1},{1,0},{2,3},{3,2},{4,5},{5,4},{6,7},{7,6},{8,9},{9,8},{10,11... | collective-permute-start | bytes 884744 | tf_op jit(solution)/shard_map/ppermute | solution.py:615
  33.9 19.2 %copy-start.27 = (bf16[256,768]{1,0:T(8,128)(2,1)}, bf16[256,768]{1,0:T(8,128)(2,1)S(1)}, u32[]{:S(2)}) copy-start(bf16[256,768]{1,0:T(8,128)(2,1)S(1)} %collective-permute-done.refs_2_) | copy-start | bytes 1179652
  33.9 1.1 copy-start.1
  35.7 46.5 %copy-start.23 = (bf16[2,768,1536]{2,1,0:T(8,128)(2,1)S(1)}, bf16[2,768,1536]{2,1,0:T(8,128)(2,1)}, u32[]{:S(2)}) copy-start(bf16[2,768,1536]{2,1,0:T(8,128)(2,1)} %refs_3_.3) | copy-start | bytes 14155780
  35.7 46.5 %copy-start.24 = (bf16[2,1536,768]{2,1,0:T(8,128)(2,1)S(1)}, bf16[2,1536,768]{2,1,0:T(8,128)(2,1)}, u32[]{:S(2)}) copy-start(bf16[2,1536,768]{2,1,0:T(8,128)(2,1)} %refs_4_.3) | copy-start | bytes 14155780
  35.7 46.5 %copy-start.29 = (s32[320,1]{1,0:T(8,128)S(1)}, s32[320,1]{1,0:T(8,128)}, u32[]{:S(2)}) copy-start(s32[320,1]{1,0:T(8,128)} %constant.37.clone.refs_1_) | copy-start | bytes 3844
  35.8 46.5 %copy-start.32 = (s32[1,320]{1,0:T(1,128)S(1)}, s32[1,320]{1,0:T(1,128)}, u32[]{:S(2)}) copy-start(s32[1,320]{1,0:T(1,128)} %constant.38.clone.refs_2_) | copy-start | bytes 3844
  40.8 1.6 copy-start.33
  43.3 38.9 %copy-start.12 = (f32[8,768]{1,0:T(8,128)}, f32[8,768]{1,0:T(8,128)S(1)}, u32[]{:S(2)}) copy-start(f32[8,768]{1,0:T(8,128)S(1)} %get-tuple-element.97.refs_12_.refs_8_.gains) | copy-start | bytes 73732
  43.3 38.9 %copy-start.37 = (bf16[512,256]{1,0:T(8,128)(2,1)}, bf16[512,256]{1,0:T(8,128)(2,1)S(1)}, u32[]{:S(2)}) copy-start(bf16[512,256]{1,0:T(8,128)(2,1)S(1)} %get-tuple-element.88.refs_4_) | copy-start | bytes 786436
  43.3 38.9 %copy-start.39 = (bf16[512,256]{1,0:T(8,128)(2,1)}, bf16[512,256]{1,0:T(8,128)(2,1)S(1)}, u32[]{:S(2)}) copy-start(bf16[512,256]{1,0:T(8,128)(2,1)S(1)} %get-tuple-element.89.refs_5_) | copy-start | bytes 786436
  43.3 38.9 %copy-start.41 = (bf16[512,256]{1,0:T(8,128)(2,1)}, bf16[512,256]{1,0:T(8,128)(2,1)S(1)}, u32[]{:S(2)}) copy-start(bf16[512,256]{1,0:T(8,128)(2,1)S(1)} %get-tuple-element.90.refs_6_) | copy-start | bytes 786436
  43.3 38.9 %copy-start.43 = (bf16[512,256]{1,0:T(8,128)(2,1)}, bf16[512,256]{1,0:T(8,128)(2,1)S(1)}, u32[]{:S(2)}) copy-start(bf16[512,256]{1,0:T(8,128)(2,1)S(1)} %get-tuple-element.109.refs_9_) | copy-start | bytes 786436
  43.4 6.8 %collective-permute-start.14 = (bf16[384,384]{1,0:T(8,128)(2,1)S(1)}, bf16[384,384]{1,0:T(8,128)(2,1)S(1)}, u32[]{:S(2)}, u32[]{:S(2)}) collective-permute-start(bf16[384,384]{1,0:T(8,128)(2,1)S(1)} %collective-permute-done.12.refs_8_), channel_id=1, source_target_pairs={{0,2},{2,0},{1,3},{3,1},{4,6},{6,4},{5,7},{7,5},{8,10},{10,8},{9,1... | collective-permute-start | bytes 884744 | tf_op jit(solution)/shard_map/ppermute | solution.py:615
  43.6 5.6 %collective-permute-start.9 = (bf16[128,384]{1,0:T(8,128)(2,1)S(1)}, bf16[128,384]{1,0:T(8,128)(2,1)S(1)}, u32[]{:S(2)}, u32[]{:S(2)}) collective-permute-start(bf16[128,384]{1,0:T(8,128)(2,1)S(1)} %get-tuple-element.92.refs_3_), channel_id=1, source_target_pairs={{0,1},{1,0},{2,3},{3,2},{4,5},{5,4},{6,7},{7,6},{8,9},{9,8},{10,11... | collective-permute-start | bytes 294920 | tf_op jit(solution)/shard_map/ppermute | solution.py:615
  44.1 6.1 %collective-permute-start.11 = (bf16[128,384]{1,0:T(8,128)(2,1)S(1)}, bf16[128,384]{1,0:T(8,128)(2,1)S(1)}, u32[]{:S(2)}, u32[]{:S(2)}) collective-permute-start(bf16[128,384]{1,0:T(8,128)(2,1)S(1)} %get-tuple-element.93), channel_id=1, source_target_pairs={{0,3},{1,2},{2,1},{3,0},{4,7},{5,6},{6,5},{7,4},{8,11},{9,10},{10,... | collective-permute-start | bytes 294920 | tf_op jit(solution)/shard_map/ppermute | solution.py:831
  45.3 4.9 %collective-permute-start.10 = (bf16[128,384]{1,0:T(8,128)(2,1)S(1)}, bf16[128,384]{1,0:T(8,128)(2,1)S(1)}, u32[]{:S(2)}, u32[]{:S(2)}) collective-permute-start(bf16[128,384]{1,0:T(8,128)(2,1)S(1)} %get-tuple-element.93), channel_id=1, source_target_pairs={{0,2},{2,0},{1,3},{3,1},{4,6},{6,4},{5,7},{7,5},{8,10},{10,8},{9,1... | collective-permute-start | bytes 294920 | tf_op jit(solution)/shard_map/ppermute | solution.py:615
  53.1 29.1 %copy-start.25 = (bf16[768,384]{1,0:T(8,128)(2,1)}, bf16[768,384]{1,0:T(8,128)(2,1)S(1)}, u32[]{:S(2)}) copy-start(bf16[768,384]{1,0:T(8,128)(2,1)S(1)} %get-tuple-element.110.refs_10_) | copy-start | bytes 1769476
  91.5 1.0 copy-start.3
  92.5 1.0 copy-start.4
  96.0 28.6 %all-to-all-start.1 = ((bf16[32,40,384]{2,1,0:T(8,128)(2,1)}), bf16[32,40,384]{2,1,0:T(8,128)(2,1)S(1)}, u32[]{:S(2)}, u32[]{:S(2)}) async-start(bf16[32,40,384]{2,1,0:T(8,128)(2,1)} %copy-done.3), calls=%async_computation.1 | async-start | bytes 1966080 | tf_op jit(solution)/shard_map/all_to_all | solution.py:915
  99.9 6.7 %copy-start.5 = (bf16[2,160,1536]{2,1,0:T(8,128)(2,1)S(1)}, bf16[2,160,1536]{2,1,0:T(8,128)(2,1)}, u32[]{:S(2)}) copy-start(bf16[2,160,1536]{2,1,0:T(8,128)(2,1)} %copy-done.4) | copy-start | bytes 2949124
  99.9 6.7 %copy-start.8 = (bf16[2,160,768]{2,1,0:T(8,128)(2,1)S(1)}, bf16[2,160,768]{2,1,0:T(8,128)(2,1)}, u32[]{:S(2)}) copy-start(bf16[2,160,768]{2,1,0:T(8,128)(2,1)} %copy-done.7) | copy-start | bytes 1474564
  99.9 24.6 %copy-start.18 = (s32[20]{0:T(128)S(1)}, s32[20]{0:T(128)}, u32[]{:S(2)}) copy-start(s32[20]{0:T(128)} %dynamic-slice_bitcast_fusion.refs_0_.meta.places) | copy-start | bytes 244
  127.8 7.2 %collective-permute-start.15 = (bf16[256,384]{1,0:T(8,128)(2,1)S(1)}, bf16[256,384]{1,0:T(8,128)(2,1)S(1)}, u32[]{:S(2)}, u32[]{:S(2)}) collective-permute-start(bf16[256,384]{1,0:T(8,128)(2,1)S(1)} %get-tuple-element.105.refs_1_), channel_id=1, source_target_pairs={{0,1},{1,0},{2,3},{3,2},{4,5},{5,4},{6,7},{7,6},{8,9},{9,8},{10,11... | collective-permute-start | bytes 589832 | tf_op jit(solution)/shard_map/ppermute | solution.py:615
  129.3 5.6 %collective-permute-start.16 = (f32[8,256]{1,0:T(8,128)S(1)}, f32[8,256]{1,0:T(8,128)S(1)}, u32[]{:S(2)}, u32[]{:S(2)}) collective-permute-start(f32[8,256]{1,0:T(8,128)S(1)} %get-tuple-element.106.refs_3_), channel_id=1, source_target_pairs={{0,1},{1,0},{2,3},{3,2},{4,5},{5,4},{6,7},{7,6},{8,9},{9,8},{10,11... | collective-permute-start | bytes 24584 | tf_op jit(solution)/shard_map/ppermute | solution.py:615
  140.6 1.1 copy-start.26
  141.6 1.0 copy-start.28
  142.6 1.9 copy-start.34
  144.5 1.1 copy-start.36
  145.7 0.9 copy-start.38
  146.6 0.9 copy-start.40
  147.6 0.9 copy-start.42
  158.5 37.4 %copy-start.14 = (f32[8,768]{1,0:T(8,128)S(1)}, f32[8,768]{1,0:T(8,128)}, u32[]{:S(2)}) copy-start(f32[8,768]{1,0:T(8,128)} %copy-done.12) | copy-start | bytes 73732
  158.5 8.5 %collective-permute-start.17 = (bf16[256,768]{1,0:T(8,128)(2,1)S(1)}, bf16[256,768]{1,0:T(8,128)(2,1)S(1)}, u32[]{:S(2)}, u32[]{:S(2)}) collective-permute-start(bf16[256,768]{1,0:T(8,128)(2,1)S(1)} %get-tuple-element.114), channel_id=1, source_target_pairs={{0,2},{2,0},{1,3},{3,1},{4,6},{6,4},{5,7},{7,5},{8,10},{10,8},{9,1... | collective-permute-start | bytes 1179656 | tf_op jit(solution)/shard_map/ppermute | solution.py:615
  158.7 4.8 %collective-permute-start.19 = (bf16[48,896]{1,0:T(8,128)(2,1)S(1)}, bf16[48,896]{1,0:T(8,128)(2,1)S(1)}, u32[]{:S(2)}, u32[]{:S(2)}) collective-permute-start(bf16[48,896]{1,0:T(8,128)(2,1)S(1)} %get-tuple-element.115), channel_id=1, source_target_pairs={{0,8},{8,16},{16,24},{24,28},{28,20},{20,12},{12,4},{4,0},{1,9},{9... | collective-permute-start | bytes 258056 | tf_op jit(solution)/shard_map/ppermute | solution.py:678
  159.8 4.5 %collective-permute-start.20 = (bf16[48,896]{1,0:T(8,128)(2,1)S(1)}, bf16[48,896]{1,0:T(8,128)(2,1)S(1)}, u32[]{:S(2)}, u32[]{:S(2)}) collective-permute-start(bf16[48,896]{1,0:T(8,128)(2,1)S(1)} %get-tuple-element.116), channel_id=1, source_target_pairs={{8,0},{16,8},{24,16},{28,24},{20,28},{12,20},{4,12},{0,4},{9,1},{1... | collective-permute-start | bytes 258056 | tf_op jit(solution)/shard_map/ppermute | solution.py:679
  164.9 5.6 %collective-permute-start.21 = (bf16[96,896]{1,0:T(8,128)(2,1)S(1)}, bf16[96,896]{1,0:T(8,128)(2,1)S(1)}, u32[]{:S(2)}, u32[]{:S(2)}) collective-permute-start(bf16[96,896]{1,0:T(8,128)(2,1)S(1)} %get-tuple-element.117), channel_id=1, source_target_pairs={{0,8},{8,16},{16,24},{24,28},{28,20},{20,12},{12,4},{4,0},{1,9},{9... | collective-permute-start | bytes 516104 | tf_op jit(solution)/shard_map/ppermute | solution.py:678
  166.1 5.4 %collective-permute-start.22 = (bf16[96,896]{1,0:T(8,128)(2,1)S(1)}, bf16[96,896]{1,0:T(8,128)(2,1)S(1)}, u32[]{:S(2)}, u32[]{:S(2)}) collective-permute-start(bf16[96,896]{1,0:T(8,128)(2,1)S(1)} %get-tuple-element.118), channel_id=1, source_target_pairs={{8,0},{16,8},{24,16},{28,24},{20,28},{12,20},{4,12},{0,4},{9,1},{1... | collective-permute-start | bytes 516104 | tf_op jit(solution)/shard_map/ppermute | solution.py:679
  167.1 18.8 %collective-permute-start.18 = (bf16[256,768]{1,0:T(8,128)(2,1)S(1)}, bf16[256,768]{1,0:T(8,128)(2,1)S(1)}, u32[]{:S(2)}, u32[]{:S(2)}) collective-permute-start(bf16[256,768]{1,0:T(8,128)(2,1)S(1)} %add_convert_fusion.near), channel_id=1, source_target_pairs={{0,1},{1,0},{2,3},{3,2},{4,5},{5,4},{6,7},{7,6},{8,9},{9,8},{10,11... | collective-permute-start | bytes 1179656 | tf_op jit(solution)/shard_map/ppermute | solution.py:615
  172.1 5.5 %collective-permute-start.23 = (bf16[96,896]{1,0:T(8,128)(2,1)S(1)}, bf16[96,896]{1,0:T(8,128)(2,1)S(1)}, u32[]{:S(2)}, u32[]{:S(2)}) collective-permute-start(bf16[96,896]{1,0:T(8,128)(2,1)S(1)} %get-tuple-element.119), channel_id=1, source_target_pairs={{0,8},{8,16},{16,24},{24,28},{28,20},{20,12},{12,4},{4,0},{1,9},{9... | collective-permute-start | bytes 516104 | tf_op jit(solution)/shard_map/ppermute | solution.py:678
  172.8 5.4 %collective-permute-start.24 = (bf16[96,896]{1,0:T(8,128)(2,1)S(1)}, bf16[96,896]{1,0:T(8,128)(2,1)S(1)}, u32[]{:S(2)}, u32[]{:S(2)}) collective-permute-start(bf16[96,896]{1,0:T(8,128)(2,1)S(1)} %get-tuple-element.120), channel_id=1, source_target_pairs={{8,0},{16,8},{24,16},{28,24},{20,28},{12,20},{4,12},{0,4},{9,1},{1... | collective-permute-start | bytes 516104 | tf_op jit(solution)/shard_map/ppermute | solution.py:679
  178.8 5.5 %collective-permute-start.25 = (bf16[96,896]{1,0:T(8,128)(2,1)S(1)}, bf16[96,896]{1,0:T(8,128)(2,1)S(1)}, u32[]{:S(2)}, u32[]{:S(2)}) collective-permute-start(bf16[96,896]{1,0:T(8,128)(2,1)S(1)} %get-tuple-element.121), channel_id=1, source_target_pairs={{0,8},{8,16},{16,24},{24,28},{28,20},{20,12},{12,4},{4,0},{1,9},{9... | collective-permute-start | bytes 516104 | tf_op jit(solution)/shard_map/ppermute | solution.py:678
  180.5 5.4 %collective-permute-start.26 = (bf16[96,896]{1,0:T(8,128)(2,1)S(1)}, bf16[96,896]{1,0:T(8,128)(2,1)S(1)}, u32[]{:S(2)}, u32[]{:S(2)}) collective-permute-start(bf16[96,896]{1,0:T(8,128)(2,1)S(1)} %get-tuple-element.122), channel_id=1, source_target_pairs={{8,0},{16,8},{24,16},{28,24},{20,28},{12,20},{4,12},{0,4},{9,1},{1... | collective-permute-start | bytes 516104 | tf_op jit(solution)/shard_map/ppermute | solution.py:679
  186.5 10.7 %collective-permute-start.27 = (f32[56,896]{1,0:T(8,128)S(1)}, f32[56,896]{1,0:T(8,128)S(1)}, u32[]{:S(2)}, u32[]{:S(2)}) collective-permute-start(f32[56,896]{1,0:T(8,128)S(1)} %get-tuple-element.125), channel_id=1, source_target_pairs={{0,2},{2,0},{1,3},{3,1},{4,6},{6,4},{5,7},{7,5},{8,10},{10,8},{9,1... | collective-permute-start | bytes 602120 | tf_op jit(solution)/shard_map/ppermute | solution.py:615
  186.6 7.8 %collective-permute-start.28 = (bf16[256,384]{1,0:T(8,128)(2,1)S(1)}, bf16[256,384]{1,0:T(8,128)(2,1)S(1)}, u32[]{:S(2)}, u32[]{:S(2)}) collective-permute-start(bf16[256,384]{1,0:T(8,128)(2,1)S(1)} %get-tuple-element.130.y_own), channel_id=1, source_target_pairs={{0,1},{1,0},{2,3},{3,2},{4,5},{5,4},{6,7},{7,6},{8,9},{9,8},{10,11... | collective-permute-start | bytes 589832 | tf_op jit(solution)/shard_map/ppermute | solution.py:615
  187.7 9.5 %collective-permute-start.29 = (f32[48,128]{1,0:T(8,128)S(1)}, f32[48,128]{1,0:T(8,128)S(1)}, u32[]{:S(2)}, u32[]{:S(2)}) collective-permute-start(f32[48,128]{1,0:T(8,128)S(1)} %get-tuple-element.136), channel_id=1, source_target_pairs={{0,1},{1,0},{2,3},{3,2},{4,5},{5,4},{6,7},{7,6},{8,9},{9,8},{10,11... | collective-permute-start | bytes 73736 | tf_op jit(solution)/shard_map/ppermute | solution.py:615
  188.7 8.5 %collective-permute-start.30 = (f32[48,128]{1,0:T(8,128)S(1)}, f32[48,128]{1,0:T(8,128)S(1)}, u32[]{:S(2)}, u32[]{:S(2)}) collective-permute-start(f32[48,128]{1,0:T(8,128)S(1)} %get-tuple-element.137), channel_id=1, source_target_pairs={{0,3},{1,2},{2,1},{3,0},{4,7},{5,6},{6,5},{7,4},{8,11},{9,10},{10,... | collective-permute-start | bytes 73736 | tf_op jit(solution)/shard_map/ppermute | solution.py:993
  (13 other events, 9.8 us)

commit v6 on v5

--- a/solution.py
+++ b/solution.py
@@ -375,10 +375,9 @@
                 ].astype(bf16)
 
 
-def weight_grads(x_rows, dpre, act, dy):
-    w_in_grad = jnp.einsum("lrd,lrf->ldf", x_rows, dpre, preferred_element_type=f32)
-    w_out_grad = jnp.einsum("lrf,lrd->lfd", act, dy, preferred_element_type=f32)
-    return w_in_grad, w_out_grad
+def expert_grads(x_rows, dpre, act, dy, w_in_grad, w_out_grad):
+    w_in_grad[0] = mm_tn(x_rows[0], dpre[0])
+    w_out_grad[0] = mm_tn(act[0], dy[0])
 
 
 def from_experts(experts, capacity, *refs):
@@ -644,19 +643,21 @@
     return np.array(rows, np.int32)
 
 
-def ring_gather(shard, count):
+def ring_gather(shard, count, side):
     _, right, left = ring_steps(count)
     shards = [shard]
     going_right, going_left = shard, shard
     for step in range(1, count // 2):
         going_right = lax.ppermute(going_right, "fsdp", right)
         going_left = lax.ppermute(going_left, "fsdp", left)
+        if step == 1:
+            going_right, going_left, side = lax.optimization_barrier((going_right, going_left, side))
         shards += [going_right, going_left]
     shards.append(lax.ppermute(going_right, "fsdp", right))
-    return shards
-
-
-def ring_sums(payload, top, bottom, count, at, meta, side):
+    return shards, side
+
+
+def ring_sums(payload, top, bottom, count, at, meta, sides):
     rows = payload.shape[0] // count
     lanes = payload.shape[1]
     half = rows // 2
@@ -677,11 +678,11 @@
     for step in range(count // 2, 0, -1):
         from_left = lax.ppermute(going_right, "fsdp", right)
         from_right = lax.ppermute(going_left, "fsdp", left)
+        if step in sides:
+            from_left, from_right, _ = lax.optimization_barrier((from_left, from_right, sides[step]))
         which = 4 + count + 2 * (count // 2 - step)
         whole = lambda dims: pl.BlockSpec(dims, lambda i, places: (0, 0))
         last = step == 1
-        if last:
-            side, from_left, from_right = lax.optimization_barrier((side, from_left, from_right))
         step_outs = outs if last else [shape((rows, lanes), bf16)] * 2
         out = pl.pallas_call(
             functools.partial(ring_last, at) if last else ring_add,
@@ -786,7 +787,7 @@
         mib=8,
     )(meta, lengths, rel_table.T)
     if aligned:
-        shards = ring_gather(shard, fsdp_count)
+        shards, (strips, far, segment) = ring_gather(shard, fsdp_count, (strips, far, segment))
         wall, wo_own = kernel_call(
             functools.partial(put_in_rows, len(shards)),
             [full((model_width, wide), bf16), full((model_width // 2, 2 * width), bf16)],
@@ -915,7 +916,22 @@
     returned = lax.all_to_all(
         outgoing, ("fsdp", "ctx", "tp"), split_axis=0, concat_axis=0, tiled=True
     ).reshape(owners * tp_count * per_owner, part_width)
-    w_in_grad, w_out_grad = weight_grads(x_rows, dpre, act, dy_rows)
+    part = 512 if hidden_width % 512 == 0 else hidden_width
+    rows_spec = pl.BlockSpec((1, slot_rows, model_width), lambda i, j: (i, 0, 0))
+    hidden_spec = pl.BlockSpec((1, slot_rows, part), lambda i, j: (i, 0, j))
+    w_in_grad, w_out_grad = kernel_call(
+        expert_grads,
+        [full(w_in.shape, f32), full(w_out.shape, f32)],
+        [rows_spec, hidden_spec, hidden_spec, rows_spec],
+        out_specs=[
+            pl.BlockSpec((1, model_width, part), lambda i, j: (i, 0, j)),
+            pl.BlockSpec((1, part, model_width), lambda i, j: (i, j, 0)),
+        ],
+        grid=(pieces, hidden_width // part),
+        flops=4 * pieces * slot_rows * model_width * hidden_width,
+        moved=24 * 1024 * 1024,
+        mib=24,
+    )(x_rows, dpre, act, dy_rows)
     returned, w_in_grad, w_out_grad = lax.optimization_barrier((returned, w_in_grad, w_out_grad))
 
     back_first = np.repeat(slot_first.reshape(owners, 1, per_owner), tp_count, axis=1).reshape(1, -1)
@@ -948,12 +964,6 @@
     )(meta, dx_own, dx_tp, part_own, part_tp, middle, cotangent, wall, gains, routes_row, keep_row)
     y_own, gate = lax.optimization_barrier((y_own, gate))
     y_tp = swap(y_own, "tp")
-    result = kernel_call(
-        add_expert,
-        [full((rows, model_width), f32)],
-        [smem] + [vmem] * 4,
-        moved=4 * 1024 * 1024,
-    )(meta, middle, gate, y_own, y_tp)[0]
     db = lax.all_gather(db_own, "ctx", axis=0, tiled=True)
 
     half = model_width // fsdp_count // 2
@@ -983,21 +993,26 @@
         meta, tokens, x_other, h1, q, k, v, probs, db, o_all, wo_full, wall, router_grad,
     )
 
+    result = kernel_call(
+        add_expert,
+        [full((rows, model_width), f32)],
+        [smem] + [vmem] * 4,
+        moved=4 * 1024 * 1024,
+    )(meta, middle, gate, y_own, y_tp)[0]
     dh1_sum = (dh1_own.astype(f32) + swap(dh1_other, "ctx").astype(f32)).astype(bf16)
     dh1_far = swap(dh1_sum, "tp")
-    own, send, own_lines, riders_own, riders_other = ring_sums(
-        payload, top, bottom, fsdp_count, wide - LANES, meta, dh1_far
-    )
-    other = swap(send, "ctx")
-    from_tp = swap(riders_own, "tp")
-    from_far = lax.ppermute(riders_other, ("ctx", "tp"), [(i, 3 - i) for i in range(4)])
     input_grad = kernel_call(
         input_backward,
         [full((rows, model_width), f32)],
         [vmem] * 5,
         moved=4 * 1024 * 1024,
     )(tokens, middle_grad, gains, dh1_sum, dh1_far)[0]
-    other, input_grad, result = lax.optimization_barrier((other, input_grad, result))
+    own, send, own_lines, riders_own, riders_other = ring_sums(
+        payload, top, bottom, fsdp_count, wide - LANES, meta, {2: result, 1: input_grad}
+    )
+    other = swap(send, "ctx")
+    from_tp = swap(riders_own, "tp")
+    from_far = lax.ppermute(riders_other, ("ctx", "tp"), [(i, 3 - i) for i in range(4)])
 
     shard = full((shard_rows, 2 * width), f32)
     query_grad, key_grad, value_grad, output_grad, router_sum, gain_one, gain_two, table_grad = kernel_call(

time: 200 us -> 194 us (0.970)
  matrix products: 11.9 us -> 0 us
  Pallas kernels: 42 us -> 49.5 us
  waiting for transfers between devices: 56.5 us -> 54.3 us
    dot_general x2 -> x0, matrix products: 11.9 us -> none  [the longest x1 6.64 us: weight_grads(): jnp.einsum('lrd,lrf->ldf', x_rows, dpre, preferred_element_type=f32)]
    pallas_call x0 -> x1, Pallas kernels: none -> 7.48 us  [body(): kernel_call(expert_grads, [full(w_in.shape, f32), full(w_out.shape, f32)]...]
    ppermute x4, waiting for transfers between devices: 11.9 us -> 6.13 us  [ring_sums(): from_left = lax.ppermute(going_right, 'fsdp', right)]
    ppermute x3, starting transfers between devices: 0.49 us -> 6.08 us  [ring_gather(): going_left = lax.ppermute(going_left, 'fsdp', left)]
    ppermute x3, starting transfers between devices: 6.31 us -> 1.33 us  [ring_gather(): going_right = lax.ppermute(going_right, 'fsdp', right)]
    ppermute x3, waiting for transfers between devices: 10.9 us -> 6.75 us  [ring_gather(): going_right = lax.ppermute(going_right, 'fsdp', right)]
    ppermute x14, waiting for transfers between devices: 14.8 us -> 18.7 us  [swap(): return lax.ppermute(value, axis, [(0, 1), (1, 0)])]
    ppermute x1, waiting for transfers between devices: 0.01 us -> 2.99 us  [ring_gather(): shards.append(lax.ppermute(going_right, 'fsdp', right))]
  transfers between devices with their start and end apart: 32 -> 32, of which waited for: 18 -> 20; matrix products, arithmetic and copies ran while one was open for 6% -> 0% of each run, Pallas kernels for 6% -> 10%
where the time goes in v6:
time: 194 us; the launch traced here: 193 us
  waiting for transfers between devices  54.3 us (28%)
  Pallas kernels  49.5 us (26%)
  starting transfers between devices  31.1 us (16%)
  blocking collectives  31 us (16%)
  local copies, waits for them, and re-layouts  25 us (13%)
    all_to_all x1, blocking collectives, body(): lax.all_to_all(sends.reshape(owners, per_owner, model_width), ('fsdp', 'c...  28.6 us
    unnamed x94, local copies, waits for them, and re-layouts  23.8 us
    ppermute x14, waiting for transfers between devices, swap(): return lax.ppermute(value, axis, [(0, 1), (1, 0)])  18.7 us
    all_to_all x1, waiting for transfers between devices, body(): lax.all_to_all(outgoing, ('fsdp', 'ctx', 'tp'), split_axis=0, concat_axis...  12.7 us
    pallas_call x1, Pallas kernels, body(): kernel_call(functools.partial(expert_kernel, owners, capacity, chunks, gr...  9.23 us
    pallas_call x1, Pallas kernels, body(): kernel_call(functools.partial(attention_backward, heads, buckets, model_w...  9.04 us
    ppermute x14, starting transfers between devices, swap(): return lax.ppermute(value, axis, [(0, 1), (1, 0)])  8.25 us
    pallas_call x1, Pallas kernels, body(): kernel_call(expert_grads, [full(w_in.shape, f32), full(w_out.shape, f32)]...  7.48 us
  transfers between devices with their start and end apart: 32, of which 20 were waited for; matrix products, arithmetic and copies ran while one was open for 0% of the time, Pallas kernels for 10%

profile of v6, /device:TPU:0, one launch (start us, length us, event | category | flops | bytes accessed | tf_op | source)
XLA Modules:
  0.0 192.9 jit_solution(71433054641597489)
XLA Ops:
  0.7 1.2 dynamic-slice_bitcast_fusion.refs_0_.meta.places
  1.9 1.7 shard_map.301
  4.0 1.1 collective-permute-done.1
  6.0 2.9 %collective-permute-start.3 = (bf16[96,896]{1,0:T(8,128)(2,1)S(1)}, bf16[96,896]{1,0:T(8,128)(2,1)S(1)}, u32[]{:S(2)}, u32[]{:S(2)}) collective-permute-start(bf16[96,896]{1,0:T(8,128)(2,1)S(1)} %pad_maximum_fusion.refs_1_), channel_id=1, source_target_pairs={{8,0},{16,8},{24,16},{28,24},{20,28},{12,20},{4,12},{0,4},{9,1},{1... | collective-permute-start | bytes 516104 | tf_op jit(solution)/shard_map/ppermute | solution.py:652
  11.0 2.3 %shard_map.302 = (f32[3,128,384]{2,1,0:T(8,128)S(1)}, f32[8,128]{1,0:T(8,128)S(1)}, s32[8,512]{1,0:T(8,128)S(1)}) custom-call(s32[20]{0:T(128)S(1)} %copy-done.9, s32[1,4]{1,0:T(1,128)S(1)} %copy-done.16, f32[6,32]{1,0:T(8,128)S(1)} %bitcast.18), custom_call_target="tpu_custom_call" | custom-call | bytes 1048576 | tf_op jit(solution)/shard_map/pallas_call | solution.py:778
  13.7 1.4 collective-permute-done.2.refs_2_
  15.5 1.6 collective-permute-start.5
  17.1 3.4 %collective-permute-done.4.refs_4_ = bf16[96,896]{1,0:T(8,128)(2,1)S(1)} collective-permute-done((bf16[96,896]{1,0:T(8,128)(2,1)S(1)}, bf16[96,896]{1,0:T(8,128)(2,1)S(1)}, u32[]{:S(2)}, u32[]{:S(2)}) %collective-permute-start.4) | collective-permute-done | bytes 172064 | tf_op jit(solution)/shard_map/ppermute | solution.py:651
  21.2 1.1 collective-permute-done.5.refs_5_
  22.3 1.6 collective-permute-start.7
  23.9 2.0 %collective-permute-done.6.refs_6_ = bf16[96,896]{1,0:T(8,128)(2,1)S(1)} collective-permute-done((bf16[96,896]{1,0:T(8,128)(2,1)S(1)}, bf16[96,896]{1,0:T(8,128)(2,1)S(1)}, u32[]{:S(2)}, u32[]{:S(2)}) %collective-permute-start.6) | collective-permute-done | bytes 172064 | tf_op jit(solution)/shard_map/ppermute | solution.py:651
  26.6 1.7 collective-permute-done.7.refs_7_
  28.3 3.0 %collective-permute-done.8.refs_8_ = bf16[96,896]{1,0:T(8,128)(2,1)S(1)} collective-permute-done((bf16[96,896]{1,0:T(8,128)(2,1)S(1)}, bf16[96,896]{1,0:T(8,128)(2,1)S(1)}, u32[]{:S(2)}, u32[]{:S(2)}) %collective-permute-start.8) | collective-permute-done | bytes 172064 | tf_op jit(solution)/shard_map/ppermute | solution.py:656
  32.8 1.6 collective-permute-start.12
  34.4 1.1 copy-done.1
  36.2 5.1 %shard_map.304 = (bf16[512,768]{1,0:T(8,128)(2,1)S(1)}, bf16[512,256]{1,0:T(8,128)(2,1)S(1)}, bf16[512,256]{1,0:T(8,128)(2,1)S(1)}, bf16[512,256]{1,0:T(8,128)(2...) custom-call(s32[20]{0:T(128)S(1)} %copy-done.11, ...), custom_call_target="tpu_custom_call" | custom-call | flops 4026531840 | bytes 8388608 | tf_op jit(solution)/shard_map/pallas_call | solution.py:806
  41.3 1.6 copy-done.35
  44.6 1.2 collective-permute-start.11
  46.2 3.5 %collective-permute-done.9.refs_4_ = bf16[128,384]{1,0:T(8,128)(2,1)S(1)} collective-permute-done((bf16[128,384]{1,0:T(8,128)(2,1)S(1)}, bf16[128,384]{1,0:T(8,128)(2,1)S(1)}, u32[]{:S(2)}, u32[]{:S(2)}) %collective-permute-start.9) | collective-permute-done | bytes 98336 | tf_op jit(solution)/shard_map/ppermute | solution.py:614
  49.7 0.9 collective-permute-done.11.refs_6_
  50.7 2.9 %shard_map.305 = (f32[256,768]{1,0:T(8,128)S(1)}, bf16[640,768]{1,0:T(8,128)(2,1)S(1)}, bf16[768,384]{1,0:T(8,128)(2,1)S(1)}) custom-call(s32[20]{0:T(128)S(1)} %copy-done.11, bf16[256,768]{1,0:T(8,128)(2,1)S(1)} %copy-done.2, bf16[256,768]{1,0:T(8,128)(2,1)S(1)} %copy-done, bf16[128,384]{1,0:T(8,128)(2,1)S(1)} %get-tuple-element.98.refs_3_, ...), custom_call_target="tpu_custom_call" | custom-call | flops 805306368 | bytes 6291456 | tf_op jit(solution)/shard_map/pallas_call | solution.py:845
  53.6 28.6 %all_to_all.10 = bf16[16,40,768]{2,1,0:T(8,128)(2,1)S(1)} all-to-all(bf16[16,40,768]{2,1,0:T(8,128)(2,1)S(1)} %bitcast.16), channel_id=1, replica_groups=mesh['fsdp'=8,'ctx'=2,'tp'=2] {'fsdp','ctx'}, dimensions={0} | all-to-all | bytes 1966080 | tf_op jit(solution)/shard_map/all_to_all | solution.py:861
  82.3 9.2 %shard_map.306 = (bf16[32,40,384]{2,1,0:T(8,128)(2,1)S(1)}, bf16[2,160,768]{2,1,0:T(8,128)(2,1)S(1)}, bf16[2,160,768]{2,1,0:T(8,128)(2,1)S(1)}, bf16[2,160,1536]...) custom-call(bf16[640,768]{1,0:T(8,128)(2,1)S(1)} %bitcast.17, s32[320,1]{1,0:T(8,128)S(1)} %copy-done.23, ...), custom_call_target="tpu_custom_call" | custom-call | flops 3019898880 | bytes 12582912 | tf_op jit(solution)/shard_map/pallas_call | solution.py:882
  91.6 1.0 copy-done.3
  92.5 0.9 copy-done.27
  93.5 0.9 copy-done.29
  96.0 3.9 %all-to-all-start.1 = ((bf16[32,40,384]{2,1,0:T(8,128)(2,1)}), bf16[32,40,384]{2,1,0:T(8,128)(2,1)S(1)}, u32[]{:S(2)}, u32[]{:S(2)}) async-start(bf16[32,40,384]{2,1,0:T(8,128)(2,1)} %copy-done.3), calls=%async_computation.1 | async-start | bytes 1966080 | tf_op jit(solution)/shard_map/all_to_all | solution.py:916
  99.9 1.2 copy-done.28
  101.1 1.2 copy-done.30
  102.3 1.0 copy-done.32
  103.3 1.0 copy-done.34
  104.4 7.5 %shard_map.307 = (f32[2,768,1536]{2,1,0:T(8,128)}, f32[2,1536,768]{2,1,0:T(8,128)}) custom-call(bf16[2,160,768]{2,1,0:T(8,128)(2,1)S(1)} %copy-done.32, bf16[2,160,1536]{2,1,0:T(8,128)(2,1)S(1)} %copy-done.30, bf16[2,160,1536]{2,1,0:T(8,128)(2,1)S(1)} %copy-done.28, bf16[2,160,768]{2,1,0:T(8,128)(2,1)S(1)} %copy-done.34), custom_call_target="tpu_custom_call" | custom-call | flops 1509949440 | bytes 25165824 | tf_op jit(solution)/shard_map/pallas_call | solution.py:922
  111.8 12.7 %all-to-all-done.1 = bf16[32,40,384]{2,1,0:T(8,128)(2,1)S(1)} async-done(((bf16[32,40,384]{2,1,0:T(8,128)(2,1)}), bf16[32,40,384]{2,1,0:T(8,128)(2,1)S(1)}, u32[]{:S(2)}, u32[]{:S(2)}) %all-to-all-start.1) | async-done | bytes 983072 | tf_op jit(solution)/shard_map/all_to_all | solution.py:916
  126.0 1.9 shard_map.308
  127.9 1.5 collective-permute-start.15
  130.0 5.1 %collective-permute-done.16.refs_4_ = f32[8,256]{1,0:T(8,128)S(1)} collective-permute-done((f32[8,256]{1,0:T(8,128)S(1)}, f32[8,256]{1,0:T(8,128)S(1)}, u32[]{:S(2)}, u32[]{:S(2)}) %collective-permute-start.16) | collective-permute-done | bytes 8224 | tf_op jit(solution)/shard_map/ppermute | solution.py:614
  135.8 2.5 %shard_map.309 = (f32[256,768]{1,0:T(8,128)S(1)}, bf16[256,768]{1,0:T(8,128)(2,1)S(1)}, bf16[768,128]{1,0:T(8,128)(2,1)S(1)}, f32[256,128]{1,0:T(8,128)S(1)}) custom-call(s32[20]{0:T(128)S(1)} %copy-done.12, bf16[256,384]{1,0:T(8,128)(2,1)S(1)} %get-tuple-element.115.refs_1_, bf16[256,384]{1,0:T(8,128)(2,1)S(1)} %collective-permute-done.15.refs_2_, ...), custom_call_target="tpu_custom_call" | custom-call | flops 150994944 | bytes 6291456 | tf_op jit(solution)/shard_map/pallas_call | solution.py:953
  138.3 2.4 %all_gather.3.refs_8_ = bf16[512,768]{1,0:T(8,128)(2,1)S(1)} all-gather(bf16[256,768]{1,0:T(8,128)(2,1)S(1)} %get-tuple-element.126), channel_id=1, replica_groups=mesh['fsdp'=8,'ctx'=2,'tp'=2] {'ctx'}, dimensions={0}, use_global_device_ids=true | all-gather | bytes 1179648 | tf_op jit(solution)/shard_map/all_gather | solution.py:967
  140.7 1.9 copy-done.36
  142.6 0.9 copy-done.40
  143.5 0.9 copy-done.42
  144.5 0.9 copy-done.44
  145.4 0.9 copy-done.46
  146.4 9.0 %shard_map.311 = (bf16[768,896]{1,0:T(8,128)(2,1)S(1)}, bf16[48,896]{1,0:T(8,128)(2,1)S(1)}, bf16[48,896]{1,0:T(8,128)(2,1)S(1)}, bf16[256,768]{1,0:T(8,128)(2,1)S(1)}, bf16[256,768]{1,0:T(8,128)(2,1)S(1)}) custom-call(s32[20]{0:T(128)S(1)} %copy-done.12, bf16[256,768]{1,0:T(8,128)(2,1)S(1)} %copy-done.2, bf16[256,768]{1,0:T(8,128)(2,1)S(1)} %copy-done.22, ...), custom_call_target="tpu_custom_call" | custom-call | flops 6039797760 | bytes 8388608 | tf_op jit(solution)/shard_map/pallas_call | solution.py:970
  155.6 1.1 collective-permute-start.20
  156.7 0.9 collective-permute-start.21
  157.7 2.8 %collective-permute-done.20.from_left = bf16[48,896]{1,0:T(8,128)(2,1)S(1)} collective-permute-done((bf16[48,896]{1,0:T(8,128)(2,1)S(1)}, bf16[48,896]{1,0:T(8,128)(2,1)S(1)}, u32[]{:S(2)}, u32[]{:S(2)}) %collective-permute-start.20) | collective-permute-done | bytes 86048 | tf_op jit(solution)/shard_map/ppermute | solution.py:679
  161.8 1.2 collective-permute-start.22
  163.0 0.9 collective-permute-start.23
  164.0 1.0 collective-permute-start.19
  165.1 1.1 collective-permute-start.17
  166.1 1.3 collective-permute-done.22.from_left
  167.4 1.0 collective-permute-done.23.from_right
  169.7 1.5 collective-permute-start.25
  171.1 6.9 %collective-permute-done.17.y_tp = bf16[256,384]{1,0:T(8,128)(2,1)S(1)} collective-permute-done((bf16[256,384]{1,0:T(8,128)(2,1)S(1)}, bf16[256,384]{1,0:T(8,128)(2,1)S(1)}, u32[]{:S(2)}, u32[]{:S(2)}) %collective-permute-start.17) | collective-permute-done | bytes 196640 | tf_op jit(solution)/shard_map/ppermute | solution.py:614
  178.0 1.6 shard_map.310
  180.2 1.2 collective-permute-start.26
  181.4 0.9 collective-permute-start.27
  182.3 1.3 shard_map.312
  183.6 2.1 %collective-permute-done.26.from_left = bf16[96,896]{1,0:T(8,128)(2,1)S(1)} collective-permute-done((bf16[96,896]{1,0:T(8,128)(2,1)S(1)}, bf16[96,896]{1,0:T(8,128)(2,1)S(1)}, u32[]{:S(2)}, u32[]{:S(2)}) %collective-permute-start.26) | collective-permute-done | bytes 172064 | tf_op jit(solution)/shard_map/ppermute | solution.py:679
  185.7 1.1 collective-permute-done.27.from_right
  188.0 1.3 collective-permute-start.30
  189.3 2.2 %collective-permute-done.29.refs_4_ = f32[48,128]{1,0:T(8,128)S(1)} collective-permute-done((f32[48,128]{1,0:T(8,128)S(1)}, f32[48,128]{1,0:T(8,128)S(1)}, u32[]{:S(2)}, u32[]{:S(2)}) %collective-permute-start.29) | collective-permute-done | bytes 24608 | tf_op jit(solution)/shard_map/ppermute | solution.py:614
  191.5 1.4 shard_map.317
  (116 shorter events, 19.2 us)
Async XLA Ops:
  3.6 1.6 collective-permute-start.1
  6.0 7.7 %collective-permute-start.3 = (bf16[96,896]{1,0:T(8,128)(2,1)S(1)}, bf16[96,896]{1,0:T(8,128)(2,1)S(1)}, u32[]{:S(2)}, u32[]{:S(2)}) collective-permute-start(bf16[96,896]{1,0:T(8,128)(2,1)S(1)} %pad_maximum_fusion.refs_1_), channel_id=1, source_target_pairs={{8,0},{16,8},{24,16},{28,24},{20,28},{12,20},{4,12},{0,4},{9,1},{1... | collective-permute-start | bytes 516104 | tf_op jit(solution)/shard_map/ppermute | solution.py:652
  8.9 6.2 %collective-permute-start.2 = (bf16[96,896]{1,0:T(8,128)(2,1)S(1)}, bf16[96,896]{1,0:T(8,128)(2,1)S(1)}, u32[]{:S(2)}, u32[]{:S(2)}) collective-permute-start(bf16[96,896]{1,0:T(8,128)(2,1)S(1)} %pad_maximum_fusion.refs_1_), channel_id=1, source_target_pairs={{0,8},{8,16},{16,24},{24,28},{28,20},{20,12},{12,4},{4,0},{1,9},{9... | collective-permute-start | bytes 516104 | tf_op jit(solution)/shard_map/ppermute | solution.py:651
  15.1 5.4 %collective-permute-start.4 = (bf16[96,896]{1,0:T(8,128)(2,1)S(1)}, bf16[96,896]{1,0:T(8,128)(2,1)S(1)}, u32[]{:S(2)}, u32[]{:S(2)}) collective-permute-start(bf16[96,896]{1,0:T(8,128)(2,1)S(1)} %collective-permute-done.2.refs_2_), channel_id=1, source_target_pairs={{0,8},{8,16},{16,24},{24,28},{28,20},{20,12},{12,4},{4,0},{1,9},{9... | collective-permute-start | bytes 516104 | tf_op jit(solution)/shard_map/ppermute | solution.py:651
  15.5 18.9 %collective-permute-start = (bf16[256,768]{1,0:T(8,128)(2,1)}, bf16[256,768]{1,0:T(8,128)(2,1)S(1)}, u32[]{:S(2)}, u32[]{:S(2)}) collective-permute-start(bf16[256,768]{1,0:T(8,128)(2,1)} %x_own.1), channel_id=1, source_target_pairs={{0,2},{2,0},{1,3},{3,1},{4,6},{6,4},{5,7},{7,5},{8,10},{10,8},{9,1... | collective-permute-start | bytes 1179656 | tf_op jit(solution)/shard_map/ppermute | solution.py:614
  15.5 6.8 %collective-permute-start.5 = (bf16[96,896]{1,0:T(8,128)(2,1)S(1)}, bf16[96,896]{1,0:T(8,128)(2,1)S(1)}, u32[]{:S(2)}, u32[]{:S(2)}) collective-permute-start(bf16[96,896]{1,0:T(8,128)(2,1)S(1)} %collective-permute-done.3.refs_3_), channel_id=1, source_target_pairs={{8,0},{16,8},{24,16},{28,24},{20,28},{12,20},{4,12},{0,4},{9,1},{1... | collective-permute-start | bytes 516104 | tf_op jit(solution)/shard_map/ppermute | solution.py:652
  20.5 5.4 %collective-permute-start.6 = (bf16[96,896]{1,0:T(8,128)(2,1)S(1)}, bf16[96,896]{1,0:T(8,128)(2,1)S(1)}, u32[]{:S(2)}, u32[]{:S(2)}) collective-permute-start(bf16[96,896]{1,0:T(8,128)(2,1)S(1)} %collective-permute-done.4.refs_4_), channel_id=1, source_target_pairs={{0,8},{8,16},{16,24},{24,28},{28,20},{20,12},{12,4},{4,0},{1,9},{9... | collective-permute-start | bytes 516104 | tf_op jit(solution)/shard_map/ppermute | solution.py:651
  22.3 6.0 %collective-permute-start.7 = (bf16[96,896]{1,0:T(8,128)(2,1)S(1)}, bf16[96,896]{1,0:T(8,128)(2,1)S(1)}, u32[]{:S(2)}, u32[]{:S(2)}) collective-permute-start(bf16[96,896]{1,0:T(8,128)(2,1)S(1)} %collective-permute-done.5.refs_5_), channel_id=1, source_target_pairs={{8,0},{16,8},{24,16},{28,24},{20,28},{12,20},{4,12},{0,4},{9,1},{1... | collective-permute-start | bytes 516104 | tf_op jit(solution)/shard_map/ppermute | solution.py:652
  25.9 5.4 %collective-permute-start.8 = (bf16[96,896]{1,0:T(8,128)(2,1)S(1)}, bf16[96,896]{1,0:T(8,128)(2,1)S(1)}, u32[]{:S(2)}, u32[]{:S(2)}) collective-permute-start(bf16[96,896]{1,0:T(8,128)(2,1)S(1)} %collective-permute-done.6.refs_6_), channel_id=1, source_target_pairs={{0,8},{8,16},{16,24},{24,28},{28,20},{20,12},{12,4},{4,0},{1,9},{9... | collective-permute-start | bytes 516104 | tf_op jit(solution)/shard_map/ppermute | solution.py:656
  32.7 18.0 %collective-permute-start.13 = (bf16[384,384]{1,0:T(8,128)(2,1)S(1)}, bf16[384,384]{1,0:T(8,128)(2,1)S(1)}, u32[]{:S(2)}, u32[]{:S(2)}) collective-permute-start(bf16[384,384]{1,0:T(8,128)(2,1)S(1)} %get-tuple-element.100.refs_7_), channel_id=1, source_target_pairs={{0,2},{2,0},{1,3},{3,1},{4,6},{6,4},{5,7},{7,5},{8,10},{10,8},{9,1... | collective-permute-start | bytes 884744 | tf_op jit(solution)/shard_map/ppermute | solution.py:614
  32.8 11.1 %collective-permute-start.12 = (bf16[384,384]{1,0:T(8,128)(2,1)S(1)}, bf16[384,384]{1,0:T(8,128)(2,1)S(1)}, u32[]{:S(2)}, u32[]{:S(2)}) collective-permute-start(bf16[384,384]{1,0:T(8,128)(2,1)S(1)} %get-tuple-element.100.refs_7_), channel_id=1, source_target_pairs={{0,1},{1,0},{2,3},{3,2},{4,5},{5,4},{6,7},{7,6},{8,9},{9,8},{10,11... | collective-permute-start | bytes 884744 | tf_op jit(solution)/shard_map/ppermute | solution.py:614
  34.4 6.9 %copy-start.21 = (bf16[256,768]{1,0:T(8,128)(2,1)}, bf16[256,768]{1,0:T(8,128)(2,1)S(1)}, u32[]{:S(2)}) copy-start(bf16[256,768]{1,0:T(8,128)(2,1)S(1)} %collective-permute-done.refs_2_) | copy-start | bytes 1179652
  34.4 1.1 copy-start.1
  36.1 14.5 %copy-start = (bf16[256,768]{1,0:T(8,128)(2,1)S(1)}, bf16[256,768]{1,0:T(8,128)(2,1)}, u32[]{:S(2)}) copy-start(bf16[256,768]{1,0:T(8,128)(2,1)} %refs_6_.2) | copy-start | bytes 1179652
  36.2 14.5 %copy-start.2 = (bf16[256,768]{1,0:T(8,128)(2,1)S(1)}, bf16[256,768]{1,0:T(8,128)(2,1)}, u32[]{:S(2)}) copy-start(bf16[256,768]{1,0:T(8,128)(2,1)} %x_own.1) | copy-start | bytes 1179652
  36.2 14.5 %copy-start.4 = (s32[640,1]{1,0:T(8,128)S(1)}, s32[640,1]{1,0:T(8,128)}, u32[]{:S(2)}) copy-start(s32[640,1]{1,0:T(8,128)} %constant.36.clone.refs_16_) | copy-start | bytes 7684
  36.2 14.5 %copy-start.5 = (s32[640,1]{1,0:T(8,128)S(1)}, s32[640,1]{1,0:T(8,128)}, u32[]{:S(2)}) copy-start(s32[640,1]{1,0:T(8,128)} %constant.35.clone.refs_15_) | copy-start | bytes 7684
  36.2 14.5 %copy-start.14 = (s32[256,1]{0,1:T(1,128)S(1)}, s32[256,1]{0,1:T(1,128)}, u32[]{:S(2)}) copy-start(s32[256,1]{0,1:T(1,128)} %param.35) | copy-start | bytes 3076
  36.2 14.5 %copy-start.15 = (s32[256]{0:T(256)S(1)}, s32[256]{0:T(256)}, u32[]{:S(2)}) copy-start(s32[256]{0:T(256)} %param.36) | copy-start | bytes 3076
  36.2 46.1 %copy-start.18 = (bf16[2,1536,768]{2,1,0:T(8,128)(2,1)S(1)}, bf16[2,1536,768]{2,1,0:T(8,128)(2,1)}, u32[]{:S(2)}) copy-start(bf16[2,1536,768]{2,1,0:T(8,128)(2,1)} %refs_4_.3) | copy-start | bytes 14155780
  41.3 1.6 copy-start.35
  43.8 38.5 %copy-start.6 = (f32[8,768]{1,0:T(8,128)}, f32[8,768]{1,0:T(8,128)S(1)}, u32[]{:S(2)}) copy-start(f32[8,768]{1,0:T(8,128)S(1)} %get-tuple-element.103.refs_12_.refs_8_.gains) | copy-start | bytes 73732
  43.8 38.5 %copy-start.39 = (bf16[512,256]{1,0:T(8,128)(2,1)}, bf16[512,256]{1,0:T(8,128)(2,1)S(1)}, u32[]{:S(2)}) copy-start(bf16[512,256]{1,0:T(8,128)(2,1)S(1)} %get-tuple-element.122.refs_4_) | copy-start | bytes 786436
  43.8 38.5 %copy-start.41 = (bf16[512,256]{1,0:T(8,128)(2,1)}, bf16[512,256]{1,0:T(8,128)(2,1)S(1)}, u32[]{:S(2)}) copy-start(bf16[512,256]{1,0:T(8,128)(2,1)S(1)} %get-tuple-element.123.refs_5_) | copy-start | bytes 786436
  43.8 38.5 %copy-start.43 = (bf16[512,256]{1,0:T(8,128)(2,1)}, bf16[512,256]{1,0:T(8,128)(2,1)S(1)}, u32[]{:S(2)}) copy-start(bf16[512,256]{1,0:T(8,128)(2,1)S(1)} %get-tuple-element.124.refs_6_) | copy-start | bytes 786436
  43.8 38.5 %copy-start.45 = (bf16[512,256]{1,0:T(8,128)(2,1)}, bf16[512,256]{1,0:T(8,128)(2,1)S(1)}, u32[]{:S(2)}) copy-start(bf16[512,256]{1,0:T(8,128)(2,1)S(1)} %get-tuple-element.127.refs_9_) | copy-start | bytes 786436
  43.8 38.5 %copy-start.17 = (bf16[2,768,1536]{2,1,0:T(8,128)(2,1)S(1)}, bf16[2,768,1536]{2,1,0:T(8,128)(2,1)}, u32[]{:S(2)}) copy-start(bf16[2,768,1536]{2,1,0:T(8,128)(2,1)} %refs_3_.3) | copy-start | bytes 14155780
  43.8 38.5 %copy-start.23 = (s32[320,1]{1,0:T(8,128)S(1)}, s32[320,1]{1,0:T(8,128)}, u32[]{:S(2)}) copy-start(s32[320,1]{1,0:T(8,128)} %constant.37.clone.refs_1_) | copy-start | bytes 3844
  43.8 38.5 %copy-start.26 = (s32[1,320]{1,0:T(1,128)S(1)}, s32[1,320]{1,0:T(1,128)}, u32[]{:S(2)}) copy-start(s32[1,320]{1,0:T(1,128)} %constant.38.clone.refs_2_) | copy-start | bytes 3844
  43.8 6.8 %collective-permute-start.14 = (bf16[384,384]{1,0:T(8,128)(2,1)S(1)}, bf16[384,384]{1,0:T(8,128)(2,1)S(1)}, u32[]{:S(2)}, u32[]{:S(2)}) collective-permute-start(bf16[384,384]{1,0:T(8,128)(2,1)S(1)} %collective-permute-done.12.refs_8_), channel_id=1, source_target_pairs={{0,2},{2,0},{1,3},{3,1},{4,6},{6,4},{5,7},{7,5},{8,10},{10,8},{9,1... | collective-permute-start | bytes 884744 | tf_op jit(solution)/shard_map/ppermute | solution.py:614
  44.1 5.6 %collective-permute-start.9 = (bf16[128,384]{1,0:T(8,128)(2,1)S(1)}, bf16[128,384]{1,0:T(8,128)(2,1)S(1)}, u32[]{:S(2)}, u32[]{:S(2)}) collective-permute-start(bf16[128,384]{1,0:T(8,128)(2,1)S(1)} %get-tuple-element.98.refs_3_), channel_id=1, source_target_pairs={{0,1},{1,0},{2,3},{3,2},{4,5},{5,4},{6,7},{7,6},{8,9},{9,8},{10,11... | collective-permute-start | bytes 294920 | tf_op jit(solution)/shard_map/ppermute | solution.py:614
  44.6 6.1 %collective-permute-start.11 = (bf16[128,384]{1,0:T(8,128)(2,1)S(1)}, bf16[128,384]{1,0:T(8,128)(2,1)S(1)}, u32[]{:S(2)}, u32[]{:S(2)}) collective-permute-start(bf16[128,384]{1,0:T(8,128)(2,1)S(1)} %get-tuple-element.99), channel_id=1, source_target_pairs={{0,3},{1,2},{2,1},{3,0},{4,7},{5,6},{6,5},{7,4},{8,11},{9,10},{10,... | collective-permute-start | bytes 294920 | tf_op jit(solution)/shard_map/ppermute | solution.py:832
  45.8 4.9 %collective-permute-start.10 = (bf16[128,384]{1,0:T(8,128)(2,1)S(1)}, bf16[128,384]{1,0:T(8,128)(2,1)S(1)}, u32[]{:S(2)}, u32[]{:S(2)}) collective-permute-start(bf16[128,384]{1,0:T(8,128)(2,1)S(1)} %get-tuple-element.99), channel_id=1, source_target_pairs={{0,2},{2,0},{1,3},{3,1},{4,6},{6,4},{5,7},{7,5},{8,10},{10,8},{9,1... | collective-permute-start | bytes 294920 | tf_op jit(solution)/shard_map/ppermute | solution.py:614
  53.6 28.7 %copy-start.19 = (bf16[768,384]{1,0:T(8,128)(2,1)}, bf16[768,384]{1,0:T(8,128)(2,1)S(1)}, u32[]{:S(2)}) copy-start(bf16[768,384]{1,0:T(8,128)(2,1)S(1)} %get-tuple-element.128.refs_10_) | copy-start | bytes 1769476
  91.5 1.0 copy-start.3
  96.0 28.6 %copy-start.12 = (s32[20]{0:T(128)S(1)}, s32[20]{0:T(128)}, u32[]{:S(2)}) copy-start(s32[20]{0:T(128)} %dynamic-slice_bitcast_fusion.refs_0_.meta.places) | copy-start | bytes 244
  96.0 28.5 %all-to-all-start.1 = ((bf16[32,40,384]{2,1,0:T(8,128)(2,1)}), bf16[32,40,384]{2,1,0:T(8,128)(2,1)S(1)}, u32[]{:S(2)}, u32[]{:S(2)}) async-start(bf16[32,40,384]{2,1,0:T(8,128)(2,1)} %copy-done.3), calls=%async_computation.1 | async-start | bytes 1966080 | tf_op jit(solution)/shard_map/all_to_all | solution.py:916
  99.9 1.2 copy-start.28
  101.1 1.2 copy-start.30
  102.3 1.0 copy-start.32
  103.3 1.0 copy-start.34
  124.6 16.1 %copy-start.20 = (bf16[768,384]{1,0:T(8,128)(2,1)S(1)}, bf16[768,384]{1,0:T(8,128)(2,1)}, u32[]{:S(2)}) copy-start(bf16[768,384]{1,0:T(8,128)(2,1)} %copy-done.19) | copy-start | bytes 1769476
  124.6 16.1 %copy-start.22 = (bf16[256,768]{1,0:T(8,128)(2,1)S(1)}, bf16[256,768]{1,0:T(8,128)(2,1)}, u32[]{:S(2)}) copy-start(bf16[256,768]{1,0:T(8,128)(2,1)} %copy-done.21) | copy-start | bytes 1179652
  126.0 14.7 %copy-start.38 = (bf16[512,768]{1,0:T(8,128)(2,1)S(1)}, bf16[512,768]{1,0:T(8,128)(2,1)}, u32[]{:S(2)}) copy-start(bf16[512,768]{1,0:T(8,128)(2,1)} %copy-done.37) | copy-start | bytes 2359300
  127.9 7.2 %collective-permute-start.15 = (bf16[256,384]{1,0:T(8,128)(2,1)S(1)}, bf16[256,384]{1,0:T(8,128)(2,1)S(1)}, u32[]{:S(2)}, u32[]{:S(2)}) collective-permute-start(bf16[256,384]{1,0:T(8,128)(2,1)S(1)} %get-tuple-element.115.refs_1_), channel_id=1, source_target_pairs={{0,1},{1,0},{2,3},{3,2},{4,5},{5,4},{6,7},{7,6},{8,9},{9,8},{10,11... | collective-permute-start | bytes 589832 | tf_op jit(solution)/shard_map/ppermute | solution.py:614
  129.4 5.7 %collective-permute-start.16 = (f32[8,256]{1,0:T(8,128)S(1)}, f32[8,256]{1,0:T(8,128)S(1)}, u32[]{:S(2)}, u32[]{:S(2)}) collective-permute-start(f32[8,256]{1,0:T(8,128)S(1)} %get-tuple-element.116.refs_3_), channel_id=1, source_target_pairs={{0,1},{1,0},{2,3},{3,2},{4,5},{5,4},{6,7},{7,6},{8,9},{9,8},{10,11... | collective-permute-start | bytes 24584 | tf_op jit(solution)/shard_map/ppermute | solution.py:614
  140.7 1.9 copy-start.36
  142.6 0.9 copy-start.40
  143.5 0.9 copy-start.42
  155.4 8.5 %collective-permute-start.18 = (bf16[256,768]{1,0:T(8,128)(2,1)S(1)}, bf16[256,768]{1,0:T(8,128)(2,1)S(1)}, u32[]{:S(2)}, u32[]{:S(2)}) collective-permute-start(bf16[256,768]{1,0:T(8,128)(2,1)S(1)} %get-tuple-element.131), channel_id=1, source_target_pairs={{0,2},{2,0},{1,3},{3,1},{4,6},{6,4},{5,7},{7,5},{8,10},{10,8},{9,1... | collective-permute-start | bytes 1179656 | tf_op jit(solution)/shard_map/ppermute | solution.py:614
  155.6 4.8 %collective-permute-start.20 = (bf16[48,896]{1,0:T(8,128)(2,1)S(1)}, bf16[48,896]{1,0:T(8,128)(2,1)S(1)}, u32[]{:S(2)}, u32[]{:S(2)}) collective-permute-start(bf16[48,896]{1,0:T(8,128)(2,1)S(1)} %get-tuple-element.133), channel_id=1, source_target_pairs={{0,8},{8,16},{16,24},{24,28},{28,20},{20,12},{12,4},{4,0},{1,9},{9... | collective-permute-start | bytes 258056 | tf_op jit(solution)/shard_map/ppermute | solution.py:679
  156.7 4.5 %collective-permute-start.21 = (bf16[48,896]{1,0:T(8,128)(2,1)S(1)}, bf16[48,896]{1,0:T(8,128)(2,1)S(1)}, u32[]{:S(2)}, u32[]{:S(2)}) collective-permute-start(bf16[48,896]{1,0:T(8,128)(2,1)S(1)} %get-tuple-element.134), channel_id=1, source_target_pairs={{8,0},{16,8},{24,16},{28,24},{20,28},{12,20},{4,12},{0,4},{9,1},{1... | collective-permute-start | bytes 258056 | tf_op jit(solution)/shard_map/ppermute | solution.py:680
  161.8 5.6 %collective-permute-start.22 = (bf16[96,896]{1,0:T(8,128)(2,1)S(1)}, bf16[96,896]{1,0:T(8,128)(2,1)S(1)}, u32[]{:S(2)}, u32[]{:S(2)}) collective-permute-start(bf16[96,896]{1,0:T(8,128)(2,1)S(1)} %get-tuple-element.135), channel_id=1, source_target_pairs={{0,8},{8,16},{16,24},{24,28},{28,20},{20,12},{12,4},{4,0},{1,9},{9... | collective-permute-start | bytes 516104 | tf_op jit(solution)/shard_map/ppermute | solution.py:679
  163.0 5.4 %collective-permute-start.23 = (bf16[96,896]{1,0:T(8,128)(2,1)S(1)}, bf16[96,896]{1,0:T(8,128)(2,1)S(1)}, u32[]{:S(2)}, u32[]{:S(2)}) collective-permute-start(bf16[96,896]{1,0:T(8,128)(2,1)S(1)} %get-tuple-element.136), channel_id=1, source_target_pairs={{8,0},{16,8},{24,16},{28,24},{20,28},{12,20},{4,12},{0,4},{9,1},{1... | collective-permute-start | bytes 516104 | tf_op jit(solution)/shard_map/ppermute | solution.py:680
  163.9 18.4 %copy-start.8 = (f32[8,768]{1,0:T(8,128)S(1)}, f32[8,768]{1,0:T(8,128)}, u32[]{:S(2)}) copy-start(f32[8,768]{1,0:T(8,128)} %copy-done.6) | copy-start | bytes 73732
  164.0 18.2 %collective-permute-start.19 = (bf16[256,768]{1,0:T(8,128)(2,1)S(1)}, bf16[256,768]{1,0:T(8,128)(2,1)S(1)}, u32[]{:S(2)}, u32[]{:S(2)}) collective-permute-start(bf16[256,768]{1,0:T(8,128)(2,1)S(1)} %add_convert_fusion.near), channel_id=1, source_target_pairs={{0,1},{1,0},{2,3},{3,2},{4,5},{5,4},{6,7},{7,6},{8,9},{9,8},{10,11... | collective-permute-start | bytes 1179656 | tf_op jit(solution)/shard_map/ppermute | solution.py:614
  165.1 12.9 %collective-permute-start.17 = (bf16[256,384]{1,0:T(8,128)(2,1)S(1)}, bf16[256,384]{1,0:T(8,128)(2,1)S(1)}, u32[]{:S(2)}, u32[]{:S(2)}) collective-permute-start(bf16[256,384]{1,0:T(8,128)(2,1)S(1)} %get-tuple-element.119.y_own), channel_id=1, source_target_pairs={{0,1},{1,0},{2,3},{3,2},{4,5},{5,4},{6,7},{7,6},{8,9},{9,8},{10,11... | collective-permute-start | bytes 589832 | tf_op jit(solution)/shard_map/ppermute | solution.py:614
  169.0 10.5 %collective-permute-start.24 = (bf16[96,896]{1,0:T(8,128)(2,1)S(1)}, bf16[96,896]{1,0:T(8,128)(2,1)S(1)}, u32[]{:S(2)}, u32[]{:S(2)}) collective-permute-start(bf16[96,896]{1,0:T(8,128)(2,1)S(1)} %get-tuple-element.137), channel_id=1, source_target_pairs={{0,8},{8,16},{16,24},{24,28},{28,20},{20,12},{12,4},{4,0},{1,9},{9... | collective-permute-start | bytes 516104 | tf_op jit(solution)/shard_map/ppermute | solution.py:679
  169.7 9.9 %collective-permute-start.25 = (bf16[96,896]{1,0:T(8,128)(2,1)S(1)}, bf16[96,896]{1,0:T(8,128)(2,1)S(1)}, u32[]{:S(2)}, u32[]{:S(2)}) collective-permute-start(bf16[96,896]{1,0:T(8,128)(2,1)S(1)} %get-tuple-element.138), channel_id=1, source_target_pairs={{8,0},{16,8},{24,16},{28,24},{20,28},{12,20},{4,12},{0,4},{9,1},{1... | collective-permute-start | bytes 516104 | tf_op jit(solution)/shard_map/ppermute | solution.py:680
  180.2 5.5 %collective-permute-start.26 = (bf16[96,896]{1,0:T(8,128)(2,1)S(1)}, bf16[96,896]{1,0:T(8,128)(2,1)S(1)}, u32[]{:S(2)}, u32[]{:S(2)}) collective-permute-start(bf16[96,896]{1,0:T(8,128)(2,1)S(1)} %get-tuple-element.141), channel_id=1, source_target_pairs={{0,8},{8,16},{16,24},{24,28},{28,20},{20,12},{12,4},{4,0},{1,9},{9... | collective-permute-start | bytes 516104 | tf_op jit(solution)/shard_map/ppermute | solution.py:679
  181.4 5.4 %collective-permute-start.27 = (bf16[96,896]{1,0:T(8,128)(2,1)S(1)}, bf16[96,896]{1,0:T(8,128)(2,1)S(1)}, u32[]{:S(2)}, u32[]{:S(2)}) collective-permute-start(bf16[96,896]{1,0:T(8,128)(2,1)S(1)} %get-tuple-element.142), channel_id=1, source_target_pairs={{8,0},{16,8},{24,16},{28,24},{20,28},{12,20},{4,12},{0,4},{9,1},{1... | collective-permute-start | bytes 516104 | tf_op jit(solution)/shard_map/ppermute | solution.py:680
  187.4 4.1 %collective-permute-start.28 = (f32[56,896]{1,0:T(8,128)S(1)}, f32[56,896]{1,0:T(8,128)S(1)}, u32[]{:S(2)}, u32[]{:S(2)}) collective-permute-start(f32[56,896]{1,0:T(8,128)S(1)} %get-tuple-element.146), channel_id=1, source_target_pairs={{0,2},{2,0},{1,3},{3,1},{4,6},{6,4},{5,7},{7,5},{8,10},{10,8},{9,1... | collective-permute-start | bytes 602120 | tf_op jit(solution)/shard_map/ppermute | solution.py:614
  187.5 4.0 %collective-permute-start.29 = (f32[48,128]{1,0:T(8,128)S(1)}, f32[48,128]{1,0:T(8,128)S(1)}, u32[]{:S(2)}, u32[]{:S(2)}) collective-permute-start(f32[48,128]{1,0:T(8,128)S(1)} %get-tuple-element.148), channel_id=1, source_target_pairs={{0,1},{1,0},{2,3},{3,2},{4,5},{5,4},{6,7},{7,6},{8,9},{9,8},{10,11... | collective-permute-start | bytes 73736 | tf_op jit(solution)/shard_map/ppermute | solution.py:614
  188.0 3.5 %collective-permute-start.30 = (f32[48,128]{1,0:T(8,128)S(1)}, f32[48,128]{1,0:T(8,128)S(1)}, u32[]{:S(2)}, u32[]{:S(2)}) collective-permute-start(f32[48,128]{1,0:T(8,128)S(1)} %get-tuple-element.149), channel_id=1, source_target_pairs={{0,3},{1,2},{2,1},{3,0},{4,7},{5,6},{6,5},{7,4},{8,11},{9,10},{10,... | collective-permute-start | bytes 73736 | tf_op jit(solution)/shard_map/ppermute | solution.py:1015
  (15 other events, 11.8 us)

commit v7 on v6

--- a/solution.py
+++ b/solution.py
@@ -20,6 +20,7 @@
 bf16 = jnp.bfloat16
 vmem = pl.BlockSpec(memory_space=pltpu.VMEM)
 smem = pl.BlockSpec(memory_space=pltpu.SMEM)
+hbm = pl.BlockSpec(memory_space=pltpu.HBM)
 
 
 def mm(left, right):
@@ -203,7 +204,16 @@
 
 def attention_forward(heads, experts, *refs):
     (meta, x_own, x_other, wall, strips, far, segment) = refs[:7]
-    (h1, q_out, k_out, v_out, o_own, o_other, o_all, probs, gains) = refs[7:]
+    kept = refs[7:12]
+    (o_own, o_other, o_all, gains) = refs[12:16]
+    (h1, q_out, k_out, v_out, probs, sems) = refs[16:]
+    copies = []
+
+    def keep(source, target):
+        copy = pltpu.make_async_copy(source, target, sems.at[len(copies)])
+        copy.start()
+        copies.append(copy)
+
     place = meta[0]
     rows = x_own.shape[0]
     group = 2 * rows
@@ -217,11 +227,14 @@
         h1[pl.ds(pl.multiple_of(start, 16), rows), :] = (
             values * rms_scale(values) * gain_one
         ).astype(bf16)
+    keep(h1, kept[0])
     qkv = mm(h1[...], wall[...])
     lanes = q_out.shape[1]
     q_out[...] = qkv[:, :lanes].astype(bf16)
     k_out[...] = pltpu.roll(qkv[:, LANES : LANES + lanes], lanes - HEAD_SIZE, 1).astype(bf16)
     v_out[...] = qkv[:, width - lanes :].astype(bf16)
+    for source, target in zip((q_out, k_out, v_out), kept[1:4]):
+        keep(source, target)
     segment_row = segment[0:1, :]
     segment_column = column_of(segment_row.astype(f32)).astype(jnp.int32)
     keys = k_out[...]
@@ -242,10 +255,14 @@
             probs[head, first : first + STRIP, :] = chances
             total = total + mm(chances.astype(bf16), values_of[head])
         o_all[first : first + STRIP, :] = total.astype(bf16)
+        at = slice(first, first + STRIP)
+        keep(probs.at[:, at, :], kept[4].at[:, at, :])
     for out, start in ((o_own, place * rows), (o_other, (1 - place) * rows)):
         values = o_all[pl.ds(pl.multiple_of(start, 16), rows), :].astype(f32)
         for index, part in enumerate(join(values[: rows // 2], values[rows // 2 :])):
             out[:, index * LANES : (index + 1) * LANES] = part.astype(bf16)
+    for copy in copies:
+        copy.wait()
 
 
 def columns_of(*lines):
@@ -381,12 +398,12 @@
 
 
 def from_experts(experts, capacity, *refs):
-    meta, rows_in, cotangent, routes_row, keep_row, slot_y, slot_x, y_out, dx_out, gate_out = refs
+    meta, rows_in, cotangent, routes_row, keep_row, slots, y_out, dx_out, gate_out = refs
     slot = column_of(slots_by_row(routes_row[...], keep_row[...], experts, capacity).astype(f32))
     slot = slot.astype(jnp.int32)
     width = rows_in.shape[1]
-    pick_y = (slot == slot_y[...]).astype(f32).astype(bf16)
-    pick_x = (slot == slot_x[...]).astype(f32).astype(bf16)
+    pick_y = (slot == slots[0:1, :]).astype(f32).astype(bf16)
+    pick_x = (slot == slots[1:2, :]).astype(f32).astype(bf16)
     dx_out[...] = mm(pick_x, rows_in[...]).astype(bf16)
     picked = mm(pick_y, rows_in[...]).astype(bf16)
     y_out[...] = picked
@@ -441,10 +458,21 @@
 
 
 def attention_backward(heads, buckets, shard, *refs):
-    (meta, x_own, x_other, h1, q_in, k_in, v_in, probs, db) = refs[:9]
-    (o_all, wo_ref, wall, router_grad) = refs[9:13]
+    (meta, x_own, x_other) = refs[:3]
+    kept = refs[3:8]
+    (db, o_all, wo_ref, wall, router_grad) = refs[8:13]
     (payload, top_out, bottom_out, dh1_own, dh1_other) = refs[13:18]
-    (sums, do_all, dq, dk, dv, dqkv, dh1) = refs[18:]
+    (sums, do_all, dq, dk, dv, dqkv, dh1) = refs[18:25]
+    (h1, q_in, k_in, v_in, probs, sems) = refs[25:]
+    blocks = q_in.shape[0] // STRIP
+    moves = [(kept[1], q_in), (kept[2], k_in), (kept[3], v_in)]
+    for block in range(blocks):
+        at = slice(block * STRIP, (block + 1) * STRIP)
+        moves.append((kept[4].at[:, at, :], probs.at[:, at, :]))
+    moves.append((kept[0], h1))
+    copies = [pltpu.make_async_copy(a, b, sems.at[i]) for i, (a, b) in enumerate(moves)]
+    for copy in copies:
+        copy.start()
     place = meta[0]
     rows = x_own.shape[0]
     group = 2 * rows
@@ -454,14 +482,16 @@
     both = mm(db[...], wo_ref[...])
     high = pltpu.roll(both[:, LANES : LANES + lanes], lanes - HEAD_SIZE, 1)
     do_all[...] = jnp.where(place == 0, both[:, :lanes], high).astype(bf16)
-    blocks = group // STRIP
     sums[...] = jnp.zeros_like(sums)
+    for copy in copies[:3]:
+        copy.wait()
     keys = k_in[...]
     values = v_in[...]
     ahead = [jnp.zeros((STRIP, STRIP), f32) for _ in range(heads)]
     behind = [jnp.zeros((STRIP, STRIP), f32) for _ in range(heads)]
     for block in range(blocks):
         at = slice(block * STRIP, (block + 1) * STRIP)
+        copies[3 + block].wait()
         dq_total = jnp.zeros((STRIP, lanes), f32)
         for head in range(heads):
             query = pick_head(q_in[at, :], head, lanes)
@@ -517,6 +547,7 @@
         line = line + jnp.where(lane == buckets // 2 - 1, jnp.sum(behind[head]), 0.0)
         riders = riders + jnp.where(row == head, pltpu.roll(line, HEAD_SIZE + 1, 1), 0.0)
     width = wall.shape[1]
+    copies[-1].wait()
     grads = mm_tn(h1[...], dqkv[...])
     payload[:, : width - LANES] = grads[:, : width - LANES].astype(bf16)
     payload[:, width - LANES : width] = (grads[:, width - LANES :] + riders).astype(bf16)
@@ -803,22 +834,26 @@
         wo_own = jnp.concatenate([upper[:, :, wide : wide + width], lower[:, :, wide : wide + width]], axis=2)
         wo_own = wo_own.reshape(-1, 2 * width)
 
-    h1, q, k, v, o_own, o_other, o_all, probs, gains = kernel_call(
+    kept_shapes = [(group, model_width)] + [(group, lanes)] * 3
+    probs_shape = (heads, group, group)
+    blocks = group // STRIP
+    kept_scratch = [pltpu.VMEM(dims, bf16) for dims in kept_shapes] + [pltpu.VMEM(probs_shape, f32)]
+    h1, q, k, v, probs, o_own, o_other, o_all, gains = kernel_call(
         functools.partial(attention_forward, heads, experts),
-        [
-            full((group, model_width), bf16),
-            full((group, lanes), bf16),
-            full((group, lanes), bf16),
-            full((group, lanes), bf16),
+        [pltpu.HBM(dims, bf16) for dims in kept_shapes]
+        + [
+            pltpu.HBM(probs_shape, f32),
             full((rows // 2, 2 * width), bf16),
             full((rows // 2, 2 * width), bf16),
             full((group, lanes), bf16),
-            full((heads, group, group), f32),
             full((8, model_width), f32),
         ],
         [smem] + [vmem] * 6,
+        out_specs=[hbm] * 5 + [vmem] * 4,
+        scratch=kept_scratch + [pltpu.SemaphoreType.DMA((4 + blocks,))],
         flops=2 * group * model_width * wide * 8,
         moved=8 * 1024 * 1024,
+        mib=20,
     )(meta, tokens, x_other, wall, strips, far, segment)
     wo_tp = swap(wo_own, "tp")
     wo_ctx = swap(wo_own, "ctx")
@@ -882,11 +917,11 @@
     outgoing, x_rows, dy_rows, act, dpre = kernel_call(
         functools.partial(expert_kernel, owners, capacity, chunks, group_owners),
         [
-            full((owners * tp_count, per_owner, part_width), bf16),
-            full((pieces, slot_rows, model_width), bf16),
-            full((pieces, slot_rows, model_width), bf16),
-            full((pieces, slot_rows, hidden_width), bf16),
-            full((pieces, slot_rows, hidden_width), bf16),
+            pltpu.HBM((owners * tp_count, per_owner, part_width), bf16),
+            pltpu.HBM((pieces, slot_rows, model_width), bf16),
+            pltpu.HBM((pieces, slot_rows, model_width), bf16),
+            pltpu.HBM((pieces, slot_rows, hidden_width), bf16),
+            pltpu.HBM((pieces, slot_rows, hidden_width), bf16),
         ],
         [
             whole(owners * per_owner, model_width),
@@ -908,7 +943,7 @@
             pltpu.VMEM((owners * per_owner, model_width), f32),
         ],
         grid=(pieces, chunks),
-        mib=24,
+        mib=24 if owners <= 16 else 60,
         flops=8 * pieces * slot_rows * model_width * hidden_width,
         moved=12 * 1024 * 1024,
     )(arrived, base[:, None], base[None, :], w_in, w_out)
@@ -943,10 +978,10 @@
             full((rows, part_width), bf16),
             full((8, rows), f32),
         ],
-        [smem] + [vmem] * 6,
+        [smem] + [vmem] * 5,
         flops=4 * rows * returned.shape[0] * part_width,
         moved=2 * 1024 * 1024,
-    )(meta, returned, cotangent, routes_row, keep_row, back_first, back_second)
+    )(meta, returned, cotangent, routes_row, keep_row, np.concatenate([back_first, back_second], axis=0))
     dx_tp = swap(dx_own, "tp")
     part_tp = swap(part_own, "tp")
 
@@ -976,7 +1011,7 @@
             full((rows, model_width), bf16),
             full((rows, model_width), bf16),
         ],
-        [smem] + [vmem] * 12,
+        [smem] + [vmem] * 2 + [hbm] * 5 + [vmem] * 5,
         scratch=[
             pltpu.VMEM((heads, STRIP, 4 * STRIP), f32),
             pltpu.VMEM((group, lanes), bf16),
@@ -985,9 +1020,11 @@
             pltpu.VMEM((group, lanes), f32),
             pltpu.VMEM((group, wide), bf16),
             pltpu.VMEM((group, model_width), f32),
+            *kept_scratch,
+            pltpu.SemaphoreType.DMA((4 + blocks,)),
         ],
         flops=2 * group * model_width * wide * 12,
-        mib=20,
+        mib=28,
         moved=8 * 1024 * 1024,
     )(
         meta, tokens, x_other, h1, q, k, v, probs, db, o_all, wo_full, wall, router_grad,
@@ -1008,7 +1045,7 @@
         moved=4 * 1024 * 1024,
     )(tokens, middle_grad, gains, dh1_sum, dh1_far)[0]
     own, send, own_lines, riders_own, riders_other = ring_sums(
-        payload, top, bottom, fsdp_count, wide - LANES, meta, {2: result, 1: input_grad}
+        payload, top, bottom, fsdp_count, wide - LANES, meta, {1: (result, input_grad)}
     )
     other = swap(send, "ctx")
     from_tp = swap(riders_own, "tp")

time: 194 us -> 187 us (0.964)
  local copies, waits for them, and re-layouts: 25 us -> 17.4 us
  Pallas kernels: 49.5 us -> 52.9 us
  waiting for transfers between devices: 54.3 us -> 51.8 us
    unnamed x94 -> x72, local copies, waits for them, and re-layouts: 23.8 us -> 16.2 us
    ppermute x14, waiting for transfers between devices: 18.7 us -> 12 us  [swap(): return lax.ppermute(value, axis, [(0, 1), (1, 0)])]
    ppermute x4, waiting for transfers between devices: 6.13 us -> 8.55 us  [ring_sums(): from_left = lax.ppermute(going_right, 'fsdp', right)]
  transfers between devices with their start and end apart: 32 -> 32, of which waited for: 20 -> 24; matrix products, arithmetic and copies ran while one was open for 0% -> 0% of each run, Pallas kernels for 10% -> 11%
where the time goes in v7:
time: 187 us; the launch traced here: 186 us
  Pallas kernels  52.9 us (28%)
  waiting for transfers between devices  51.8 us (28%)
  starting transfers between devices  31.2 us (17%)
  blocking collectives  31 us (17%)
  local copies, waits for them, and re-layouts  17.4 us (9%)
    all_to_all x1, blocking collectives, body(): lax.all_to_all(sends.reshape(owners, per_owner, model_width), ('fsdp', 'c...  28.6 us
    unnamed x72, local copies, waits for them, and re-layouts  16.2 us
    all_to_all x1, waiting for transfers between devices, body(): lax.all_to_all(outgoing, ('fsdp', 'ctx', 'tp'), split_axis=0, concat_axis...  12.7 us
    ppermute x14, waiting for transfers between devices, swap(): return lax.ppermute(value, axis, [(0, 1), (1, 0)])  12 us
    pallas_call x1, Pallas kernels, body(): kernel_call(functools.partial(attention_backward, heads, buckets, model_w...  10.5 us
    pallas_call x1, Pallas kernels, body(): kernel_call(functools.partial(expert_kernel, owners, capacity, chunks, gr...  10.4 us
    ppermute x14, starting transfers between devices, swap(): return lax.ppermute(value, axis, [(0, 1), (1, 0)])  8.78 us
    ppermute x4, waiting for transfers between devices, ring_sums(): from_left = lax.ppermute(going_right, 'fsdp', right)  8.55 us
  transfers between devices with their start and end apart: 32, of which 24 were waited for; matrix products, arithmetic and copies ran while one was open for 0% of the time, Pallas kernels for 11%

profile of v7, /device:TPU:0, one launch (start us, length us, event | category | flops | bytes accessed | tf_op | source)
XLA Modules:
  0.0 186.2 jit_solution(17740016544536916684)
XLA Ops:
  0.7 1.2 dynamic-slice_bitcast_fusion.refs_0_.meta.places
  1.9 1.7 shard_map.292
  4.0 1.1 collective-permute-done.1
  5.1 0.9 pad_maximum_fusion.refs_1_
  6.0 2.9 %collective-permute-start.3 = (bf16[96,896]{1,0:T(8,128)(2,1)S(1)}, bf16[96,896]{1,0:T(8,128)(2,1)S(1)}, u32[]{:S(2)}, u32[]{:S(2)}) collective-permute-start(bf16[96,896]{1,0:T(8,128)(2,1)S(1)} %pad_maximum_fusion.refs_1_), channel_id=1, source_target_pairs={{8,0},{16,8},{24,16},{28,24},{20,28},{12,20},{4,12},{0,4},{9,1},{1... | collective-permute-start | bytes 516104 | tf_op jit(solution)/shard_map/ppermute | solution.py:683
  11.0 2.3 %shard_map.293 = (f32[3,128,384]{2,1,0:T(8,128)S(1)}, f32[8,128]{1,0:T(8,128)S(1)}, s32[8,512]{1,0:T(8,128)S(1)}) custom-call(s32[20]{0:T(128)S(1)} %copy-done.8, s32[1,4]{1,0:T(1,128)S(1)} %copy-done.15, f32[6,32]{1,0:T(8,128)S(1)} %bitcast.18), custom_call_target="tpu_custom_call" | custom-call | bytes 1048576 | tf_op jit(solution)/shard_map/pallas_call | solution.py:809
  13.7 1.4 collective-permute-done.2.refs_2_
  15.5 1.6 collective-permute-start.5
  17.1 3.4 %collective-permute-done.4.refs_4_ = bf16[96,896]{1,0:T(8,128)(2,1)S(1)} collective-permute-done((bf16[96,896]{1,0:T(8,128)(2,1)S(1)}, bf16[96,896]{1,0:T(8,128)(2,1)S(1)}, u32[]{:S(2)}, u32[]{:S(2)}) %collective-permute-start.4) | collective-permute-done | bytes 172064 | tf_op jit(solution)/shard_map/ppermute | solution.py:682
  20.5 0.8 collective-permute-start.6
  21.2 1.1 collective-permute-done.5.refs_5_
  22.3 1.6 collective-permute-start.7
  23.9 2.0 %collective-permute-done.6.refs_6_ = bf16[96,896]{1,0:T(8,128)(2,1)S(1)} collective-permute-done((bf16[96,896]{1,0:T(8,128)(2,1)S(1)}, bf16[96,896]{1,0:T(8,128)(2,1)S(1)}, u32[]{:S(2)}, u32[]{:S(2)}) %collective-permute-start.6) | collective-permute-done | bytes 172064 | tf_op jit(solution)/shard_map/ppermute | solution.py:682
  25.9 0.8 collective-permute-start.8
  26.6 1.7 collective-permute-done.7.refs_7_
  28.3 3.0 %collective-permute-done.8.refs_8_ = bf16[96,896]{1,0:T(8,128)(2,1)S(1)} collective-permute-done((bf16[96,896]{1,0:T(8,128)(2,1)S(1)}, bf16[96,896]{1,0:T(8,128)(2,1)S(1)}, u32[]{:S(2)}, u32[]{:S(2)}) %collective-permute-start.8) | collective-permute-done | bytes 172064 | tf_op jit(solution)/shard_map/ppermute | solution.py:687
  31.9 0.7 shard_map.294
  32.8 1.6 collective-permute-start.12
  34.4 1.1 copy-done.1
  36.2 5.8 %shard_map.295 = (bf16[512,768]{1,0:T(8,128)(2,1)}, bf16[512,256]{1,0:T(8,128)(2,1)}, bf16[512,256]{1,0:T(8,128)(2,1)}, bf16[512,256]{1,0:T(8,128)(2,1)}, f32[3,...) custom-call(s32[20]{0:T(128)S(1)} %copy-done.10, ...), custom_call_target="tpu_custom_call" | custom-call | flops 4026531840 | bytes 8388608 | tf_op jit(solution)/shard_map/pallas_call | solution.py:841
  42.3 1.4 collective-permute-start.9
  44.4 3.5 %collective-permute-done.9.refs_4_ = bf16[128,384]{1,0:T(8,128)(2,1)S(1)} collective-permute-done((bf16[128,384]{1,0:T(8,128)(2,1)S(1)}, bf16[128,384]{1,0:T(8,128)(2,1)S(1)}, u32[]{:S(2)}, u32[]{:S(2)}) %collective-permute-start.9) | collective-permute-done | bytes 98336 | tf_op jit(solution)/shard_map/ppermute | solution.py:645
  47.9 1.2 collective-permute-done.11.refs_6_
  49.1 2.9 %shard_map.296 = (f32[256,768]{1,0:T(8,128)S(1)}, bf16[640,768]{1,0:T(8,128)(2,1)S(1)}, bf16[768,384]{1,0:T(8,128)(2,1)S(1)}) custom-call(s32[20]{0:T(128)S(1)} %copy-done.10, bf16[256,768]{1,0:T(8,128)(2,1)S(1)} %copy-done.2, bf16[256,768]{1,0:T(8,128)(2,1)S(1)} %copy-done, bf16[128,384]{1,0:T(8,128)(2,1)S(1)} %get-tuple-element.96.refs_3_, ...), custom_call_target="tpu_custom_call" | custom-call | flops 805306368 | bytes 6291456 | tf_op jit(solution)/shard_map/pallas_call | solution.py:880
  52.0 28.6 %all_to_all.10 = bf16[16,40,768]{2,1,0:T(8,128)(2,1)S(1)} all-to-all(bf16[16,40,768]{2,1,0:T(8,128)(2,1)S(1)} %bitcast.16), channel_id=1, replica_groups=mesh['fsdp'=8,'ctx'=2,'tp'=2] {'fsdp','ctx'}, dimensions={0} | all-to-all | bytes 1966080 | tf_op jit(solution)/shard_map/all_to_all | solution.py:896
  80.7 10.4 %shard_map.297 = (bf16[32,40,384]{2,1,0:T(8,128)(2,1)}, bf16[2,160,768]{2,1,0:T(8,128)(2,1)}, bf16[2,160,768]{2,1,0:T(8,128)(2,1)}, bf16[2,160,1536]{2,1,0:T(8,128)(2,1)}, bf16[2,160,1536]{2,1,0:T(8,128)(2,1)}) custom-call(bf16[640,768]{1,0:T(8,128)(2,1)S(1)} %bitcast.17, s32[320,1]{1,0:T(8,128)S(1)} %copy-done.22, s32[1,320]{1,0:T(1,128)S(1)} %copy-done.24, ...), custom_call_target="tpu_custom_call" | custom-call | flops 3019898880 | bytes 12582912 | tf_op jit(solution)/shard_map/pallas_call | solution.py:917
  91.1 4.9 %all-to-all-start.1 = ((bf16[32,40,384]{2,1,0:T(8,128)(2,1)}), bf16[32,40,384]{2,1,0:T(8,128)(2,1)S(1)}, u32[]{:S(2)}, u32[]{:S(2)}) async-start(bf16[32,40,384]{2,1,0:T(8,128)(2,1)} %get-tuple-element.104), calls=%async_computation.1 | async-start | bytes 1966080 | tf_op jit(solution)/shard_map/all_to_all | solution.py:951
  96.0 1.2 copy-done.25
  97.2 1.2 copy-done.26
  98.4 1.0 copy-done.27
  99.4 1.0 copy-done.28
  100.5 7.5 %shard_map.298 = (f32[2,768,1536]{2,1,0:T(8,128)}, f32[2,1536,768]{2,1,0:T(8,128)}) custom-call(bf16[2,160,768]{2,1,0:T(8,128)(2,1)S(1)} %copy-done.27, bf16[2,160,1536]{2,1,0:T(8,128)(2,1)S(1)} %copy-done.26, bf16[2,160,1536]{2,1,0:T(8,128)(2,1)S(1)} %copy-done.25, bf16[2,160,768]{2,1,0:T(8,128)(2,1)S(1)} %copy-done.28), custom_call_target="tpu_custom_call" | custom-call | flops 1509949440 | bytes 25165824 | tf_op jit(solution)/shard_map/pallas_call | solution.py:957
  107.9 12.7 %all-to-all-done.1 = bf16[32,40,384]{2,1,0:T(8,128)(2,1)S(1)} async-done(((bf16[32,40,384]{2,1,0:T(8,128)(2,1)}), bf16[32,40,384]{2,1,0:T(8,128)(2,1)S(1)}, u32[]{:S(2)}, u32[]{:S(2)}) %all-to-all-start.1) | async-done | bytes 983072 | tf_op jit(solution)/shard_map/all_to_all | solution.py:951
  120.7 0.8 copy-done.23
  121.4 1.9 %shard_map.299 = (bf16[256,384]{1,0:T(8,128)(2,1)S(1)}, bf16[256,384]{1,0:T(8,128)(2,1)S(1)}, f32[8,256]{1,0:T(8,128)S(1)}) custom-call(s32[20]{0:T(128)S(1)} %copy-done.11, bf16[1280,384]{1,0:T(8,128)(2,1)S(1)} %bitcast.15, bf16[256,768]{1,0:T(8,128)(2,1)S(1)} %copy-done, s32[1,256]{1,0:T(1,128)S(1)} %bitcast.20, s32[1,256]{1,0:T(1,128)S(1)} %bitcast.23, ...), custom_call_target="tpu_custom_call" | custom-call | flops 503316480 | bytes 2097152 | tf_op jit(solution)/shard_map/pallas_call | solution.py:974
  123.3 1.5 collective-permute-start.15
  125.4 5.1 %collective-permute-done.16.refs_4_ = f32[8,256]{1,0:T(8,128)S(1)} collective-permute-done((f32[8,256]{1,0:T(8,128)S(1)}, f32[8,256]{1,0:T(8,128)S(1)}, u32[]{:S(2)}, u32[]{:S(2)}) %collective-permute-start.16) | collective-permute-done | bytes 8224 | tf_op jit(solution)/shard_map/ppermute | solution.py:645
  130.5 0.7 copy-done.6
  131.2 2.5 %shard_map.300 = (f32[256,768]{1,0:T(8,128)S(1)}, bf16[256,768]{1,0:T(8,128)(2,1)S(1)}, bf16[768,128]{1,0:T(8,128)(2,1)S(1)}, f32[256,128]{1,0:T(8,128)S(1)}) custom-call(s32[20]{0:T(128)S(1)} %copy-done.11, bf16[256,384]{1,0:T(8,128)(2,1)S(1)} %get-tuple-element.113.refs_1_, bf16[256,384]{1,0:T(8,128)(2,1)S(1)} %collective-permute-done.15.refs_2_, ...), custom_call_target="tpu_custom_call" | custom-call | flops 150994944 | bytes 6291456 | tf_op jit(solution)/shard_map/pallas_call | solution.py:988
  133.7 2.4 %all_gather.3.refs_8_ = bf16[512,768]{1,0:T(8,128)(2,1)S(1)} all-gather(bf16[256,768]{1,0:T(8,128)(2,1)S(1)} %get-tuple-element.124), channel_id=1, replica_groups=mesh['fsdp'=8,'ctx'=2,'tp'=2] {'ctx'}, dimensions={0}, use_global_device_ids=true | all-gather | bytes 1179648 | tf_op jit(solution)/shard_map/all_gather | solution.py:1002
  136.1 1.9 %copy-done.29 = f32[3,512,512]{2,1,0:T(8,128)S(1)} copy-done((f32[3,512,512]{2,1,0:T(8,128)S(1)}, f32[3,512,512]{2,1,0:T(8,128)}, u32[]{:S(2)}) %copy-start.29) | copy-done | bytes 3145752
  138.0 0.9 copy-done.31
  139.0 0.9 copy-done.32
  139.9 0.9 copy-done.33
  140.9 0.9 copy-done.35
  141.8 10.5 %shard_map.302 = (bf16[768,896]{1,0:T(8,128)(2,1)S(1)}, bf16[48,896]{1,0:T(8,128)(2,1)S(1)}, bf16[48,896]{1,0:T(8,128)(2,1)S(1)}, bf16[256,768]{1,0:T(8,128)(2,1)S(1)}, bf16[256,768]{1,0:T(8,128)(2,1)S(1)}) custom-call(s32[20]{0:T(128)S(1)} %copy-done.11, bf16[256,768]{1,0:T(8,128)(2,1)S(1)} %copy-done.2, bf16[256,768]{1,0:T(8,128)(2,1)S(1)} %copy-done.21, ...), custom_call_target="tpu_custom_call" | custom-call | flops 6039797760 | bytes 8388608 | tf_op jit(solution)/shard_map/pallas_call | solution.py:1005
  152.5 1.1 collective-permute-start.20
  153.6 1.0 collective-permute-start.21
  154.6 2.8 %collective-permute-done.20.from_left = bf16[48,896]{1,0:T(8,128)(2,1)S(1)} collective-permute-done((bf16[48,896]{1,0:T(8,128)(2,1)S(1)}, bf16[48,896]{1,0:T(8,128)(2,1)S(1)}, u32[]{:S(2)}, u32[]{:S(2)}) %collective-permute-start.20) | collective-permute-done | bytes 86048 | tf_op jit(solution)/shard_map/ppermute | solution.py:710
  157.4 0.8 collective-permute-done.21.from_right
  158.7 1.2 collective-permute-start.22
  159.9 0.9 collective-permute-start.23
  160.9 1.0 collective-permute-start.19
  161.9 2.4 %collective-permute-done.22.from_left = bf16[96,896]{1,0:T(8,128)(2,1)S(1)} collective-permute-done((bf16[96,896]{1,0:T(8,128)(2,1)S(1)}, bf16[96,896]{1,0:T(8,128)(2,1)S(1)}, u32[]{:S(2)}, u32[]{:S(2)}) %collective-permute-start.22) | collective-permute-done | bytes 172064 | tf_op jit(solution)/shard_map/ppermute | solution.py:710
  164.3 1.0 collective-permute-done.23.from_right
  166.6 1.5 collective-permute-start.25
  168.3 3.1 %collective-permute-done.24.from_left = bf16[96,896]{1,0:T(8,128)(2,1)S(1)} collective-permute-done((bf16[96,896]{1,0:T(8,128)(2,1)S(1)}, bf16[96,896]{1,0:T(8,128)(2,1)S(1)}, u32[]{:S(2)}, u32[]{:S(2)}) %collective-permute-start.24) | collective-permute-done | bytes 172064 | tf_op jit(solution)/shard_map/ppermute | solution.py:710
  172.6 1.6 collective-permute-start.26
  174.9 1.6 shard_map.301
  176.5 1.3 shard_map.303
  178.1 1.6 collective-permute-done.27.from_right
  180.4 1.1 collective-permute-start.29
  182.2 2.0 %collective-permute-done.29.refs_4_ = f32[48,128]{1,0:T(8,128)S(1)} collective-permute-done((f32[48,128]{1,0:T(8,128)S(1)}, f32[48,128]{1,0:T(8,128)S(1)}, u32[]{:S(2)}, u32[]{:S(2)}) %collective-permute-start.29) | collective-permute-done | bytes 24608 | tf_op jit(solution)/shard_map/ppermute | solution.py:645
  184.8 1.4 shard_map.308
  (94 shorter events, 12.9 us)
Async XLA Ops:
  3.6 1.6 collective-permute-start.1
  6.0 7.7 %collective-permute-start.3 = (bf16[96,896]{1,0:T(8,128)(2,1)S(1)}, bf16[96,896]{1,0:T(8,128)(2,1)S(1)}, u32[]{:S(2)}, u32[]{:S(2)}) collective-permute-start(bf16[96,896]{1,0:T(8,128)(2,1)S(1)} %pad_maximum_fusion.refs_1_), channel_id=1, source_target_pairs={{8,0},{16,8},{24,16},{28,24},{20,28},{12,20},{4,12},{0,4},{9,1},{1... | collective-permute-start | bytes 516104 | tf_op jit(solution)/shard_map/ppermute | solution.py:683
  8.9 6.2 %collective-permute-start.2 = (bf16[96,896]{1,0:T(8,128)(2,1)S(1)}, bf16[96,896]{1,0:T(8,128)(2,1)S(1)}, u32[]{:S(2)}, u32[]{:S(2)}) collective-permute-start(bf16[96,896]{1,0:T(8,128)(2,1)S(1)} %pad_maximum_fusion.refs_1_), channel_id=1, source_target_pairs={{0,8},{8,16},{16,24},{24,28},{28,20},{20,12},{12,4},{4,0},{1,9},{9... | collective-permute-start | bytes 516104 | tf_op jit(solution)/shard_map/ppermute | solution.py:682
  9.7 0.7 copy-start.12
  15.1 5.4 %collective-permute-start.4 = (bf16[96,896]{1,0:T(8,128)(2,1)S(1)}, bf16[96,896]{1,0:T(8,128)(2,1)S(1)}, u32[]{:S(2)}, u32[]{:S(2)}) collective-permute-start(bf16[96,896]{1,0:T(8,128)(2,1)S(1)} %collective-permute-done.2.refs_2_), channel_id=1, source_target_pairs={{0,8},{8,16},{16,24},{24,28},{28,20},{20,12},{12,4},{4,0},{1,9},{9... | collective-permute-start | bytes 516104 | tf_op jit(solution)/shard_map/ppermute | solution.py:682
  15.5 18.9 %collective-permute-start = (bf16[256,768]{1,0:T(8,128)(2,1)}, bf16[256,768]{1,0:T(8,128)(2,1)S(1)}, u32[]{:S(2)}, u32[]{:S(2)}) collective-permute-start(bf16[256,768]{1,0:T(8,128)(2,1)} %x_own.1), channel_id=1, source_target_pairs={{0,2},{2,0},{1,3},{3,1},{4,6},{6,4},{5,7},{7,5},{8,10},{10,8},{9,1... | collective-permute-start | bytes 1179656 | tf_op jit(solution)/shard_map/ppermute | solution.py:645
  15.5 6.8 %collective-permute-start.5 = (bf16[96,896]{1,0:T(8,128)(2,1)S(1)}, bf16[96,896]{1,0:T(8,128)(2,1)S(1)}, u32[]{:S(2)}, u32[]{:S(2)}) collective-permute-start(bf16[96,896]{1,0:T(8,128)(2,1)S(1)} %collective-permute-done.3.refs_3_), channel_id=1, source_target_pairs={{8,0},{16,8},{24,16},{28,24},{20,28},{12,20},{4,12},{0,4},{9,1},{1... | collective-permute-start | bytes 516104 | tf_op jit(solution)/shard_map/ppermute | solution.py:683
  20.5 5.4 %collective-permute-start.6 = (bf16[96,896]{1,0:T(8,128)(2,1)S(1)}, bf16[96,896]{1,0:T(8,128)(2,1)S(1)}, u32[]{:S(2)}, u32[]{:S(2)}) collective-permute-start(bf16[96,896]{1,0:T(8,128)(2,1)S(1)} %collective-permute-done.4.refs_4_), channel_id=1, source_target_pairs={{0,8},{8,16},{16,24},{24,28},{28,20},{20,12},{12,4},{4,0},{1,9},{9... | collective-permute-start | bytes 516104 | tf_op jit(solution)/shard_map/ppermute | solution.py:682
  22.3 6.0 %collective-permute-start.7 = (bf16[96,896]{1,0:T(8,128)(2,1)S(1)}, bf16[96,896]{1,0:T(8,128)(2,1)S(1)}, u32[]{:S(2)}, u32[]{:S(2)}) collective-permute-start(bf16[96,896]{1,0:T(8,128)(2,1)S(1)} %collective-permute-done.5.refs_5_), channel_id=1, source_target_pairs={{8,0},{16,8},{24,16},{28,24},{20,28},{12,20},{4,12},{0,4},{9,1},{1... | collective-permute-start | bytes 516104 | tf_op jit(solution)/shard_map/ppermute | solution.py:683
  25.9 5.4 %collective-permute-start.8 = (bf16[96,896]{1,0:T(8,128)(2,1)S(1)}, bf16[96,896]{1,0:T(8,128)(2,1)S(1)}, u32[]{:S(2)}, u32[]{:S(2)}) collective-permute-start(bf16[96,896]{1,0:T(8,128)(2,1)S(1)} %collective-permute-done.6.refs_6_), channel_id=1, source_target_pairs={{0,8},{8,16},{16,24},{24,28},{28,20},{20,12},{12,4},{4,0},{1,9},{9... | collective-permute-start | bytes 516104 | tf_op jit(solution)/shard_map/ppermute | solution.py:687
  32.7 16.4 %collective-permute-start.13 = (bf16[384,384]{1,0:T(8,128)(2,1)S(1)}, bf16[384,384]{1,0:T(8,128)(2,1)S(1)}, u32[]{:S(2)}, u32[]{:S(2)}) collective-permute-start(bf16[384,384]{1,0:T(8,128)(2,1)S(1)} %get-tuple-element.98.refs_7_), channel_id=1, source_target_pairs={{0,2},{2,0},{1,3},{3,1},{4,6},{6,4},{5,7},{7,5},{8,10},{10,8},{9,1... | collective-permute-start | bytes 884744 | tf_op jit(solution)/shard_map/ppermute | solution.py:645
  32.8 9.4 %collective-permute-start.12 = (bf16[384,384]{1,0:T(8,128)(2,1)S(1)}, bf16[384,384]{1,0:T(8,128)(2,1)S(1)}, u32[]{:S(2)}, u32[]{:S(2)}) collective-permute-start(bf16[384,384]{1,0:T(8,128)(2,1)S(1)} %get-tuple-element.98.refs_7_), channel_id=1, source_target_pairs={{0,1},{1,0},{2,3},{3,2},{4,5},{5,4},{6,7},{7,6},{8,9},{9,8},{10,11... | collective-permute-start | bytes 884744 | tf_op jit(solution)/shard_map/ppermute | solution.py:645
  34.4 7.6 %copy-start.20 = (bf16[256,768]{1,0:T(8,128)(2,1)}, bf16[256,768]{1,0:T(8,128)(2,1)S(1)}, u32[]{:S(2)}) copy-start(bf16[256,768]{1,0:T(8,128)(2,1)S(1)} %collective-permute-done.refs_2_) | copy-start | bytes 1179652
  34.4 1.1 copy-start.1
  36.1 12.9 %copy-start = (bf16[256,768]{1,0:T(8,128)(2,1)S(1)}, bf16[256,768]{1,0:T(8,128)(2,1)}, u32[]{:S(2)}) copy-start(bf16[256,768]{1,0:T(8,128)(2,1)} %refs_6_.1) | copy-start | bytes 1179652
  36.2 12.9 %copy-start.2 = (bf16[256,768]{1,0:T(8,128)(2,1)S(1)}, bf16[256,768]{1,0:T(8,128)(2,1)}, u32[]{:S(2)}) copy-start(bf16[256,768]{1,0:T(8,128)(2,1)} %x_own.1) | copy-start | bytes 1179652
  36.2 12.9 %copy-start.3 = (s32[640,1]{1,0:T(8,128)S(1)}, s32[640,1]{1,0:T(8,128)}, u32[]{:S(2)}) copy-start(s32[640,1]{1,0:T(8,128)} %constant.34.clone.refs_16_) | copy-start | bytes 7684
  36.2 12.9 %copy-start.4 = (s32[640,1]{1,0:T(8,128)S(1)}, s32[640,1]{1,0:T(8,128)}, u32[]{:S(2)}) copy-start(s32[640,1]{1,0:T(8,128)} %constant.33.clone.refs_15_) | copy-start | bytes 7684
  36.2 12.9 %copy-start.13 = (s32[256,1]{0,1:T(1,128)S(1)}, s32[256,1]{0,1:T(1,128)}, u32[]{:S(2)}) copy-start(s32[256,1]{0,1:T(1,128)} %param.34) | copy-start | bytes 3076
  36.2 12.9 %copy-start.14 = (s32[256]{0:T(256)S(1)}, s32[256]{0:T(256)}, u32[]{:S(2)}) copy-start(s32[256]{0:T(256)} %param.35) | copy-start | bytes 3076
  36.2 44.4 %copy-start.17 = (bf16[2,1536,768]{2,1,0:T(8,128)(2,1)S(1)}, bf16[2,1536,768]{2,1,0:T(8,128)(2,1)}, u32[]{:S(2)}) copy-start(bf16[2,1536,768]{2,1,0:T(8,128)(2,1)} %refs_4_.3) | copy-start | bytes 14155780
  42.0 38.6 %copy-start.5 = (f32[8,768]{1,0:T(8,128)}, f32[8,768]{1,0:T(8,128)S(1)}, u32[]{:S(2)}) copy-start(f32[8,768]{1,0:T(8,128)S(1)} %get-tuple-element.101.refs_12_.refs_8_.gains) | copy-start | bytes 73732
  42.0 38.6 %copy-start.34 = (bf16[512,256]{1,0:T(8,128)(2,1)}, bf16[512,256]{1,0:T(8,128)(2,1)S(1)}, u32[]{:S(2)}) copy-start(bf16[512,256]{1,0:T(8,128)(2,1)S(1)} %get-tuple-element.125.refs_9_) | copy-start | bytes 786436
  42.0 38.6 %copy-start.16 = (bf16[2,768,1536]{2,1,0:T(8,128)(2,1)S(1)}, bf16[2,768,1536]{2,1,0:T(8,128)(2,1)}, u32[]{:S(2)}) copy-start(bf16[2,768,1536]{2,1,0:T(8,128)(2,1)} %refs_3_.3) | copy-start | bytes 14155780
  42.0 38.6 %copy-start.22 = (s32[320,1]{1,0:T(8,128)S(1)}, s32[320,1]{1,0:T(8,128)}, u32[]{:S(2)}) copy-start(s32[320,1]{1,0:T(8,128)} %constant.35.clone.refs_1_) | copy-start | bytes 3844
  42.0 38.6 %copy-start.24 = (s32[1,320]{1,0:T(1,128)S(1)}, s32[1,320]{1,0:T(1,128)}, u32[]{:S(2)}) copy-start(s32[1,320]{1,0:T(1,128)} %constant.36.clone.refs_2_) | copy-start | bytes 3844
  42.2 6.9 %collective-permute-start.14 = (bf16[384,384]{1,0:T(8,128)(2,1)S(1)}, bf16[384,384]{1,0:T(8,128)(2,1)S(1)}, u32[]{:S(2)}, u32[]{:S(2)}) collective-permute-start(bf16[384,384]{1,0:T(8,128)(2,1)S(1)} %collective-permute-done.12.refs_8_), channel_id=1, source_target_pairs={{0,2},{2,0},{1,3},{3,1},{4,6},{6,4},{5,7},{7,5},{8,10},{10,8},{9,1... | collective-permute-start | bytes 884744 | tf_op jit(solution)/shard_map/ppermute | solution.py:645
  42.3 5.6 %collective-permute-start.9 = (bf16[128,384]{1,0:T(8,128)(2,1)S(1)}, bf16[128,384]{1,0:T(8,128)(2,1)S(1)}, u32[]{:S(2)}, u32[]{:S(2)}) collective-permute-start(bf16[128,384]{1,0:T(8,128)(2,1)S(1)} %get-tuple-element.96.refs_3_), channel_id=1, source_target_pairs={{0,1},{1,0},{2,3},{3,2},{4,5},{5,4},{6,7},{7,6},{8,9},{9,8},{10,11... | collective-permute-start | bytes 294920 | tf_op jit(solution)/shard_map/ppermute | solution.py:645
  43.7 5.3 %collective-permute-start.11 = (bf16[128,384]{1,0:T(8,128)(2,1)S(1)}, bf16[128,384]{1,0:T(8,128)(2,1)S(1)}, u32[]{:S(2)}, u32[]{:S(2)}) collective-permute-start(bf16[128,384]{1,0:T(8,128)(2,1)S(1)} %get-tuple-element.97), channel_id=1, source_target_pairs={{0,3},{1,2},{2,1},{3,0},{4,7},{5,6},{6,5},{7,4},{8,11},{9,10},{10,... | collective-permute-start | bytes 294920 | tf_op jit(solution)/shard_map/ppermute | solution.py:867
  44.1 5.0 %collective-permute-start.10 = (bf16[128,384]{1,0:T(8,128)(2,1)S(1)}, bf16[128,384]{1,0:T(8,128)(2,1)S(1)}, u32[]{:S(2)}, u32[]{:S(2)}) collective-permute-start(bf16[128,384]{1,0:T(8,128)(2,1)S(1)} %get-tuple-element.97), channel_id=1, source_target_pairs={{0,2},{2,0},{1,3},{3,1},{4,6},{6,4},{5,7},{7,5},{8,10},{10,8},{9,1... | collective-permute-start | bytes 294920 | tf_op jit(solution)/shard_map/ppermute | solution.py:645
  52.0 28.6 %copy-start.18 = (bf16[768,384]{1,0:T(8,128)(2,1)}, bf16[768,384]{1,0:T(8,128)(2,1)S(1)}, u32[]{:S(2)}) copy-start(bf16[768,384]{1,0:T(8,128)(2,1)S(1)} %get-tuple-element.126.refs_10_) | copy-start | bytes 1769476
  91.1 29.6 %copy-start.11 = (s32[20]{0:T(128)S(1)}, s32[20]{0:T(128)}, u32[]{:S(2)}) copy-start(s32[20]{0:T(128)} %dynamic-slice_bitcast_fusion.refs_0_.meta.places) | copy-start | bytes 244
  91.1 29.6 %all-to-all-start.1 = ((bf16[32,40,384]{2,1,0:T(8,128)(2,1)}), bf16[32,40,384]{2,1,0:T(8,128)(2,1)S(1)}, u32[]{:S(2)}, u32[]{:S(2)}) async-start(bf16[32,40,384]{2,1,0:T(8,128)(2,1)} %get-tuple-element.104), calls=%async_computation.1 | async-start | bytes 1966080 | tf_op jit(solution)/shard_map/all_to_all | solution.py:951
  96.0 1.2 copy-start.25
  97.2 1.2 copy-start.26
  98.4 1.0 copy-start.27
  99.4 1.0 copy-start.28
  120.6 15.5 %copy-start.19 = (bf16[768,384]{1,0:T(8,128)(2,1)S(1)}, bf16[768,384]{1,0:T(8,128)(2,1)}, u32[]{:S(2)}) copy-start(bf16[768,384]{1,0:T(8,128)(2,1)} %copy-done.18) | copy-start | bytes 1769476
  120.6 15.5 %copy-start.21 = (bf16[256,768]{1,0:T(8,128)(2,1)S(1)}, bf16[256,768]{1,0:T(8,128)(2,1)}, u32[]{:S(2)}) copy-start(bf16[256,768]{1,0:T(8,128)(2,1)} %copy-done.20) | copy-start | bytes 1179652
  120.7 0.8 copy-start.23
  121.4 14.7 %copy-start.30 = (bf16[512,768]{1,0:T(8,128)(2,1)S(1)}, bf16[512,768]{1,0:T(8,128)(2,1)}, u32[]{:S(2)}) copy-start(bf16[512,768]{1,0:T(8,128)(2,1)} %get-tuple-element.119.refs_3_) | copy-start | bytes 2359300
  123.3 7.2 %collective-permute-start.15 = (bf16[256,384]{1,0:T(8,128)(2,1)S(1)}, bf16[256,384]{1,0:T(8,128)(2,1)S(1)}, u32[]{:S(2)}, u32[]{:S(2)}) collective-permute-start(bf16[256,384]{1,0:T(8,128)(2,1)S(1)} %get-tuple-element.113.refs_1_), channel_id=1, source_target_pairs={{0,1},{1,0},{2,3},{3,2},{4,5},{5,4},{6,7},{7,6},{8,9},{9,8},{10,11... | collective-permute-start | bytes 589832 | tf_op jit(solution)/shard_map/ppermute | solution.py:645
  124.8 5.6 %collective-permute-start.16 = (f32[8,256]{1,0:T(8,128)S(1)}, f32[8,256]{1,0:T(8,128)S(1)}, u32[]{:S(2)}, u32[]{:S(2)}) collective-permute-start(f32[8,256]{1,0:T(8,128)S(1)} %get-tuple-element.114.refs_3_), channel_id=1, source_target_pairs={{0,1},{1,0},{2,3},{3,2},{4,5},{5,4},{6,7},{7,6},{8,9},{9,8},{10,11... | collective-permute-start | bytes 24584 | tf_op jit(solution)/shard_map/ppermute | solution.py:645
  130.5 0.7 copy-start.6
  136.1 1.9 %copy-start.29 = (f32[3,512,512]{2,1,0:T(8,128)S(1)}, f32[3,512,512]{2,1,0:T(8,128)}, u32[]{:S(2)}) copy-start(f32[3,512,512]{2,1,0:T(8,128)} %get-tuple-element.123.refs_7_) | copy-start | bytes 9437188
  138.0 0.9 copy-start.31
  139.0 0.9 copy-start.32
  139.9 0.9 copy-start.33
  140.9 0.9 copy-start.35
  152.3 8.5 %collective-permute-start.18 = (bf16[256,768]{1,0:T(8,128)(2,1)S(1)}, bf16[256,768]{1,0:T(8,128)(2,1)S(1)}, u32[]{:S(2)}, u32[]{:S(2)}) collective-permute-start(bf16[256,768]{1,0:T(8,128)(2,1)S(1)} %get-tuple-element.129), channel_id=1, source_target_pairs={{0,2},{2,0},{1,3},{3,1},{4,6},{6,4},{5,7},{7,5},{8,10},{10,8},{9,1... | collective-permute-start | bytes 1179656 | tf_op jit(solution)/shard_map/ppermute | solution.py:645
  152.5 4.8 %collective-permute-start.20 = (bf16[48,896]{1,0:T(8,128)(2,1)S(1)}, bf16[48,896]{1,0:T(8,128)(2,1)S(1)}, u32[]{:S(2)}, u32[]{:S(2)}) collective-permute-start(bf16[48,896]{1,0:T(8,128)(2,1)S(1)} %get-tuple-element.131), channel_id=1, source_target_pairs={{0,8},{8,16},{16,24},{24,28},{28,20},{20,12},{12,4},{4,0},{1,9},{9... | collective-permute-start | bytes 258056 | tf_op jit(solution)/shard_map/ppermute | solution.py:710
  153.6 4.5 %collective-permute-start.21 = (bf16[48,896]{1,0:T(8,128)(2,1)S(1)}, bf16[48,896]{1,0:T(8,128)(2,1)S(1)}, u32[]{:S(2)}, u32[]{:S(2)}) collective-permute-start(bf16[48,896]{1,0:T(8,128)(2,1)S(1)} %get-tuple-element.132), channel_id=1, source_target_pairs={{8,0},{16,8},{24,16},{28,24},{20,28},{12,20},{4,12},{0,4},{9,1},{1... | collective-permute-start | bytes 258056 | tf_op jit(solution)/shard_map/ppermute | solution.py:711
  158.7 5.6 %collective-permute-start.22 = (bf16[96,896]{1,0:T(8,128)(2,1)S(1)}, bf16[96,896]{1,0:T(8,128)(2,1)S(1)}, u32[]{:S(2)}, u32[]{:S(2)}) collective-permute-start(bf16[96,896]{1,0:T(8,128)(2,1)S(1)} %get-tuple-element.133), channel_id=1, source_target_pairs={{0,8},{8,16},{16,24},{24,28},{28,20},{20,12},{12,4},{4,0},{1,9},{9... | collective-permute-start | bytes 516104 | tf_op jit(solution)/shard_map/ppermute | solution.py:710
  159.9 5.4 %collective-permute-start.23 = (bf16[96,896]{1,0:T(8,128)(2,1)S(1)}, bf16[96,896]{1,0:T(8,128)(2,1)S(1)}, u32[]{:S(2)}, u32[]{:S(2)}) collective-permute-start(bf16[96,896]{1,0:T(8,128)(2,1)S(1)} %get-tuple-element.134), channel_id=1, source_target_pairs={{8,0},{16,8},{24,16},{28,24},{20,28},{12,20},{4,12},{0,4},{9,1},{1... | collective-permute-start | bytes 516104 | tf_op jit(solution)/shard_map/ppermute | solution.py:711
  160.8 15.7 %copy-start.7 = (f32[8,768]{1,0:T(8,128)S(1)}, f32[8,768]{1,0:T(8,128)}, u32[]{:S(2)}) copy-start(f32[8,768]{1,0:T(8,128)} %copy-done.5) | copy-start | bytes 73732
  160.9 15.6 %collective-permute-start.19 = (bf16[256,768]{1,0:T(8,128)(2,1)S(1)}, bf16[256,768]{1,0:T(8,128)(2,1)S(1)}, u32[]{:S(2)}, u32[]{:S(2)}) collective-permute-start(bf16[256,768]{1,0:T(8,128)(2,1)S(1)} %add_convert_fusion.near), channel_id=1, source_target_pairs={{0,1},{1,0},{2,3},{3,2},{4,5},{5,4},{6,7},{7,6},{8,9},{9,8},{10,11... | collective-permute-start | bytes 1179656 | tf_op jit(solution)/shard_map/ppermute | solution.py:645
  165.9 5.5 %collective-permute-start.24 = (bf16[96,896]{1,0:T(8,128)(2,1)S(1)}, bf16[96,896]{1,0:T(8,128)(2,1)S(1)}, u32[]{:S(2)}, u32[]{:S(2)}) collective-permute-start(bf16[96,896]{1,0:T(8,128)(2,1)S(1)} %get-tuple-element.135), channel_id=1, source_target_pairs={{0,8},{8,16},{16,24},{24,28},{28,20},{20,12},{12,4},{4,0},{1,9},{9... | collective-permute-start | bytes 516104 | tf_op jit(solution)/shard_map/ppermute | solution.py:710
  166.6 5.4 %collective-permute-start.25 = (bf16[96,896]{1,0:T(8,128)(2,1)S(1)}, bf16[96,896]{1,0:T(8,128)(2,1)S(1)}, u32[]{:S(2)}, u32[]{:S(2)}) collective-permute-start(bf16[96,896]{1,0:T(8,128)(2,1)S(1)} %get-tuple-element.136), channel_id=1, source_target_pairs={{8,0},{16,8},{24,16},{28,24},{20,28},{12,20},{4,12},{0,4},{9,1},{1... | collective-permute-start | bytes 516104 | tf_op jit(solution)/shard_map/ppermute | solution.py:711
  168.0 6.8 %collective-permute-start.17 = (bf16[256,384]{1,0:T(8,128)(2,1)S(1)}, bf16[256,384]{1,0:T(8,128)(2,1)S(1)}, u32[]{:S(2)}, u32[]{:S(2)}) collective-permute-start(bf16[256,384]{1,0:T(8,128)(2,1)S(1)} %get-tuple-element.117.y_own), channel_id=1, source_target_pairs={{0,1},{1,0},{2,3},{3,2},{4,5},{5,4},{6,7},{7,6},{8,9},{9,8},{10,11... | collective-permute-start | bytes 589832 | tf_op jit(solution)/shard_map/ppermute | solution.py:645
  172.6 5.5 %collective-permute-start.26 = (bf16[96,896]{1,0:T(8,128)(2,1)S(1)}, bf16[96,896]{1,0:T(8,128)(2,1)S(1)}, u32[]{:S(2)}, u32[]{:S(2)}) collective-permute-start(bf16[96,896]{1,0:T(8,128)(2,1)S(1)} %get-tuple-element.137), channel_id=1, source_target_pairs={{0,8},{8,16},{16,24},{24,28},{28,20},{20,12},{12,4},{4,0},{1,9},{9... | collective-permute-start | bytes 516104 | tf_op jit(solution)/shard_map/ppermute | solution.py:710
  174.3 5.4 %collective-permute-start.27 = (bf16[96,896]{1,0:T(8,128)(2,1)S(1)}, bf16[96,896]{1,0:T(8,128)(2,1)S(1)}, u32[]{:S(2)}, u32[]{:S(2)}) collective-permute-start(bf16[96,896]{1,0:T(8,128)(2,1)S(1)} %get-tuple-element.138), channel_id=1, source_target_pairs={{8,0},{16,8},{24,16},{28,24},{20,28},{12,20},{4,12},{0,4},{9,1},{1... | collective-permute-start | bytes 516104 | tf_op jit(solution)/shard_map/ppermute | solution.py:711
  180.3 4.5 %collective-permute-start.28 = (f32[56,896]{1,0:T(8,128)S(1)}, f32[56,896]{1,0:T(8,128)S(1)}, u32[]{:S(2)}, u32[]{:S(2)}) collective-permute-start(f32[56,896]{1,0:T(8,128)S(1)} %get-tuple-element.142), channel_id=1, source_target_pairs={{0,2},{2,0},{1,3},{3,1},{4,6},{6,4},{5,7},{7,5},{8,10},{10,8},{9,1... | collective-permute-start | bytes 602120 | tf_op jit(solution)/shard_map/ppermute | solution.py:645
  180.4 3.9 %collective-permute-start.29 = (f32[48,128]{1,0:T(8,128)S(1)}, f32[48,128]{1,0:T(8,128)S(1)}, u32[]{:S(2)}, u32[]{:S(2)}) collective-permute-start(f32[48,128]{1,0:T(8,128)S(1)} %get-tuple-element.144), channel_id=1, source_target_pairs={{0,1},{1,0},{2,3},{3,2},{4,5},{5,4},{6,7},{7,6},{8,9},{9,8},{10,11... | collective-permute-start | bytes 73736 | tf_op jit(solution)/shard_map/ppermute | solution.py:645
  181.5 3.3 %collective-permute-start.30 = (f32[48,128]{1,0:T(8,128)S(1)}, f32[48,128]{1,0:T(8,128)S(1)}, u32[]{:S(2)}, u32[]{:S(2)}) collective-permute-start(f32[48,128]{1,0:T(8,128)S(1)} %get-tuple-element.145), channel_id=1, source_target_pairs={{0,3},{1,2},{2,1},{3,0},{4,7},{5,6},{6,5},{7,4},{8,11},{9,10},{10,... | collective-permute-start | bytes 73736 | tf_op jit(solution)/shard_map/ppermute | solution.py:1052
  (4 other events, 2.6 us)

commit v8 on v7

--- a/solution.py
+++ b/solution.py
@@ -1024,7 +1024,7 @@
             pltpu.SemaphoreType.DMA((4 + blocks,)),
         ],
         flops=2 * group * model_width * wide * 12,
-        mib=28,
+        mib=60,
         moved=8 * 1024 * 1024,
     )(
         meta, tokens, x_other, h1, q, k, v, probs, db, o_all, wo_full, wall, router_grad,

time: 187 us -> 184 us (0.984)
  local copies, waits for them, and re-layouts: 17.4 us -> 11.5 us
  Pallas kernels: 52.9 us -> 55.6 us
    unnamed x72 -> x62, local copies, waits for them, and re-layouts: 16.2 us -> 10.3 us
    pallas_call x1, Pallas kernels: 10.5 us -> 13.2 us  [body(): kernel_call(functools.partial(attention_backward, heads, buckets, model_w...]
  transfers between devices with their start and end apart: 32 -> 32, of which waited for: 24 -> 23; matrix products, arithmetic and copies ran while one was open for 0% -> 1% of each run, Pallas kernels for 11% -> 11%
where the time goes in v8:
time: 184 us; the launch traced here: 183 us
  Pallas kernels  55.6 us (30%)
  waiting for transfers between devices  50.9 us (28%)
  starting transfers between devices  31.2 us (17%)
  blocking collectives  31.1 us (17%)
  local copies, waits for them, and re-layouts  11.5 us (6%)
  other arithmetic  2.01 us (1%)
    all_to_all x1, blocking collectives, body(): lax.all_to_all(sends.reshape(owners, per_owner, model_width), ('fsdp', 'c...  28.6 us
    pallas_call x1, Pallas kernels, body(): kernel_call(functools.partial(attention_backward, heads, buckets, model_w...  13.2 us
    ppermute x14, waiting for transfers between devices, swap(): return lax.ppermute(value, axis, [(0, 1), (1, 0)])  13.1 us
    all_to_all x1, waiting for transfers between devices, body(): lax.all_to_all(outgoing, ('fsdp', 'ctx', 'tp'), split_axis=0, concat_axis...  12.7 us
    pallas_call x1, Pallas kernels, body(): kernel_call(functools.partial(expert_kernel, owners, capacity, chunks, gr...  10.5 us
    unnamed x62, local copies, waits for them, and re-layouts  10.3 us
    ppermute x14, starting transfers between devices, swap(): return lax.ppermute(value, axis, [(0, 1), (1, 0)])  8.78 us
    pallas_call x1, Pallas kernels, body(): kernel_call(expert_grads, [full(w_in.shape, f32), full(w_out.shape, f32)]...  7.47 us
  transfers between devices with their start and end apart: 32, of which 23 were waited for; matrix products, arithmetic and copies ran while one was open for 1% of the time, Pallas kernels for 11%

profile of v8, /device:TPU:0, one launch (start us, length us, event | category | flops | bytes accessed | tf_op | source)
XLA Modules:
  0.0 183.4 jit_solution(8961455279334917593)
XLA Ops:
  0.7 1.2 dynamic-slice_bitcast_fusion.refs_0_.meta.places
  1.9 1.7 shard_map.292
  4.0 1.1 collective-permute-done.1
  5.1 0.9 pad_maximum_fusion.refs_1_
  6.0 2.9 %collective-permute-start.3 = (bf16[96,896]{1,0:T(8,128)(2,1)S(1)}, bf16[96,896]{1,0:T(8,128)(2,1)S(1)}, u32[]{:S(2)}, u32[]{:S(2)}) collective-permute-start(bf16[96,896]{1,0:T(8,128)(2,1)S(1)} %pad_maximum_fusion.refs_1_), channel_id=1, source_target_pairs={{8,0},{16,8},{24,16},{28,24},{20,28},{12,20},{4,12},{0,4},{9,1},{1... | collective-permute-start | bytes 516104 | tf_op jit(solution)/shard_map/ppermute | solution.py:683
  9.7 0.7 copy-done.14
  10.4 0.7 copy-done.17
  11.0 2.3 %shard_map.293 = (f32[3,128,384]{2,1,0:T(8,128)S(1)}, f32[8,128]{1,0:T(8,128)S(1)}, s32[8,512]{1,0:T(8,128)S(1)}) custom-call(s32[20]{0:T(128)S(1)} %copy-done.9, s32[1,4]{1,0:T(1,128)S(1)} %copy-done.17, f32[6,32]{1,0:T(8,128)S(1)} %bitcast.18), custom_call_target="tpu_custom_call" | custom-call | bytes 1048576 | tf_op jit(solution)/shard_map/pallas_call | solution.py:809
  13.7 1.4 collective-permute-done.2.refs_2_
  15.5 1.6 collective-permute-start.5
  17.1 3.4 %collective-permute-done.4.refs_4_ = bf16[96,896]{1,0:T(8,128)(2,1)S(1)} collective-permute-done((bf16[96,896]{1,0:T(8,128)(2,1)S(1)}, bf16[96,896]{1,0:T(8,128)(2,1)S(1)}, u32[]{:S(2)}, u32[]{:S(2)}) %collective-permute-start.4) | collective-permute-done | bytes 172064 | tf_op jit(solution)/shard_map/ppermute | solution.py:682
  20.5 0.8 collective-permute-start.6
  21.2 1.1 collective-permute-done.5.refs_5_
  22.3 1.6 collective-permute-start.7
  23.9 2.0 %collective-permute-done.6.refs_6_ = bf16[96,896]{1,0:T(8,128)(2,1)S(1)} collective-permute-done((bf16[96,896]{1,0:T(8,128)(2,1)S(1)}, bf16[96,896]{1,0:T(8,128)(2,1)S(1)}, u32[]{:S(2)}, u32[]{:S(2)}) %collective-permute-start.6) | collective-permute-done | bytes 172064 | tf_op jit(solution)/shard_map/ppermute | solution.py:682
  25.9 0.8 collective-permute-start.8
  26.6 1.7 collective-permute-done.7.refs_7_
  28.3 3.0 %collective-permute-done.8.refs_8_ = bf16[96,896]{1,0:T(8,128)(2,1)S(1)} collective-permute-done((bf16[96,896]{1,0:T(8,128)(2,1)S(1)}, bf16[96,896]{1,0:T(8,128)(2,1)S(1)}, u32[]{:S(2)}, u32[]{:S(2)}) %collective-permute-start.8) | collective-permute-done | bytes 172064 | tf_op jit(solution)/shard_map/ppermute | solution.py:687
  31.3 0.7 copy-done.10
  31.9 0.7 shard_map.294
  32.8 1.6 collective-permute-start.12
  34.4 1.1 copy-done.4
  36.2 5.8 %shard_map.295 = (bf16[512,768]{1,0:T(8,128)(2,1)}, bf16[512,256]{1,0:T(8,128)(2,1)}, bf16[512,256]{1,0:T(8,128)(2,1)}, bf16[512,256]{1,0:T(8,128)(2,1)}, f32[3,...) custom-call(s32[20]{0:T(128)S(1)} %copy-done.11, ...), custom_call_target="tpu_custom_call" | custom-call | flops 4026531840 | bytes 8388608 | tf_op jit(solution)/shard_map/pallas_call | solution.py:841
  42.3 1.4 collective-permute-start.9
  44.4 3.5 %collective-permute-done.9.refs_4_ = bf16[128,384]{1,0:T(8,128)(2,1)S(1)} collective-permute-done((bf16[128,384]{1,0:T(8,128)(2,1)S(1)}, bf16[128,384]{1,0:T(8,128)(2,1)S(1)}, u32[]{:S(2)}, u32[]{:S(2)}) %collective-permute-start.9) | collective-permute-done | bytes 98336 | tf_op jit(solution)/shard_map/ppermute | solution.py:645
  47.9 1.2 collective-permute-done.11.refs_6_
  49.1 2.9 %shard_map.296 = (f32[256,768]{1,0:T(8,128)S(1)}, bf16[640,768]{1,0:T(8,128)(2,1)S(1)}, bf16[768,384]{1,0:T(8,128)(2,1)S(1)}) custom-call(s32[20]{0:T(128)S(1)} %copy-done.11, bf16[256,768]{1,0:T(8,128)(2,1)S(1)} %copy-done.5, bf16[256,768]{1,0:T(8,128)(2,1)S(1)} %copy-done.3, bf16[128,384]{1,0:T(8,128)(2,1)S(1)} %get-tuple-element.96.refs_3_, ...), custom_call_target="tpu_custom_call" | custom-call | flops 805306368 | bytes 6291456 | tf_op jit(solution)/shard_map/pallas_call | solution.py:880
  52.0 28.6 %all_to_all.10 = bf16[16,40,768]{2,1,0:T(8,128)(2,1)S(1)} all-to-all(bf16[16,40,768]{2,1,0:T(8,128)(2,1)S(1)} %bitcast.16), channel_id=1, replica_groups=mesh['fsdp'=8,'ctx'=2,'tp'=2] {'fsdp','ctx'}, dimensions={0} | all-to-all | bytes 1966080 | tf_op jit(solution)/shard_map/all_to_all | solution.py:896
  80.7 10.5 %shard_map.297 = (bf16[32,40,384]{2,1,0:T(8,128)(2,1)}, bf16[2,160,768]{2,1,0:T(8,128)(2,1)}, bf16[2,160,768]{2,1,0:T(8,128)(2,1)}, bf16[2,160,1536]{2,1,0:T(8,128)(2,1)}, bf16[2,160,1536]{2,1,0:T(8,128)(2,1)}) custom-call(bf16[640,768]{1,0:T(8,128)(2,1)S(1)} %bitcast.17, s32[320,1]{1,0:T(8,128)S(1)} %copy-done.23, s32[1,320]{1,0:T(1,128)S(1)} %copy-done.25, ...), custom_call_target="tpu_custom_call" | custom-call | flops 3019898880 | bytes 12582912 | tf_op jit(solution)/shard_map/pallas_call | solution.py:917
  91.2 4.9 %all-to-all-start.1 = ((bf16[32,40,384]{2,1,0:T(8,128)(2,1)}), bf16[32,40,384]{2,1,0:T(8,128)(2,1)S(1)}, u32[]{:S(2)}, u32[]{:S(2)}) async-start(bf16[32,40,384]{2,1,0:T(8,128)(2,1)} %get-tuple-element.104), calls=%async_computation.1 | async-start | bytes 1966080 | tf_op jit(solution)/shard_map/all_to_all | solution.py:951
  96.1 1.2 copy-done.26
  97.3 1.2 copy-done.27
  98.5 1.0 copy-done.28
  99.5 1.0 copy-done.29
  100.5 7.5 %shard_map.298 = (f32[2,768,1536]{2,1,0:T(8,128)}, f32[2,1536,768]{2,1,0:T(8,128)}) custom-call(bf16[2,160,768]{2,1,0:T(8,128)(2,1)S(1)} %copy-done.28, bf16[2,160,1536]{2,1,0:T(8,128)(2,1)S(1)} %copy-done.27, bf16[2,160,1536]{2,1,0:T(8,128)(2,1)S(1)} %copy-done.26, bf16[2,160,768]{2,1,0:T(8,128)(2,1)S(1)} %copy-done.29), custom_call_target="tpu_custom_call" | custom-call | flops 1509949440 | bytes 25165824 | tf_op jit(solution)/shard_map/pallas_call | solution.py:957
  108.0 12.7 %all-to-all-done.1 = bf16[32,40,384]{2,1,0:T(8,128)(2,1)S(1)} async-done(((bf16[32,40,384]{2,1,0:T(8,128)(2,1)}), bf16[32,40,384]{2,1,0:T(8,128)(2,1)S(1)}, u32[]{:S(2)}, u32[]{:S(2)}) %all-to-all-start.1) | async-done | bytes 983072 | tf_op jit(solution)/shard_map/all_to_all | solution.py:951
  120.7 1.9 %shard_map.299 = (bf16[256,384]{1,0:T(8,128)(2,1)S(1)}, bf16[256,384]{1,0:T(8,128)(2,1)S(1)}, f32[8,256]{1,0:T(8,128)S(1)}) custom-call(s32[20]{0:T(128)S(1)} %copy-done.12, bf16[1280,384]{1,0:T(8,128)(2,1)S(1)} %bitcast.15, bf16[256,768]{1,0:T(8,128)(2,1)S(1)} %copy-done.3, s32[1,256]{1,0:T(1,128)S(1)} %bitcast.20, s32[1,256]{1,0:T(1,128)S(1)} %bitcast.23, ...), custom_call_target="tpu_custom_call" | custom-call | flops 503316480 | bytes 2097152 | tf_op jit(solution)/shard_map/pallas_call | solution.py:974
  122.6 1.5 collective-permute-start.15
  124.7 5.1 %collective-permute-done.16.refs_4_ = f32[8,256]{1,0:T(8,128)S(1)} collective-permute-done((f32[8,256]{1,0:T(8,128)S(1)}, f32[8,256]{1,0:T(8,128)S(1)}, u32[]{:S(2)}, u32[]{:S(2)}) %collective-permute-start.16) | collective-permute-done | bytes 8224 | tf_op jit(solution)/shard_map/ppermute | solution.py:645
  129.8 2.5 %shard_map.300 = (f32[256,768]{1,0:T(8,128)S(1)}, bf16[256,768]{1,0:T(8,128)(2,1)S(1)}, bf16[768,128]{1,0:T(8,128)(2,1)S(1)}, f32[256,128]{1,0:T(8,128)S(1)}) custom-call(s32[20]{0:T(128)S(1)} %copy-done.12, bf16[256,384]{1,0:T(8,128)(2,1)S(1)} %get-tuple-element.113.refs_1_, bf16[256,384]{1,0:T(8,128)(2,1)S(1)} %collective-permute-done.15.refs_2_, ...), custom_call_target="tpu_custom_call" | custom-call | flops 150994944 | bytes 6291456 | tf_op jit(solution)/shard_map/pallas_call | solution.py:988
  132.3 2.5 %all_gather.3.refs_8_ = bf16[512,768]{1,0:T(8,128)(2,1)} all-gather(bf16[256,768]{1,0:T(8,128)(2,1)S(1)} %get-tuple-element.124), channel_id=1, replica_groups=mesh['fsdp'=8,'ctx'=2,'tp'=2] {'ctx'}, dimensions={0}, use_global_device_ids=true | all-gather | bytes 1179648 | tf_op jit(solution)/shard_map/all_gather | solution.py:1002
  134.8 13.2 %shard_map.302 = (bf16[768,896]{1,0:T(8,128)(2,1)}, bf16[48,896]{1,0:T(8,128)(2,1)}, bf16[48,896]{1,0:T(8,128)(2,1)}, bf16[256,768]{1,0:T(8,128)(2,1)}, bf16[256,768]{1,0:T(8,128)(2,1)}) custom-call(s32[20]{0:T(128)} %dynamic-slice_bitcast_fusion.refs_0_.meta.places, bf16[256,768]{1,0:T(8,128)(2,1)} %x_own.1, bf16[256,768]{1,0:T(8,128)(2,1)} %copy-done.21, ...), custom_call_target="tpu_custom_call" | custom-call | flops 6039797760 | bytes 8388608 | tf_op jit(solution)/shard_map/pallas_call | solution.py:1005
  148.2 1.1 collective-permute-start.20
  149.3 1.0 collective-permute-start.21
  150.3 3.0 %collective-permute-done.20.from_left = bf16[48,896]{1,0:T(8,128)(2,1)S(1)} collective-permute-done((bf16[48,896]{1,0:T(8,128)(2,1)}, bf16[48,896]{1,0:T(8,128)(2,1)S(1)}, u32[]{:S(2)}, u32[]{:S(2)}) %collective-permute-start.20) | collective-permute-done | bytes 86048 | tf_op jit(solution)/shard_map/ppermute | solution.py:710
  153.2 0.8 collective-permute-done.21.from_right
  154.0 1.3 copy-done
  156.0 1.2 collective-permute-start.22
  157.1 0.9 collective-permute-start.23
  158.0 1.1 add_convert_fusion.near
  159.2 1.0 collective-permute-start.19
  160.2 1.3 collective-permute-done.22.from_left
  161.5 1.0 collective-permute-done.23.from_right
  163.8 1.4 collective-permute-start.25
  165.5 3.1 %collective-permute-done.24.from_left = bf16[96,896]{1,0:T(8,128)(2,1)S(1)} collective-permute-done((bf16[96,896]{1,0:T(8,128)(2,1)S(1)}, bf16[96,896]{1,0:T(8,128)(2,1)S(1)}, u32[]{:S(2)}, u32[]{:S(2)}) %collective-permute-start.24) | collective-permute-done | bytes 172064 | tf_op jit(solution)/shard_map/ppermute | solution.py:710
  169.8 1.6 collective-permute-start.26
  171.9 1.2 collective-permute-done.17.y_tp
  173.2 1.6 shard_map.301
  174.7 1.3 shard_map.303
  176.0 0.9 collective-permute-done.27.from_right
  177.6 1.1 collective-permute-start.29
  178.7 0.7 collective-permute-start.30
  179.5 2.0 %collective-permute-done.29.refs_4_ = f32[48,128]{1,0:T(8,128)S(1)} collective-permute-done((f32[48,128]{1,0:T(8,128)S(1)}, f32[48,128]{1,0:T(8,128)S(1)}, u32[]{:S(2)}, u32[]{:S(2)}) %collective-permute-start.29) | collective-permute-done | bytes 24608 | tf_op jit(solution)/shard_map/ppermute | solution.py:645
  182.0 1.4 shard_map.308
  (84 shorter events, 9.6 us)
Async XLA Ops:
  3.6 1.6 collective-permute-start.1
  6.0 7.7 %collective-permute-start.3 = (bf16[96,896]{1,0:T(8,128)(2,1)S(1)}, bf16[96,896]{1,0:T(8,128)(2,1)S(1)}, u32[]{:S(2)}, u32[]{:S(2)}) collective-permute-start(bf16[96,896]{1,0:T(8,128)(2,1)S(1)} %pad_maximum_fusion.refs_1_), channel_id=1, source_target_pairs={{8,0},{16,8},{24,16},{28,24},{20,28},{12,20},{4,12},{0,4},{9,1},{1... | collective-permute-start | bytes 516104 | tf_op jit(solution)/shard_map/ppermute | solution.py:683
  8.9 6.2 %collective-permute-start.2 = (bf16[96,896]{1,0:T(8,128)(2,1)S(1)}, bf16[96,896]{1,0:T(8,128)(2,1)S(1)}, u32[]{:S(2)}, u32[]{:S(2)}) collective-permute-start(bf16[96,896]{1,0:T(8,128)(2,1)S(1)} %pad_maximum_fusion.refs_1_), channel_id=1, source_target_pairs={{0,8},{8,16},{16,24},{24,28},{28,20},{20,12},{12,4},{4,0},{1,9},{9... | collective-permute-start | bytes 516104 | tf_op jit(solution)/shard_map/ppermute | solution.py:682
  9.0 0.7 copy-start.9
  9.7 0.7 copy-start.14
  10.4 0.7 copy-start.17
  15.1 5.4 %collective-permute-start.4 = (bf16[96,896]{1,0:T(8,128)(2,1)S(1)}, bf16[96,896]{1,0:T(8,128)(2,1)S(1)}, u32[]{:S(2)}, u32[]{:S(2)}) collective-permute-start(bf16[96,896]{1,0:T(8,128)(2,1)S(1)} %collective-permute-done.2.refs_2_), channel_id=1, source_target_pairs={{0,8},{8,16},{16,24},{24,28},{28,20},{20,12},{12,4},{4,0},{1,9},{9... | collective-permute-start | bytes 516104 | tf_op jit(solution)/shard_map/ppermute | solution.py:682
  15.5 18.9 %collective-permute-start = (bf16[256,768]{1,0:T(8,128)(2,1)}, bf16[256,768]{1,0:T(8,128)(2,1)S(1)}, u32[]{:S(2)}, u32[]{:S(2)}) collective-permute-start(bf16[256,768]{1,0:T(8,128)(2,1)} %x_own.1), channel_id=1, source_target_pairs={{0,2},{2,0},{1,3},{3,1},{4,6},{6,4},{5,7},{7,5},{8,10},{10,8},{9,1... | collective-permute-start | bytes 1179656 | tf_op jit(solution)/shard_map/ppermute | solution.py:645
  15.5 6.8 %collective-permute-start.5 = (bf16[96,896]{1,0:T(8,128)(2,1)S(1)}, bf16[96,896]{1,0:T(8,128)(2,1)S(1)}, u32[]{:S(2)}, u32[]{:S(2)}) collective-permute-start(bf16[96,896]{1,0:T(8,128)(2,1)S(1)} %collective-permute-done.3.refs_3_), channel_id=1, source_target_pairs={{8,0},{16,8},{24,16},{28,24},{20,28},{12,20},{4,12},{0,4},{9,1},{1... | collective-permute-start | bytes 516104 | tf_op jit(solution)/shard_map/ppermute | solution.py:683
  20.5 5.4 %collective-permute-start.6 = (bf16[96,896]{1,0:T(8,128)(2,1)S(1)}, bf16[96,896]{1,0:T(8,128)(2,1)S(1)}, u32[]{:S(2)}, u32[]{:S(2)}) collective-permute-start(bf16[96,896]{1,0:T(8,128)(2,1)S(1)} %collective-permute-done.4.refs_4_), channel_id=1, source_target_pairs={{0,8},{8,16},{16,24},{24,28},{28,20},{20,12},{12,4},{4,0},{1,9},{9... | collective-permute-start | bytes 516104 | tf_op jit(solution)/shard_map/ppermute | solution.py:682
  22.3 6.0 %collective-permute-start.7 = (bf16[96,896]{1,0:T(8,128)(2,1)S(1)}, bf16[96,896]{1,0:T(8,128)(2,1)S(1)}, u32[]{:S(2)}, u32[]{:S(2)}) collective-permute-start(bf16[96,896]{1,0:T(8,128)(2,1)S(1)} %collective-permute-done.5.refs_5_), channel_id=1, source_target_pairs={{8,0},{16,8},{24,16},{28,24},{20,28},{12,20},{4,12},{0,4},{9,1},{1... | collective-permute-start | bytes 516104 | tf_op jit(solution)/shard_map/ppermute | solution.py:683
  25.9 5.4 %collective-permute-start.8 = (bf16[96,896]{1,0:T(8,128)(2,1)S(1)}, bf16[96,896]{1,0:T(8,128)(2,1)S(1)}, u32[]{:S(2)}, u32[]{:S(2)}) collective-permute-start(bf16[96,896]{1,0:T(8,128)(2,1)S(1)} %collective-permute-done.6.refs_6_), channel_id=1, source_target_pairs={{0,8},{8,16},{16,24},{24,28},{28,20},{20,12},{12,4},{4,0},{1,9},{9... | collective-permute-start | bytes 516104 | tf_op jit(solution)/shard_map/ppermute | solution.py:687
  31.3 0.7 copy-start.10
  32.7 97.1 %copy-start.2 = (bf16[768,640]{1,0:T(8,128)(2,1)}, bf16[768,640]{1,0:T(8,128)(2,1)S(1)}, u32[]{:S(2)}) copy-start(bf16[768,640]{1,0:T(8,128)(2,1)S(1)} %get-tuple-element.92.refs_3_.refs_11_.refs_7_) | copy-start | bytes 2949124
  32.7 16.4 %collective-permute-start.13 = (bf16[384,384]{1,0:T(8,128)(2,1)S(1)}, bf16[384,384]{1,0:T(8,128)(2,1)S(1)}, u32[]{:S(2)}, u32[]{:S(2)}) collective-permute-start(bf16[384,384]{1,0:T(8,128)(2,1)S(1)} %get-tuple-element.98.refs_7_), channel_id=1, source_target_pairs={{0,2},{2,0},{1,3},{3,1},{4,6},{6,4},{5,7},{7,5},{8,10},{10,8},{9,1... | collective-permute-start | bytes 884744 | tf_op jit(solution)/shard_map/ppermute | solution.py:645
  32.8 9.4 %collective-permute-start.12 = (bf16[384,384]{1,0:T(8,128)(2,1)S(1)}, bf16[384,384]{1,0:T(8,128)(2,1)S(1)}, u32[]{:S(2)}, u32[]{:S(2)}) collective-permute-start(bf16[384,384]{1,0:T(8,128)(2,1)S(1)} %get-tuple-element.98.refs_7_), channel_id=1, source_target_pairs={{0,1},{1,0},{2,3},{3,2},{4,5},{5,4},{6,7},{7,6},{8,9},{9,8},{10,11... | collective-permute-start | bytes 884744 | tf_op jit(solution)/shard_map/ppermute | solution.py:645
  34.4 7.6 %copy-start.21 = (bf16[256,768]{1,0:T(8,128)(2,1)}, bf16[256,768]{1,0:T(8,128)(2,1)S(1)}, u32[]{:S(2)}) copy-start(bf16[256,768]{1,0:T(8,128)(2,1)S(1)} %collective-permute-done.refs_2_) | copy-start | bytes 1179652
  34.4 1.1 copy-start.4
  35.5 0.7 copy-start.11
  36.2 12.9 %copy-start.3 = (bf16[256,768]{1,0:T(8,128)(2,1)S(1)}, bf16[256,768]{1,0:T(8,128)(2,1)}, u32[]{:S(2)}) copy-start(bf16[256,768]{1,0:T(8,128)(2,1)} %refs_6_.1) | copy-start | bytes 1179652
  36.2 12.9 %copy-start.5 = (bf16[256,768]{1,0:T(8,128)(2,1)S(1)}, bf16[256,768]{1,0:T(8,128)(2,1)}, u32[]{:S(2)}) copy-start(bf16[256,768]{1,0:T(8,128)(2,1)} %x_own.1) | copy-start | bytes 1179652
  36.2 12.9 %copy-start.7 = (s32[640,1]{1,0:T(8,128)S(1)}, s32[640,1]{1,0:T(8,128)}, u32[]{:S(2)}) copy-start(s32[640,1]{1,0:T(8,128)} %constant.34.clone.refs_16_) | copy-start | bytes 7684
  36.2 12.9 %copy-start.8 = (s32[640,1]{1,0:T(8,128)S(1)}, s32[640,1]{1,0:T(8,128)}, u32[]{:S(2)}) copy-start(s32[640,1]{1,0:T(8,128)} %constant.33.clone.refs_15_) | copy-start | bytes 7684
  36.2 12.9 %copy-start.15 = (s32[256,1]{0,1:T(1,128)S(1)}, s32[256,1]{0,1:T(1,128)}, u32[]{:S(2)}) copy-start(s32[256,1]{0,1:T(1,128)} %param.34) | copy-start | bytes 3076
  36.2 12.9 %copy-start.16 = (s32[256]{0:T(256)S(1)}, s32[256]{0:T(256)}, u32[]{:S(2)}) copy-start(s32[256]{0:T(256)} %param.35) | copy-start | bytes 3076
  36.2 44.4 %copy-start.19 = (bf16[2,1536,768]{2,1,0:T(8,128)(2,1)S(1)}, bf16[2,1536,768]{2,1,0:T(8,128)(2,1)}, u32[]{:S(2)}) copy-start(bf16[2,1536,768]{2,1,0:T(8,128)(2,1)} %refs_4_.3) | copy-start | bytes 14155780
  42.0 38.6 %copy-start.30 = (bf16[512,256]{1,0:T(8,128)(2,1)}, bf16[512,256]{1,0:T(8,128)(2,1)S(1)}, u32[]{:S(2)}) copy-start(bf16[512,256]{1,0:T(8,128)(2,1)S(1)} %get-tuple-element.125.refs_9_) | copy-start | bytes 786436
  42.0 38.6 %copy-start.18 = (bf16[2,768,1536]{2,1,0:T(8,128)(2,1)S(1)}, bf16[2,768,1536]{2,1,0:T(8,128)(2,1)}, u32[]{:S(2)}) copy-start(bf16[2,768,1536]{2,1,0:T(8,128)(2,1)} %refs_3_.3) | copy-start | bytes 14155780
  42.0 38.6 %copy-start.23 = (s32[320,1]{1,0:T(8,128)S(1)}, s32[320,1]{1,0:T(8,128)}, u32[]{:S(2)}) copy-start(s32[320,1]{1,0:T(8,128)} %constant.35.clone.refs_1_) | copy-start | bytes 3844
  42.0 38.6 %copy-start.25 = (s32[1,320]{1,0:T(1,128)S(1)}, s32[1,320]{1,0:T(1,128)}, u32[]{:S(2)}) copy-start(s32[1,320]{1,0:T(1,128)} %constant.36.clone.refs_2_) | copy-start | bytes 3844
  42.2 6.9 %collective-permute-start.14 = (bf16[384,384]{1,0:T(8,128)(2,1)S(1)}, bf16[384,384]{1,0:T(8,128)(2,1)S(1)}, u32[]{:S(2)}, u32[]{:S(2)}) collective-permute-start(bf16[384,384]{1,0:T(8,128)(2,1)S(1)} %collective-permute-done.12.refs_8_), channel_id=1, source_target_pairs={{0,2},{2,0},{1,3},{3,1},{4,6},{6,4},{5,7},{7,5},{8,10},{10,8},{9,1... | collective-permute-start | bytes 884744 | tf_op jit(solution)/shard_map/ppermute | solution.py:645
  42.3 5.6 %collective-permute-start.9 = (bf16[128,384]{1,0:T(8,128)(2,1)S(1)}, bf16[128,384]{1,0:T(8,128)(2,1)S(1)}, u32[]{:S(2)}, u32[]{:S(2)}) collective-permute-start(bf16[128,384]{1,0:T(8,128)(2,1)S(1)} %get-tuple-element.96.refs_3_), channel_id=1, source_target_pairs={{0,1},{1,0},{2,3},{3,2},{4,5},{5,4},{6,7},{7,6},{8,9},{9,8},{10,11... | collective-permute-start | bytes 294920 | tf_op jit(solution)/shard_map/ppermute | solution.py:645
  43.7 5.3 %collective-permute-start.11 = (bf16[128,384]{1,0:T(8,128)(2,1)S(1)}, bf16[128,384]{1,0:T(8,128)(2,1)S(1)}, u32[]{:S(2)}, u32[]{:S(2)}) collective-permute-start(bf16[128,384]{1,0:T(8,128)(2,1)S(1)} %get-tuple-element.97), channel_id=1, source_target_pairs={{0,3},{1,2},{2,1},{3,0},{4,7},{5,6},{6,5},{7,4},{8,11},{9,10},{10,... | collective-permute-start | bytes 294920 | tf_op jit(solution)/shard_map/ppermute | solution.py:867
  44.1 5.0 %collective-permute-start.10 = (bf16[128,384]{1,0:T(8,128)(2,1)S(1)}, bf16[128,384]{1,0:T(8,128)(2,1)S(1)}, u32[]{:S(2)}, u32[]{:S(2)}) collective-permute-start(bf16[128,384]{1,0:T(8,128)(2,1)S(1)} %get-tuple-element.97), channel_id=1, source_target_pairs={{0,2},{2,0},{1,3},{3,1},{4,6},{6,4},{5,7},{7,5},{8,10},{10,8},{9,1... | collective-permute-start | bytes 294920 | tf_op jit(solution)/shard_map/ppermute | solution.py:645
  52.0 39.1 %copy-start.20 = (bf16[768,384]{1,0:T(8,128)(2,1)}, bf16[768,384]{1,0:T(8,128)(2,1)S(1)}, u32[]{:S(2)}) copy-start(bf16[768,384]{1,0:T(8,128)(2,1)S(1)} %get-tuple-element.126.refs_10_) | copy-start | bytes 1769476
  91.1 29.6 %copy-start.12 = (s32[20]{0:T(128)S(1)}, s32[20]{0:T(128)}, u32[]{:S(2)}) copy-start(s32[20]{0:T(128)} %dynamic-slice_bitcast_fusion.refs_0_.meta.places) | copy-start | bytes 244
  91.1 29.6 %copy-start.24 = (s32[2,1280]{1,0:T(2,128)S(1)}, s32[2,1280]{1,0:T(2,128)}, u32[]{:S(2)}) copy-start(s32[2,1280]{1,0:T(2,128)} %constant.37.clone.refs_5_) | copy-start | bytes 30724
  91.2 29.6 %all-to-all-start.1 = ((bf16[32,40,384]{2,1,0:T(8,128)(2,1)}), bf16[32,40,384]{2,1,0:T(8,128)(2,1)S(1)}, u32[]{:S(2)}, u32[]{:S(2)}) async-start(bf16[32,40,384]{2,1,0:T(8,128)(2,1)} %get-tuple-element.104), calls=%async_computation.1 | async-start | bytes 1966080 | tf_op jit(solution)/shard_map/all_to_all | solution.py:951
  96.1 1.2 copy-start.26
  97.3 1.2 copy-start.27
  98.5 1.0 copy-start.28
  99.5 1.0 copy-start.29
  122.6 7.2 %collective-permute-start.15 = (bf16[256,384]{1,0:T(8,128)(2,1)S(1)}, bf16[256,384]{1,0:T(8,128)(2,1)S(1)}, u32[]{:S(2)}, u32[]{:S(2)}) collective-permute-start(bf16[256,384]{1,0:T(8,128)(2,1)S(1)} %get-tuple-element.113.refs_1_), channel_id=1, source_target_pairs={{0,1},{1,0},{2,3},{3,2},{4,5},{5,4},{6,7},{7,6},{8,9},{9,8},{10,11... | collective-permute-start | bytes 589832 | tf_op jit(solution)/shard_map/ppermute | solution.py:645
  124.1 5.7 %collective-permute-start.16 = (f32[8,256]{1,0:T(8,128)S(1)}, f32[8,256]{1,0:T(8,128)S(1)}, u32[]{:S(2)}, u32[]{:S(2)}) collective-permute-start(f32[8,256]{1,0:T(8,128)S(1)} %get-tuple-element.114.refs_3_), channel_id=1, source_target_pairs={{0,1},{1,0},{2,3},{3,2},{4,5},{5,4},{6,7},{7,6},{8,9},{9,8},{10,11... | collective-permute-start | bytes 24584 | tf_op jit(solution)/shard_map/ppermute | solution.py:645
  132.3 2.5 %copy-start.22 = (bf16[768,128]{1,0:T(8,128)(2,1)}, bf16[768,128]{1,0:T(8,128)(2,1)S(1)}, u32[]{:S(2)}) copy-start(bf16[768,128]{1,0:T(8,128)(2,1)S(1)} %get-tuple-element.127.refs_12_) | copy-start | bytes 589828
  134.8 19.2 %copy-start.13 = (s32[20]{0:T(128)S(1)}, s32[20]{0:T(128)}, u32[]{:S(2)}) copy-start(s32[20]{0:T(128)} %dynamic-slice_bitcast_fusion.refs_0_.meta.places) | copy-start | bytes 244
  148.0 10.0 %collective-permute-start.18 = (bf16[256,768]{1,0:T(8,128)(2,1)}, bf16[256,768]{1,0:T(8,128)(2,1)S(1)}, u32[]{:S(2)}, u32[]{:S(2)}) collective-permute-start(bf16[256,768]{1,0:T(8,128)(2,1)} %get-tuple-element.129), channel_id=1, source_target_pairs={{0,2},{2,0},{1,3},{3,1},{4,6},{6,4},{5,7},{7,5},{8,10},{10,8},{9,1... | collective-permute-start | bytes 1179656 | tf_op jit(solution)/shard_map/ppermute | solution.py:645
  148.2 5.0 %collective-permute-start.20 = (bf16[48,896]{1,0:T(8,128)(2,1)}, bf16[48,896]{1,0:T(8,128)(2,1)S(1)}, u32[]{:S(2)}, u32[]{:S(2)}) collective-permute-start(bf16[48,896]{1,0:T(8,128)(2,1)} %get-tuple-element.131), channel_id=1, source_target_pairs={{0,8},{8,16},{16,24},{24,28},{28,20},{20,12},{12,4},{4,0},{1,9},{9... | collective-permute-start | bytes 258056 | tf_op jit(solution)/shard_map/ppermute | solution.py:710
  149.3 4.7 %collective-permute-start.21 = (bf16[48,896]{1,0:T(8,128)(2,1)}, bf16[48,896]{1,0:T(8,128)(2,1)S(1)}, u32[]{:S(2)}, u32[]{:S(2)}) collective-permute-start(bf16[48,896]{1,0:T(8,128)(2,1)} %get-tuple-element.132), channel_id=1, source_target_pairs={{8,0},{16,8},{24,16},{28,24},{20,28},{12,20},{4,12},{0,4},{9,1},{1... | collective-permute-start | bytes 258056 | tf_op jit(solution)/shard_map/ppermute | solution.py:711
  154.0 1.3 copy-start
  155.4 7.2 %copy-start.1 = (bf16[768,896]{1,0:T(8,128)(2,1)S(1)}, bf16[768,896]{1,0:T(8,128)(2,1)}, u32[]{:S(2)}) copy-start(bf16[768,896]{1,0:T(8,128)(2,1)} %get-tuple-element.130.right_mine.left_mine.mine) | copy-start | bytes 4128772
  156.0 5.6 %collective-permute-start.22 = (bf16[96,896]{1,0:T(8,128)(2,1)S(1)}, bf16[96,896]{1,0:T(8,128)(2,1)S(1)}, u32[]{:S(2)}, u32[]{:S(2)}) collective-permute-start(bf16[96,896]{1,0:T(8,128)(2,1)S(1)} %get-tuple-element.133), channel_id=1, source_target_pairs={{0,8},{8,16},{16,24},{24,28},{28,20},{20,12},{12,4},{4,0},{1,9},{9... | collective-permute-start | bytes 516104 | tf_op jit(solution)/shard_map/ppermute | solution.py:710
  157.1 5.4 %collective-permute-start.23 = (bf16[96,896]{1,0:T(8,128)(2,1)S(1)}, bf16[96,896]{1,0:T(8,128)(2,1)S(1)}, u32[]{:S(2)}, u32[]{:S(2)}) collective-permute-start(bf16[96,896]{1,0:T(8,128)(2,1)S(1)} %get-tuple-element.134), channel_id=1, source_target_pairs={{8,0},{16,8},{24,16},{28,24},{20,28},{12,20},{4,12},{0,4},{9,1},{1... | collective-permute-start | bytes 516104 | tf_op jit(solution)/shard_map/ppermute | solution.py:711
  158.0 16.7 %copy-start.6 = (bf16[256,768]{1,0:T(8,128)(2,1)S(1)}, bf16[256,768]{1,0:T(8,128)(2,1)}, u32[]{:S(2)}) copy-start(bf16[256,768]{1,0:T(8,128)(2,1)} %x_own.1) | copy-start | bytes 1179652
  159.2 15.5 %collective-permute-start.19 = (bf16[256,768]{1,0:T(8,128)(2,1)S(1)}, bf16[256,768]{1,0:T(8,128)(2,1)S(1)}, u32[]{:S(2)}, u32[]{:S(2)}) collective-permute-start(bf16[256,768]{1,0:T(8,128)(2,1)S(1)} %add_convert_fusion.near), channel_id=1, source_target_pairs={{0,1},{1,0},{2,3},{3,2},{4,5},{5,4},{6,7},{7,6},{8,9},{9,8},{10,11... | collective-permute-start | bytes 1179656 | tf_op jit(solution)/shard_map/ppermute | solution.py:645
  163.2 5.5 %collective-permute-start.24 = (bf16[96,896]{1,0:T(8,128)(2,1)S(1)}, bf16[96,896]{1,0:T(8,128)(2,1)S(1)}, u32[]{:S(2)}, u32[]{:S(2)}) collective-permute-start(bf16[96,896]{1,0:T(8,128)(2,1)S(1)} %get-tuple-element.135), channel_id=1, source_target_pairs={{0,8},{8,16},{16,24},{24,28},{28,20},{20,12},{12,4},{4,0},{1,9},{9... | collective-permute-start | bytes 516104 | tf_op jit(solution)/shard_map/ppermute | solution.py:710
  163.8 5.4 %collective-permute-start.25 = (bf16[96,896]{1,0:T(8,128)(2,1)S(1)}, bf16[96,896]{1,0:T(8,128)(2,1)S(1)}, u32[]{:S(2)}, u32[]{:S(2)}) collective-permute-start(bf16[96,896]{1,0:T(8,128)(2,1)S(1)} %get-tuple-element.136), channel_id=1, source_target_pairs={{8,0},{16,8},{24,16},{28,24},{20,28},{12,20},{4,12},{0,4},{9,1},{1... | collective-permute-start | bytes 516104 | tf_op jit(solution)/shard_map/ppermute | solution.py:711
  165.3 7.9 %collective-permute-start.17 = (bf16[256,384]{1,0:T(8,128)(2,1)S(1)}, bf16[256,384]{1,0:T(8,128)(2,1)S(1)}, u32[]{:S(2)}, u32[]{:S(2)}) collective-permute-start(bf16[256,384]{1,0:T(8,128)(2,1)S(1)} %get-tuple-element.117.y_own), channel_id=1, source_target_pairs={{0,1},{1,0},{2,3},{3,2},{4,5},{5,4},{6,7},{7,6},{8,9},{9,8},{10,11... | collective-permute-start | bytes 589832 | tf_op jit(solution)/shard_map/ppermute | solution.py:645
  169.8 6.2 %collective-permute-start.26 = (bf16[96,896]{1,0:T(8,128)(2,1)S(1)}, bf16[96,896]{1,0:T(8,128)(2,1)S(1)}, u32[]{:S(2)}, u32[]{:S(2)}) collective-permute-start(bf16[96,896]{1,0:T(8,128)(2,1)S(1)} %get-tuple-element.137), channel_id=1, source_target_pairs={{0,8},{8,16},{16,24},{24,28},{28,20},{20,12},{12,4},{4,0},{1,9},{9... | collective-permute-start | bytes 516104 | tf_op jit(solution)/shard_map/ppermute | solution.py:710
  171.5 5.4 %collective-permute-start.27 = (bf16[96,896]{1,0:T(8,128)(2,1)S(1)}, bf16[96,896]{1,0:T(8,128)(2,1)S(1)}, u32[]{:S(2)}, u32[]{:S(2)}) collective-permute-start(bf16[96,896]{1,0:T(8,128)(2,1)S(1)} %get-tuple-element.138), channel_id=1, source_target_pairs={{8,0},{16,8},{24,16},{28,24},{20,28},{12,20},{4,12},{0,4},{9,1},{1... | collective-permute-start | bytes 516104 | tf_op jit(solution)/shard_map/ppermute | solution.py:711
  177.5 4.5 %collective-permute-start.28 = (f32[56,896]{1,0:T(8,128)S(1)}, f32[56,896]{1,0:T(8,128)S(1)}, u32[]{:S(2)}, u32[]{:S(2)}) collective-permute-start(f32[56,896]{1,0:T(8,128)S(1)} %get-tuple-element.142), channel_id=1, source_target_pairs={{0,2},{2,0},{1,3},{3,1},{4,6},{6,4},{5,7},{7,5},{8,10},{10,8},{9,1... | collective-permute-start | bytes 602120 | tf_op jit(solution)/shard_map/ppermute | solution.py:645
  177.6 3.9 %collective-permute-start.29 = (f32[48,128]{1,0:T(8,128)S(1)}, f32[48,128]{1,0:T(8,128)S(1)}, u32[]{:S(2)}, u32[]{:S(2)}) collective-permute-start(f32[48,128]{1,0:T(8,128)S(1)} %get-tuple-element.144), channel_id=1, source_target_pairs={{0,1},{1,0},{2,3},{3,2},{4,5},{5,4},{6,7},{7,6},{8,9},{9,8},{10,11... | collective-permute-start | bytes 73736 | tf_op jit(solution)/shard_map/ppermute | solution.py:645
  178.7 3.3 %collective-permute-start.30 = (f32[48,128]{1,0:T(8,128)S(1)}, f32[48,128]{1,0:T(8,128)S(1)}, u32[]{:S(2)}, u32[]{:S(2)}) collective-permute-start(f32[48,128]{1,0:T(8,128)S(1)} %get-tuple-element.145), channel_id=1, source_target_pairs={{0,3},{1,2},{2,1},{3,0},{4,7},{5,6},{6,5},{7,4},{8,11},{9,10},{10,... | collective-permute-start | bytes 73736 | tf_op jit(solution)/shard_map/ppermute | solution.py:1052
